TPU v7x, 256 devices: a whole 4x4x8 slice. The times are simulated.
256 devices in a mesh: row: 32 (over z, x), col: 8 (over y, core).
Axes of the slice: x: 4, y: 4, z: 8, core: 2. Of those that a mesh axis runs over, the one named last changes fastest.
Arguments:
- noise: bfloat16 [8192, 4096], P('row', 'col'), may hold values from -6 to 6
- data: bfloat16 [8192, 4096], P('col', 'row'), may hold values from -6 to 6
Outputs:
- potential_noise: float32 [8192], P('row')
- potential_data: float32 [8192], P('col')
- velocity: bfloat16 [8192, 4096], P('row', 'col')
All inputs are finite; a program needn't handle non-finite values.
Results may differ from a plain program's by a relative error of at most 0.0075.
Values may be sent and summed in bfloat16 or wider, within the bound.
No kernel may reach another device: no remote copies, remote signals or barrier semaphores. Data moves between devices by JAX's collectives and lax.ppermute only.
A program may use at most 64 MiB of HBM per device.

v0:
```python
import jax
import jax.numpy as jnp
from jax import lax
from jax.sharding import PartitionSpec as P

ITERS = 3


eps_scale = 0.01


def noise_lse(scores):
    local_peak = jnp.max(scores, axis=1)
    peak = lax.pmax(local_peak, "col")
    total = lax.psum(jnp.sum(jnp.exp(scores - peak[:, None]), axis=1), "col")
    return peak + jnp.log(total)


def data_lse(scores):
    local_peak = jnp.max(scores, axis=0)
    peak = lax.pmax(local_peak, "row")
    total = lax.psum(jnp.sum(jnp.exp(scores - peak[None, :]), axis=0), "row")
    return peak + jnp.log(total)


def body(noise, data):
    data_full = lax.all_gather(data, "row", axis=1, tiled=True)
    wide = data_full.astype(jnp.float32)
    sq_data = jnp.sum(wide * wide, axis=1)
    rows = noise.shape[0]
    count = data_full.shape[0]
    width = data_full.shape[1]
    piece = lax.all_gather(noise, "col", axis=1, tiled=True)
    gram = lax.dot_general(
        piece, data_full, (((1,), (1,)), ((), ())), preferred_element_type=jnp.float32
    )
    flat = piece.astype(jnp.float32)
    gram, sq_noise = (gram, jnp.sum(flat * flat, axis=1))
    cost = (sq_noise[:, None] + sq_data[None, :] - 2.0 * gram) / width
    noise_total = rows * lax.axis_size("row")
    data_total = count * lax.axis_size("col")
    pot_f = jnp.zeros((rows,), jnp.float32)
    pot_g = jnp.zeros((count,), jnp.float32)
    for step in range(ITERS):
        pot_f = -eps_scale * jnp.log(jnp.float32(noise_total)) - eps_scale * noise_lse(
            (pot_g[None, :] - cost) / eps_scale
        )
        pot_g = -eps_scale * jnp.log(jnp.float32(data_total)) - eps_scale * data_lse(
            (pot_f[:, None] - cost) / eps_scale
        )
    weights = (noise_total * jnp.exp((pot_f[:, None] + pot_g[None, :] - cost) / eps_scale)).astype(
        jnp.bfloat16
    )
    share = noise.shape[1]
    partial_sum = jnp.dot(weights, data_full, preferred_element_type=jnp.float32)
    whole = lax.psum(partial_sum.astype(jnp.bfloat16), "col").astype(jnp.float32)
    target = lax.dynamic_slice_in_dim(whole, lax.axis_index("col") * share, share, 1)
    velocity = (target - noise.astype(jnp.float32)).astype(jnp.bfloat16)
    return (pot_f, pot_g, velocity)


def solution(mesh):
    in_specs = (P("row", "col"), P("col", "row"))
    out_specs = (P("row"), P("col"), P("row", "col"))
    return jax.shard_map(body, mesh=mesh, in_specs=in_specs, out_specs=out_specs, check_vma=False)
```

profile of v0, /device:TPU:1, one launch (start us, length us, event | category | flops | bytes accessed | tf_op | source)
XLA Modules:
  0.0 738.5 jit_solution(4635166947434853166)
XLA Ops:
  7.2 0.7 all-gather.3.cloned.1.call-update
  7.9 0.7 all-gather.5.cloned.1.call-update
  8.7 33.1 %all-gather.3.cloned.1.call-done = bf16[256,4096]{1,0:T(8,128)(2,1)} async-done(((bf16[256,512]{1,0:T(8,128)(2,1)}), bf16[256,4096]{1,0:T(8,128)(2,1)}) %all-gather.3.cloned.1.call-update) | async-done | bytes 2097168 | tf_op jit(solution)/shard_map/all_gather | solution.py:33
  41.8 2.2 multiply_reduce_fusion.1
  44.1 101.3 %all-gather.5.cloned.1.call-done = bf16[1024,4096]{1,0:T(8,128)(2,1)} async-done(((bf16[1024,128]{1,0:T(8,128)(2,1)}), bf16[1024,4096]{1,0:T(8,128)(2,1)}) %all-gather.5.cloned.1.call-update) | async-done | bytes 8388624 | tf_op jit(solution)/shard_map/all_gather | solution.py:27
  145.4 5.2 multiply_reduce_fusion
  150.6 0.5 copy-done
  151.2 2.9 fusion.2
  154.0 14.9 %pmax.42 = f32[256]{0:T(256)S(1)} all-reduce(f32[256]{0:T(256)S(1)} %get-tuple-element.3), channel_id=1, replica_groups=mesh['row'=32,'col'=8] {'col'}, use_global_device_ids=true, to_apply=%region_3.0 | all-reduce | flops 256 | bytes 2048 | tf_op jit(solution)/shard_map/pmax | solution.py:14
  169.3 12.4 %psum.49 = f32[256]{0:T(256)S(1)} all-reduce(f32[256]{0:T(256)S(1)} %exponential_reduce_fusion.5), channel_id=1, replica_groups=mesh['row'=32,'col'=8] {'col'}, use_global_device_ids=true, to_apply=%region_5.0 | all-reduce | flops 256 | bytes 2048 | tf_op jit(solution)/shard_map/psum | solution.py:15
  181.9 58.9 %pmax.43 = f32[1024]{0:T(1024)S(1)} all-reduce(f32[1024]{0:T(1024)S(1)} %fusion.3), channel_id=1, replica_groups=mesh['row'=32,'col'=8] {'row'}, use_global_device_ids=true, to_apply=%region_7.0 | all-reduce | flops 1024 | bytes 8192 | tf_op jit(solution)/shard_map/pmax | solution.py:21
  241.1 55.9 %psum.50 = f32[1024]{0:T(1024)S(1)} all-reduce(f32[1024]{0:T(1024)S(1)} %exponential_reduce_fusion.4), channel_id=1, replica_groups=mesh['row'=32,'col'=8] {'row'}, use_global_device_ids=true, to_apply=%region_9.0 | all-reduce | flops 1024 | bytes 8192 | tf_op jit(solution)/shard_map/psum | solution.py:22
  297.2 40.2 %pmax.44 = f32[256]{0:T(256)S(1)} all-reduce(f32[256]{0:T(256)S(1)} %fusion.4), channel_id=1, replica_groups=mesh['row'=32,'col'=8] {'col'}, use_global_device_ids=true, to_apply=%region_11.0 | all-reduce | flops 256 | bytes 2048 | tf_op jit(solution)/shard_map/pmax | solution.py:14
  337.7 12.4 %psum.51 = f32[256]{0:T(256)S(1)} all-reduce(f32[256]{0:T(256)S(1)} %exponential_reduce_fusion.3), channel_id=1, replica_groups=mesh['row'=32,'col'=8] {'col'}, use_global_device_ids=true, to_apply=%region_13.0 | all-reduce | flops 256 | bytes 2048 | tf_op jit(solution)/shard_map/psum | solution.py:15
  350.3 57.4 %pmax.45 = f32[1024]{0:T(1024)S(1)} all-reduce(f32[1024]{0:T(1024)S(1)} %fusion.5), channel_id=1, replica_groups=mesh['row'=32,'col'=8] {'row'}, use_global_device_ids=true, to_apply=%region_15.0 | all-reduce | flops 1024 | bytes 8192 | tf_op jit(solution)/shard_map/pmax | solution.py:21
  408.1 56.1 %psum.52 = f32[1024]{0:T(1024)S(1)} all-reduce(f32[1024]{0:T(1024)S(1)} %exponential_reduce_fusion.2), channel_id=1, replica_groups=mesh['row'=32,'col'=8] {'row'}, use_global_device_ids=true, to_apply=%region_17.0 | all-reduce | flops 1024 | bytes 8192 | tf_op jit(solution)/shard_map/psum | solution.py:22
  464.4 40.2 %pmax.46 = f32[256]{0:T(256)S(1)} all-reduce(f32[256]{0:T(256)S(1)} %fusion.6), channel_id=1, replica_groups=mesh['row'=32,'col'=8] {'col'}, use_global_device_ids=true, to_apply=%region_19.0 | all-reduce | flops 256 | bytes 2048 | tf_op jit(solution)/shard_map/pmax | solution.py:14
  504.6 0.3 exponential_reduce_fusion.1
  504.9 12.4 %psum.53 = f32[256]{0:T(256)S(1)} all-reduce(f32[256]{0:T(256)S(1)} %exponential_reduce_fusion.1), channel_id=1, replica_groups=mesh['row'=32,'col'=8] {'col'}, use_global_device_ids=true, to_apply=%region_21.0 | all-reduce | flops 256 | bytes 2048 | tf_op jit(solution)/shard_map/psum | solution.py:15
  517.5 57.4 %pmax.47 = f32[1024]{0:T(1024)S(1)} all-reduce(f32[1024]{0:T(1024)S(1)} %fusion.7), channel_id=1, replica_groups=mesh['row'=32,'col'=8] {'row'}, use_global_device_ids=true, to_apply=%region_23.0 | all-reduce | flops 1024 | bytes 8192 | tf_op jit(solution)/shard_map/pmax | solution.py:21
  575.2 56.1 %psum.54 = f32[1024]{0:T(1024)S(1)} all-reduce(f32[1024]{0:T(1024)S(1)} %exponential_reduce_fusion), channel_id=1, replica_groups=mesh['row'=32,'col'=8] {'row'}, use_global_device_ids=true, to_apply=%region_25.0 | all-reduce | flops 1024 | bytes 8192 | tf_op jit(solution)/shard_map/psum | solution.py:22
  631.3 7.3 convolution_convert_fusion
  638.7 91.5 %all-reduce.2.cloned.1.call-done = bf16[256,4096]{1,0:T(8,128)(2,1)} async-done(((bf16[256,4096]{1,0:T(8,128)(2,1)}), bf16[256,4096]{1,0:T(8,128)(2,1)}) %all-reduce.2.cloned.1.call-update) | async-done | bytes 2097168 | tf_op jit(solution)/shard_map/psum | solution.py:56
  730.2 1.7 subtract_convert_fusion
  (29 shorter events, 2.7 us)
Async XLA Ops:
  7.2 34.7 %all-gather.3.cloned.1.call-start = ((), (), s32[]{:S(2)}) async-start(), calls=%async_computation | async-start | bytes 2359296 | tf_op jit(solution)/shard_map/all_gather | solution.py:33
  7.9 137.5 %all-gather.5.cloned.1.call-start = ((), (), s32[]{:S(2)}) async-start(), calls=%async_computation.1 | async-start | bytes 8650752 | tf_op jit(solution)/shard_map/all_gather | solution.py:27
  8.6 721.6 %all-reduce.2.cloned.1.call-start = ((), (), s32[]{:S(2)}) async-start(), calls=%async_computation.2 | async-start | bytes 4194304 | tf_op jit(solution)/shard_map/psum | solution.py:56
  41.8 108.8 %copy-start.1 = (bf16[256,4096]{1,0:T(8,128)(2,1)S(1)}, bf16[256,4096]{1,0:T(8,128)(2,1)}, u32[]{:S(2)}) copy-start(bf16[256,4096]{1,0:T(8,128)(2,1)} %all-gather.3.cloned.1.call-done) | copy-start | bytes 6291460
  145.4 5.8 copy-start
  517.3 121.3 %copy-start.3 = (f32[256]{0:T(256)}, f32[256]{0:T(256)S(1)}, u32[]{:S(2)}) copy-start(f32[256]{0:T(256)S(1)} %multiply_subtract_fusion.3) | copy-start | bytes 3076
  631.3 7.3 copy-start.4
  631.3 98.9 %copy-start.2 = (bf16[256,512]{1,0:T(8,128)(2,1)S(1)}, bf16[256,512]{1,0:T(8,128)(2,1)}, u32[]{:S(2)}) copy-start(bf16[256,512]{1,0:T(8,128)(2,1)} %param.2) | copy-start | bytes 786436
Sparse Core Ops, SparseCore 0:
  9.8 31.9 all-gather.2
  44.3 101.0 all-gather.4
  638.8 91.3 all-reduce.1
where the time goes:
time: 740 us; the launch traced here: 738 us
  blocking collectives  474 us (64%)
  waiting for transfers between devices  227 us (31%)
  between operations  13.8 us (2%)
  other arithmetic  12 us (2%)
  matrix products  10.2 us (1%)
    pmax x3, blocking collectives, data_lse(): peak = lax.pmax(local_peak, 'row')  174 us
    psum x3, blocking collectives, data_lse(): total = lax.psum(jnp.sum(jnp.exp(scores - peak[None, :]), axis=0), 'row')  168 us
    all_gather x1, waiting for transfers between devices, body(): data_full = lax.all_gather(data, 'row', axis=1, tiled=True)  101 us
    pmax x3, blocking collectives, noise_lse(): peak = lax.pmax(local_peak, 'col')  95.3 us
    psum x1, waiting for transfers between devices, body(): lax.psum(partial_sum.astype(jnp.bfloat16), 'col').astype(jnp.float32)  91.5 us
    psum x3, blocking collectives, noise_lse(): total = lax.psum(jnp.sum(jnp.exp(scores - peak[:, None]), axis=1), 'col')  37.3 us
    all_gather x1, waiting for transfers between devices, body(): piece = lax.all_gather(noise, 'col', axis=1, tiled=True)  33.1 us
  transfers between devices with their start and end apart: 3, of which 3 were waited for; matrix products, arithmetic and copies ran while one was open for 0% of the time, Pallas kernels for 0%

commit v1 on v0

v1 whole, which is shorter than its diff:
```python
import jax
import jax.numpy as jnp
from jax import lax
from jax.sharding import Mesh, PartitionSpec as P

ITERS = 3
EPS = 0.01


def shift(x, axis, by):
    n = lax.axis_size(axis)
    return lax.ppermute(x, axis, [(j, (j + by) % n) for j in range(n)])


def merge(parts):
    top = parts[0]
    for part in parts[1:]:
        top = jnp.maximum(top, part)
    total = sum(jnp.exp(part - top) for part in parts)
    return top + jnp.log(total)


def merge_along(lse, axis):
    return merge([lse] + [shift(lse, axis, by) for by in range(1, lax.axis_size(axis))])


def local_lse(scores, axis):
    peak = jnp.max(scores, axis=axis, keepdims=True)
    total = jnp.sum(jnp.exp(scores - peak), axis=axis)
    return jnp.squeeze(peak, axis) + jnp.log(total)


def noise_lse(scores):
    return merge_along(merge_along(local_lse(scores, 1), "core"), "y")


def data_lse(scores):
    mine = local_lse(scores, 0)
    n = lax.axis_size("z") * lax.axis_size("x")
    parts = lax.all_to_all(jnp.broadcast_to(mine[None], (n, mine.shape[0])), ("z", "x"), 0, 0)
    top = jnp.max(parts, axis=0)
    return top + jnp.log(jnp.sum(jnp.exp(parts - top[None]), axis=0))


def body(noise, data):
    width = noise.shape[1] * 8
    data_full = lax.all_gather(data, ("z", "x"), axis=1, tiled=True)
    noise_full = lax.all_gather(noise, ("y", "core"), axis=1, tiled=True)
    wide = data_full.astype(jnp.float32)
    flat = noise_full.astype(jnp.float32)
    sq_data = jnp.sum(wide * wide, axis=1)
    sq_noise = jnp.sum(flat * flat, axis=1)
    gram = lax.dot_general(
        noise_full, data_full, (((1,), (1,)), ((), ())), preferred_element_type=jnp.float32
    )
    cost = (sq_noise[:, None] + sq_data[None, :] - 2.0 * gram) / width
    noise_total = noise.shape[0] * 32
    data_total = data.shape[0] * 8
    pot_g = jnp.zeros((data.shape[0],), jnp.float32)
    for _ in range(ITERS):
        pot_f = -EPS * jnp.log(jnp.float32(noise_total)) - EPS * noise_lse((pot_g[None, :] - cost) / EPS)
        pot_g = -EPS * jnp.log(jnp.float32(data_total)) - EPS * data_lse((pot_f[:, None] - cost) / EPS)
    weights = (noise_total * jnp.exp((pot_f[:, None] + pot_g[None, :] - cost) / EPS)).astype(jnp.bfloat16)
    partial = jnp.dot(weights, data_full, preferred_element_type=jnp.float32)
    rows, share = noise.shape
    partial = partial.reshape(rows, 4, 2, share)
    core = lax.axis_index("core")
    keep = lax.dynamic_index_in_dim(partial, core, 2, keepdims=False)
    give = lax.dynamic_index_in_dim(partial, 1 - core, 2, keepdims=False).astype(jnp.bfloat16)
    pair = keep + shift(give, "core", 1).astype(jnp.float32)
    y = lax.axis_index("y")
    target = lax.dynamic_index_in_dim(pair, y, 1, keepdims=False)
    for by in range(1, 4):
        part = lax.dynamic_index_in_dim(pair, lax.rem(y + by, 4), 1, keepdims=False)
        target = target + shift(part.astype(jnp.bfloat16), "y", by).astype(jnp.float32)
    velocity = (target - noise.astype(jnp.float32)).astype(jnp.bfloat16)
    return pot_f, pot_g, velocity


def solution(mesh):
    fine = Mesh(mesh.devices.reshape(8, 4, 4, 2), ("z", "x", "y", "core"))
    row, col = ("z", "x"), ("y", "core")
    return jax.shard_map(
        body,
        mesh=fine,
        in_specs=(P(row, col), P(col, row)),
        out_specs=(P(row), P(col), P(row, col)),
        check_vma=False,
    )
```

time: 740 us -> 282 us (0.38)
  blocking collectives: 474 us -> 27.3 us
  waiting for transfers between devices: 227 us -> 167 us
  starting transfers between devices: 0.11 us -> 31.7 us
  local copies, waits for them, and re-layouts: 0.56 us -> 17.4 us
    pmax x6 -> x0, blocking collectives: 269 us -> none  [the longest x3 174 us: data_lse(): peak = lax.pmax(local_peak, 'row')]
    psum x6 -> x0, blocking collectives: 205 us -> none  [the longest x3 168 us: data_lse(): total = lax.psum(jnp.sum(jnp.exp(scores - peak[None, :]), axis=0), 'row')]
    psum x1 -> x0, waiting for transfers between devices: 91.5 us -> none  [body(): lax.psum(partial_sum.astype(jnp.bfloat16), 'col').astype(jnp.float32)]
    ppermute x0 -> x16, starting transfers between devices: none -> 27.7 us  [shift(): return lax.ppermute(x, axis, [(j, (j + by) % n) for j in range(n)])]
    all_to_all x0 -> x2, blocking collectives: none -> 27.3 us  [data_lse(): lax.all_to_all(jnp.broadcast_to(mine[None], (n, mine.shape[0])), ('z', 'x...]
    ppermute x0 -> x16, waiting for transfers between devices: none -> 21.8 us  [shift(): return lax.ppermute(x, axis, [(j, (j + by) % n) for j in range(n)])]
    all_to_all x0 -> x1, waiting for transfers between devices: none -> 9.4 us  [data_lse(): lax.all_to_all(jnp.broadcast_to(mine[None], (n, mine.shape[0])), ('z', 'x...]
    dynamic_slice x0 -> x2, local copies, waits for them, and re-layouts: none -> 8.68 us  [the longest x1 4.35 us: body(): keep = lax.dynamic_index_in_dim(partial, core, 2, keepdims=False)]
  transfers between devices with their start and end apart: 3 -> 19, of which waited for: 3 -> 16; matrix products, arithmetic and copies ran while one was open for 0% -> 2% of each run, Pallas kernels for 0% -> 0%
where the time goes in v1:
time: 282 us
  waiting for transfers between devices  167 us (59%)
  starting transfers between devices  31.7 us (11%)
  blocking collectives  27.3 us (10%)
  local copies, waits for them, and re-layouts  17.4 us (6%)
  between operations  14.3 us (5%)
  other arithmetic  13.4 us (5%)
  matrix products  10.7 us (4%)
    all_gather x1, waiting for transfers between devices, body(): data_full = lax.all_gather(data, ('z', 'x'), axis=1, tiled=True)  101 us
    all_gather x1, waiting for transfers between devices, body(): noise_full = lax.all_gather(noise, ('y', 'core'), axis=1, tiled=True)  33.2 us
    ppermute x16, starting transfers between devices, shift(): return lax.ppermute(x, axis, [(j, (j + by) % n) for j in range(n)])  27.7 us
    all_to_all x2, blocking collectives, data_lse(): lax.all_to_all(jnp.broadcast_to(mine[None], (n, mine.shape[0])), ('z', 'x...  27.3 us
    ppermute x16, waiting for transfers between devices, shift(): return lax.ppermute(x, axis, [(j, (j + by) % n) for j in range(n)])  21.8 us
    all_to_all x1, waiting for transfers between devices, data_lse(): lax.all_to_all(jnp.broadcast_to(mine[None], (n, mine.shape[0])), ('z', 'x...  9.4 us
    dot_general x1, matrix products, body(): partial = jnp.dot(weights, data_full, preferred_element_type=jnp.float32)  7.85 us
    reshape x1, local copies, waits for them, and re-layouts, body(): partial = partial.reshape(rows, 4, 2, share)  6.58 us
  transfers between devices with their start and end apart: 19, of which 16 were waited for; matrix products, arithmetic and copies ran while one was open for 2% of the time, Pallas kernels for 0%

profile of v1, /device:TPU:1, one launch (start us, length us, event | category | flops | bytes accessed | tf_op | source)
XLA Modules:
  0.0 281.9 jit_solution(13511681515554797688)
XLA Ops:
  8.6 33.2 %all-gather.3.cloned.1.call-done = bf16[256,4096]{1,0:T(8,128)(2,1)} async-done(((bf16[256,512]{1,0:T(8,128)(2,1)}), bf16[256,4096]{1,0:T(8,128)(2,1)}) %all-gather.3.cloned.1.call-update) | async-done | bytes 2097168 | tf_op jit(solution)/shard_map/all_gather | solution.py:48
  41.8 2.2 multiply_reduce_fusion.1
  44.1 101.3 %all-gather.5.cloned.1.call-done = bf16[1024,4096]{1,0:T(8,128)(2,1)} async-done(((bf16[1024,128]{1,0:T(8,128)(2,1)}), bf16[1024,4096]{1,0:T(8,128)(2,1)}) %all-gather.5.cloned.1.call-update) | async-done | bytes 8388624 | tf_op jit(solution)/shard_map/all_gather | solution.py:47
  145.4 5.2 %multiply_reduce_fusion = f32[1024]{0:T(1024)S(1)} fusion(bf16[1024,4096]{1,0:T(8,128)(2,1)} %all-gather.5.cloned.1.call-done), kind=kLoop, calls=%fused_computation | loop fusion | flops 12581888 | bytes 8392704 | tf_op jit(solution)/shard_map/reduce_sum | solution.py:51
  151.2 2.9 %fusion.3 = (f32[256]{0:T(256)S(1)}, f32[256,1024]{1,0:T(8,128)S(1)}) fusion(bf16[256,4096]{1,0:T(8,128)(2,1)S(1)} %copy-done.1, bf16[1024,4096]{1,0:T(8,128)(2,1)S(1)} %copy-done, f32[1024]{0:T(1024)S(1)} %multiply_reduce_fusion, f32[256]{0:T(256)S(1)} %multiply_reduce_fusion.1), kind=kOutput, calls=%fused_computation.21 | convolution fusion | flops 2149318400 | bytes 11540480 | tf_op jit(solution)/shard_map/dot_general | solution.py:53
  154.4 3.2 %collective-permute-start = (f32[256]{0:T(256)S(1)}, f32[256]{0:T(256)S(1)}, u32[]{:S(2)}, u32[]{:S(2)}) collective-permute-start(f32[256]{0:T(256)S(1)} %log_add_fusion.8), channel_id=1, source_target_pairs={{0,1},{1,0},{2,3},{3,2},{4,5},{5,4},{6,7},{7,6},{8,9},{9,8},{10,11... | collective-permute-start | bytes 3080 | tf_op jit(solution)/shard_map/ppermute | solution.py:12
  159.7 2.4 collective-permute-start.2
  165.4 15.0 %all_to_all.27 = f32[32,1,1024]{2,1,0:T(1,128)S(1)} all-to-all(f32[32,1,1024]{2,1,0:T(1,128)S(1)} %broadcast_in_dim.6), channel_id=1, replica_groups=mesh['z'=8,'x'=4,'y'=4,'core'=2] {'z','x'}, dimensions={0} | all-to-all | bytes 262144 | tf_op jit(solution)/shard_map/all_to_all | solution.py:40
  181.2 3.4 %collective-permute-start.4 = (f32[256]{0:T(256)S(1)}, f32[256]{0:T(256)S(1)}, u32[]{:S(2)}, u32[]{:S(2)}) collective-permute-start(f32[256]{0:T(256)S(1)} %log_add_fusion.6), channel_id=1, source_target_pairs={{0,1},{1,0},{2,3},{3,2},{4,5},{5,4},{6,7},{7,6},{8,9},{9,8},{10,11... | collective-permute-start | bytes 3080 | tf_op jit(solution)/shard_map/ppermute | solution.py:12
  185.5 3.5 %collective-permute-start.6 = (f32[256]{0:T(256)S(1)}, f32[256]{0:T(256)S(1)}, u32[]{:S(2)}, u32[]{:S(2)}) collective-permute-start(f32[256]{0:T(256)S(1)} %log_add_fusion.5), channel_id=1, source_target_pairs={{0,4},{2,6},{4,0},{6,2},{1,5},{3,7},{5,1},{7,3},{8,12},{10,14},{12... | collective-permute-start | bytes 3080 | tf_op jit(solution)/shard_map/ppermute | solution.py:12
  189.9 1.5 collective-permute-done.7
  192.0 12.3 %all_to_all.28 = f32[32,1,1024]{2,1,0:T(1,128)S(1)} all-to-all(f32[32,1,1024]{2,1,0:T(1,128)S(1)} %broadcast_in_dim.7), channel_id=1, replica_groups=mesh['z'=8,'x'=4,'y'=4,'core'=2] {'z','x'}, dimensions={0} | all-to-all | bytes 262144 | tf_op jit(solution)/shard_map/all_to_all | solution.py:40
  205.0 3.6 %collective-permute-start.8 = (f32[256]{0:T(256)S(1)}, f32[256]{0:T(256)S(1)}, u32[]{:S(2)}, u32[]{:S(2)}) collective-permute-start(f32[256]{0:T(256)S(1)} %log_add_fusion.4), channel_id=1, source_target_pairs={{0,1},{1,0},{2,3},{3,2},{4,5},{5,4},{6,7},{7,6},{8,9},{9,8},{10,11... | collective-permute-start | bytes 3080 | tf_op jit(solution)/shard_map/ppermute | solution.py:12
  213.5 1.7 collective-permute-done.9
  216.5 3.9 %all-to-all-start.2 = ((f32[32,1,1024]{2,1,0:T(1,128)}), f32[32,1,1024]{2,1,0:T(1,128)S(1)}, u32[]{:S(2)}, u32[]{:S(2)}) async-start(f32[32,1,1024]{2,1,0:T(1,128)} %broadcast_in_dim.8), calls=%async_computation.2 | async-start | bytes 262144 | tf_op jit(solution)/shard_map/all_to_all | solution.py:40
  220.3 9.4 %all-to-all-done.2 = f32[32,1,1024]{2,1,0:T(1,128)S(1)} async-done(((f32[32,1,1024]{2,1,0:T(1,128)}), f32[32,1,1024]{2,1,0:T(1,128)S(1)}, u32[]{:S(2)}, u32[]{:S(2)}) %all-to-all-start.2) | async-done | bytes 131104 | tf_op jit(solution)/shard_map/all_to_all | solution.py:40
  229.9 7.9 %fusion.9 = f32[256,4096]{1,0:T(8,128)} fusion(bf16[1024,4096]{1,0:T(8,128)(2,1)} %all-gather.5.cloned.1.call-done, f32[256,1024]{1,0:T(8,128)S(1)} %get-tuple-element.7, f32[1024]{0:T(1024)S(1)} %multiply_subtract_fusion, f32[256]{0:T(256)S(1)} %multiply_subtract_fusion.3), kind=kOutput, calls=%fused_computation.27 | convolution fusion | flops 2148794368 | bytes 13636608 | tf_op jit(solution)/shard_map/dot_general | solution.py:64
  237.8 6.6 %reshape.87 = f32[256,4,2,512]{3,2,1,0:T(2,128)} reshape(f32[256,4096]{1,0:T(8,128)} %fusion.9) | data formatting | bytes 8388608 | tf_op jit(solution)/shard_map/reshape | solution.py:66
  244.3 4.3 %constant_dynamic-slice_fusion = bf16[256,4,1,512]{3,2,1,0:T(2,128)(2,1)S(1)} fusion(f32[256,4,2,512]{3,2,1,0:T(2,128)} %reshape.87, s32[]{:T(128)S(6)} %select_n.21), kind=kLoop, calls=%fused_computation.58 | loop fusion | bytes 2097156 | tf_op jit(solution)/shard_map/jit(dynamic_index_in_dim)/dynamic_slice | solution.py:69
  249.3 3.5 %collective-permute-start.12 = (bf16[256,4,512]{2,0,1:T(8,128)(2,1)S(1)}, bf16[256,4,512]{2,0,1:T(8,128)(2,1)S(1)}, u32[]{:S(2)}, u32[]{:S(2)}) collective-permute-start(bf16[256,4,512]{2,0,1:T(8,128)(2,1)S(1)} %bitcast.42), channel_id=1, source_target_pairs={{0,1},{1,0},{2,3},{3,2},{4,5},{5,4},{6,7},{7,6},{8,9},{9,8},{10,11... | collective-permute-start | bytes 3145736 | tf_op jit(solution)/shard_map/ppermute | solution.py:12
  252.7 4.3 %constant_dynamic-slice_fusion.1 = f32[256,4,1,512]{3,2,1,0:T(1,128)S(1)} fusion(f32[256,4,2,512]{3,2,1,0:T(2,128)} %reshape.87, s32[]{:T(128)S(6)} %select_n.20), kind=kLoop, calls=%fused_computation.59 | loop fusion | bytes 4194308 | tf_op jit(solution)/shard_map/jit(dynamic_index_in_dim)/dynamic_slice | solution.py:68
  259.0 1.6 collective-permute-start.15
  260.7 12.0 %collective-permute-done.13 = bf16[256,512]{1,0:T(8,128)(2,1)S(1)} collective-permute-done((bf16[256,512]{1,0:T(8,128)(2,1)S(1)}, bf16[256,512]{1,0:T(8,128)(2,1)S(1)}, u32[]{:S(2)}, u32[]{:S(2)}) %collective-permute-start.13) | collective-permute-done | bytes 262176 | tf_op jit(solution)/shard_map/ppermute | solution.py:12
  273.1 1.9 fusion.13
  (74 shorter events, 20.8 us)
Async XLA Ops:
  7.2 34.7 %all-gather.3.cloned.1.call-start = ((), (), s32[]{:S(2)}) async-start(), calls=%async_computation.3 | async-start | bytes 2359296 | tf_op jit(solution)/shard_map/all_gather | solution.py:48
  7.9 137.5 %all-gather.5.cloned.1.call-start = ((), (), s32[]{:S(2)}) async-start(), calls=%async_computation.4 | async-start | bytes 8650752 | tf_op jit(solution)/shard_map/all_gather | solution.py:47
  41.8 108.8 %copy-start.1 = (bf16[256,4096]{1,0:T(8,128)(2,1)S(1)}, bf16[256,4096]{1,0:T(8,128)(2,1)}, u32[]{:S(2)}) copy-start(bf16[256,4096]{1,0:T(8,128)(2,1)} %all-gather.3.cloned.1.call-done) | copy-start | bytes 6291460
  145.4 5.8 %copy-start = (bf16[1024,4096]{1,0:T(8,128)(2,1)S(1)}, bf16[1024,4096]{1,0:T(8,128)(2,1)}, u32[]{:S(2)}) copy-start(bf16[1024,4096]{1,0:T(8,128)(2,1)} %all-gather.5.cloned.1.call-done) | copy-start | bytes 25165828
  154.4 4.0 %collective-permute-start = (f32[256]{0:T(256)S(1)}, f32[256]{0:T(256)S(1)}, u32[]{:S(2)}, u32[]{:S(2)}) collective-permute-start(f32[256]{0:T(256)S(1)} %log_add_fusion.8), channel_id=1, source_target_pairs={{0,1},{1,0},{2,3},{3,2},{4,5},{5,4},{6,7},{7,6},{8,9},{9,8},{10,11... | collective-permute-start | bytes 3080 | tf_op jit(solution)/shard_map/ppermute | solution.py:12
  158.4 4.9 %collective-permute-start.1 = (f32[256]{0:T(256)S(1)}, f32[256]{0:T(256)S(1)}, u32[]{:S(2)}, u32[]{:S(2)}) collective-permute-start(f32[256]{0:T(256)S(1)} %log_add_fusion.7), channel_id=1, source_target_pairs={{0,2},{2,4},{4,6},{6,0},{1,3},{3,5},{5,7},{7,1},{8,10},{10,12},{12... | collective-permute-start | bytes 3080 | tf_op jit(solution)/shard_map/ppermute | solution.py:12
  159.7 3.9 %collective-permute-start.2 = (f32[256]{0:T(256)S(1)}, f32[256]{0:T(256)S(1)}, u32[]{:S(2)}, u32[]{:S(2)}) collective-permute-start(f32[256]{0:T(256)S(1)} %log_add_fusion.7), channel_id=1, source_target_pairs={{0,4},{2,6},{4,0},{6,2},{1,5},{3,7},{5,1},{7,3},{8,12},{10,14},{12... | collective-permute-start | bytes 3080 | tf_op jit(solution)/shard_map/ppermute | solution.py:12
  162.1 2.7 collective-permute-start.3
  181.2 4.2 %collective-permute-start.4 = (f32[256]{0:T(256)S(1)}, f32[256]{0:T(256)S(1)}, u32[]{:S(2)}, u32[]{:S(2)}) collective-permute-start(f32[256]{0:T(256)S(1)} %log_add_fusion.6), channel_id=1, source_target_pairs={{0,1},{1,0},{2,3},{3,2},{4,5},{5,4},{6,7},{7,6},{8,9},{9,8},{10,11... | collective-permute-start | bytes 3080 | tf_op jit(solution)/shard_map/ppermute | solution.py:12
  185.4 3.7 %collective-permute-start.5 = (f32[256]{0:T(256)S(1)}, f32[256]{0:T(256)S(1)}, u32[]{:S(2)}, u32[]{:S(2)}) collective-permute-start(f32[256]{0:T(256)S(1)} %log_add_fusion.5), channel_id=1, source_target_pairs={{0,2},{2,4},{4,6},{6,0},{1,3},{3,5},{5,7},{7,1},{8,10},{10,12},{12... | collective-permute-start | bytes 3080 | tf_op jit(solution)/shard_map/ppermute | solution.py:12
  185.5 4.4 %collective-permute-start.6 = (f32[256]{0:T(256)S(1)}, f32[256]{0:T(256)S(1)}, u32[]{:S(2)}, u32[]{:S(2)}) collective-permute-start(f32[256]{0:T(256)S(1)} %log_add_fusion.5), channel_id=1, source_target_pairs={{0,4},{2,6},{4,0},{6,2},{1,5},{3,7},{5,1},{7,3},{8,12},{10,14},{12... | collective-permute-start | bytes 3080 | tf_op jit(solution)/shard_map/ppermute | solution.py:12
  189.0 2.4 collective-permute-start.7
  205.0 4.4 %collective-permute-start.8 = (f32[256]{0:T(256)S(1)}, f32[256]{0:T(256)S(1)}, u32[]{:S(2)}, u32[]{:S(2)}) collective-permute-start(f32[256]{0:T(256)S(1)} %log_add_fusion.4), channel_id=1, source_target_pairs={{0,1},{1,0},{2,3},{3,2},{4,5},{5,4},{6,7},{7,6},{8,9},{9,8},{10,11... | collective-permute-start | bytes 3080 | tf_op jit(solution)/shard_map/ppermute | solution.py:12
  209.4 4.0 %collective-permute-start.10 = (f32[256]{0:T(256)S(1)}, f32[256]{0:T(256)S(1)}, u32[]{:S(2)}, u32[]{:S(2)}) collective-permute-start(f32[256]{0:T(256)S(1)} %log_add_fusion.3), channel_id=1, source_target_pairs={{0,4},{2,6},{4,0},{6,2},{1,5},{3,7},{5,1},{7,3},{8,12},{10,14},{12... | collective-permute-start | bytes 3080 | tf_op jit(solution)/shard_map/ppermute | solution.py:12
  210.8 2.7 collective-permute-start.11
  211.6 3.6 %collective-permute-start.9 = (f32[256]{0:T(256)S(1)}, f32[256]{0:T(256)S(1)}, u32[]{:S(2)}, u32[]{:S(2)}) collective-permute-start(f32[256]{0:T(256)S(1)} %log_add_fusion.3), channel_id=1, source_target_pairs={{0,2},{2,4},{4,6},{6,0},{1,3},{3,5},{5,7},{7,1},{8,10},{10,12},{12... | collective-permute-start | bytes 3080 | tf_op jit(solution)/shard_map/ppermute | solution.py:12
  215.2 22.5 %copy-start.3 = (f32[256]{0:T(256)}, f32[256]{0:T(256)S(1)}, u32[]{:S(2)}) copy-start(f32[256]{0:T(256)S(1)} %multiply_subtract_fusion.3) | copy-start | bytes 3076
  216.5 13.3 %all-to-all-start.2 = ((f32[32,1,1024]{2,1,0:T(1,128)}), f32[32,1,1024]{2,1,0:T(1,128)S(1)}, u32[]{:S(2)}, u32[]{:S(2)}) async-start(f32[32,1,1024]{2,1,0:T(1,128)} %broadcast_in_dim.8), calls=%async_computation.2 | async-start | bytes 262144 | tf_op jit(solution)/shard_map/all_to_all | solution.py:40
  229.9 7.9 %copy-start.4 = (f32[1024]{0:T(1024)}, f32[1024]{0:T(1024)S(1)}, u32[]{:S(2)}) copy-start(f32[1024]{0:T(1024)S(1)} %multiply_subtract_fusion) | copy-start | bytes 12292
  249.3 7.8 %collective-permute-start.12 = (bf16[256,4,512]{2,0,1:T(8,128)(2,1)S(1)}, bf16[256,4,512]{2,0,1:T(8,128)(2,1)S(1)}, u32[]{:S(2)}, u32[]{:S(2)}) collective-permute-start(bf16[256,4,512]{2,0,1:T(8,128)(2,1)S(1)} %bitcast.42), channel_id=1, source_target_pairs={{0,1},{1,0},{2,3},{3,2},{4,5},{5,4},{6,7},{7,6},{8,9},{9,8},{10,11... | collective-permute-start | bytes 3145736 | tf_op jit(solution)/shard_map/ppermute | solution.py:12
  257.1 16.0 %copy-start.2 = (bf16[256,512]{1,0:T(8,128)(2,1)S(1)}, bf16[256,512]{1,0:T(8,128)(2,1)}, u32[]{:S(2)}) copy-start(bf16[256,512]{1,0:T(8,128)(2,1)} %param.2) | copy-start | bytes 786436
  257.9 14.8 %collective-permute-start.13 = (bf16[256,512]{1,0:T(8,128)(2,1)S(1)}, bf16[256,512]{1,0:T(8,128)(2,1)S(1)}, u32[]{:S(2)}, u32[]{:S(2)}) collective-permute-start(bf16[256,512]{1,0:T(8,128)(2,1)S(1)} %get-tuple-element.3), channel_id=1, source_target_pairs={{0,2},{2,4},{4,6},{6,0},{1,3},{3,5},{5,7},{7,1},{8,10},{10,12},{12... | collective-permute-start | bytes 786440 | tf_op jit(solution)/shard_map/ppermute | solution.py:12
  258.0 14.7 %collective-permute-start.14 = (bf16[256,512]{1,0:T(8,128)(2,1)S(1)}, bf16[256,512]{1,0:T(8,128)(2,1)}, u32[]{:S(2)}, u32[]{:S(2)}) collective-permute-start(bf16[256,512]{1,0:T(8,128)(2,1)S(1)} %get-tuple-element.5), channel_id=1, source_target_pairs={{0,4},{2,6},{4,0},{6,2},{1,5},{3,7},{5,1},{7,3},{8,12},{10,14},{12... | collective-permute-start | bytes 786440 | tf_op jit(solution)/shard_map/ppermute | solution.py:12
  259.0 14.1 %collective-permute-start.15 = (bf16[256,512]{1,0:T(8,128)(2,1)S(1)}, bf16[256,512]{1,0:T(8,128)(2,1)}, u32[]{:S(2)}, u32[]{:S(2)}) collective-permute-start(bf16[256,512]{1,0:T(8,128)(2,1)S(1)} %get-tuple-element.4), channel_id=1, source_target_pairs={{0,6},{2,0},{4,2},{6,4},{1,7},{3,1},{5,3},{7,5},{8,14},{10,8},{12,... | collective-permute-start | bytes 786440 | tf_op jit(solution)/shard_map/ppermute | solution.py:12
Sparse Core Ops, SparseCore 0:
  9.8 31.9 all-gather.2
  44.3 101.0 all-gather.4

commit v2 on v1

v2 whole, which is shorter than its diff:
```python
import functools
import math

import jax
import jax.numpy as jnp
from jax import lax
from jax.experimental import pallas as pl
from jax.experimental.pallas import tpu as pltpu
from jax.sharding import Mesh, PartitionSpec as P

ITERS = 3
EPS = 0.01
LOG2E = math.log2(math.e)
Z, X, Y, C = 8, 4, 4, 2
ROWS, SHARE = 256, 512
COUNT, SLICE = 1024, 128
WIDTH = 4096
QUARTER = COUNT // X
TALL = ROWS * X
CHUNKS = TALL // 128
GROUP = X * Y * C
TOTAL = 8192
UNIT = LOG2E / (WIDTH * EPS)
LOG2N = math.log2(TOTAL)
F32, BF16 = jnp.float32, jnp.bfloat16
VMEM = pl.BlockSpec(memory_space=pltpu.VMEM)
SMEM = pl.BlockSpec(memory_space=pltpu.SMEM)


def shift(x, axis, by):
    n = {"z": Z, "x": X, "y": Y, "core": C}[axis]
    return lax.ppermute(x, axis, [(j, (j + by) % n) for j in range(n)])


def params(mib):
    return pltpu.CompilerParams(vmem_limit_bytes=mib * 2**20)


def ring_z(x):
    forward = backward = x
    got = [x]
    for _ in range(1, Z // 2):
        forward, backward = shift(forward, "z", 1), shift(backward, "z", -1)
        got += [forward, backward]
    cut = x.shape[0] // 2
    return got + [shift(forward[:cut], "z", 1), shift(backward[cut:], "z", -1)]


def squares(ref, pieces):
    total = None
    for view in pieces:
        part = ref[view].astype(F32)
        total = part * part if total is None else total + part * part
    return total


def assemble_kernel(place, *refs):
    ins, (out_ref, sq_ref) = refs[:-2], refs[-2:]
    z = place[0]
    plan = [(0, 0)] + [(r, 0) for s in range(1, Z // 2) for r in (-s, s)] + [(Z // 2, 0), (Z // 2, X // 2)]
    for ref, (rel, first) in zip(ins, plan, strict=True):
        piece = lax.rem(z + rel + Z, Z)
        for n in range(ref.shape[0]):
            lanes = pl.ds(pl.multiple_of(piece * SHARE + (first + n) * SLICE, SLICE), SLICE)
            out_ref[:, lanes] = ref[n]
    step = 64
    for start in range(0, QUARTER, step):
        rows = pl.ds(start, step)
        total = squares(out_ref, [(rows, pl.ds(lane, 128)) for lane in range(0, WIDTH, 128)])
        sq_ref[rows, :] = jnp.broadcast_to(jnp.sum(total, axis=1, keepdims=True), (step, 128))


def assemble(place, parts):
    return pl.pallas_call(
        assemble_kernel,
        out_shape=(jax.ShapeDtypeStruct((QUARTER, WIDTH), BF16), jax.ShapeDtypeStruct((QUARTER, 128), F32)),
        in_specs=[SMEM] + [VMEM] * len(parts),
        out_specs=(VMEM, VMEM),
        compiler_params=params(16),
        cost_estimate=pl.CostEstimate(flops=2 * QUARTER * WIDTH, bytes_accessed=4 * 2**20, transcendentals=0),
        name="assemble",
    )(place, *parts)


def lse(t, axis):
    top = jnp.max(t, axis=axis, keepdims=True)
    return top + jnp.log2(jnp.sum(jnp.exp2(t - top), axis=axis, keepdims=True))


def merged(ref):
    parts = ref[...]
    top = jnp.max(parts, axis=0)
    return top + jnp.log2(jnp.sum(jnp.exp2(parts - top[None]), axis=0))


def chunk(r):
    return pl.ds(r * 128, 128)


def score_kernel(place, data_ref, sq_ref, noise_ref, q_ref, out_ref, sqn_ref, lse_ref):
    n = pl.program_id(0)
    gram = jnp.zeros((QUARTER, ROWS), F32)
    for p in range(Y * C):
        gram = gram + lax.dot_general(
            data_ref[:, pl.ds(p * SHARE, SHARE)], noise_ref[0, p], (((1,), (1,)), ((), ())), preferred_element_type=F32
        )
    gram = gram * (2.0 * UNIT)
    q_ref[:, pl.ds(pl.multiple_of(n * ROWS, ROWS), ROWS)] = gram
    t = gram - UNIT * jnp.concatenate([sq_ref[...]] * 2, axis=1)
    rows = lse(t, 0)
    lse_ref[pl.ds(2 * n, 1), :] = rows[:, :128]
    lse_ref[pl.ds(2 * n + 1, 1), :] = rows[:, 128:]

    @pl.when(n == place[1])
    def _():
        views = [(0, p, slice(None), pl.ds(lane, 128)) for p in range(Y * C) for lane in range(0, SHARE, 128)]
        total = squares(noise_ref, views)
        sqn_ref[...] = jnp.sum(jnp.transpose(total), axis=0, keepdims=True)

    @pl.when(n == X - 1)
    def _():
        out_ref[...] = jnp.broadcast_to(lse_ref[...][None], (GROUP, CHUNKS, 128))


def score(place, data, sq, noise):
    whole = lambda n, place: (0, 0)
    return pl.pallas_call(
        score_kernel,
        grid_spec=pltpu.PrefetchScalarGridSpec(
            num_scalar_prefetch=1,
            grid=(X,),
            in_specs=[
                pl.BlockSpec((QUARTER, WIDTH), whole),
                pl.BlockSpec((QUARTER, 128), whole),
                pl.BlockSpec((1, Y * C, ROWS, SHARE), lambda n, place: (n, 0, 0, 0)),
            ],
            out_specs=(
                pl.BlockSpec((QUARTER, TALL), whole),
                pl.BlockSpec((GROUP, CHUNKS, 128), lambda n, place: (0, 0, 0)),
                pl.BlockSpec((1, ROWS), whole),
            ),
            scratch_shapes=[pltpu.VMEM((CHUNKS, 128), F32)],
        ),
        out_shape=(
            jax.ShapeDtypeStruct((QUARTER, TALL), F32),
            jax.ShapeDtypeStruct((GROUP, CHUNKS, 128), F32),
            jax.ShapeDtypeStruct((1, ROWS), F32),
        ),
        compiler_params=params(58),
        name="score",
    )(place, data, sq, noise)


def to_column(g):
    return jnp.concatenate([jnp.transpose(jnp.broadcast_to(g[r : r + 1], (128, 128))) for r in range(2)], axis=0)


def noise_kernel(q_ref, part_ref, out_ref, lse_ref, g_ref):
    g_ref[...] = to_column(-LOG2N - merged(part_ref))
    for r in range(CHUNKS):
        lse_ref[pl.ds(r, 1), :] = lse(q_ref[:, chunk(r)] + g_ref[...], 0)
    out_ref[...] = jnp.broadcast_to(lse_ref[...][None], (GROUP, CHUNKS, 128))


def noise_lse(q, parts):
    return pl.pallas_call(
        noise_kernel,
        out_shape=jax.ShapeDtypeStruct((GROUP, CHUNKS, 128), F32),
        in_specs=[VMEM] * 2,
        out_specs=VMEM,
        scratch_shapes=[pltpu.VMEM((CHUNKS, 128), F32), pltpu.VMEM((QUARTER, 128), F32)],
        compiler_params=params(16),
        name="noise_lse",
    )(q, parts)


def data_kernel(q_ref, part_ref, out_ref, f_ref, lane_ref):
    f_ref[...] = -LOG2N - merged(part_ref)
    step = 32
    for start in range(0, QUARTER, step):
        rows = pl.ds(start, step)
        t = [q_ref[rows, chunk(r)] + f_ref[pl.ds(r, 1), :] for r in range(CHUNKS)]
        top = functools.reduce(jnp.maximum, t)
        lane_ref[rows, :] = top + jnp.log2(sum(jnp.exp2(part - top) for part in t))
    row = lse(jnp.transpose(lane_ref[...]), 0)
    tile = jnp.concatenate([row[:, :128], row[:, 128:], jnp.zeros((6, 128), F32)], axis=0)
    out_ref[...] = jnp.broadcast_to(tile[None], (Z, 8, 128))


def data_lse(q, parts):
    return pl.pallas_call(
        data_kernel,
        out_shape=(jax.ShapeDtypeStruct((Z, 8, 128), F32), jax.ShapeDtypeStruct((CHUNKS, 128), F32)),
        in_specs=[VMEM] * 2,
        out_specs=(VMEM, VMEM),
        scratch_shapes=[pltpu.VMEM((QUARTER, 128), F32)],
        compiler_params=params(16),
        name="data_lse",
    )(q, parts)


def weights_kernel(q_ref, f_ref, part_ref, sq_ref, w_ref, pot_ref):
    g = -LOG2N - merged(part_ref)
    column = to_column(g) + LOG2N
    for r in range(CHUNKS):
        w = jnp.exp2((q_ref[:, chunk(r)] + f_ref[pl.ds(r, 1), :]) + column)
        w_ref[r // 2, pl.ds(r % 2 * 128, 128), :] = jnp.transpose(w).astype(BF16)
    row = jnp.concatenate([g[0:1], g[1:2]], axis=1)
    pot_ref[...] = row * (EPS / LOG2E) + jnp.transpose(sq_ref[...])[0:1, :] * (1.0 / WIDTH)


def weigh(q, f, parts, sq):
    return pl.pallas_call(
        weights_kernel,
        out_shape=(jax.ShapeDtypeStruct((X, ROWS, QUARTER), BF16), jax.ShapeDtypeStruct((1, QUARTER), F32)),
        in_specs=[VMEM] * 4,
        out_specs=(VMEM, VMEM),
        compiler_params=params(16),
        name="weights",
    )(q, f, parts, sq)


def transport_kernel(place, w_ref, data_ref, out_ref):
    total = jnp.dot(w_ref[0], data_ref[0], preferred_element_type=F32)
    for n in range(1, X):
        total = total + jnp.dot(w_ref[n], data_ref[n], preferred_element_type=F32)
    out_ref[0] = total.astype(out_ref.dtype)


def transport(place, w, data, mine):
    def piece(s, place):
        core = place[3] if mine else 1 - place[3]
        return (0, 0, lax.rem(place[2] + s, Y) * C + core)

    return pl.pallas_call(
        transport_kernel,
        grid_spec=pltpu.PrefetchScalarGridSpec(
            num_scalar_prefetch=1,
            grid=(Y,),
            in_specs=[
                pl.BlockSpec((X, ROWS, QUARTER), lambda s, place: (0, 0, 0)),
                pl.BlockSpec((X, QUARTER, SHARE), piece),
            ],
            out_specs=pl.BlockSpec((1, ROWS, SHARE), lambda s, place: (s, 0, 0)),
        ),
        out_shape=jax.ShapeDtypeStruct((Y, ROWS, SHARE), F32 if mine else BF16),
        compiler_params=params(58),
        cost_estimate=pl.CostEstimate(flops=ROWS * COUNT * WIDTH, bytes_accessed=8 * 2**20, transcendentals=0),
        name="keep" if mine else "give",
    )(place, w, data)


def body(noise, data):
    z, x, y, c = (lax.axis_index(a) for a in ("z", "x", "y", "core"))
    place = jnp.stack([z, x, y, c]).astype(jnp.int32)
    noise_all = lax.all_gather(noise, ("x", "y", "core")).reshape(X, Y * C, ROWS, SHARE)
    mine = lax.all_to_all(data.reshape(X, QUARTER, SLICE), "x", 0, 0)
    samples, sq = assemble(place, ring_z(mine))
    data_all = lax.all_gather(samples, "x")
    q, rows, sq_noise = score(place, samples, sq, noise_all)
    for step in range(ITERS):
        if step:
            rows = noise_lse(q, columns)
        columns, f = data_lse(q, lax.all_to_all(rows, ("x", "y", "core"), 0, 0))
        columns = lax.all_to_all(columns, "z", 0, 0)
    w, pot_g = weigh(q, f, columns, sq)
    w = lax.all_to_all(w, "x", 0, 0)
    give = transport(place, w, data_all, False)
    got = shift(give, "core", 1)
    keep = transport(place, w, data_all, True)
    both = keep + got.astype(F32)
    target = both[0]
    for by in (2, 1, 3):
        target = target + shift(both[by].astype(BF16), "y", by).astype(F32)
    velocity = (target - noise.astype(F32)).astype(BF16)
    own = lax.dynamic_slice_in_dim(f, 2 * x, 2, 0).reshape(ROWS)
    pot_f = own * (EPS / LOG2E) + sq_noise[0] / WIDTH
    turn = jnp.stack([shift(pot_g[0], "x", by) if by else pot_g[0] for by in range(X)])
    pot_g = jnp.concatenate([lax.dynamic_index_in_dim(turn, lax.rem(x - j + X, X), 0, False) for j in range(X)])
    return pot_f, pot_g, velocity


def solution(mesh):
    fine = Mesh(mesh.devices.reshape(Z, X, Y, C), ("z", "x", "y", "core"))
    row, col = ("z", "x"), ("y", "core")
    return jax.shard_map(
        body,
        mesh=fine,
        in_specs=(P(row, col), P(col, row)),
        out_specs=(P(row), P(col), P(row, col)),
        check_vma=False,
    )
```

time: 282 us -> 215 us (0.76)
  waiting for transfers between devices: 167 us -> 56.7 us
  blocking collectives: 27.3 us -> 83.4 us
  Pallas kernels: 0 us -> 26.7 us
  local copies, waits for them, and re-layouts: 17.4 us -> 2.79 us
  matrix products: 10.7 us -> 0 us
  other arithmetic: 13.4 us -> 4.15 us
  starting transfers between devices: 31.7 us -> 24.6 us
    all_gather x2, waiting for transfers between devices: 135 us -> 22.5 us  [the longest x1 22.5 us: body(): lax.all_gather(noise, ('x', 'y', 'core')).reshape(X, Y * C, ROWS, SHARE)]
    all_to_all x2 -> x7, blocking collectives: 27.3 us -> 83.4 us  [the longest x3 41.1 us: body(): columns, f = data_lse(q, lax.all_to_all(rows, ('x', 'y', 'core'), 0, 0))]
    pallas_call x0 -> x10, Pallas kernels: none -> 26.7 us  [the longest x2 11.6 us: transport(): pl.pallas_call(transport_kernel, grid_spec=pltpu.PrefetchScalarGridSpec(n...]
    dot_general x2 -> x0, matrix products: 10.7 us -> none  [the longest x1 7.85 us: body(): partial = jnp.dot(weights, data_full, preferred_element_type=jnp.float32)]
    reduce_sum x11 -> x0, other arithmetic: 9.48 us -> none  [the longest x1 5.22 us: body(): sq_data = jnp.sum(wide * wide, axis=1)]
    dynamic_slice x2 -> x1, local copies, waits for them, and re-layouts: 8.68 us -> 0.01 us  [body(): lax.dynamic_index_in_dim(turn, lax.rem(x - j + X, X), 0, False)]
    ppermute x16 -> x15, starting transfers between devices: 27.7 us -> 21.1 us  [shift(): return lax.ppermute(x, axis, [(j, (j + by) % n) for j in range(n)])]
    reshape x1 -> x0, local copies, waits for them, and re-layouts: 6.58 us -> none  [body(): partial = partial.reshape(rows, 4, 2, share)]
  transfers between devices with their start and end apart: 19 -> 18, of which waited for: 16 -> 9; matrix products, arithmetic and copies ran while one was open for 2% -> 2% of each run, Pallas kernels for 0% -> 10%
where the time goes in v2:
time: 215 us; the launch traced here: 213 us
  blocking collectives  83.4 us (39%)
  waiting for transfers between devices  56.7 us (26%)
  Pallas kernels  26.7 us (12%)
  starting transfers between devices  24.6 us (11%)
  between operations  14.2 us (7%)
  other arithmetic  4.15 us (2%)
  local copies, waits for them, and re-layouts  2.79 us (1%)
    all_to_all x3, blocking collectives, body(): columns, f = data_lse(q, lax.all_to_all(rows, ('x', 'y', 'core'), 0, 0))  41.1 us
    all_to_all x3, blocking collectives, body(): columns = lax.all_to_all(columns, 'z', 0, 0)  31.9 us
    ppermute x15, waiting for transfers between devices, shift(): return lax.ppermute(x, axis, [(j, (j + by) % n) for j in range(n)])  25.6 us
    all_gather x1, waiting for transfers between devices, body(): lax.all_gather(noise, ('x', 'y', 'core')).reshape(X, Y * C, ROWS, SHARE)  22.5 us
    ppermute x15, starting transfers between devices, shift(): return lax.ppermute(x, axis, [(j, (j + by) % n) for j in range(n)])  21.1 us
    pallas_call x2, Pallas kernels, transport(): pl.pallas_call(transport_kernel, grid_spec=pltpu.PrefetchScalarGridSpec(n...  11.6 us
    all_to_all x1, blocking collectives, body(): mine = lax.all_to_all(data.reshape(X, QUARTER, SLICE), 'x', 0, 0)  10.4 us
    pallas_call x1, Pallas kernels, score(): pl.pallas_call(score_kernel, grid_spec=pltpu.PrefetchScalarGridSpec(num_s...  8.69 us
  transfers between devices with their start and end apart: 18, of which 9 were waited for; matrix products, arithmetic and copies ran while one was open for 2% of the time, Pallas kernels for 10%

profile of v2, /device:TPU:1, one launch (start us, length us, event | category | flops | bytes accessed | tf_op | source)
XLA Modules:
  0.0 212.5 jit_solution(9777742142197254718)
XLA Ops:
  7.9 10.4 %all_to_all.40.refs_0_ = bf16[4,256,128]{2,1,0:T(8,128)(2,1)S(1)} all-to-all(bf16[4,256,128]{2,1,0:T(8,128)(2,1)} %bitcast.44), channel_id=1, replica_groups=mesh['z'=8,'x'=4,'y'=4,'core'=2] {'x'}, dimensions={0} | all-to-all | bytes 524288 | tf_op jit(solution)/shard_map/all_to_all | solution.py:257
  20.0 3.9 %collective-permute-start.1 = (bf16[4,256,128]{2,1,0:T(8,128)(2,1)S(1)}, bf16[4,256,128]{2,1,0:T(8,128)(2,1)S(1)}, u32[]{:S(2)}, u32[]{:S(2)}) collective-permute-start(bf16[4,256,128]{2,1,0:T(8,128)(2,1)S(1)} %all_to_all.40.refs_0_), channel_id=1, source_target_pairs={{0,224},{32,0},{64,32},{96,64},{128,96},{160,128},{192,160},{224,1... | collective-permute-start | bytes 786440 | tf_op jit(solution)/shard_map/ppermute | solution.py:32
  23.9 4.5 %collective-permute-done.refs_1_ = bf16[4,256,128]{2,1,0:T(8,128)(2,1)S(1)} collective-permute-done((bf16[4,256,128]{2,1,0:T(8,128)(2,1)S(1)}, bf16[4,256,128]{2,1,0:T(8,128)(2,1)S(1)}, u32[]{:S(2)}, u32[]{:S(2)}) %collective-permute-start) | collective-permute-done | bytes 262176 | tf_op jit(solution)/shard_map/ppermute | solution.py:32
  28.5 2.7 %collective-permute-start.3 = (bf16[4,256,128]{2,1,0:T(8,128)(2,1)S(1)}, bf16[4,256,128]{2,1,0:T(8,128)(2,1)S(1)}, u32[]{:S(2)}, u32[]{:S(2)}) collective-permute-start(bf16[4,256,128]{2,1,0:T(8,128)(2,1)S(1)} %collective-permute-done.1.refs_2_), channel_id=1, source_target_pairs={{0,224},{32,0},{64,32},{96,64},{128,96},{160,128},{192,160},{224,1... | collective-permute-start | bytes 786440 | tf_op jit(solution)/shard_map/ppermute | solution.py:32
  31.1 3.8 %collective-permute-done.2.refs_3_ = bf16[4,256,128]{2,1,0:T(8,128)(2,1)S(1)} collective-permute-done((bf16[4,256,128]{2,1,0:T(8,128)(2,1)S(1)}, bf16[4,256,128]{2,1,0:T(8,128)(2,1)S(1)}, u32[]{:S(2)}, u32[]{:S(2)}) %collective-permute-start.2) | collective-permute-done | bytes 262176 | tf_op jit(solution)/shard_map/ppermute | solution.py:32
  34.9 2.8 %collective-permute-start.5 = (bf16[4,256,128]{2,1,0:T(8,128)(2,1)S(1)}, bf16[4,256,128]{2,1,0:T(8,128)(2,1)S(1)}, u32[]{:S(2)}, u32[]{:S(2)}) collective-permute-start(bf16[4,256,128]{2,1,0:T(8,128)(2,1)S(1)} %collective-permute-done.3.refs_4_), channel_id=1, source_target_pairs={{0,224},{32,0},{64,32},{96,64},{128,96},{160,128},{192,160},{224,1... | collective-permute-start | bytes 786440 | tf_op jit(solution)/shard_map/ppermute | solution.py:32
  37.7 3.7 %collective-permute-done.4.refs_5_ = bf16[4,256,128]{2,1,0:T(8,128)(2,1)S(1)} collective-permute-done((bf16[4,256,128]{2,1,0:T(8,128)(2,1)S(1)}, bf16[4,256,128]{2,1,0:T(8,128)(2,1)S(1)}, u32[]{:S(2)}, u32[]{:S(2)}) %collective-permute-start.4) | collective-permute-done | bytes 262176 | tf_op jit(solution)/shard_map/ppermute | solution.py:32
  41.5 2.7 %collective-permute-start.7 = (bf16[2,256,128]{2,1,0:T(8,128)(2,1)S(1)}, bf16[2,256,128]{2,1,0:T(8,128)(2,1)S(1)}, u32[]{:S(2)}, u32[]{:S(2)}) collective-permute-start(bf16[2,256,128]{2,1,0:T(8,128)(2,1)S(1)} %slice.28), channel_id=1, source_target_pairs={{0,224},{32,0},{64,32},{96,64},{128,96},{160,128},{192,160},{224,1... | collective-permute-start | bytes 393224 | tf_op jit(solution)/shard_map/ppermute | solution.py:32
  44.3 2.8 %collective-permute-done.6.refs_7_ = bf16[2,256,128]{2,1,0:T(8,128)(2,1)S(1)} collective-permute-done((bf16[2,256,128]{2,1,0:T(8,128)(2,1)S(1)}, bf16[2,256,128]{2,1,0:T(8,128)(2,1)S(1)}, u32[]{:S(2)}, u32[]{:S(2)}) %collective-permute-start.6) | collective-permute-done | bytes 131104 | tf_op jit(solution)/shard_map/ppermute | solution.py:32
  50.3 22.5 %all-gather.5.cloned.1.call-done = bf16[8192,512]{1,0:T(8,128)(2,1)} async-done(((bf16[256,512]{1,0:T(8,128)(2,1)}), bf16[8192,512]{1,0:T(8,128)(2,1)}) %all-gather.5.cloned.1.call-update) | async-done | bytes 8388624 | tf_op jit(solution)/shard_map/all_gather | solution.py:256
  72.7 8.7 %score.1 = (f32[256,1024]{1,0:T(8,128)}, f32[32,8,128]{2,1,0:T(8,128)}, f32[1,256]{1,0:T(1,128)}) custom-call(s32[4]{0:T(128)} %copy-done.4, bf16[256,4096]{1,0:T(8,128)(2,1)} %get-tuple-element.14.data_ref, f32[256,128]{1,0:T(8,128)} %copy-done.2, bf16[4,8,256,512]{3,2,1,0:T(8,128)(2,1)} %bitcast.43), custom_call_target="tpu_custom_call" | custom-call | tf_op jit(solution)/shard_map/score/pallas_call | solution.py:127
  81.4 13.0 %all_to_all.41.part_ref = f32[32,8,128]{2,1,0:T(8,128)S(1)} all-to-all(f32[32,8,128]{2,1,0:T(8,128)} %get-tuple-element.17), channel_id=1, replica_groups=mesh['z'=8,'x'=4,'y'=4,'core'=2] {'x','y','core'}, dimensions={0} | all-to-all | bytes 262144 | tf_op jit(solution)/shard_map/all_to_all | solution.py:264
  96.5 13.5 %all_to_all.42.part_ref = f32[8,8,128]{2,1,0:T(8,128)S(1)} all-to-all(f32[8,8,128]{2,1,0:T(8,128)S(1)} %get-tuple-element.18), channel_id=1, replica_groups=mesh['z'=8,'x'=4,'y'=4,'core'=2] {'z'}, dimensions={0} | all-to-all | bytes 65536 | tf_op jit(solution)/shard_map/all_to_all | solution.py:265
  110.3 14.3 %all_to_all.43.part_ref = f32[32,8,128]{2,1,0:T(8,128)S(1)} all-to-all(f32[32,8,128]{2,1,0:T(8,128)S(1)} %noise_lse.2), channel_id=1, replica_groups=mesh['z'=8,'x'=4,'y'=4,'core'=2] {'x','y','core'}, dimensions={0} | all-to-all | bytes 262144 | tf_op jit(solution)/shard_map/all_to_all | solution.py:264
  125.5 9.2 %all_to_all.44.part_ref = f32[8,8,128]{2,1,0:T(8,128)S(1)} all-to-all(f32[8,8,128]{2,1,0:T(8,128)S(1)} %get-tuple-element.19), channel_id=1, replica_groups=mesh['z'=8,'x'=4,'y'=4,'core'=2] {'z'}, dimensions={0} | all-to-all | bytes 65536 | tf_op jit(solution)/shard_map/all_to_all | solution.py:265
  135.1 13.7 %all_to_all.45.part_ref = f32[32,8,128]{2,1,0:T(8,128)S(1)} all-to-all(f32[32,8,128]{2,1,0:T(8,128)S(1)} %noise_lse.3), channel_id=1, replica_groups=mesh['z'=8,'x'=4,'y'=4,'core'=2] {'x','y','core'}, dimensions={0} | all-to-all | bytes 262144 | tf_op jit(solution)/shard_map/all_to_all | solution.py:264
  149.2 9.2 %all_to_all.46.part_ref = f32[8,8,128]{2,1,0:T(8,128)S(1)} all-to-all(f32[8,8,128]{2,1,0:T(8,128)S(1)} %get-tuple-element.22), channel_id=1, replica_groups=mesh['z'=8,'x'=4,'y'=4,'core'=2] {'z'}, dimensions={0} | all-to-all | bytes 65536 | tf_op jit(solution)/shard_map/all_to_all | solution.py:265
  159.6 3.5 %all-to-all-start.7 = ((bf16[4,256,256]{2,1,0:T(8,128)(2,1)}), bf16[4,256,256]{2,1,0:T(8,128)(2,1)S(1)}, u32[]{:S(2)}, u32[]{:S(2)}) async-start(bf16[4,256,256]{2,1,0:T(8,128)(2,1)} %get-tuple-element.24), calls=%async_computation.7 | async-start | bytes 1048576 | tf_op jit(solution)/shard_map/all_to_all | solution.py:267
  163.1 8.0 %all-to-all-done.7.w_ref = bf16[4,256,256]{2,1,0:T(8,128)(2,1)S(1)} async-done(((bf16[4,256,256]{2,1,0:T(8,128)(2,1)}), bf16[4,256,256]{2,1,0:T(8,128)(2,1)S(1)}, u32[]{:S(2)}, u32[]{:S(2)}) %all-to-all-start.7) | async-done | bytes 524320 | tf_op jit(solution)/shard_map/all_to_all | solution.py:267
  171.9 5.8 %give.1 = bf16[4,256,512]{2,1,0:T(8,128)(2,1)} custom-call(s32[4]{0:T(128)} %copy-done.4, bf16[4,256,256]{2,1,0:T(8,128)(2,1)} %copy-done.5, bf16[4,256,4096]{2,1,0:T(8,128)(2,1)} %bitcast.41), custom_call_target="tpu_custom_call" | custom-call | flops 1073741824 | bytes 8388608 | tf_op jit(solution)/shard_map/give/pallas_call | solution.py:235
  182.7 5.9 %keep.1 = f32[4,256,512]{2,1,0:T(8,128)} custom-call(s32[4]{0:T(128)} %copy-done.4, bf16[4,256,256]{2,1,0:T(8,128)(2,1)} %copy-done.5, bf16[4,256,4096]{2,1,0:T(8,128)(2,1)} %bitcast.42), custom_call_target="tpu_custom_call" | custom-call | flops 1073741824 | bytes 8388608 | tf_op jit(solution)/shard_map/keep/pallas_call | solution.py:235
  194.0 4.0 %collective-permute-done.14 = bf16[256,512]{1,0:T(8,128)(2,1)S(1)} collective-permute-done((bf16[256,512]{1,0:T(8,128)(2,1)S(1)}, bf16[256,512]{1,0:T(8,128)(2,1)S(1)}, u32[]{:S(2)}, u32[]{:S(2)}) %collective-permute-start.14) | collective-permute-done | bytes 262176 | tf_op jit(solution)/shard_map/ppermute | solution.py:32
  198.0 2.6 %collective-permute-done.13 = bf16[256,512]{1,0:T(8,128)(2,1)S(1)} collective-permute-done((bf16[256,512]{1,0:T(8,128)(2,1)S(1)}, bf16[256,512]{1,0:T(8,128)(2,1)S(1)}, u32[]{:S(2)}, u32[]{:S(2)}) %collective-permute-start.13) | collective-permute-done | bytes 262176 | tf_op jit(solution)/shard_map/ppermute | solution.py:32
  200.6 4.2 %collective-permute-done.12 = bf16[256,512]{1,0:T(8,128)(2,1)S(1)} collective-permute-done((bf16[256,512]{1,0:T(8,128)(2,1)S(1)}, bf16[256,512]{1,0:T(8,128)(2,1)S(1)}, u32[]{:S(2)}, u32[]{:S(2)}) %collective-permute-start.12) | collective-permute-done | bytes 262176 | tf_op jit(solution)/shard_map/ppermute | solution.py:32
  (58 shorter events, 23.1 us)
Async XLA Ops:
  7.2 65.6 %all-gather.5.cloned.1.call-start = ((), (), s32[]{:S(2)}) async-start(), calls=%async_computation.8 | async-start | bytes 8650752 | tf_op jit(solution)/shard_map/all_gather | solution.py:256
  7.9 155.2 %all-gather.7.cloned.1.call-start = ((), (), s32[]{:S(2)}) async-start(), calls=%async_computation.9 | async-start | bytes 10485760 | tf_op jit(solution)/shard_map/all_gather | solution.py:259
  18.3 10.1 %collective-permute-start = (bf16[4,256,128]{2,1,0:T(8,128)(2,1)S(1)}, bf16[4,256,128]{2,1,0:T(8,128)(2,1)S(1)}, u32[]{:S(2)}, u32[]{:S(2)}) collective-permute-start(bf16[4,256,128]{2,1,0:T(8,128)(2,1)S(1)} %all_to_all.40.refs_0_), channel_id=1, source_target_pairs={{0,32},{32,64},{64,96},{96,128},{128,160},{160,192},{192,224},{224... | collective-permute-start | bytes 786440 | tf_op jit(solution)/shard_map/ppermute | solution.py:32
  20.0 8.5 %collective-permute-start.1 = (bf16[4,256,128]{2,1,0:T(8,128)(2,1)S(1)}, bf16[4,256,128]{2,1,0:T(8,128)(2,1)S(1)}, u32[]{:S(2)}, u32[]{:S(2)}) collective-permute-start(bf16[4,256,128]{2,1,0:T(8,128)(2,1)S(1)} %all_to_all.40.refs_0_), channel_id=1, source_target_pairs={{0,224},{32,0},{64,32},{96,64},{128,96},{160,128},{192,160},{224,1... | collective-permute-start | bytes 786440 | tf_op jit(solution)/shard_map/ppermute | solution.py:32
  28.5 6.4 %collective-permute-start.2 = (bf16[4,256,128]{2,1,0:T(8,128)(2,1)S(1)}, bf16[4,256,128]{2,1,0:T(8,128)(2,1)S(1)}, u32[]{:S(2)}, u32[]{:S(2)}) collective-permute-start(bf16[4,256,128]{2,1,0:T(8,128)(2,1)S(1)} %collective-permute-done.refs_1_), channel_id=1, source_target_pairs={{0,32},{32,64},{64,96},{96,128},{128,160},{160,192},{192,224},{224... | collective-permute-start | bytes 786440 | tf_op jit(solution)/shard_map/ppermute | solution.py:32
  28.5 6.4 %collective-permute-start.3 = (bf16[4,256,128]{2,1,0:T(8,128)(2,1)S(1)}, bf16[4,256,128]{2,1,0:T(8,128)(2,1)S(1)}, u32[]{:S(2)}, u32[]{:S(2)}) collective-permute-start(bf16[4,256,128]{2,1,0:T(8,128)(2,1)S(1)} %collective-permute-done.1.refs_2_), channel_id=1, source_target_pairs={{0,224},{32,0},{64,32},{96,64},{128,96},{160,128},{192,160},{224,1... | collective-permute-start | bytes 786440 | tf_op jit(solution)/shard_map/ppermute | solution.py:32
  34.9 6.4 %collective-permute-start.4 = (bf16[4,256,128]{2,1,0:T(8,128)(2,1)S(1)}, bf16[4,256,128]{2,1,0:T(8,128)(2,1)S(1)}, u32[]{:S(2)}, u32[]{:S(2)}) collective-permute-start(bf16[4,256,128]{2,1,0:T(8,128)(2,1)S(1)} %collective-permute-done.2.refs_3_), channel_id=1, source_target_pairs={{0,32},{32,64},{64,96},{96,128},{128,160},{160,192},{192,224},{224... | collective-permute-start | bytes 786440 | tf_op jit(solution)/shard_map/ppermute | solution.py:32
  34.9 6.5 %collective-permute-start.5 = (bf16[4,256,128]{2,1,0:T(8,128)(2,1)S(1)}, bf16[4,256,128]{2,1,0:T(8,128)(2,1)S(1)}, u32[]{:S(2)}, u32[]{:S(2)}) collective-permute-start(bf16[4,256,128]{2,1,0:T(8,128)(2,1)S(1)} %collective-permute-done.3.refs_4_), channel_id=1, source_target_pairs={{0,224},{32,0},{64,32},{96,64},{128,96},{160,128},{192,160},{224,1... | collective-permute-start | bytes 786440 | tf_op jit(solution)/shard_map/ppermute | solution.py:32
  41.4 5.7 %collective-permute-start.6 = (bf16[2,256,128]{2,1,0:T(8,128)(2,1)S(1)}, bf16[2,256,128]{2,1,0:T(8,128)(2,1)S(1)}, u32[]{:S(2)}, u32[]{:S(2)}) collective-permute-start(bf16[2,256,128]{2,1,0:T(8,128)(2,1)S(1)} %slice.27), channel_id=1, source_target_pairs={{0,32},{32,64},{64,96},{96,128},{128,160},{160,192},{192,224},{224... | collective-permute-start | bytes 393224 | tf_op jit(solution)/shard_map/ppermute | solution.py:32
  41.5 5.6 %collective-permute-start.7 = (bf16[2,256,128]{2,1,0:T(8,128)(2,1)S(1)}, bf16[2,256,128]{2,1,0:T(8,128)(2,1)S(1)}, u32[]{:S(2)}, u32[]{:S(2)}) collective-permute-start(bf16[2,256,128]{2,1,0:T(8,128)(2,1)S(1)} %slice.28), channel_id=1, source_target_pairs={{0,224},{32,0},{64,32},{96,64},{128,96},{160,128},{192,160},{224,1... | collective-permute-start | bytes 393224 | tf_op jit(solution)/shard_map/ppermute | solution.py:32
  44.3 6.0 %copy-start.4 = (s32[4]{0:T(128)}, s32[4]{0:T(128)S(1)}, u32[]{:S(2)}) copy-start(s32[4]{0:T(128)S(1)} %pad_add_fusion.place) | copy-start | bytes 52
  94.5 1.2 copy-start
  110.3 48.1 %copy-start.1 = (f32[256,1024]{1,0:T(8,128)S(1)}, f32[256,1024]{1,0:T(8,128)}, u32[]{:S(2)}) copy-start(f32[256,1024]{1,0:T(8,128)} %get-tuple-element.16.q_ref) | copy-start | bytes 3145732
  110.3 48.0 %copy-start.3 = (f32[256,128]{1,0:T(8,128)S(1)}, f32[256,128]{1,0:T(8,128)}, u32[]{:S(2)}) copy-start(f32[256,128]{1,0:T(8,128)} %copy-done.2) | copy-start | bytes 393220
  159.6 11.5 %all-to-all-start.7 = ((bf16[4,256,256]{2,1,0:T(8,128)(2,1)}), bf16[4,256,256]{2,1,0:T(8,128)(2,1)S(1)}, u32[]{:S(2)}, u32[]{:S(2)}) async-start(bf16[4,256,256]{2,1,0:T(8,128)(2,1)} %get-tuple-element.24), calls=%async_computation.7 | async-start | bytes 1048576 | tf_op jit(solution)/shard_map/all_to_all | solution.py:267
  171.9 8.1 %copy-start.7 = (f32[1,256]{1,0:T(1,128)S(1)}, f32[1,256]{1,0:T(1,128)}, u32[]{:S(2)}) copy-start(f32[1,256]{1,0:T(1,128)} %get-tuple-element.21) | copy-start | bytes 3076
  177.6 10.9 %collective-permute-start.11 = (bf16[4,256,512]{2,1,0:T(8,128)(2,1)}, bf16[4,256,512]{2,1,0:T(8,128)(2,1)S(1)}, u32[]{:S(2)}, u32[]{:S(2)}) collective-permute-start(bf16[4,256,512]{2,1,0:T(8,128)(2,1)} %give.1), channel_id=1, source_target_pairs={{0,1},{1,0},{2,3},{3,2},{4,5},{5,4},{6,7},{7,6},{8,9},{9,8},{10,11... | collective-permute-start | bytes 3145736 | tf_op jit(solution)/shard_map/ppermute | solution.py:32
  180.6 11.6 %collective-permute-start.10 = (f32[256]{0:T(256)S(1)}, f32[256]{0:T(256)S(1)}, u32[]{:S(2)}, u32[]{:S(2)}) collective-permute-start(f32[256]{0:T(256)S(1)} %bitcast.38), channel_id=1, source_target_pairs={{0,24},{8,0},{16,8},{24,16},{1,25},{9,1},{17,9},{25,17},{2,26},{10... | collective-permute-start | bytes 3080 | tf_op jit(solution)/shard_map/ppermute | solution.py:32
  181.5 11.9 %collective-permute-start.9 = (f32[256]{0:T(256)S(1)}, f32[256]{0:T(256)S(1)}, u32[]{:S(2)}, u32[]{:S(2)}) collective-permute-start(f32[256]{0:T(256)S(1)} %bitcast.39), channel_id=1, source_target_pairs={{0,16},{8,24},{16,0},{24,8},{1,17},{9,25},{17,1},{25,9},{2,18},{10... | collective-permute-start | bytes 3080 | tf_op jit(solution)/shard_map/ppermute | solution.py:32
  182.6 10.7 %collective-permute-start.8 = (f32[256]{0:T(256)S(1)}, f32[256]{0:T(256)S(1)}, u32[]{:S(2)}, u32[]{:S(2)}) collective-permute-start(f32[256]{0:T(256)S(1)} %bitcast.40), channel_id=1, source_target_pairs={{0,8},{8,16},{16,24},{24,0},{1,9},{9,17},{17,25},{25,1},{2,10},{10... | collective-permute-start | bytes 3080 | tf_op jit(solution)/shard_map/ppermute | solution.py:32
  188.5 16.3 %copy-start.6 = (bf16[256,512]{1,0:T(8,128)(2,1)S(1)}, bf16[256,512]{1,0:T(8,128)(2,1)}, u32[]{:S(2)}) copy-start(bf16[256,512]{1,0:T(8,128)(2,1)} %param.2) | copy-start | bytes 786436
  190.6 7.4 %collective-permute-start.14 = (bf16[256,512]{1,0:T(8,128)(2,1)S(1)}, bf16[256,512]{1,0:T(8,128)(2,1)S(1)}, u32[]{:S(2)}, u32[]{:S(2)}) collective-permute-start(bf16[256,512]{1,0:T(8,128)(2,1)S(1)} %get-tuple-element.28), channel_id=1, source_target_pairs={{0,6},{2,0},{4,2},{6,4},{1,7},{3,1},{5,3},{7,5},{8,14},{10,8},{12,... | collective-permute-start | bytes 786440 | tf_op jit(solution)/shard_map/ppermute | solution.py:32
  191.7 8.9 %collective-permute-start.13 = (bf16[256,512]{1,0:T(8,128)(2,1)S(1)}, bf16[256,512]{1,0:T(8,128)(2,1)S(1)}, u32[]{:S(2)}, u32[]{:S(2)}) collective-permute-start(bf16[256,512]{1,0:T(8,128)(2,1)S(1)} %get-tuple-element.29), channel_id=1, source_target_pairs={{0,2},{2,4},{4,6},{6,0},{1,3},{3,5},{5,7},{7,1},{8,10},{10,12},{12... | collective-permute-start | bytes 786440 | tf_op jit(solution)/shard_map/ppermute | solution.py:32
  192.2 12.7 %collective-permute-start.12 = (bf16[256,512]{1,0:T(8,128)(2,1)S(1)}, bf16[256,512]{1,0:T(8,128)(2,1)S(1)}, u32[]{:S(2)}, u32[]{:S(2)}) collective-permute-start(bf16[256,512]{1,0:T(8,128)(2,1)S(1)} %get-tuple-element.27), channel_id=1, source_target_pairs={{0,4},{2,6},{4,0},{6,2},{1,5},{3,7},{5,1},{7,3},{8,12},{10,14},{12... | collective-permute-start | bytes 786440 | tf_op jit(solution)/shard_map/ppermute | solution.py:32
  (2 other events, 1.5 us)
Sparse Core Ops, SparseCore 0:
  10.6 62.1 all-gather.4
  74.5 88.0 all-gather.6

commit v3 on v2

v3 whole, which is shorter than its diff:
```python
import functools
import math

import jax
import jax.numpy as jnp
from jax import lax
from jax.experimental import pallas as pl
from jax.experimental.pallas import tpu as pltpu
from jax.sharding import Mesh, PartitionSpec as P

ITERS = 3
EPS = 0.01
LOG2E = math.log2(math.e)
Z, X, Y, C = 8, 4, 4, 2
ROWS, SHARE = 256, 512
COUNT, SLICE = 1024, 128
WIDTH = 4096
QUARTER = COUNT // X
TALL = ROWS * X
CHUNKS = TALL // 128
GROUP = X * Y * C
TOTAL = 8192
UNIT = LOG2E / (WIDTH * EPS)
LOG2N = math.log2(TOTAL)
F32, BF16 = jnp.float32, jnp.bfloat16
VMEM = pl.BlockSpec(memory_space=pltpu.VMEM)
SMEM = pl.BlockSpec(memory_space=pltpu.SMEM)


def shift(x, axis, by):
    n = {"z": Z, "x": X, "y": Y, "core": C}[axis]
    return lax.ppermute(x, axis, [(j, (j + by) % n) for j in range(n)])


def params(mib):
    return pltpu.CompilerParams(vmem_limit_bytes=mib * 2**20)


def ring_z(x):
    forward = backward = x
    got = [x]
    for _ in range(1, Z // 2):
        forward, backward = shift(forward, "z", 1), shift(backward, "z", -1)
        got += [forward, backward]
    cut = x.shape[0] // 2
    return got + [shift(forward[:cut], "z", 1), shift(backward[cut:], "z", -1)]


def squares(ref, pieces):
    total = None
    for view in pieces:
        part = ref[view].astype(F32)
        total = part * part if total is None else total + part * part
    return total


def slot_of(place, piece):
    core, y = lax.rem(piece, C), lax.div(piece, C)
    return lax.rem(core - place[3] + C, C) * Y + lax.rem(y - place[2] + Y, Y)


def assemble_kernel(place, *refs):
    ins, (out_ref, sq_ref) = refs[:-2], refs[-2:]
    z = place[0]
    plan = [(0, 0)] + [(r, 0) for s in range(1, Z // 2) for r in (-s, s)] + [(Z // 2, 0), (Z // 2, X // 2)]
    for ref, (rel, first) in zip(ins, plan, strict=True):
        slot = slot_of(place, lax.rem(z + rel + Z, Z))
        for n in range(ref.shape[0]):
            out_ref[slot, :, pl.ds((first + n) * SLICE, SLICE)] = ref[n]
    step = 64
    for start in range(0, QUARTER, step):
        rows = pl.ds(start, step)
        views = [(p, rows, pl.ds(lane, 128)) for p in range(Y * C) for lane in range(0, SHARE, 128)]
        total = squares(out_ref, views)
        sq_ref[rows, :] = jnp.broadcast_to(jnp.sum(total, axis=1, keepdims=True), (step, 128))


def assemble(place, parts):
    return pl.pallas_call(
        assemble_kernel,
        out_shape=(jax.ShapeDtypeStruct((Y * C, QUARTER, SHARE), BF16), jax.ShapeDtypeStruct((QUARTER, 128), F32)),
        in_specs=[SMEM] + [VMEM] * len(parts),
        out_specs=(VMEM, VMEM),
        compiler_params=params(16),
        cost_estimate=pl.CostEstimate(flops=2 * QUARTER * WIDTH, bytes_accessed=4 * 2**20, transcendentals=0),
        name="assemble",
    )(place, *parts)


def lse(t, axis):
    top = jnp.max(t, axis=axis, keepdims=True)
    return top + jnp.log2(jnp.sum(jnp.exp2(t - top), axis=axis, keepdims=True))


def merged(ref):
    parts = ref[...]
    top = jnp.max(parts, axis=0)
    return top + jnp.log2(jnp.sum(jnp.exp2(parts - top[None]), axis=0))


def chunk(r):
    return pl.ds(r * 128, 128)


def score_kernel(place, data_ref, sq_ref, noise_ref, q_ref, out_ref, sqn_ref, lse_ref):
    data = jnp.concatenate([data_ref[slot_of(place, p)] for p in range(Y * C)], axis=1)
    for n in range(X):
        block = jnp.concatenate([noise_ref[n, p] for p in range(Y * C)], axis=1)
        gram = lax.dot_general(data, block, (((1,), (1,)), ((), ())), preferred_element_type=F32)
        gram = gram * (2.0 * UNIT)
        q_ref[:, pl.ds(n * ROWS, ROWS)] = gram
        t = gram - UNIT * jnp.concatenate([sq_ref[...]] * 2, axis=1)
        rows = lse(t, 0)
        lse_ref[pl.ds(2 * n, 1), :] = rows[:, :128]
        lse_ref[pl.ds(2 * n + 1, 1), :] = rows[:, 128:]
    out_ref[...] = jnp.broadcast_to(lse_ref[...][None], (GROUP, CHUNKS, 128))
    x = place[1]
    views = [(x, p, slice(None), pl.ds(lane, 128)) for p in range(Y * C) for lane in range(0, SHARE, 128)]
    sqn_ref[...] = jnp.sum(jnp.transpose(squares(noise_ref, views)), axis=0, keepdims=True)


def score(place, data, sq, noise):
    return pl.pallas_call(
        score_kernel,
        out_shape=(
            jax.ShapeDtypeStruct((QUARTER, TALL), F32),
            jax.ShapeDtypeStruct((GROUP, CHUNKS, 128), F32),
            jax.ShapeDtypeStruct((1, ROWS), F32),
        ),
        in_specs=[SMEM] + [VMEM] * 3,
        out_specs=(VMEM,) * 3,
        scratch_shapes=[pltpu.VMEM((CHUNKS, 128), F32)],
        compiler_params=params(32),
        name="score",
    )(place, data, sq, noise)


def to_column(g):
    return jnp.concatenate([jnp.transpose(jnp.broadcast_to(g[r : r + 1], (128, 128))) for r in range(2)], axis=0)


def noise_kernel(q_ref, part_ref, out_ref, lse_ref, g_ref):
    g_ref[...] = to_column(-LOG2N - merged(part_ref))
    for r in range(CHUNKS):
        lse_ref[pl.ds(r, 1), :] = lse(q_ref[:, chunk(r)] + g_ref[...], 0)
    out_ref[...] = jnp.broadcast_to(lse_ref[...][None], (GROUP, CHUNKS, 128))


def noise_lse(q, parts):
    return pl.pallas_call(
        noise_kernel,
        out_shape=jax.ShapeDtypeStruct((GROUP, CHUNKS, 128), F32),
        in_specs=[VMEM] * 2,
        out_specs=VMEM,
        scratch_shapes=[pltpu.VMEM((CHUNKS, 128), F32), pltpu.VMEM((QUARTER, 128), F32)],
        compiler_params=params(16),
        name="noise_lse",
    )(q, parts)


def data_kernel(q_ref, part_ref, out_ref, f_ref, lane_ref):
    f_ref[...] = -LOG2N - merged(part_ref)
    row = data_row(q_ref, f_ref, lane_ref)
    out_ref[...] = jnp.broadcast_to(two_rows(row)[None], (Z, 8, 128))


def data_row(q_ref, f_ref, lane_ref):
    step = 32
    for start in range(0, QUARTER, step):
        rows = pl.ds(start, step)
        t = [q_ref[rows, chunk(r)] + f_ref[pl.ds(r, 1), :] for r in range(CHUNKS)]
        top = functools.reduce(jnp.maximum, t)
        lane_ref[rows, :] = top + jnp.log2(sum(jnp.exp2(part - top) for part in t))
    return lse(jnp.transpose(lane_ref[...]), 0)


def two_rows(*rows):
    halves = [half for row in rows for half in (row[:, :128], row[:, 128:])]
    return jnp.concatenate(halves + [jnp.zeros((8 - len(halves), 128), F32)], axis=0)


def data_lse(q, parts):
    return pl.pallas_call(
        data_kernel,
        out_shape=(jax.ShapeDtypeStruct((Z, 8, 128), F32), jax.ShapeDtypeStruct((CHUNKS, 128), F32)),
        in_specs=[VMEM] * 2,
        out_specs=(VMEM, VMEM),
        scratch_shapes=[pltpu.VMEM((QUARTER, 128), F32)],
        compiler_params=params(16),
        name="data_lse",
    )(q, parts)


def last_kernel(place, q_ref, part_ref, sq_ref, out_ref, f_ref, *refs):
    w_refs, lane_ref = refs[:X], refs[X]
    f_ref[...] = -LOG2N - merged(part_ref)
    tile = two_rows(data_row(q_ref, f_ref, lane_ref), jnp.transpose(sq_ref[...])[0:1, :])
    out_ref[...] = jnp.broadcast_to(tile[None], (Z * X, 8, 128))
    column = to_column(tile)
    for by in range(X):
        block = lax.rem(place[1] + by, X)
        for h in range(2):
            lanes = pl.ds(pl.multiple_of(block * ROWS + h * 128, 128), 128)
            w = jnp.exp2((q_ref[:, lanes] + f_ref[pl.ds(2 * block + h, 1), :]) - column)
            w_refs[by][:, pl.ds(h * 128, 128)] = w.astype(BF16)


def last_lse(place, q, parts, sq):
    return pl.pallas_call(
        last_kernel,
        out_shape=(jax.ShapeDtypeStruct((Z * X, 8, 128), F32), jax.ShapeDtypeStruct((CHUNKS, 128), F32))
        + (jax.ShapeDtypeStruct((QUARTER, ROWS), BF16),) * X,
        in_specs=[SMEM] + [VMEM] * 3,
        out_specs=(VMEM,) * (2 + X),
        scratch_shapes=[pltpu.VMEM((QUARTER, 128), F32)],
        compiler_params=params(16),
        name="last_lse",
    )(place, q, parts, sq)


def give_kernel(place, part_ref, *refs):
    w_refs, (data_ref, out_ref, w_ref, pot_ref) = refs[:X], refs[X:]

    @pl.when(pl.program_id(0) == 0)
    def _():
        scale(place, part_ref, w_refs, w_ref, pot_ref)

    transport(w_ref, data_ref, out_ref)


def scale(place, part_ref, w_refs, w_ref, pot_ref):
    z, x = place[0], place[1]
    for n in range(X):
        parts = jnp.stack([part_ref[k * X + n, 0:4, :] for k in range(Z)])
        top = jnp.max(parts, axis=0)
        total = top + jnp.log2(jnp.sum(jnp.exp2(parts - top[None]), axis=0))
        pot_ref[pl.ds(2 * n, 2), :] = (-LOG2N - total[0:2]) * (EPS / LOG2E) + parts[0, 2:4] * (1.0 / WIDTH)
    for by in range(X):
        n = lax.rem(x - by + X, X)
        parts = jnp.stack([part_ref[k * X + n] for k in range(Z)])
        top = jnp.max(parts, axis=0)
        total = top + jnp.log2(jnp.sum(jnp.exp2(parts - top[None]), axis=0))
        factor = to_column(jnp.exp2(part_ref[z * X + n] - total))
        rows = pl.ds(pl.multiple_of(n * QUARTER, QUARTER), QUARTER)
        for h in range(2):
            w = w_refs[by][:, pl.ds(h * 128, 128)].astype(F32) * factor
            w_ref[rows, pl.ds(h * 128, 128)] = w.astype(BF16)


def transport(w_ref, data_ref, out_ref):
    block = jnp.concatenate([data_ref[n, 0] for n in range(X)], axis=0)
    total = lax.dot_general(w_ref[...], block, (((0,), (0,)), ((), ())), preferred_element_type=F32)
    out_ref[0] = total.astype(out_ref.dtype)


HALF_COST = pl.CostEstimate(flops=ROWS * COUNT * WIDTH, bytes_accessed=5 * 2**20, transcendentals=0)


def half_of(which):
    return pl.BlockSpec((X, 1, QUARTER, SHARE), lambda s: (0, which * Y + s, 0, 0))


PIECE = pl.BlockSpec((1, ROWS, SHARE), lambda s: (s, 0, 0))


def give(place, parts, blocks, data):
    return pl.pallas_call(
        give_kernel,
        grid=(Y,),
        out_shape=(
            jax.ShapeDtypeStruct((Y, ROWS, SHARE), BF16),
            jax.ShapeDtypeStruct((COUNT, ROWS), BF16),
            jax.ShapeDtypeStruct((2 * X, 128), F32),
        ),
        in_specs=[SMEM] + [VMEM] * (1 + X) + [half_of(1)],
        out_specs=(PIECE, VMEM, VMEM),
        compiler_params=params(53),
        cost_estimate=HALF_COST,
        name="give",
    )(place, parts, *blocks, data)


def keep(w, data):
    return pl.pallas_call(
        transport,
        grid=(Y,),
        out_shape=jax.ShapeDtypeStruct((Y, ROWS, SHARE), F32),
        in_specs=[VMEM, half_of(0)],
        out_specs=PIECE,
        compiler_params=params(53),
        cost_estimate=HALF_COST,
        name="keep",
    )(w, data)


def body(noise, data):
    z, x, y, c = (lax.axis_index(a) for a in ("z", "x", "y", "core"))
    place = jnp.stack([z, x, y, c]).astype(jnp.int32)
    noise_all = lax.all_gather(noise, ("x", "y", "core")).reshape(X, Y * C, ROWS, SHARE)
    swapped = lax.all_to_all(data.reshape(X, QUARTER, SLICE), "x", 0, 0)
    samples, sq = assemble(place, ring_z(swapped))
    data_all = lax.all_gather(samples, "x")
    q, rows, sq_noise = score(place, samples, sq, noise_all)
    for step in range(ITERS):
        if step:
            rows = noise_lse(q, columns)
        parts = lax.all_to_all(rows, ("x", "y", "core"), 0, 0)
        if step < ITERS - 1:
            columns, f = data_lse(q, parts)
            columns = lax.all_to_all(columns, "z", 0, 0)
    columns, f, *blocks = last_lse(place, q, parts, sq)
    blocks = [blocks[0]] + [shift(blocks[by], "x", by) for by in range(1, X)]
    columns = lax.all_to_all(columns, ("z", "x"), 0, 0)
    theirs, w, pot_g = give(place, columns, blocks, data_all)
    got = shift(theirs, "core", 1)
    mine = keep(w, data_all)
    both = mine + got.astype(F32)
    target = both[0]
    for by in (2, 1, 3):
        target = target + shift(both[by].astype(BF16), "y", by).astype(F32)
    velocity = (target - noise.astype(F32)).astype(BF16)
    own = lax.dynamic_slice_in_dim(f, 2 * x, 2, 0).reshape(ROWS)
    pot_f = own * (EPS / LOG2E) + sq_noise[0] / WIDTH
    return pot_f, pot_g.reshape(COUNT), velocity


def solution(mesh):
    fine = Mesh(mesh.devices.reshape(Z, X, Y, C), ("z", "x", "y", "core"))
    row, col = ("z", "x"), ("y", "core")
    return jax.shard_map(
        body,
        mesh=fine,
        in_specs=(P(row, col), P(col, row)),
        out_specs=(P(row), P(col), P(row, col)),
        check_vma=False,
    )
```

time: 215 us -> 209 us (0.972)
  blocking collectives: 83.4 us -> 74.1 us
  waiting for transfers between devices: 56.7 us -> 63.2 us
  Pallas kernels: 26.7 us -> 21 us
  starting transfers between devices: 24.6 us -> 27.7 us
    all_gather x1, waiting for transfers between devices: 0.02 us -> 12.3 us  [body(): data_all = lax.all_gather(samples, 'x')]
    all_to_all x3 -> x2, blocking collectives: 31.9 us -> 22.7 us  [body(): columns = lax.all_to_all(columns, 'z', 0, 0)]
    all_to_all x1, waiting for transfers between devices: 7.98 us -> 0.01 us  [body(): columns = lax.all_to_all(columns, ('z', 'x'), 0, 0)]
    pallas_call x5, Pallas kernels: 24 us -> 18.6 us  [the longest x1 5.19 us: give(): pl.pallas_call(give_kernel, grid=(Y,), out_shape=(jax.ShapeDtypeStruct((Y...]
    ppermute x15, starting transfers between devices: 21.1 us -> 23.8 us  [shift(): return lax.ppermute(x, axis, [(j, (j + by) % n) for j in range(n)])]
    unnamed x16 -> x6, local copies, waits for them, and re-layouts: 2.71 us -> 4.43 us
  transfers between devices with their start and end apart: 18 -> 18, of which waited for: 9 -> 8; matrix products, arithmetic and copies ran while one was open for 2% -> 0% of each run, Pallas kernels for 10% -> 8%
where the time goes in v3:
time: 209 us; the launch traced here: 208 us
  blocking collectives  74.1 us (35%)
  waiting for transfers between devices  63.2 us (30%)
  starting transfers between devices  27.7 us (13%)
  Pallas kernels  21 us (10%)
  between operations  14.1 us (7%)
  local copies, waits for them, and re-layouts  4.5 us (2%)
  other arithmetic  3.54 us (2%)
    all_to_all x3, blocking collectives, body(): parts = lax.all_to_all(rows, ('x', 'y', 'core'), 0, 0)  41 us
    ppermute x15, waiting for transfers between devices, shift(): return lax.ppermute(x, axis, [(j, (j + by) % n) for j in range(n)])  26.9 us
    ppermute x15, starting transfers between devices, shift(): return lax.ppermute(x, axis, [(j, (j + by) % n) for j in range(n)])  23.8 us
    all_gather x1, waiting for transfers between devices, body(): lax.all_gather(noise, ('x', 'y', 'core')).reshape(X, Y * C, ROWS, SHARE)  23.3 us
    all_to_all x2, blocking collectives, body(): columns = lax.all_to_all(columns, 'z', 0, 0)  22.7 us
    all_gather x1, waiting for transfers between devices, body(): data_all = lax.all_gather(samples, 'x')  12.3 us
    all_to_all x1, blocking collectives, body(): swapped = lax.all_to_all(data.reshape(X, QUARTER, SLICE), 'x', 0, 0)  10.4 us
    pallas_call x1, Pallas kernels, give(): pl.pallas_call(give_kernel, grid=(Y,), out_shape=(jax.ShapeDtypeStruct((Y...  5.19 us
  transfers between devices with their start and end apart: 18, of which 8 were waited for; matrix products, arithmetic and copies ran while one was open for 0% of the time, Pallas kernels for 8%

profile of v3, /device:TPU:1, one launch (start us, length us, event | category | flops | bytes accessed | tf_op | source)
XLA Modules:
  0.0 208.1 jit_solution(6321304140126509431)
XLA Ops:
  7.9 10.4 %all_to_all.35.refs_0_ = bf16[4,256,128]{2,1,0:T(8,128)(2,1)S(1)} all-to-all(bf16[4,256,128]{2,1,0:T(8,128)(2,1)} %bitcast.32), channel_id=1, replica_groups=mesh['z'=8,'x'=4,'y'=4,'core'=2] {'x'}, dimensions={0} | all-to-all | bytes 524288 | tf_op jit(solution)/shard_map/all_to_all | solution.py:300
  20.0 3.9 %collective-permute-start.1 = (bf16[4,256,128]{2,1,0:T(8,128)(2,1)S(1)}, bf16[4,256,128]{2,1,0:T(8,128)(2,1)S(1)}, u32[]{:S(2)}, u32[]{:S(2)}) collective-permute-start(bf16[4,256,128]{2,1,0:T(8,128)(2,1)S(1)} %all_to_all.35.refs_0_), channel_id=1, source_target_pairs={{0,224},{32,0},{64,32},{96,64},{128,96},{160,128},{192,160},{224,1... | collective-permute-start | bytes 786440 | tf_op jit(solution)/shard_map/ppermute | solution.py:32
  23.9 4.5 %collective-permute-done.refs_1_ = bf16[4,256,128]{2,1,0:T(8,128)(2,1)S(1)} collective-permute-done((bf16[4,256,128]{2,1,0:T(8,128)(2,1)S(1)}, bf16[4,256,128]{2,1,0:T(8,128)(2,1)S(1)}, u32[]{:S(2)}, u32[]{:S(2)}) %collective-permute-start) | collective-permute-done | bytes 262176 | tf_op jit(solution)/shard_map/ppermute | solution.py:32
  28.5 2.7 %collective-permute-start.3 = (bf16[4,256,128]{2,1,0:T(8,128)(2,1)S(1)}, bf16[4,256,128]{2,1,0:T(8,128)(2,1)S(1)}, u32[]{:S(2)}, u32[]{:S(2)}) collective-permute-start(bf16[4,256,128]{2,1,0:T(8,128)(2,1)S(1)} %collective-permute-done.1.refs_2_), channel_id=1, source_target_pairs={{0,224},{32,0},{64,32},{96,64},{128,96},{160,128},{192,160},{224,1... | collective-permute-start | bytes 786440 | tf_op jit(solution)/shard_map/ppermute | solution.py:32
  31.1 3.8 %collective-permute-done.2.refs_3_ = bf16[4,256,128]{2,1,0:T(8,128)(2,1)S(1)} collective-permute-done((bf16[4,256,128]{2,1,0:T(8,128)(2,1)S(1)}, bf16[4,256,128]{2,1,0:T(8,128)(2,1)S(1)}, u32[]{:S(2)}, u32[]{:S(2)}) %collective-permute-start.2) | collective-permute-done | bytes 262176 | tf_op jit(solution)/shard_map/ppermute | solution.py:32
  34.9 2.8 %collective-permute-start.5 = (bf16[4,256,128]{2,1,0:T(8,128)(2,1)S(1)}, bf16[4,256,128]{2,1,0:T(8,128)(2,1)S(1)}, u32[]{:S(2)}, u32[]{:S(2)}) collective-permute-start(bf16[4,256,128]{2,1,0:T(8,128)(2,1)S(1)} %collective-permute-done.3.refs_4_), channel_id=1, source_target_pairs={{0,224},{32,0},{64,32},{96,64},{128,96},{160,128},{192,160},{224,1... | collective-permute-start | bytes 786440 | tf_op jit(solution)/shard_map/ppermute | solution.py:32
  37.7 3.7 %collective-permute-done.4.refs_5_ = bf16[4,256,128]{2,1,0:T(8,128)(2,1)S(1)} collective-permute-done((bf16[4,256,128]{2,1,0:T(8,128)(2,1)S(1)}, bf16[4,256,128]{2,1,0:T(8,128)(2,1)S(1)}, u32[]{:S(2)}, u32[]{:S(2)}) %collective-permute-start.4) | collective-permute-done | bytes 262176 | tf_op jit(solution)/shard_map/ppermute | solution.py:32
  41.5 2.7 %collective-permute-start.7 = (bf16[2,256,128]{2,1,0:T(8,128)(2,1)S(1)}, bf16[2,256,128]{2,1,0:T(8,128)(2,1)S(1)}, u32[]{:S(2)}, u32[]{:S(2)}) collective-permute-start(bf16[2,256,128]{2,1,0:T(8,128)(2,1)S(1)} %slice.28), channel_id=1, source_target_pairs={{0,224},{32,0},{64,32},{96,64},{128,96},{160,128},{192,160},{224,1... | collective-permute-start | bytes 393224 | tf_op jit(solution)/shard_map/ppermute | solution.py:32
  44.3 2.8 %collective-permute-done.6.refs_7_ = bf16[2,256,128]{2,1,0:T(8,128)(2,1)S(1)} collective-permute-done((bf16[2,256,128]{2,1,0:T(8,128)(2,1)S(1)}, bf16[2,256,128]{2,1,0:T(8,128)(2,1)S(1)}, u32[]{:S(2)}, u32[]{:S(2)}) %collective-permute-start.6) | collective-permute-done | bytes 131104 | tf_op jit(solution)/shard_map/ppermute | solution.py:32
  49.4 23.3 %all-gather.5.cloned.1.call-done = bf16[8192,512]{1,0:T(8,128)(2,1)} async-done(((bf16[256,512]{1,0:T(8,128)(2,1)}), bf16[8192,512]{1,0:T(8,128)(2,1)}) %all-gather.5.cloned.1.call-update) | async-done | bytes 8388624 | tf_op jit(solution)/shard_map/all_gather | solution.py:299
  72.7 3.4 %copy-done = bf16[8192,512]{1,0:T(8,128)(2,1)S(1)} copy-done((bf16[8192,512]{1,0:T(8,128)(2,1)S(1)}, bf16[8192,512]{1,0:T(8,128)(2,1)}, u32[]{:S(2)}) %copy-start) | copy-done | bytes 8388632
  76.1 4.4 %score.1 = (f32[256,1024]{1,0:T(8,128)S(1)}, f32[32,8,128]{2,1,0:T(8,128)S(1)}, f32[1,256]{1,0:T(1,128)S(1)}) custom-call(s32[4]{0:T(128)S(1)} %pad_add_fusion.place, bf16[8,256,512]{2,1,0:T(8,128)(2,1)} %get-tuple-element.19.data_ref, f32[256,128]{1,0:T(8,128)S(1)} %get-tuple-element.20.sq_ref, bf16[4,8,256,512]{3,2,1,0:T(8,128)(2,1)S(1)} %bitcast.29), custom_call_target="tpu_custom_call" | custom-call | tf_op jit(solution)/shard_map/score/pallas_call | solution.py:123
  80.5 13.0 %all_to_all.36.part_ref = f32[32,8,128]{2,1,0:T(8,128)S(1)} all-to-all(f32[32,8,128]{2,1,0:T(8,128)S(1)} %get-tuple-element.22), channel_id=1, replica_groups=mesh['z'=8,'x'=4,'y'=4,'core'=2] {'x','y','core'}, dimensions={0} | all-to-all | bytes 262144 | tf_op jit(solution)/shard_map/all_to_all | solution.py:307
  94.3 13.5 %all_to_all.37.part_ref = f32[8,8,128]{2,1,0:T(8,128)S(1)} all-to-all(f32[8,8,128]{2,1,0:T(8,128)S(1)} %get-tuple-element.23), channel_id=1, replica_groups=mesh['z'=8,'x'=4,'y'=4,'core'=2] {'z'}, dimensions={0} | all-to-all | bytes 65536 | tf_op jit(solution)/shard_map/all_to_all | solution.py:310
  108.2 14.1 %all_to_all.38.part_ref = f32[32,8,128]{2,1,0:T(8,128)S(1)} all-to-all(f32[32,8,128]{2,1,0:T(8,128)S(1)} %noise_lse.2), channel_id=1, replica_groups=mesh['z'=8,'x'=4,'y'=4,'core'=2] {'x','y','core'}, dimensions={0} | all-to-all | bytes 262144 | tf_op jit(solution)/shard_map/all_to_all | solution.py:307
  123.1 9.2 %all_to_all.39.part_ref = f32[8,8,128]{2,1,0:T(8,128)S(1)} all-to-all(f32[8,8,128]{2,1,0:T(8,128)S(1)} %get-tuple-element.24), channel_id=1, replica_groups=mesh['z'=8,'x'=4,'y'=4,'core'=2] {'z'}, dimensions={0} | all-to-all | bytes 65536 | tf_op jit(solution)/shard_map/all_to_all | solution.py:310
  132.7 13.9 %all_to_all.40.part_ref = f32[32,8,128]{2,1,0:T(8,128)S(1)} all-to-all(f32[32,8,128]{2,1,0:T(8,128)S(1)} %noise_lse.3), channel_id=1, replica_groups=mesh['z'=8,'x'=4,'y'=4,'core'=2] {'x','y','core'}, dimensions={0} | all-to-all | bytes 262144 | tf_op jit(solution)/shard_map/all_to_all | solution.py:307
  148.2 3.9 %all-to-all-start.6 = ((f32[32,8,128]{2,1,0:T(8,128)}), f32[32,8,128]{2,1,0:T(8,128)S(1)}, u32[]{:S(2)}, u32[]{:S(2)}) async-start(f32[32,8,128]{2,1,0:T(8,128)} %get-tuple-element.27), calls=%async_computation.6 | async-start | bytes 262144 | tf_op jit(solution)/shard_map/all_to_all | solution.py:313
  156.9 12.3 %all-gather.7.cloned.1.call-done = bf16[32,256,512]{2,1,0:T(8,128)(2,1)} async-done(((bf16[8,256,512]{2,1,0:T(8,128)(2,1)}), bf16[32,256,512]{2,1,0:T(8,128)(2,1)}) %all-gather.7.cloned.1.call-update) | async-done | bytes 8388624 | tf_op jit(solution)/shard_map/all_gather | solution.py:302
  169.2 5.2 %give.1 = (bf16[4,256,512]{2,1,0:T(8,128)(2,1)}, bf16[1024,256]{1,0:T(8,128)(2,1)}, f32[8,128]{1,0:T(8,128)}) custom-call(s32[4]{0:T(128)S(1)} %pad_add_fusion.place, f32[32,8,128]{2,1,0:T(8,128)S(1)} %all-to-all-done.6.part_ref, bf16[256,256]{1,0:T(8,128)(2,1)S(1)} %get-tuple-element.28.refs_0_, bf16[256,256]{1,0:T(8,128)(2,1)S(1)} %collective-permute-done.8.refs_1_, ...), custom_call_target="tpu_custom_call" | custom-call | flops 1073741824 | bytes 5242880 | tf_op jit(solution)/shard_map/give/pallas_call | solution.py:267
  176.2 5.1 %keep.1 = f32[4,256,512]{2,1,0:T(8,128)} custom-call(bf16[1024,256]{1,0:T(8,128)(2,1)S(1)} %copy-done.1, bf16[4,8,256,512]{3,2,1,0:T(8,128)(2,1)} %bitcast.31), custom_call_target="tpu_custom_call" | custom-call | flops 1073741824 | bytes 5242880 | tf_op jit(solution)/shard_map/keep/pallas_call | solution.py:284
  183.4 2.5 %collective-permute-start.14 = (bf16[256,512]{1,0:T(8,128)(2,1)S(1)}, bf16[256,512]{1,0:T(8,128)(2,1)S(1)}, u32[]{:S(2)}, u32[]{:S(2)}) collective-permute-start(bf16[256,512]{1,0:T(8,128)(2,1)S(1)} %get-tuple-element.38), channel_id=1, source_target_pairs={{0,6},{2,0},{4,2},{6,4},{1,7},{3,1},{5,3},{7,5},{8,14},{10,8},{12,... | collective-permute-start | bytes 786440 | tf_op jit(solution)/shard_map/ppermute | solution.py:32
  188.3 8.9 %collective-permute-done.14 = bf16[256,512]{1,0:T(8,128)(2,1)S(1)} collective-permute-done((bf16[256,512]{1,0:T(8,128)(2,1)S(1)}, bf16[256,512]{1,0:T(8,128)(2,1)S(1)}, u32[]{:S(2)}, u32[]{:S(2)}) %collective-permute-start.14) | collective-permute-done | bytes 262176 | tf_op jit(solution)/shard_map/ppermute | solution.py:32
  197.2 3.2 %collective-permute-done.13 = bf16[256,512]{1,0:T(8,128)(2,1)S(1)} collective-permute-done((bf16[256,512]{1,0:T(8,128)(2,1)S(1)}, bf16[256,512]{1,0:T(8,128)(2,1)S(1)}, u32[]{:S(2)}, u32[]{:S(2)}) %collective-permute-start.13) | collective-permute-done | bytes 262176 | tf_op jit(solution)/shard_map/ppermute | solution.py:32
  (43 shorter events, 20.8 us)
Async XLA Ops:
  7.2 65.6 %all-gather.5.cloned.1.call-start = ((), (), s32[]{:S(2)}) async-start(), calls=%async_computation.7 | async-start | bytes 8650752 | tf_op jit(solution)/shard_map/all_gather | solution.py:299
  7.9 161.2 %all-gather.7.cloned.1.call-start = ((), (), s32[]{:S(2)}) async-start(), calls=%async_computation.8 | async-start | bytes 10485760 | tf_op jit(solution)/shard_map/all_gather | solution.py:302
  18.3 10.1 %collective-permute-start = (bf16[4,256,128]{2,1,0:T(8,128)(2,1)S(1)}, bf16[4,256,128]{2,1,0:T(8,128)(2,1)S(1)}, u32[]{:S(2)}, u32[]{:S(2)}) collective-permute-start(bf16[4,256,128]{2,1,0:T(8,128)(2,1)S(1)} %all_to_all.35.refs_0_), channel_id=1, source_target_pairs={{0,32},{32,64},{64,96},{96,128},{128,160},{160,192},{192,224},{224... | collective-permute-start | bytes 786440 | tf_op jit(solution)/shard_map/ppermute | solution.py:32
  20.0 8.5 %collective-permute-start.1 = (bf16[4,256,128]{2,1,0:T(8,128)(2,1)S(1)}, bf16[4,256,128]{2,1,0:T(8,128)(2,1)S(1)}, u32[]{:S(2)}, u32[]{:S(2)}) collective-permute-start(bf16[4,256,128]{2,1,0:T(8,128)(2,1)S(1)} %all_to_all.35.refs_0_), channel_id=1, source_target_pairs={{0,224},{32,0},{64,32},{96,64},{128,96},{160,128},{192,160},{224,1... | collective-permute-start | bytes 786440 | tf_op jit(solution)/shard_map/ppermute | solution.py:32
  28.5 6.4 %collective-permute-start.2 = (bf16[4,256,128]{2,1,0:T(8,128)(2,1)S(1)}, bf16[4,256,128]{2,1,0:T(8,128)(2,1)S(1)}, u32[]{:S(2)}, u32[]{:S(2)}) collective-permute-start(bf16[4,256,128]{2,1,0:T(8,128)(2,1)S(1)} %collective-permute-done.refs_1_), channel_id=1, source_target_pairs={{0,32},{32,64},{64,96},{96,128},{128,160},{160,192},{192,224},{224... | collective-permute-start | bytes 786440 | tf_op jit(solution)/shard_map/ppermute | solution.py:32
  28.5 6.4 %collective-permute-start.3 = (bf16[4,256,128]{2,1,0:T(8,128)(2,1)S(1)}, bf16[4,256,128]{2,1,0:T(8,128)(2,1)S(1)}, u32[]{:S(2)}, u32[]{:S(2)}) collective-permute-start(bf16[4,256,128]{2,1,0:T(8,128)(2,1)S(1)} %collective-permute-done.1.refs_2_), channel_id=1, source_target_pairs={{0,224},{32,0},{64,32},{96,64},{128,96},{160,128},{192,160},{224,1... | collective-permute-start | bytes 786440 | tf_op jit(solution)/shard_map/ppermute | solution.py:32
  34.9 6.4 %collective-permute-start.4 = (bf16[4,256,128]{2,1,0:T(8,128)(2,1)S(1)}, bf16[4,256,128]{2,1,0:T(8,128)(2,1)S(1)}, u32[]{:S(2)}, u32[]{:S(2)}) collective-permute-start(bf16[4,256,128]{2,1,0:T(8,128)(2,1)S(1)} %collective-permute-done.2.refs_3_), channel_id=1, source_target_pairs={{0,32},{32,64},{64,96},{96,128},{128,160},{160,192},{192,224},{224... | collective-permute-start | bytes 786440 | tf_op jit(solution)/shard_map/ppermute | solution.py:32
  34.9 6.5 %collective-permute-start.5 = (bf16[4,256,128]{2,1,0:T(8,128)(2,1)S(1)}, bf16[4,256,128]{2,1,0:T(8,128)(2,1)S(1)}, u32[]{:S(2)}, u32[]{:S(2)}) collective-permute-start(bf16[4,256,128]{2,1,0:T(8,128)(2,1)S(1)} %collective-permute-done.3.refs_4_), channel_id=1, source_target_pairs={{0,224},{32,0},{64,32},{96,64},{128,96},{160,128},{192,160},{224,1... | collective-permute-start | bytes 786440 | tf_op jit(solution)/shard_map/ppermute | solution.py:32
  41.4 5.7 %collective-permute-start.6 = (bf16[2,256,128]{2,1,0:T(8,128)(2,1)S(1)}, bf16[2,256,128]{2,1,0:T(8,128)(2,1)S(1)}, u32[]{:S(2)}, u32[]{:S(2)}) collective-permute-start(bf16[2,256,128]{2,1,0:T(8,128)(2,1)S(1)} %slice.27), channel_id=1, source_target_pairs={{0,32},{32,64},{64,96},{96,128},{128,160},{160,192},{192,224},{224... | collective-permute-start | bytes 393224 | tf_op jit(solution)/shard_map/ppermute | solution.py:32
  41.5 5.6 %collective-permute-start.7 = (bf16[2,256,128]{2,1,0:T(8,128)(2,1)S(1)}, bf16[2,256,128]{2,1,0:T(8,128)(2,1)S(1)}, u32[]{:S(2)}, u32[]{:S(2)}) collective-permute-start(bf16[2,256,128]{2,1,0:T(8,128)(2,1)S(1)} %slice.28), channel_id=1, source_target_pairs={{0,224},{32,0},{64,32},{96,64},{128,96},{160,128},{192,160},{224,1... | collective-permute-start | bytes 393224 | tf_op jit(solution)/shard_map/ppermute | solution.py:32
  72.7 3.4 %copy-start = (bf16[8192,512]{1,0:T(8,128)(2,1)S(1)}, bf16[8192,512]{1,0:T(8,128)(2,1)}, u32[]{:S(2)}) copy-start(bf16[8192,512]{1,0:T(8,128)(2,1)} %all-gather.5.cloned.1.call-done) | copy-start | bytes 25165828
  148.2 20.9 %all-to-all-start.6 = ((f32[32,8,128]{2,1,0:T(8,128)}), f32[32,8,128]{2,1,0:T(8,128)S(1)}, u32[]{:S(2)}, u32[]{:S(2)}) async-start(f32[32,8,128]{2,1,0:T(8,128)} %get-tuple-element.27), calls=%async_computation.6 | async-start | bytes 262144 | tf_op jit(solution)/shard_map/all_to_all | solution.py:313
  152.1 17.1 %collective-permute-start.8 = (bf16[256,256]{1,0:T(8,128)(2,1)S(1)}, bf16[256,256]{1,0:T(8,128)(2,1)S(1)}, u32[]{:S(2)}, u32[]{:S(2)}) collective-permute-start(bf16[256,256]{1,0:T(8,128)(2,1)S(1)} %get-tuple-element.29), channel_id=1, source_target_pairs={{0,8},{8,16},{16,24},{24,0},{1,9},{9,17},{17,25},{25,1},{2,10},{10... | collective-permute-start | bytes 393224 | tf_op jit(solution)/shard_map/ppermute | solution.py:32
  153.3 15.9 %collective-permute-start.9 = (bf16[256,256]{1,0:T(8,128)(2,1)S(1)}, bf16[256,256]{1,0:T(8,128)(2,1)S(1)}, u32[]{:S(2)}, u32[]{:S(2)}) collective-permute-start(bf16[256,256]{1,0:T(8,128)(2,1)S(1)} %get-tuple-element.30), channel_id=1, source_target_pairs={{0,16},{8,24},{16,0},{24,8},{1,17},{9,25},{17,1},{25,9},{2,18},{10... | collective-permute-start | bytes 393224 | tf_op jit(solution)/shard_map/ppermute | solution.py:32
  155.7 13.5 %collective-permute-start.10 = (bf16[256,256]{1,0:T(8,128)(2,1)S(1)}, bf16[256,256]{1,0:T(8,128)(2,1)S(1)}, u32[]{:S(2)}, u32[]{:S(2)}) collective-permute-start(bf16[256,256]{1,0:T(8,128)(2,1)S(1)} %get-tuple-element.31), channel_id=1, source_target_pairs={{0,24},{8,0},{16,8},{24,16},{1,25},{9,1},{17,9},{25,17},{2,26},{10... | collective-permute-start | bytes 393224 | tf_op jit(solution)/shard_map/ppermute | solution.py:32
  174.3 7.0 %collective-permute-start.11 = (bf16[4,256,512]{2,1,0:T(8,128)(2,1)}, bf16[4,256,512]{2,1,0:T(8,128)(2,1)S(1)}, u32[]{:S(2)}, u32[]{:S(2)}) collective-permute-start(bf16[4,256,512]{2,1,0:T(8,128)(2,1)} %get-tuple-element.34), channel_id=1, source_target_pairs={{0,1},{1,0},{2,3},{3,2},{4,5},{5,4},{6,7},{7,6},{8,9},{9,8},{10,11... | collective-permute-start | bytes 3145736 | tf_op jit(solution)/shard_map/ppermute | solution.py:32
  175.2 1.0 copy-start.1
  181.3 19.1 %copy-start.2 = (bf16[256,512]{1,0:T(8,128)(2,1)S(1)}, bf16[256,512]{1,0:T(8,128)(2,1)}, u32[]{:S(2)}) copy-start(bf16[256,512]{1,0:T(8,128)(2,1)} %param.2) | copy-start | bytes 786436
  183.4 13.7 %collective-permute-start.14 = (bf16[256,512]{1,0:T(8,128)(2,1)S(1)}, bf16[256,512]{1,0:T(8,128)(2,1)S(1)}, u32[]{:S(2)}, u32[]{:S(2)}) collective-permute-start(bf16[256,512]{1,0:T(8,128)(2,1)S(1)} %get-tuple-element.38), channel_id=1, source_target_pairs={{0,6},{2,0},{4,2},{6,4},{1,7},{3,1},{5,3},{7,5},{8,14},{10,8},{12,... | collective-permute-start | bytes 786440 | tf_op jit(solution)/shard_map/ppermute | solution.py:32
  186.0 14.4 %collective-permute-start.13 = (bf16[256,512]{1,0:T(8,128)(2,1)S(1)}, bf16[256,512]{1,0:T(8,128)(2,1)S(1)}, u32[]{:S(2)}, u32[]{:S(2)}) collective-permute-start(bf16[256,512]{1,0:T(8,128)(2,1)S(1)} %get-tuple-element.39), channel_id=1, source_target_pairs={{0,2},{2,4},{4,6},{6,0},{1,3},{3,5},{5,7},{7,1},{8,10},{10,12},{12... | collective-permute-start | bytes 786440 | tf_op jit(solution)/shard_map/ppermute | solution.py:32
  186.0 14.4 %collective-permute-start.12 = (bf16[256,512]{1,0:T(8,128)(2,1)S(1)}, bf16[256,512]{1,0:T(8,128)(2,1)S(1)}, u32[]{:S(2)}, u32[]{:S(2)}) collective-permute-start(bf16[256,512]{1,0:T(8,128)(2,1)S(1)} %get-tuple-element.37), channel_id=1, source_target_pairs={{0,4},{2,6},{4,0},{6,2},{1,5},{3,7},{5,1},{7,3},{8,12},{10,14},{12... | collective-permute-start | bytes 786440 | tf_op jit(solution)/shard_map/ppermute | solution.py:32
Sparse Core Ops, SparseCore 0:
  10.6 62.1 all-gather.4
  74.5 94.5 all-gather.6

commit v4 on v3

--- a/solution.py
+++ b/solution.py
@@ -19,6 +19,7 @@
 TALL = ROWS * X
 CHUNKS = TALL // 128
 GROUP = X * Y * C
+CUT = ROWS // 2
 TOTAL = 8192
 UNIT = LOG2E / (WIDTH * EPS)
 LOG2N = math.log2(TOTAL)
@@ -36,14 +37,34 @@
     return pltpu.CompilerParams(vmem_limit_bytes=mib * 2**20)
 
 
-def ring_z(x):
-    forward = backward = x
-    got = [x]
-    for _ in range(1, Z // 2):
-        forward, backward = shift(forward, "z", 1), shift(backward, "z", -1)
-        got += [forward, backward]
-    cut = x.shape[0] // 2
-    return got + [shift(forward[:cut], "z", 1), shift(backward[cut:], "z", -1)]
+def both_ways(forward, backward, axis):
+    return shift(forward, axis, 1), shift(backward, axis, -1)
+
+
+def halves(forward, backward, axis):
+    cut = forward.shape[0] // 2
+    return both_ways(forward[:cut], backward[cut:], axis)
+
+
+def gather(noise, data):
+    hold = lax.optimization_barrier
+    across = shift(noise, "x", 1), shift(noise, "x", -1), shift(noise, "x", 2)
+    swapped = lax.all_to_all(data.reshape(X, QUARTER, SLICE), "x", 0, 0)
+    swapped, *across = hold((swapped, *across))
+    block = jnp.stack([noise, *across])
+    y1 = both_ways(block, block, "y")
+    z1 = both_ways(swapped, swapped, "z")
+    z2 = both_ways(*z1, "z")
+    y1, z2 = hold((y1, z2))
+    y2 = halves(*y1, "y")
+    z3 = both_ways(*z2, "z")
+    mine = [block, *y1]
+    theirs = [shift(block, "core", 1)]
+    y2, z3, theirs = hold((y2, z3, theirs))
+    z4 = halves(*z3, "z")
+    mine += y2
+    theirs += [shift(part, "core", 1) for part in mine[1:]]
+    return mine + theirs, [swapped, *z1, *z2, *z3, *z4]
 
 
 def squares(ref, pieces):
@@ -102,37 +123,80 @@
     return pl.ds(r * 128, 128)
 
 
-def score_kernel(place, data_ref, sq_ref, noise_ref, q_ref, out_ref, sqn_ref, lse_ref):
-    data = jnp.concatenate([data_ref[slot_of(place, p)] for p in range(Y * C)], axis=1)
-    for n in range(X):
-        block = jnp.concatenate([noise_ref[n, p] for p in range(Y * C)], axis=1)
-        gram = lax.dot_general(data, block, (((1,), (1,)), ((), ())), preferred_element_type=F32)
-        gram = gram * (2.0 * UNIT)
-        q_ref[:, pl.ds(n * ROWS, ROWS)] = gram
-        t = gram - UNIT * jnp.concatenate([sq_ref[...]] * 2, axis=1)
-        rows = lse(t, 0)
-        lse_ref[pl.ds(2 * n, 1), :] = rows[:, :128]
-        lse_ref[pl.ds(2 * n + 1, 1), :] = rows[:, 128:]
-    out_ref[...] = jnp.broadcast_to(lse_ref[...][None], (GROUP, CHUNKS, 128))
-    x = place[1]
-    views = [(x, p, slice(None), pl.ds(lane, 128)) for p in range(Y * C) for lane in range(0, SHARE, 128)]
-    sqn_ref[...] = jnp.sum(jnp.transpose(squares(noise_ref, views)), axis=0, keepdims=True)
-
-
-def score(place, data, sq, noise):
-    return pl.pallas_call(
-        score_kernel,
+def scored(data_ref, order, blocks, sq_ref):
+    data = jnp.concatenate([data_ref[p] for p in order], axis=1)
+    gram = lax.dot_general(
+        data, jnp.concatenate(blocks, axis=1), (((1,), (1,)), ((), ())), preferred_element_type=F32
+    ) * (2.0 * UNIT)
+    return gram, lse(gram - UNIT * jnp.concatenate([sq_ref[...]] * (gram.shape[1] // 128), axis=1), 0)
+
+
+def low_kernel(place, data_ref, sq_ref, *refs):
+    ins, (q_ref, lse_ref, sqn_ref) = refs[:-3], refs[-3:]
+    blocks, order = [], []
+    for core in range(C):
+        own, before, after, top, low = ins[5 * core : 5 * core + 5]
+        for s, part in ((0, own), (Y - 1, before), (1, after)):
+            blocks.append(part[...].reshape(X * CUT, SHARE))
+            order.append(core * Y + s)
+        blocks.append(jnp.concatenate([top[...], low[...]], axis=0).reshape(X * CUT, SHARE))
+        order.append(core * Y + Y // 2)
+    gram, rows = scored(data_ref, order, blocks, sq_ref)
+    for n, rel in enumerate((0, -1, 1, 2)):
+        block = lax.rem(place[1] + rel + X, X)
+        q_ref[:, pl.ds(pl.multiple_of(block * 128, 128), 128)] = gram[:, n * 128 : (n + 1) * 128]
+        lse_ref[pl.ds(block, 1), :] = rows[:, n * 128 : (n + 1) * 128]
+    total = None
+    for core in range(C):
+        own, before, after, top, _ = ins[5 * core : 5 * core + 5]
+        for part in (own, before, after, top):
+            more = squares(part, [(0, slice(None), pl.ds(lane, 128)) for lane in range(0, SHARE, 128)])
+            total = more if total is None else total + more
+    sqn_ref[...] = jnp.sum(jnp.transpose(total), axis=0, keepdims=True)
+
+
+def low_score(place, data, sq, parts):
+    return pl.pallas_call(
+        low_kernel,
+        out_shape=(
+            jax.ShapeDtypeStruct((QUARTER, X * CUT), F32),
+            jax.ShapeDtypeStruct((X, 128), F32),
+            jax.ShapeDtypeStruct((1, 128), F32),
+        ),
+        in_specs=[SMEM] + [VMEM] * (2 + len(parts)),
+        out_specs=(VMEM,) * 3,
+        compiler_params=params(24),
+        cost_estimate=pl.CostEstimate(flops=QUARTER * TALL * WIDTH, bytes_accessed=6 * 2**20, transcendentals=0),
+        name="low_score",
+    )(place, data, sq, *parts)
+
+
+def high_kernel(place, data_ref, sq_ref, noise_ref, low_ref, low_lse_ref, low_sqn_ref, q_ref, out_ref, sqn_ref):
+    order = [slot_of(place, p) for p in range(Y * C)]
+    blocks = [noise_ref[:, p].reshape(X * CUT, SHARE) for p in range(Y * C)]
+    gram, rows = scored(data_ref, order, blocks, sq_ref)
+    q_ref[:, : X * CUT] = gram
+    q_ref[:, X * CUT :] = low_ref[...]
+    parts = [rows[:, n * 128 : (n + 1) * 128] for n in range(X)] + [low_lse_ref[...]]
+    out_ref[...] = jnp.broadcast_to(jnp.concatenate(parts, axis=0)[None], (GROUP, CHUNKS, 128))
+    views = [(place[1], p, slice(None), pl.ds(lane, 128)) for p in range(Y * C) for lane in range(0, SHARE, 128)]
+    own = jnp.sum(jnp.transpose(squares(noise_ref, views)), axis=0, keepdims=True)
+    sqn_ref[...] = jnp.concatenate([own, low_sqn_ref[...]], axis=0)
+
+
+def score(place, data, sq, noise, low):
+    return pl.pallas_call(
+        high_kernel,
         out_shape=(
             jax.ShapeDtypeStruct((QUARTER, TALL), F32),
             jax.ShapeDtypeStruct((GROUP, CHUNKS, 128), F32),
-            jax.ShapeDtypeStruct((1, ROWS), F32),
+            jax.ShapeDtypeStruct((2, 128), F32),
         ),
-        in_specs=[SMEM] + [VMEM] * 3,
+        in_specs=[SMEM] + [VMEM] * 6,
         out_specs=(VMEM,) * 3,
-        scratch_shapes=[pltpu.VMEM((CHUNKS, 128), F32)],
-        compiler_params=params(32),
+        compiler_params=params(24),
         name="score",
-    )(place, data, sq, noise)
+    )(place, data, sq, noise, *low)
 
 
 def to_column(g):
@@ -200,8 +264,8 @@
     for by in range(X):
         block = lax.rem(place[1] + by, X)
         for h in range(2):
-            lanes = pl.ds(pl.multiple_of(block * ROWS + h * 128, 128), 128)
-            w = jnp.exp2((q_ref[:, lanes] + f_ref[pl.ds(2 * block + h, 1), :]) - column)
+            lanes = pl.ds(pl.multiple_of((h * X + block) * 128, 128), 128)
+            w = jnp.exp2((q_ref[:, lanes] + f_ref[pl.ds(h * X + block, 1), :]) - column)
             w_refs[by][:, pl.ds(h * 128, 128)] = w.astype(BF16)
 
 
@@ -240,16 +304,17 @@
         parts = jnp.stack([part_ref[k * X + n] for k in range(Z)])
         top = jnp.max(parts, axis=0)
         total = top + jnp.log2(jnp.sum(jnp.exp2(parts - top[None]), axis=0))
-        factor = to_column(jnp.exp2(part_ref[z * X + n] - total))
-        rows = pl.ds(pl.multiple_of(n * QUARTER, QUARTER), QUARTER)
+        factor = jnp.exp2(part_ref[z * X + n] - total)
+        factor = jnp.concatenate([factor[0:1], factor[1:2]], axis=1)
+        lanes = pl.ds(pl.multiple_of(n * QUARTER, QUARTER), QUARTER)
         for h in range(2):
-            w = w_refs[by][:, pl.ds(h * 128, 128)].astype(F32) * factor
-            w_ref[rows, pl.ds(h * 128, 128)] = w.astype(BF16)
+            w = jnp.transpose(w_refs[by][:, pl.ds(h * 128, 128)].astype(F32)) * factor
+            w_ref[pl.ds(h * 128, 128), lanes] = w.astype(BF16)
 
 
 def transport(w_ref, data_ref, out_ref):
     block = jnp.concatenate([data_ref[n, 0] for n in range(X)], axis=0)
-    total = lax.dot_general(w_ref[...], block, (((0,), (0,)), ((), ())), preferred_element_type=F32)
+    total = jnp.dot(w_ref[...], block, preferred_element_type=F32)
     out_ref[0] = total.astype(out_ref.dtype)
 
 
@@ -269,7 +334,7 @@
         grid=(Y,),
         out_shape=(
             jax.ShapeDtypeStruct((Y, ROWS, SHARE), BF16),
-            jax.ShapeDtypeStruct((COUNT, ROWS), BF16),
+            jax.ShapeDtypeStruct((ROWS, COUNT), BF16),
             jax.ShapeDtypeStruct((2 * X, 128), F32),
         ),
         in_specs=[SMEM] + [VMEM] * (1 + X) + [half_of(1)],
@@ -296,11 +361,12 @@
 def body(noise, data):
     z, x, y, c = (lax.axis_index(a) for a in ("z", "x", "y", "core"))
     place = jnp.stack([z, x, y, c]).astype(jnp.int32)
-    noise_all = lax.all_gather(noise, ("x", "y", "core")).reshape(X, Y * C, ROWS, SHARE)
-    swapped = lax.all_to_all(data.reshape(X, QUARTER, SLICE), "x", 0, 0)
-    samples, sq = assemble(place, ring_z(swapped))
+    noise_all = lax.all_gather(noise[:CUT], ("x", "y", "core")).reshape(X, Y * C, CUT, SHARE)
+    noise_low, data_parts = gather(noise[CUT:], data)
+    samples, sq = assemble(place, data_parts)
     data_all = lax.all_gather(samples, "x")
-    q, rows, sq_noise = score(place, samples, sq, noise_all)
+    low = low_score(place, samples, sq, noise_low)
+    q, rows, sq_noise = score(place, samples, sq, noise_all, low)
     for step in range(ITERS):
         if step:
             rows = noise_lse(q, columns)
@@ -319,8 +385,8 @@
     for by in (2, 1, 3):
         target = target + shift(both[by].astype(BF16), "y", by).astype(F32)
     velocity = (target - noise.astype(F32)).astype(BF16)
-    own = lax.dynamic_slice_in_dim(f, 2 * x, 2, 0).reshape(ROWS)
-    pot_f = own * (EPS / LOG2E) + sq_noise[0] / WIDTH
+    own = lax.dynamic_index_in_dim(f.reshape(2, X, 128), x, 1, False)
+    pot_f = (own * (EPS / LOG2E) + sq_noise / WIDTH).reshape(ROWS)
     return pot_f, pot_g.reshape(COUNT), velocity
 
 

time: 209 us -> 209 us (level)
  starting transfers between devices: 27.7 us -> 54 us
  waiting for transfers between devices: 63.2 us -> 37.2 us
  blocking collectives: 74.1 us -> 63.8 us
  local copies, waits for them, and re-layouts: 4.5 us -> 12.6 us
  Pallas kernels: 21 us -> 23.1 us
    all_gather x1, waiting for transfers between devices: 23.3 us -> 0.02 us  [body(): lax.all_gather(noise[:CUT], ('x', 'y', 'core'))]
    ppermute x15 -> x27, starting transfers between devices: 23.8 us -> 45.3 us  [shift(): return lax.ppermute(x, axis, [(j, (j + by) % n) for j in range(n)])]
    all_gather x1, waiting for transfers between devices: 12.3 us -> 0.01 us  [body(): data_all = lax.all_gather(samples, 'x')]
    all_to_all x1 -> x0, blocking collectives: 10.4 us -> none  [body(): swapped = lax.all_to_all(data.reshape(X, QUARTER, SLICE), 'x', 0, 0)]
    ppermute x15 -> x27, waiting for transfers between devices: 26.9 us -> 37.1 us  [shift(): return lax.ppermute(x, axis, [(j, (j + by) % n) for j in range(n)])]
    unnamed x6 -> x26, local copies, waits for them, and re-layouts: 4.43 us -> 9.5 us
    all_to_all x0 -> x1, starting transfers between devices: none -> 4.85 us  [gather(): swapped = lax.all_to_all(data.reshape(X, QUARTER, SLICE), 'x', 0, 0)]
    slice x2 -> x5, local copies, waits for them, and re-layouts: 0.02 us -> 2.99 us  [the longest x1 1.64 us: body(): noise[:CUT]]
  transfers between devices with their start and end apart: 18 -> 31, of which waited for: 8 -> 16; matrix products, arithmetic and copies ran while one was open for 0% -> 1% of each run, Pallas kernels for 8% -> 9%
where the time goes in v4:
time: 209 us
  blocking collectives  63.8 us (31%)
  starting transfers between devices  54 us (26%)
  waiting for transfers between devices  37.2 us (18%)
  Pallas kernels  23.1 us (11%)
  between operations  14.2 us (7%)
  local copies, waits for them, and re-layouts  12.6 us (6%)
  other arithmetic  3.69 us (2%)
    ppermute x27, starting transfers between devices, shift(): return lax.ppermute(x, axis, [(j, (j + by) % n) for j in range(n)])  45.3 us
    all_to_all x3, blocking collectives, body(): parts = lax.all_to_all(rows, ('x', 'y', 'core'), 0, 0)  41.4 us
    ppermute x27, waiting for transfers between devices, shift(): return lax.ppermute(x, axis, [(j, (j + by) % n) for j in range(n)])  37.1 us
    all_to_all x2, blocking collectives, body(): columns = lax.all_to_all(columns, 'z', 0, 0)  22.4 us
    unnamed x26, local copies, waits for them, and re-layouts  9.5 us
    pallas_call x1, Pallas kernels, give(): pl.pallas_call(give_kernel, grid=(Y,), out_shape=(jax.ShapeDtypeStruct((Y...  5.09 us
    pallas_call x1, Pallas kernels, keep(): pl.pallas_call(transport, grid=(Y,), out_shape=jax.ShapeDtypeStruct((Y, R...  5.01 us
    all_to_all x1, starting transfers between devices, gather(): swapped = lax.all_to_all(data.reshape(X, QUARTER, SLICE), 'x', 0, 0)  4.85 us
  transfers between devices with their start and end apart: 31, of which 16 were waited for; matrix products, arithmetic and copies ran while one was open for 1% of the time, Pallas kernels for 9%

profile of v4, /device:TPU:1, one launch (start us, length us, event | category | flops | bytes accessed | tf_op | source)
XLA Modules:
  0.0 208.6 jit_solution(8219179907949259925)
XLA Ops:
  8.9 4.9 %all-to-all-start = ((bf16[4,256,128]{2,1,0:T(8,128)(2,1)}), bf16[4,256,128]{2,1,0:T(8,128)(2,1)S(1)}, u32[]{:S(2)}, u32[]{:S(2)}) async-start(bf16[4,256,128]{2,1,0:T(8,128)(2,1)} %bitcast.43), calls=%async_computation | async-start | bytes 524288 | tf_op jit(solution)/shard_map/all_to_all | solution.py:52
  18.2 3.0 %collective-permute-done = bf16[128,512]{1,0:T(8,128)(2,1)S(1)} collective-permute-done((bf16[128,512]{1,0:T(8,128)(2,1)S(1)}, bf16[128,512]{1,0:T(8,128)(2,1)S(1)}, u32[]{:S(2)}, u32[]{:S(2)}) %collective-permute-start) | collective-permute-done | bytes 131104 | tf_op jit(solution)/shard_map/ppermute | solution.py:33
  21.2 2.9 %collective-permute-done.2 = bf16[128,512]{1,0:T(8,128)(2,1)S(1)} collective-permute-done((bf16[128,512]{1,0:T(8,128)(2,1)S(1)}, bf16[128,512]{1,0:T(8,128)(2,1)S(1)}, u32[]{:S(2)}, u32[]{:S(2)}) %collective-permute-start.2) | collective-permute-done | bytes 131104 | tf_op jit(solution)/shard_map/ppermute | solution.py:33
  29.4 3.9 %collective-permute-start.4 = (bf16[4,256,128]{2,1,0:T(8,128)(2,1)S(1)}, bf16[4,256,128]{2,1,0:T(8,128)(2,1)S(1)}, u32[]{:S(2)}, u32[]{:S(2)}) collective-permute-start(bf16[4,256,128]{2,1,0:T(8,128)(2,1)S(1)} %all-to-all-done.refs_0_), channel_id=1, source_target_pairs={{0,224},{32,0},{64,32},{96,64},{128,96},{160,128},{192,160},{224,1... | collective-permute-start | bytes 786440 | tf_op jit(solution)/shard_map/ppermute | solution.py:33
  36.7 3.5 %collective-permute-start.8 = (bf16[4,256,128]{2,1,0:T(8,128)(2,1)S(1)}, bf16[4,256,128]{2,1,0:T(8,128)(2,1)S(1)}, u32[]{:S(2)}, u32[]{:S(2)}) collective-permute-start(bf16[4,256,128]{2,1,0:T(8,128)(2,1)S(1)} %collective-permute-done.4.refs_2_), channel_id=1, source_target_pairs={{0,224},{32,0},{64,32},{96,64},{128,96},{160,128},{192,160},{224,1... | collective-permute-start | bytes 786440 | tf_op jit(solution)/shard_map/ppermute | solution.py:33
  40.9 3.6 %collective-permute-start.13 = (bf16[4,128,512]{2,1,0:T(8,128)(2,1)S(1)}, bf16[4,128,512]{2,1,0:T(8,128)(2,1)S(1)}, u32[]{:S(2)}, u32[]{:S(2)}) collective-permute-start(bf16[4,128,512]{2,1,0:T(8,128)(2,1)S(1)} %pad_maximum_fusion.refs_0_), channel_id=1, source_target_pairs={{0,1},{1,0},{2,3},{3,2},{4,5},{5,4},{6,7},{7,6},{8,9},{9,8},{10,11... | collective-permute-start | bytes 1572872 | tf_op jit(solution)/shard_map/ppermute | solution.py:33
  44.8 2.7 %collective-permute-start.10 = (bf16[2,128,512]{2,1,0:T(8,128)(2,1)S(1)}, bf16[2,128,512]{2,1,0:T(8,128)(2,1)S(1)}, u32[]{:S(2)}, u32[]{:S(2)}) collective-permute-start(bf16[2,128,512]{2,1,0:T(8,128)(2,1)S(1)} %slice.35), channel_id=1, source_target_pairs={{0,6},{2,0},{4,2},{6,4},{1,7},{3,1},{5,3},{7,5},{8,14},{10,8},{12,... | collective-permute-start | bytes 786440 | tf_op jit(solution)/shard_map/ppermute | solution.py:33
  47.4 2.7 %collective-permute-start.12 = (bf16[4,256,128]{2,1,0:T(8,128)(2,1)S(1)}, bf16[4,256,128]{2,1,0:T(8,128)(2,1)S(1)}, u32[]{:S(2)}, u32[]{:S(2)}) collective-permute-start(bf16[4,256,128]{2,1,0:T(8,128)(2,1)S(1)} %collective-permute-done.8.refs_4_), channel_id=1, source_target_pairs={{0,224},{32,0},{64,32},{96,64},{128,96},{160,128},{192,160},{224,1... | collective-permute-start | bytes 786440 | tf_op jit(solution)/shard_map/ppermute | solution.py:33
  51.1 3.1 %collective-permute-done.11.refs_5_ = bf16[4,256,128]{2,1,0:T(8,128)(2,1)S(1)} collective-permute-done((bf16[4,256,128]{2,1,0:T(8,128)(2,1)S(1)}, bf16[4,256,128]{2,1,0:T(8,128)(2,1)S(1)}, u32[]{:S(2)}, u32[]{:S(2)}) %collective-permute-start.11) | collective-permute-done | bytes 262176 | tf_op jit(solution)/shard_map/ppermute | solution.py:33
  65.6 2.6 %assemble.1 = (bf16[8,256,512]{2,1,0:T(8,128)(2,1)}, f32[256,128]{1,0:T(8,128)S(1)}) custom-call(s32[4]{0:T(128)S(1)} %pad_add_fusion.place, bf16[4,256,128]{2,1,0:T(8,128)(2,1)S(1)} %all-to-all-done.refs_0_, bf16[4,256,128]{2,1,0:T(8,128)(2,1)S(1)} %collective-permute-done.3.refs_1_, bf16[4,256,128]{2,1,0:T(8,128)(2,1)S(1)} %copy-done.5, ...), custom_call_target="tpu_custom_call" | custom-call | flops 2097152 | bytes 4194304 | tf_op jit(solution)/shard_map/assemble/pallas_call | solution.py:100
  68.2 7.0 %collective-permute-start.16 = (bf16[4,128,512]{2,1,0:T(8,128)(2,1)S(1)}, bf16[4,128,512]{2,1,0:T(8,128)(2,1)S(1)}, u32[]{:S(2)}, u32[]{:S(2)}) collective-permute-start(bf16[4,128,512]{2,1,0:T(8,128)(2,1)S(1)} %collective-permute-done.5.refs_1_), channel_id=1, source_target_pairs={{0,1},{1,0},{2,3},{3,2},{4,5},{5,4},{6,7},{7,6},{8,9},{9,8},{10,11... | collective-permute-start | bytes 1572872 | tf_op jit(solution)/shard_map/ppermute | solution.py:33
  79.3 3.1 %low_score.1 = (f32[256,512]{1,0:T(8,128)S(1)}, f32[4,128]{1,0:T(4,128)S(1)}, f32[1,128]{1,0:T(1,128)S(1)}) custom-call(s32[4]{0:T(128)S(1)} %pad_add_fusion.place, bf16[8,256,512]{2,1,0:T(8,128)(2,1)} %get-tuple-element.45.data_ref, f32[256,128]{1,0:T(8,128)S(1)} %get-tuple-element.46.sq_ref, bf16[4,128,512]{2,1,0:T(8,128)(2,1)S(1)} %pad_maximum_fusion.refs_0_, ...), custom_call_target="tpu_custom_call" | custom-call | flops 1073741824 | bytes 6291456 | tf_op jit(solution)/shard_map/low_score/pallas_call | solution.py:159
  84.8 3.4 %score.1 = (f32[256,1024]{1,0:T(8,128)S(1)}, f32[32,8,128]{2,1,0:T(8,128)S(1)}, f32[2,128]{1,0:T(2,128)S(1)}) custom-call(s32[4]{0:T(128)S(1)} %pad_add_fusion.place, bf16[8,256,512]{2,1,0:T(8,128)(2,1)} %get-tuple-element.45.data_ref, f32[256,128]{1,0:T(8,128)S(1)} %get-tuple-element.46.sq_ref, bf16[4,8,128,512]{3,2,1,0:T(8,128)(2,1)S(1)} %bitcast.39, ...), custom_call_target="tpu_custom_call" | custom-call | tf_op jit(solution)/shard_map/score/pallas_call | solution.py:188
  88.2 13.6 %all_to_all.35.part_ref = f32[32,8,128]{2,1,0:T(8,128)S(1)} all-to-all(f32[32,8,128]{2,1,0:T(8,128)S(1)} %get-tuple-element.54), channel_id=1, replica_groups=mesh['z'=8,'x'=4,'y'=4,'core'=2] {'x','y','core'}, dimensions={0} | all-to-all | bytes 262144 | tf_op jit(solution)/shard_map/all_to_all | solution.py:373
  102.6 13.2 %all_to_all.36.part_ref = f32[8,8,128]{2,1,0:T(8,128)S(1)} all-to-all(f32[8,8,128]{2,1,0:T(8,128)S(1)} %get-tuple-element.55), channel_id=1, replica_groups=mesh['z'=8,'x'=4,'y'=4,'core'=2] {'z'}, dimensions={0} | all-to-all | bytes 65536 | tf_op jit(solution)/shard_map/all_to_all | solution.py:376
  116.2 14.0 %all_to_all.37.part_ref = f32[32,8,128]{2,1,0:T(8,128)S(1)} all-to-all(f32[32,8,128]{2,1,0:T(8,128)S(1)} %noise_lse.2), channel_id=1, replica_groups=mesh['z'=8,'x'=4,'y'=4,'core'=2] {'x','y','core'}, dimensions={0} | all-to-all | bytes 262144 | tf_op jit(solution)/shard_map/all_to_all | solution.py:373
  131.0 9.2 %all_to_all.38.part_ref = f32[8,8,128]{2,1,0:T(8,128)S(1)} all-to-all(f32[8,8,128]{2,1,0:T(8,128)S(1)} %get-tuple-element.56), channel_id=1, replica_groups=mesh['z'=8,'x'=4,'y'=4,'core'=2] {'z'}, dimensions={0} | all-to-all | bytes 65536 | tf_op jit(solution)/shard_map/all_to_all | solution.py:376
  140.6 13.7 %all_to_all.39.part_ref = f32[32,8,128]{2,1,0:T(8,128)S(1)} all-to-all(f32[32,8,128]{2,1,0:T(8,128)S(1)} %noise_lse.3), channel_id=1, replica_groups=mesh['z'=8,'x'=4,'y'=4,'core'=2] {'x','y','core'}, dimensions={0} | all-to-all | bytes 262144 | tf_op jit(solution)/shard_map/all_to_all | solution.py:373
  155.9 3.9 %all-to-all-start.6 = ((f32[32,8,128]{2,1,0:T(8,128)}), f32[32,8,128]{2,1,0:T(8,128)S(1)}, u32[]{:S(2)}, u32[]{:S(2)}) async-start(f32[32,8,128]{2,1,0:T(8,128)} %get-tuple-element.59), calls=%async_computation.6 | async-start | bytes 262144 | tf_op jit(solution)/shard_map/all_to_all | solution.py:379
  167.0 3.9 %collective-permute-done.21.refs_2_ = bf16[256,256]{1,0:T(8,128)(2,1)S(1)} collective-permute-done((bf16[256,256]{1,0:T(8,128)(2,1)S(1)}, bf16[256,256]{1,0:T(8,128)(2,1)S(1)}, u32[]{:S(2)}, u32[]{:S(2)}) %collective-permute-start.21) | collective-permute-done | bytes 131104 | tf_op jit(solution)/shard_map/ppermute | solution.py:33
  170.9 5.1 %give.1 = (bf16[4,256,512]{2,1,0:T(8,128)(2,1)}, bf16[256,1024]{1,0:T(8,128)(2,1)}, f32[8,128]{1,0:T(8,128)}) custom-call(s32[4]{0:T(128)S(1)} %pad_add_fusion.place, f32[32,8,128]{2,1,0:T(8,128)S(1)} %all-to-all-done.6.part_ref, bf16[256,256]{1,0:T(8,128)(2,1)S(1)} %get-tuple-element.60.refs_0_, bf16[256,256]{1,0:T(8,128)(2,1)S(1)} %collective-permute-done.20.refs_1_, ...), custom_call_target="tpu_custom_call" | custom-call | flops 1073741824 | bytes 5242880 | tf_op jit(solution)/shard_map/give/pallas_call | solution.py:332
  178.1 5.0 %keep.1 = f32[4,256,512]{2,1,0:T(8,128)} custom-call(bf16[256,1024]{1,0:T(8,128)(2,1)S(1)} %copy-done.1, bf16[4,8,256,512]{3,2,1,0:T(8,128)(2,1)} %bitcast.42), custom_call_target="tpu_custom_call" | custom-call | flops 1073741824 | bytes 5242880 | tf_op jit(solution)/shard_map/keep/pallas_call | solution.py:349
  188.6 4.6 %collective-permute-done.26 = bf16[256,512]{1,0:T(8,128)(2,1)S(1)} collective-permute-done((bf16[256,512]{1,0:T(8,128)(2,1)S(1)}, bf16[256,512]{1,0:T(8,128)(2,1)S(1)}, u32[]{:S(2)}, u32[]{:S(2)}) %collective-permute-start.26) | collective-permute-done | bytes 262176 | tf_op jit(solution)/shard_map/ppermute | solution.py:33
  193.3 7.5 %collective-permute-done.25 = bf16[256,512]{1,0:T(8,128)(2,1)S(1)} collective-permute-done((bf16[256,512]{1,0:T(8,128)(2,1)S(1)}, bf16[256,512]{1,0:T(8,128)(2,1)S(1)}, u32[]{:S(2)}, u32[]{:S(2)}) %collective-permute-start.25) | collective-permute-done | bytes 262176 | tf_op jit(solution)/shard_map/ppermute | solution.py:33
  (93 shorter events, 54.3 us)
Async XLA Ops:
  7.2 75.3 %all-gather.5.cloned.1.call-start = ((), (), s32[]{:S(2)}) async-start(), calls=%async_computation.7 | async-start | bytes 4325376 | tf_op jit(solution)/shard_map/all_gather | solution.py:364
  8.9 15.2 %all-to-all-start = ((bf16[4,256,128]{2,1,0:T(8,128)(2,1)}), bf16[4,256,128]{2,1,0:T(8,128)(2,1)S(1)}, u32[]{:S(2)}, u32[]{:S(2)}) async-start(bf16[4,256,128]{2,1,0:T(8,128)(2,1)} %bitcast.43), calls=%async_computation | async-start | bytes 524288 | tf_op jit(solution)/shard_map/all_to_all | solution.py:52
  13.7 157.2 %all-gather.7.cloned.1.call-start = ((), (), s32[]{:S(2)}) async-start(), calls=%async_computation.8 | async-start | bytes 10485760 | tf_op jit(solution)/shard_map/all_gather | solution.py:367
  13.7 7.4 %collective-permute-start = (bf16[128,512]{1,0:T(8,128)(2,1)S(1)}, bf16[128,512]{1,0:T(8,128)(2,1)S(1)}, u32[]{:S(2)}, u32[]{:S(2)}) collective-permute-start(bf16[128,512]{1,0:T(8,128)(2,1)S(1)} %get-tuple-element.74), channel_id=1, source_target_pairs={{0,8},{8,16},{16,24},{24,0},{1,9},{9,17},{17,25},{25,1},{2,10},{10... | collective-permute-start | bytes 393224 | tf_op jit(solution)/shard_map/ppermute | solution.py:33
  16.4 7.6 %collective-permute-start.2 = (bf16[128,512]{1,0:T(8,128)(2,1)S(1)}, bf16[128,512]{1,0:T(8,128)(2,1)S(1)}, u32[]{:S(2)}, u32[]{:S(2)}) collective-permute-start(bf16[128,512]{1,0:T(8,128)(2,1)S(1)} %get-tuple-element.74), channel_id=1, source_target_pairs={{0,16},{8,24},{16,0},{24,8},{1,17},{9,25},{17,1},{25,9},{2,18},{10... | collective-permute-start | bytes 393224 | tf_op jit(solution)/shard_map/ppermute | solution.py:33
  24.0 10.8 %collective-permute-start.3 = (bf16[4,256,128]{2,1,0:T(8,128)(2,1)S(1)}, bf16[4,256,128]{2,1,0:T(8,128)(2,1)S(1)}, u32[]{:S(2)}, u32[]{:S(2)}) collective-permute-start(bf16[4,256,128]{2,1,0:T(8,128)(2,1)S(1)} %all-to-all-done.refs_0_), channel_id=1, source_target_pairs={{0,32},{32,64},{64,96},{96,128},{128,160},{160,192},{192,224},{224... | collective-permute-start | bytes 786440 | tf_op jit(solution)/shard_map/ppermute | solution.py:33
  26.5 18.0 %collective-permute-start.5 = (bf16[4,128,512]{2,1,0:T(8,128)(2,1)S(1)}, bf16[4,128,512]{2,1,0:T(8,128)(2,1)S(1)}, u32[]{:S(2)}, u32[]{:S(2)}) collective-permute-start(bf16[4,128,512]{2,1,0:T(8,128)(2,1)S(1)} %pad_maximum_fusion.refs_0_), channel_id=1, source_target_pairs={{0,2},{2,4},{4,6},{6,0},{1,3},{3,5},{5,7},{7,1},{8,10},{10,12},{12... | collective-permute-start | bytes 1572872 | tf_op jit(solution)/shard_map/ppermute | solution.py:33
  27.9 16.6 %collective-permute-start.6 = (bf16[4,128,512]{2,1,0:T(8,128)(2,1)S(1)}, bf16[4,128,512]{2,1,0:T(8,128)(2,1)S(1)}, u32[]{:S(2)}, u32[]{:S(2)}) collective-permute-start(bf16[4,128,512]{2,1,0:T(8,128)(2,1)S(1)} %pad_maximum_fusion.refs_0_), channel_id=1, source_target_pairs={{0,6},{2,0},{4,2},{6,4},{1,7},{3,1},{5,3},{7,5},{8,14},{10,8},{12,... | collective-permute-start | bytes 1572872 | tf_op jit(solution)/shard_map/ppermute | solution.py:33
  29.4 7.3 %collective-permute-start.4 = (bf16[4,256,128]{2,1,0:T(8,128)(2,1)S(1)}, bf16[4,256,128]{2,1,0:T(8,128)(2,1)S(1)}, u32[]{:S(2)}, u32[]{:S(2)}) collective-permute-start(bf16[4,256,128]{2,1,0:T(8,128)(2,1)S(1)} %all-to-all-done.refs_0_), channel_id=1, source_target_pairs={{0,224},{32,0},{64,32},{96,64},{128,96},{160,128},{192,160},{224,1... | collective-permute-start | bytes 786440 | tf_op jit(solution)/shard_map/ppermute | solution.py:33
  34.8 9.7 %collective-permute-start.7 = (bf16[4,256,128]{2,1,0:T(8,128)(2,1)S(1)}, bf16[4,256,128]{2,1,0:T(8,128)(2,1)S(1)}, u32[]{:S(2)}, u32[]{:S(2)}) collective-permute-start(bf16[4,256,128]{2,1,0:T(8,128)(2,1)S(1)} %collective-permute-done.3.refs_1_), channel_id=1, source_target_pairs={{0,32},{32,64},{64,96},{96,128},{128,160},{160,192},{192,224},{224... | collective-permute-start | bytes 786440 | tf_op jit(solution)/shard_map/ppermute | solution.py:33
  36.7 7.8 %collective-permute-start.8 = (bf16[4,256,128]{2,1,0:T(8,128)(2,1)S(1)}, bf16[4,256,128]{2,1,0:T(8,128)(2,1)S(1)}, u32[]{:S(2)}, u32[]{:S(2)}) collective-permute-start(bf16[4,256,128]{2,1,0:T(8,128)(2,1)S(1)} %collective-permute-done.4.refs_2_), channel_id=1, source_target_pairs={{0,224},{32,0},{64,32},{96,64},{128,96},{160,128},{192,160},{224,1... | collective-permute-start | bytes 786440 | tf_op jit(solution)/shard_map/ppermute | solution.py:33
  40.9 9.2 %collective-permute-start.13 = (bf16[4,128,512]{2,1,0:T(8,128)(2,1)S(1)}, bf16[4,128,512]{2,1,0:T(8,128)(2,1)S(1)}, u32[]{:S(2)}, u32[]{:S(2)}) collective-permute-start(bf16[4,128,512]{2,1,0:T(8,128)(2,1)S(1)} %pad_maximum_fusion.refs_0_), channel_id=1, source_target_pairs={{0,1},{1,0},{2,3},{3,2},{4,5},{5,4},{6,7},{7,6},{8,9},{9,8},{10,11... | collective-permute-start | bytes 1572872 | tf_op jit(solution)/shard_map/ppermute | solution.py:33
  44.6 6.5 %collective-permute-start.9 = (bf16[2,128,512]{2,1,0:T(8,128)(2,1)S(1)}, bf16[2,128,512]{2,1,0:T(8,128)(2,1)S(1)}, u32[]{:S(2)}, u32[]{:S(2)}) collective-permute-start(bf16[2,128,512]{2,1,0:T(8,128)(2,1)S(1)} %slice.34), channel_id=1, source_target_pairs={{0,2},{2,4},{4,6},{6,0},{1,3},{3,5},{5,7},{7,1},{8,10},{10,12},{12... | collective-permute-start | bytes 786440 | tf_op jit(solution)/shard_map/ppermute | solution.py:33
  47.4 6.7 %collective-permute-start.11 = (bf16[4,256,128]{2,1,0:T(8,128)(2,1)S(1)}, bf16[4,256,128]{2,1,0:T(8,128)(2,1)S(1)}, u32[]{:S(2)}, u32[]{:S(2)}) collective-permute-start(bf16[4,256,128]{2,1,0:T(8,128)(2,1)S(1)} %collective-permute-done.7.refs_3_), channel_id=1, source_target_pairs={{0,32},{32,64},{64,96},{96,128},{128,160},{160,192},{192,224},{224... | collective-permute-start | bytes 786440 | tf_op jit(solution)/shard_map/ppermute | solution.py:33
  47.4 6.7 %collective-permute-start.12 = (bf16[4,256,128]{2,1,0:T(8,128)(2,1)S(1)}, bf16[4,256,128]{2,1,0:T(8,128)(2,1)S(1)}, u32[]{:S(2)}, u32[]{:S(2)}) collective-permute-start(bf16[4,256,128]{2,1,0:T(8,128)(2,1)S(1)} %collective-permute-done.8.refs_4_), channel_id=1, source_target_pairs={{0,224},{32,0},{64,32},{96,64},{128,96},{160,128},{192,160},{224,1... | collective-permute-start | bytes 786440 | tf_op jit(solution)/shard_map/ppermute | solution.py:33
  68.2 8.6 %collective-permute-start.16 = (bf16[4,128,512]{2,1,0:T(8,128)(2,1)S(1)}, bf16[4,128,512]{2,1,0:T(8,128)(2,1)S(1)}, u32[]{:S(2)}, u32[]{:S(2)}) collective-permute-start(bf16[4,128,512]{2,1,0:T(8,128)(2,1)S(1)} %collective-permute-done.5.refs_1_), channel_id=1, source_target_pairs={{0,1},{1,0},{2,3},{3,2},{4,5},{5,4},{6,7},{7,6},{8,9},{9,8},{10,11... | collective-permute-start | bytes 1572872 | tf_op jit(solution)/shard_map/ppermute | solution.py:33
  155.9 15.0 %all-to-all-start.6 = ((f32[32,8,128]{2,1,0:T(8,128)}), f32[32,8,128]{2,1,0:T(8,128)S(1)}, u32[]{:S(2)}, u32[]{:S(2)}) async-start(f32[32,8,128]{2,1,0:T(8,128)} %get-tuple-element.59), calls=%async_computation.6 | async-start | bytes 262144 | tf_op jit(solution)/shard_map/all_to_all | solution.py:379
  159.8 7.2 %collective-permute-start.20 = (bf16[256,256]{1,0:T(8,128)(2,1)S(1)}, bf16[256,256]{1,0:T(8,128)(2,1)S(1)}, u32[]{:S(2)}, u32[]{:S(2)}) collective-permute-start(bf16[256,256]{1,0:T(8,128)(2,1)S(1)} %get-tuple-element.61), channel_id=1, source_target_pairs={{0,8},{8,16},{16,24},{24,0},{1,9},{9,17},{17,25},{25,1},{2,10},{10... | collective-permute-start | bytes 393224 | tf_op jit(solution)/shard_map/ppermute | solution.py:33
  161.0 9.9 %collective-permute-start.21 = (bf16[256,256]{1,0:T(8,128)(2,1)S(1)}, bf16[256,256]{1,0:T(8,128)(2,1)S(1)}, u32[]{:S(2)}, u32[]{:S(2)}) collective-permute-start(bf16[256,256]{1,0:T(8,128)(2,1)S(1)} %get-tuple-element.62), channel_id=1, source_target_pairs={{0,16},{8,24},{16,0},{24,8},{1,17},{9,25},{17,1},{25,9},{2,18},{10... | collective-permute-start | bytes 393224 | tf_op jit(solution)/shard_map/ppermute | solution.py:33
  163.4 7.5 %collective-permute-start.22 = (bf16[256,256]{1,0:T(8,128)(2,1)S(1)}, bf16[256,256]{1,0:T(8,128)(2,1)S(1)}, u32[]{:S(2)}, u32[]{:S(2)}) collective-permute-start(bf16[256,256]{1,0:T(8,128)(2,1)S(1)} %get-tuple-element.63), channel_id=1, source_target_pairs={{0,24},{8,0},{16,8},{24,16},{1,25},{9,1},{17,9},{25,17},{2,26},{10... | collective-permute-start | bytes 393224 | tf_op jit(solution)/shard_map/ppermute | solution.py:33
  176.0 7.1 %collective-permute-start.23 = (bf16[4,256,512]{2,1,0:T(8,128)(2,1)}, bf16[4,256,512]{2,1,0:T(8,128)(2,1)S(1)}, u32[]{:S(2)}, u32[]{:S(2)}) collective-permute-start(bf16[4,256,512]{2,1,0:T(8,128)(2,1)} %get-tuple-element.66), channel_id=1, source_target_pairs={{0,1},{1,0},{2,3},{3,2},{4,5},{5,4},{6,7},{7,6},{8,9},{9,8},{10,11... | collective-permute-start | bytes 3145736 | tf_op jit(solution)/shard_map/ppermute | solution.py:33
  185.2 8.0 %collective-permute-start.26 = (bf16[256,512]{1,0:T(8,128)(2,1)S(1)}, bf16[256,512]{1,0:T(8,128)(2,1)S(1)}, u32[]{:S(2)}, u32[]{:S(2)}) collective-permute-start(bf16[256,512]{1,0:T(8,128)(2,1)S(1)} %get-tuple-element.70), channel_id=1, source_target_pairs={{0,6},{2,0},{4,2},{6,4},{1,7},{3,1},{5,3},{7,5},{8,14},{10,8},{12,... | collective-permute-start | bytes 786440 | tf_op jit(solution)/shard_map/ppermute | solution.py:33
  186.4 14.5 %collective-permute-start.25 = (bf16[256,512]{1,0:T(8,128)(2,1)S(1)}, bf16[256,512]{1,0:T(8,128)(2,1)S(1)}, u32[]{:S(2)}, u32[]{:S(2)}) collective-permute-start(bf16[256,512]{1,0:T(8,128)(2,1)S(1)} %get-tuple-element.71), channel_id=1, source_target_pairs={{0,2},{2,4},{4,6},{6,0},{1,3},{3,5},{5,7},{7,1},{8,10},{10,12},{12... | collective-permute-start | bytes 786440 | tf_op jit(solution)/shard_map/ppermute | solution.py:33
  186.8 14.0 %collective-permute-start.24 = (bf16[256,512]{1,0:T(8,128)(2,1)S(1)}, bf16[256,512]{1,0:T(8,128)(2,1)S(1)}, u32[]{:S(2)}, u32[]{:S(2)}) collective-permute-start(bf16[256,512]{1,0:T(8,128)(2,1)S(1)} %get-tuple-element.69), channel_id=1, source_target_pairs={{0,4},{2,6},{4,0},{6,2},{1,5},{3,7},{5,1},{7,3},{8,12},{10,14},{12... | collective-permute-start | bytes 786440 | tf_op jit(solution)/shard_map/ppermute | solution.py:33
  (20 other events, 80.6 us)
Sparse Core Ops, SparseCore 0:
  10.6 56.5 all-gather.4
  69.0 93.8 all-gather.6

commit v5 on v3

--- a/solution.py
+++ b/solution.py
@@ -218,14 +218,23 @@
     )(place, q, parts, sq)
 
 
+HALF_COST = pl.CostEstimate(flops=ROWS * COUNT * WIDTH, bytes_accessed=5 * 2**20, transcendentals=0)
+
+
+def transport(w_ref, data_ref, first, out_ref):
+    for s in range(Y):
+        block = jnp.concatenate([data_ref[n, first + s] for n in range(X)], axis=0)
+        out_ref[s] = jnp.dot(w_ref[...], block, preferred_element_type=F32).astype(out_ref.dtype)
+
+
 def give_kernel(place, part_ref, *refs):
     w_refs, (data_ref, out_ref, w_ref, pot_ref) = refs[:X], refs[X:]
-
-    @pl.when(pl.program_id(0) == 0)
-    def _():
-        scale(place, part_ref, w_refs, w_ref, pot_ref)
-
-    transport(w_ref, data_ref, out_ref)
+    scale(place, part_ref, w_refs, w_ref, pot_ref)
+    transport(w_ref, data_ref, Y, out_ref)
+
+
+def keep_kernel(w_ref, data_ref, out_ref):
+    transport(w_ref, data_ref, 0, out_ref)
 
 
 def scale(place, part_ref, w_refs, w_ref, pot_ref):
@@ -240,41 +249,25 @@
         parts = jnp.stack([part_ref[k * X + n] for k in range(Z)])
         top = jnp.max(parts, axis=0)
         total = top + jnp.log2(jnp.sum(jnp.exp2(parts - top[None]), axis=0))
-        factor = to_column(jnp.exp2(part_ref[z * X + n] - total))
-        rows = pl.ds(pl.multiple_of(n * QUARTER, QUARTER), QUARTER)
+        factor = jnp.exp2(part_ref[z * X + n] - total)
+        factor = jnp.concatenate([factor[0:1], factor[1:2]], axis=1)
+        lanes = pl.ds(pl.multiple_of(n * QUARTER, QUARTER), QUARTER)
         for h in range(2):
-            w = w_refs[by][:, pl.ds(h * 128, 128)].astype(F32) * factor
-            w_ref[rows, pl.ds(h * 128, 128)] = w.astype(BF16)
-
-
-def transport(w_ref, data_ref, out_ref):
-    block = jnp.concatenate([data_ref[n, 0] for n in range(X)], axis=0)
-    total = lax.dot_general(w_ref[...], block, (((0,), (0,)), ((), ())), preferred_element_type=F32)
-    out_ref[0] = total.astype(out_ref.dtype)
-
-
-HALF_COST = pl.CostEstimate(flops=ROWS * COUNT * WIDTH, bytes_accessed=5 * 2**20, transcendentals=0)
-
-
-def half_of(which):
-    return pl.BlockSpec((X, 1, QUARTER, SHARE), lambda s: (0, which * Y + s, 0, 0))
-
-
-PIECE = pl.BlockSpec((1, ROWS, SHARE), lambda s: (s, 0, 0))
+            w = jnp.transpose(w_refs[by][:, pl.ds(h * 128, 128)].astype(F32)) * factor
+            w_ref[pl.ds(h * 128, 128), lanes] = w.astype(BF16)
 
 
 def give(place, parts, blocks, data):
     return pl.pallas_call(
         give_kernel,
-        grid=(Y,),
         out_shape=(
             jax.ShapeDtypeStruct((Y, ROWS, SHARE), BF16),
-            jax.ShapeDtypeStruct((COUNT, ROWS), BF16),
+            jax.ShapeDtypeStruct((ROWS, COUNT), BF16),
             jax.ShapeDtypeStruct((2 * X, 128), F32),
         ),
-        in_specs=[SMEM] + [VMEM] * (1 + X) + [half_of(1)],
-        out_specs=(PIECE, VMEM, VMEM),
-        compiler_params=params(53),
+        in_specs=[SMEM] + [VMEM] * (2 + X),
+        out_specs=(VMEM,) * 3,
+        compiler_params=params(24),
         cost_estimate=HALF_COST,
         name="give",
     )(place, parts, *blocks, data)
@@ -282,15 +275,32 @@
 
 def keep(w, data):
     return pl.pallas_call(
-        transport,
-        grid=(Y,),
+        keep_kernel,
         out_shape=jax.ShapeDtypeStruct((Y, ROWS, SHARE), F32),
-        in_specs=[VMEM, half_of(0)],
-        out_specs=PIECE,
-        compiler_params=params(53),
+        in_specs=[VMEM] * 2,
+        out_specs=VMEM,
+        compiler_params=params(24),
         cost_estimate=HALF_COST,
         name="keep",
     )(w, data)
+
+
+def join_kernel(mine_ref, got_ref, own_ref, *out_refs):
+    own_ref[...] = mine_ref[0] + got_ref[0].astype(F32)
+    for s, ref in enumerate(out_refs, 1):
+        ref[...] = (mine_ref[s] + got_ref[s].astype(F32)).astype(BF16)
+
+
+def join(mine, got):
+    return pl.pallas_call(
+        join_kernel,
+        out_shape=(jax.ShapeDtypeStruct((ROWS, SHARE), F32),)
+        + (jax.ShapeDtypeStruct((ROWS, SHARE), BF16),) * (Y - 1),
+        in_specs=[VMEM] * 2,
+        out_specs=(VMEM,) * Y,
+        compiler_params=params(16),
+        name="join",
+    )(mine, got)
 
 
 def body(noise, data):
@@ -313,11 +323,9 @@
     columns = lax.all_to_all(columns, ("z", "x"), 0, 0)
     theirs, w, pot_g = give(place, columns, blocks, data_all)
     got = shift(theirs, "core", 1)
-    mine = keep(w, data_all)
-    both = mine + got.astype(F32)
-    target = both[0]
+    target, *rest = join(keep(w, data_all), got)
     for by in (2, 1, 3):
-        target = target + shift(both[by].astype(BF16), "y", by).astype(F32)
+        target = target + shift(rest[by - 1], "y", by).astype(F32)
     velocity = (target - noise.astype(F32)).astype(BF16)
     own = lax.dynamic_slice_in_dim(f, 2 * x, 2, 0).reshape(ROWS)
     pot_f = own * (EPS / LOG2E) + sq_noise[0] / WIDTH

time: 209 us -> 206 us (0.986)
  Pallas kernels: 21 us -> 14.6 us
  local copies, waits for them, and re-layouts: 4.5 us -> 10.2 us
    pallas_call x2 -> x3, Pallas kernels: 10.3 us -> 3.99 us  [the longest x1 2.57 us: give(): pl.pallas_call(give_kernel, out_shape=(jax.ShapeDtypeStruct((Y, ROWS, SHA...]
    unnamed x6 -> x8, local copies, waits for them, and re-layouts: 4.43 us -> 10.1 us
  transfers between devices with their start and end apart: 18 -> 18, of which waited for: 8 -> 8; matrix products, arithmetic and copies ran while one was open for 0% -> 0% of each run, Pallas kernels for 8% -> 6%
where the time goes in v5:
time: 206 us; the launch traced here: 205 us
  blocking collectives  74.1 us (36%)
  waiting for transfers between devices  63.2 us (31%)
  starting transfers between devices  27.7 us (13%)
  Pallas kernels  14.6 us (7%)
  between operations  14.2 us (7%)
  local copies, waits for them, and re-layouts  10.2 us (5%)
    all_to_all x3, blocking collectives, body(): parts = lax.all_to_all(rows, ('x', 'y', 'core'), 0, 0)  41 us
    ppermute x15, waiting for transfers between devices, shift(): return lax.ppermute(x, axis, [(j, (j + by) % n) for j in range(n)])  26.9 us
    ppermute x15, starting transfers between devices, shift(): return lax.ppermute(x, axis, [(j, (j + by) % n) for j in range(n)])  23.8 us
    all_gather x1, waiting for transfers between devices, body(): lax.all_gather(noise, ('x', 'y', 'core')).reshape(X, Y * C, ROWS, SHARE)  23.3 us
    all_to_all x2, blocking collectives, body(): columns = lax.all_to_all(columns, 'z', 0, 0)  22.7 us
    all_gather x1, waiting for transfers between devices, body(): data_all = lax.all_gather(samples, 'x')  12.3 us
    all_to_all x1, blocking collectives, body(): swapped = lax.all_to_all(data.reshape(X, QUARTER, SLICE), 'x', 0, 0)  10.4 us
    unnamed x8, local copies, waits for them, and re-layouts  10.1 us
  transfers between devices with their start and end apart: 18, of which 8 were waited for; matrix products, arithmetic and copies ran while one was open for 0% of the time, Pallas kernels for 6%

profile of v5, /device:TPU:1, one launch (start us, length us, event | category | flops | bytes accessed | tf_op | source)
XLA Modules:
  0.0 205.5 jit_solution(14937435241202585357)
XLA Ops:
  7.9 10.4 %all_to_all.35.refs_0_ = bf16[4,256,128]{2,1,0:T(8,128)(2,1)S(1)} all-to-all(bf16[4,256,128]{2,1,0:T(8,128)(2,1)} %bitcast.14), channel_id=1, replica_groups=mesh['z'=8,'x'=4,'y'=4,'core'=2] {'x'}, dimensions={0} | all-to-all | bytes 524288 | tf_op jit(solution)/shard_map/all_to_all | solution.py:310
  20.0 3.9 %collective-permute-start.1 = (bf16[4,256,128]{2,1,0:T(8,128)(2,1)S(1)}, bf16[4,256,128]{2,1,0:T(8,128)(2,1)S(1)}, u32[]{:S(2)}, u32[]{:S(2)}) collective-permute-start(bf16[4,256,128]{2,1,0:T(8,128)(2,1)S(1)} %all_to_all.35.refs_0_), channel_id=1, source_target_pairs={{0,224},{32,0},{64,32},{96,64},{128,96},{160,128},{192,160},{224,1... | collective-permute-start | bytes 786440 | tf_op jit(solution)/shard_map/ppermute | solution.py:32
  23.9 4.5 %collective-permute-done.refs_1_ = bf16[4,256,128]{2,1,0:T(8,128)(2,1)S(1)} collective-permute-done((bf16[4,256,128]{2,1,0:T(8,128)(2,1)S(1)}, bf16[4,256,128]{2,1,0:T(8,128)(2,1)S(1)}, u32[]{:S(2)}, u32[]{:S(2)}) %collective-permute-start) | collective-permute-done | bytes 262176 | tf_op jit(solution)/shard_map/ppermute | solution.py:32
  28.5 2.7 %collective-permute-start.3 = (bf16[4,256,128]{2,1,0:T(8,128)(2,1)S(1)}, bf16[4,256,128]{2,1,0:T(8,128)(2,1)S(1)}, u32[]{:S(2)}, u32[]{:S(2)}) collective-permute-start(bf16[4,256,128]{2,1,0:T(8,128)(2,1)S(1)} %collective-permute-done.1.refs_2_), channel_id=1, source_target_pairs={{0,224},{32,0},{64,32},{96,64},{128,96},{160,128},{192,160},{224,1... | collective-permute-start | bytes 786440 | tf_op jit(solution)/shard_map/ppermute | solution.py:32
  31.1 3.8 %collective-permute-done.2.refs_3_ = bf16[4,256,128]{2,1,0:T(8,128)(2,1)S(1)} collective-permute-done((bf16[4,256,128]{2,1,0:T(8,128)(2,1)S(1)}, bf16[4,256,128]{2,1,0:T(8,128)(2,1)S(1)}, u32[]{:S(2)}, u32[]{:S(2)}) %collective-permute-start.2) | collective-permute-done | bytes 262176 | tf_op jit(solution)/shard_map/ppermute | solution.py:32
  34.9 2.8 %collective-permute-start.5 = (bf16[4,256,128]{2,1,0:T(8,128)(2,1)S(1)}, bf16[4,256,128]{2,1,0:T(8,128)(2,1)S(1)}, u32[]{:S(2)}, u32[]{:S(2)}) collective-permute-start(bf16[4,256,128]{2,1,0:T(8,128)(2,1)S(1)} %collective-permute-done.3.refs_4_), channel_id=1, source_target_pairs={{0,224},{32,0},{64,32},{96,64},{128,96},{160,128},{192,160},{224,1... | collective-permute-start | bytes 786440 | tf_op jit(solution)/shard_map/ppermute | solution.py:32
  37.7 3.7 %collective-permute-done.4.refs_5_ = bf16[4,256,128]{2,1,0:T(8,128)(2,1)S(1)} collective-permute-done((bf16[4,256,128]{2,1,0:T(8,128)(2,1)S(1)}, bf16[4,256,128]{2,1,0:T(8,128)(2,1)S(1)}, u32[]{:S(2)}, u32[]{:S(2)}) %collective-permute-start.4) | collective-permute-done | bytes 262176 | tf_op jit(solution)/shard_map/ppermute | solution.py:32
  41.5 2.7 %collective-permute-start.7 = (bf16[2,256,128]{2,1,0:T(8,128)(2,1)S(1)}, bf16[2,256,128]{2,1,0:T(8,128)(2,1)S(1)}, u32[]{:S(2)}, u32[]{:S(2)}) collective-permute-start(bf16[2,256,128]{2,1,0:T(8,128)(2,1)S(1)} %slice.9), channel_id=1, source_target_pairs={{0,224},{32,0},{64,32},{96,64},{128,96},{160,128},{192,160},{224,1... | collective-permute-start | bytes 393224 | tf_op jit(solution)/shard_map/ppermute | solution.py:32
  44.3 2.8 %collective-permute-done.6.refs_7_ = bf16[2,256,128]{2,1,0:T(8,128)(2,1)S(1)} collective-permute-done((bf16[2,256,128]{2,1,0:T(8,128)(2,1)S(1)}, bf16[2,256,128]{2,1,0:T(8,128)(2,1)S(1)}, u32[]{:S(2)}, u32[]{:S(2)}) %collective-permute-start.6) | collective-permute-done | bytes 131104 | tf_op jit(solution)/shard_map/ppermute | solution.py:32
  49.4 23.3 %all-gather.5.cloned.1.call-done = bf16[8192,512]{1,0:T(8,128)(2,1)} async-done(((bf16[256,512]{1,0:T(8,128)(2,1)}), bf16[8192,512]{1,0:T(8,128)(2,1)}) %all-gather.5.cloned.1.call-update) | async-done | bytes 8388624 | tf_op jit(solution)/shard_map/all_gather | solution.py:309
  72.7 3.4 %copy-done.2 = bf16[8192,512]{1,0:T(8,128)(2,1)S(1)} copy-done((bf16[8192,512]{1,0:T(8,128)(2,1)S(1)}, bf16[8192,512]{1,0:T(8,128)(2,1)}, u32[]{:S(2)}) %copy-start.2) | copy-done | bytes 8388632
  76.1 4.4 %score.1 = (f32[256,1024]{1,0:T(8,128)S(1)}, f32[32,8,128]{2,1,0:T(8,128)S(1)}, f32[1,256]{1,0:T(1,128)S(1)}) custom-call(s32[4]{0:T(128)S(1)} %pad_add_fusion.place, bf16[8,256,512]{2,1,0:T(8,128)(2,1)} %get-tuple-element.23.data_ref, f32[256,128]{1,0:T(8,128)S(1)} %get-tuple-element.24.sq_ref, bf16[4,8,256,512]{3,2,1,0:T(8,128)(2,1)S(1)} %bitcast.13), custom_call_target="tpu_custom_call" | custom-call | tf_op jit(solution)/shard_map/score/pallas_call | solution.py:123
  80.5 13.0 %all_to_all.36.part_ref = f32[32,8,128]{2,1,0:T(8,128)S(1)} all-to-all(f32[32,8,128]{2,1,0:T(8,128)S(1)} %get-tuple-element.26), channel_id=1, replica_groups=mesh['z'=8,'x'=4,'y'=4,'core'=2] {'x','y','core'}, dimensions={0} | all-to-all | bytes 262144 | tf_op jit(solution)/shard_map/all_to_all | solution.py:317
  94.3 13.5 %all_to_all.37.part_ref = f32[8,8,128]{2,1,0:T(8,128)S(1)} all-to-all(f32[8,8,128]{2,1,0:T(8,128)S(1)} %get-tuple-element.27), channel_id=1, replica_groups=mesh['z'=8,'x'=4,'y'=4,'core'=2] {'z'}, dimensions={0} | all-to-all | bytes 65536 | tf_op jit(solution)/shard_map/all_to_all | solution.py:320
  108.2 14.1 %all_to_all.38.part_ref = f32[32,8,128]{2,1,0:T(8,128)S(1)} all-to-all(f32[32,8,128]{2,1,0:T(8,128)S(1)} %noise_lse.2), channel_id=1, replica_groups=mesh['z'=8,'x'=4,'y'=4,'core'=2] {'x','y','core'}, dimensions={0} | all-to-all | bytes 262144 | tf_op jit(solution)/shard_map/all_to_all | solution.py:317
  123.1 9.2 %all_to_all.39.part_ref = f32[8,8,128]{2,1,0:T(8,128)S(1)} all-to-all(f32[8,8,128]{2,1,0:T(8,128)S(1)} %get-tuple-element.28), channel_id=1, replica_groups=mesh['z'=8,'x'=4,'y'=4,'core'=2] {'z'}, dimensions={0} | all-to-all | bytes 65536 | tf_op jit(solution)/shard_map/all_to_all | solution.py:320
  132.7 13.9 %all_to_all.40.part_ref = f32[32,8,128]{2,1,0:T(8,128)S(1)} all-to-all(f32[32,8,128]{2,1,0:T(8,128)S(1)} %noise_lse.3), channel_id=1, replica_groups=mesh['z'=8,'x'=4,'y'=4,'core'=2] {'x','y','core'}, dimensions={0} | all-to-all | bytes 262144 | tf_op jit(solution)/shard_map/all_to_all | solution.py:317
  148.2 3.9 %all-to-all-start.6 = ((f32[32,8,128]{2,1,0:T(8,128)}), f32[32,8,128]{2,1,0:T(8,128)S(1)}, u32[]{:S(2)}, u32[]{:S(2)}) async-start(f32[32,8,128]{2,1,0:T(8,128)} %get-tuple-element.31), calls=%async_computation.6 | async-start | bytes 262144 | tf_op jit(solution)/shard_map/all_to_all | solution.py:323
  156.9 12.3 %all-gather.7.cloned.1.call-done = bf16[32,256,512]{2,1,0:T(8,128)(2,1)} async-done(((bf16[8,256,512]{2,1,0:T(8,128)(2,1)}), bf16[32,256,512]{2,1,0:T(8,128)(2,1)}) %all-gather.7.cloned.1.call-update) | async-done | bytes 8388624 | tf_op jit(solution)/shard_map/all_gather | solution.py:312
  169.2 3.4 %copy-done = bf16[32,256,512]{2,1,0:T(8,128)(2,1)S(1)} copy-done((bf16[32,256,512]{2,1,0:T(8,128)(2,1)S(1)}, bf16[32,256,512]{2,1,0:T(8,128)(2,1)}, u32[]{:S(2)}) %copy-start) | copy-done | bytes 8388632
  172.5 2.6 %give.1 = (bf16[4,256,512]{2,1,0:T(8,128)(2,1)S(1)}, bf16[256,1024]{1,0:T(8,128)(2,1)S(1)}, f32[8,128]{1,0:T(8,128)}) custom-call(s32[4]{0:T(128)S(1)} %pad_add_fusion.place, f32[32,8,128]{2,1,0:T(8,128)S(1)} %all-to-all-done.6.part_ref, bf16[256,256]{1,0:T(8,128)(2,1)S(1)} %get-tuple-element.32.refs_0_, ...), custom_call_target="tpu_custom_call" | custom-call | flops 1073741824 | bytes 5242880 | tf_op jit(solution)/shard_map/give/pallas_call | solution.py:261
  175.9 3.4 %copy-done.1 = bf16[32,256,512]{2,1,0:T(8,128)(2,1)S(1)} copy-done((bf16[32,256,512]{2,1,0:T(8,128)(2,1)S(1)}, bf16[32,256,512]{2,1,0:T(8,128)(2,1)}, u32[]{:S(2)}) %copy-start.1) | copy-done | bytes 8388632
  185.6 8.9 %collective-permute-done.14 = bf16[256,512]{1,0:T(8,128)(2,1)S(1)} collective-permute-done((bf16[256,512]{1,0:T(8,128)(2,1)S(1)}, bf16[256,512]{1,0:T(8,128)(2,1)S(1)}, u32[]{:S(2)}, u32[]{:S(2)}) %collective-permute-start.14) | collective-permute-done | bytes 262176 | tf_op jit(solution)/shard_map/ppermute | solution.py:32
  194.5 3.2 %collective-permute-done.13 = bf16[256,512]{1,0:T(8,128)(2,1)S(1)} collective-permute-done((bf16[256,512]{1,0:T(8,128)(2,1)S(1)}, bf16[256,512]{1,0:T(8,128)(2,1)S(1)}, u32[]{:S(2)}, u32[]{:S(2)}) %collective-permute-start.13) | collective-permute-done | bytes 262176 | tf_op jit(solution)/shard_map/ppermute | solution.py:32
  (44 shorter events, 21.6 us)
Async XLA Ops:
  7.2 65.6 %all-gather.5.cloned.1.call-start = ((), (), s32[]{:S(2)}) async-start(), calls=%async_computation.7 | async-start | bytes 8650752 | tf_op jit(solution)/shard_map/all_gather | solution.py:309
  7.9 161.2 %all-gather.7.cloned.1.call-start = ((), (), s32[]{:S(2)}) async-start(), calls=%async_computation.8 | async-start | bytes 10485760 | tf_op jit(solution)/shard_map/all_gather | solution.py:312
  18.3 10.1 %collective-permute-start = (bf16[4,256,128]{2,1,0:T(8,128)(2,1)S(1)}, bf16[4,256,128]{2,1,0:T(8,128)(2,1)S(1)}, u32[]{:S(2)}, u32[]{:S(2)}) collective-permute-start(bf16[4,256,128]{2,1,0:T(8,128)(2,1)S(1)} %all_to_all.35.refs_0_), channel_id=1, source_target_pairs={{0,32},{32,64},{64,96},{96,128},{128,160},{160,192},{192,224},{224... | collective-permute-start | bytes 786440 | tf_op jit(solution)/shard_map/ppermute | solution.py:32
  20.0 8.5 %collective-permute-start.1 = (bf16[4,256,128]{2,1,0:T(8,128)(2,1)S(1)}, bf16[4,256,128]{2,1,0:T(8,128)(2,1)S(1)}, u32[]{:S(2)}, u32[]{:S(2)}) collective-permute-start(bf16[4,256,128]{2,1,0:T(8,128)(2,1)S(1)} %all_to_all.35.refs_0_), channel_id=1, source_target_pairs={{0,224},{32,0},{64,32},{96,64},{128,96},{160,128},{192,160},{224,1... | collective-permute-start | bytes 786440 | tf_op jit(solution)/shard_map/ppermute | solution.py:32
  28.5 6.4 %collective-permute-start.2 = (bf16[4,256,128]{2,1,0:T(8,128)(2,1)S(1)}, bf16[4,256,128]{2,1,0:T(8,128)(2,1)S(1)}, u32[]{:S(2)}, u32[]{:S(2)}) collective-permute-start(bf16[4,256,128]{2,1,0:T(8,128)(2,1)S(1)} %collective-permute-done.refs_1_), channel_id=1, source_target_pairs={{0,32},{32,64},{64,96},{96,128},{128,160},{160,192},{192,224},{224... | collective-permute-start | bytes 786440 | tf_op jit(solution)/shard_map/ppermute | solution.py:32
  28.5 6.4 %collective-permute-start.3 = (bf16[4,256,128]{2,1,0:T(8,128)(2,1)S(1)}, bf16[4,256,128]{2,1,0:T(8,128)(2,1)S(1)}, u32[]{:S(2)}, u32[]{:S(2)}) collective-permute-start(bf16[4,256,128]{2,1,0:T(8,128)(2,1)S(1)} %collective-permute-done.1.refs_2_), channel_id=1, source_target_pairs={{0,224},{32,0},{64,32},{96,64},{128,96},{160,128},{192,160},{224,1... | collective-permute-start | bytes 786440 | tf_op jit(solution)/shard_map/ppermute | solution.py:32
  34.9 6.4 %collective-permute-start.4 = (bf16[4,256,128]{2,1,0:T(8,128)(2,1)S(1)}, bf16[4,256,128]{2,1,0:T(8,128)(2,1)S(1)}, u32[]{:S(2)}, u32[]{:S(2)}) collective-permute-start(bf16[4,256,128]{2,1,0:T(8,128)(2,1)S(1)} %collective-permute-done.2.refs_3_), channel_id=1, source_target_pairs={{0,32},{32,64},{64,96},{96,128},{128,160},{160,192},{192,224},{224... | collective-permute-start | bytes 786440 | tf_op jit(solution)/shard_map/ppermute | solution.py:32
  34.9 6.5 %collective-permute-start.5 = (bf16[4,256,128]{2,1,0:T(8,128)(2,1)S(1)}, bf16[4,256,128]{2,1,0:T(8,128)(2,1)S(1)}, u32[]{:S(2)}, u32[]{:S(2)}) collective-permute-start(bf16[4,256,128]{2,1,0:T(8,128)(2,1)S(1)} %collective-permute-done.3.refs_4_), channel_id=1, source_target_pairs={{0,224},{32,0},{64,32},{96,64},{128,96},{160,128},{192,160},{224,1... | collective-permute-start | bytes 786440 | tf_op jit(solution)/shard_map/ppermute | solution.py:32
  41.4 5.7 %collective-permute-start.6 = (bf16[2,256,128]{2,1,0:T(8,128)(2,1)S(1)}, bf16[2,256,128]{2,1,0:T(8,128)(2,1)S(1)}, u32[]{:S(2)}, u32[]{:S(2)}) collective-permute-start(bf16[2,256,128]{2,1,0:T(8,128)(2,1)S(1)} %slice.8), channel_id=1, source_target_pairs={{0,32},{32,64},{64,96},{96,128},{128,160},{160,192},{192,224},{224... | collective-permute-start | bytes 393224 | tf_op jit(solution)/shard_map/ppermute | solution.py:32
  41.5 5.6 %collective-permute-start.7 = (bf16[2,256,128]{2,1,0:T(8,128)(2,1)S(1)}, bf16[2,256,128]{2,1,0:T(8,128)(2,1)S(1)}, u32[]{:S(2)}, u32[]{:S(2)}) collective-permute-start(bf16[2,256,128]{2,1,0:T(8,128)(2,1)S(1)} %slice.9), channel_id=1, source_target_pairs={{0,224},{32,0},{64,32},{96,64},{128,96},{160,128},{192,160},{224,1... | collective-permute-start | bytes 393224 | tf_op jit(solution)/shard_map/ppermute | solution.py:32
  72.7 3.4 %copy-start.2 = (bf16[8192,512]{1,0:T(8,128)(2,1)S(1)}, bf16[8192,512]{1,0:T(8,128)(2,1)}, u32[]{:S(2)}) copy-start(bf16[8192,512]{1,0:T(8,128)(2,1)} %all-gather.5.cloned.1.call-done) | copy-start | bytes 25165828
  148.2 20.9 %all-to-all-start.6 = ((f32[32,8,128]{2,1,0:T(8,128)}), f32[32,8,128]{2,1,0:T(8,128)S(1)}, u32[]{:S(2)}, u32[]{:S(2)}) async-start(f32[32,8,128]{2,1,0:T(8,128)} %get-tuple-element.31), calls=%async_computation.6 | async-start | bytes 262144 | tf_op jit(solution)/shard_map/all_to_all | solution.py:323
  152.1 17.1 %collective-permute-start.8 = (bf16[256,256]{1,0:T(8,128)(2,1)S(1)}, bf16[256,256]{1,0:T(8,128)(2,1)S(1)}, u32[]{:S(2)}, u32[]{:S(2)}) collective-permute-start(bf16[256,256]{1,0:T(8,128)(2,1)S(1)} %get-tuple-element.33), channel_id=1, source_target_pairs={{0,8},{8,16},{16,24},{24,0},{1,9},{9,17},{17,25},{25,1},{2,10},{10... | collective-permute-start | bytes 393224 | tf_op jit(solution)/shard_map/ppermute | solution.py:32
  153.3 15.9 %collective-permute-start.9 = (bf16[256,256]{1,0:T(8,128)(2,1)S(1)}, bf16[256,256]{1,0:T(8,128)(2,1)S(1)}, u32[]{:S(2)}, u32[]{:S(2)}) collective-permute-start(bf16[256,256]{1,0:T(8,128)(2,1)S(1)} %get-tuple-element.34), channel_id=1, source_target_pairs={{0,16},{8,24},{16,0},{24,8},{1,17},{9,25},{17,1},{25,9},{2,18},{10... | collective-permute-start | bytes 393224 | tf_op jit(solution)/shard_map/ppermute | solution.py:32
  155.7 13.5 %collective-permute-start.10 = (bf16[256,256]{1,0:T(8,128)(2,1)S(1)}, bf16[256,256]{1,0:T(8,128)(2,1)S(1)}, u32[]{:S(2)}, u32[]{:S(2)}) collective-permute-start(bf16[256,256]{1,0:T(8,128)(2,1)S(1)} %get-tuple-element.35), channel_id=1, source_target_pairs={{0,24},{8,0},{16,8},{24,16},{1,25},{9,1},{17,9},{25,17},{2,26},{10... | collective-permute-start | bytes 393224 | tf_op jit(solution)/shard_map/ppermute | solution.py:32
  169.2 3.4 %copy-start = (bf16[32,256,512]{2,1,0:T(8,128)(2,1)S(1)}, bf16[32,256,512]{2,1,0:T(8,128)(2,1)}, u32[]{:S(2)}) copy-start(bf16[32,256,512]{2,1,0:T(8,128)(2,1)} %all-gather.7.cloned.1.call-done) | copy-start | bytes 25165828
  172.5 25.2 %copy-start.3 = (bf16[256,512]{1,0:T(8,128)(2,1)S(1)}, bf16[256,512]{1,0:T(8,128)(2,1)}, u32[]{:S(2)}) copy-start(bf16[256,512]{1,0:T(8,128)(2,1)} %param.2) | copy-start | bytes 786436
  175.1 5.5 %collective-permute-start.11 = (bf16[4,256,512]{2,1,0:T(8,128)(2,1)S(1)}, bf16[4,256,512]{2,1,0:T(8,128)(2,1)S(1)}, u32[]{:S(2)}, u32[]{:S(2)}) collective-permute-start(bf16[4,256,512]{2,1,0:T(8,128)(2,1)S(1)} %get-tuple-element.38), channel_id=1, source_target_pairs={{0,1},{1,0},{2,3},{3,2},{4,5},{5,4},{6,7},{7,6},{8,9},{9,8},{10,11... | collective-permute-start | bytes 3145736 | tf_op jit(solution)/shard_map/ppermute | solution.py:32
  175.9 3.4 %copy-start.1 = (bf16[32,256,512]{2,1,0:T(8,128)(2,1)S(1)}, bf16[32,256,512]{2,1,0:T(8,128)(2,1)}, u32[]{:S(2)}) copy-start(bf16[32,256,512]{2,1,0:T(8,128)(2,1)} %all-gather.7.cloned.1.call-done) | copy-start | bytes 25165828
  180.8 13.8 %collective-permute-start.14 = (bf16[256,512]{1,0:T(8,128)(2,1)S(1)}, bf16[256,512]{1,0:T(8,128)(2,1)S(1)}, u32[]{:S(2)}, u32[]{:S(2)}) collective-permute-start(bf16[256,512]{1,0:T(8,128)(2,1)S(1)} %get-tuple-element.42), channel_id=1, source_target_pairs={{0,6},{2,0},{4,2},{6,4},{1,7},{3,1},{5,3},{7,5},{8,14},{10,8},{12,... | collective-permute-start | bytes 786440 | tf_op jit(solution)/shard_map/ppermute | solution.py:32
  183.3 14.4 %collective-permute-start.13 = (bf16[256,512]{1,0:T(8,128)(2,1)S(1)}, bf16[256,512]{1,0:T(8,128)(2,1)S(1)}, u32[]{:S(2)}, u32[]{:S(2)}) collective-permute-start(bf16[256,512]{1,0:T(8,128)(2,1)S(1)} %get-tuple-element.41), channel_id=1, source_target_pairs={{0,2},{2,4},{4,6},{6,0},{1,3},{3,5},{5,7},{7,1},{8,10},{10,12},{12... | collective-permute-start | bytes 786440 | tf_op jit(solution)/shard_map/ppermute | solution.py:32
  183.3 14.4 %collective-permute-start.12 = (bf16[256,512]{1,0:T(8,128)(2,1)S(1)}, bf16[256,512]{1,0:T(8,128)(2,1)S(1)}, u32[]{:S(2)}, u32[]{:S(2)}) collective-permute-start(bf16[256,512]{1,0:T(8,128)(2,1)S(1)} %get-tuple-element.40), channel_id=1, source_target_pairs={{0,4},{2,6},{4,0},{6,2},{1,5},{3,7},{5,1},{7,3},{8,12},{10,14},{12... | collective-permute-start | bytes 786440 | tf_op jit(solution)/shard_map/ppermute | solution.py:32
Sparse Core Ops, SparseCore 0:
  10.6 62.1 all-gather.4
  74.5 94.5 all-gather.6

commit v6 on v5

v6 whole, which is shorter than its diff:
```python
import functools
import math

import jax
import jax.numpy as jnp
from jax import lax
from jax.experimental import pallas as pl
from jax.experimental.pallas import tpu as pltpu
from jax.sharding import Mesh, PartitionSpec as P

ITERS = 3
EPS = 0.01
LOG2E = math.log2(math.e)
Z, X, Y, C = 8, 4, 4, 2
ROWS, SHARE = 256, 512
COUNT, SLICE = 1024, 128
WIDTH = 4096
QUARTER = COUNT // X
TALL = ROWS * X
CHUNKS = TALL // 128
GROUP = X * Y * C
CUT = ROWS // 2
AROUND = (0, -1, 1, 2)
TOTAL = 8192
UNIT = LOG2E / (WIDTH * EPS)
LOG2N = math.log2(TOTAL)
F32, BF16 = jnp.float32, jnp.bfloat16
VMEM = pl.BlockSpec(memory_space=pltpu.VMEM)
SMEM = pl.BlockSpec(memory_space=pltpu.SMEM)


def shift(x, axis, by):
    n = {"z": Z, "x": X, "y": Y, "core": C}[axis]
    return lax.ppermute(x, axis, [(j, (j + by) % n) for j in range(n)])


def params(mib):
    return pltpu.CompilerParams(vmem_limit_bytes=mib * 2**20)


def both_ways(forward, backward, axis):
    return shift(forward, axis, 1), shift(backward, axis, -1)


def halves(forward, backward, axis):
    cut = forward.shape[0] // 2
    return both_ways(forward[:cut], backward[cut:], axis)


def around(block, axis):
    return [block, shift(block, axis, 1), shift(block, axis, -1), shift(block, axis, 2)]


def gather_noise(noise):
    hold = lax.optimization_barrier
    across, along = hold((around(noise[:CUT], "x"), around(noise[CUT:], "y")))
    across, along = jnp.stack(across), jnp.stack(along)
    y1, x1 = hold((both_ways(across, across, "y"), both_ways(along, along, "x")))
    return [across, *y1, *halves(*y1, "y"), along, *x1, *halves(*x1, "x")]


def squares(ref, pieces):
    total = None
    for view in pieces:
        part = ref[view].astype(F32)
        total = part * part if total is None else total + part * part
    return total


def lse(t, axis):
    top = jnp.max(t, axis=axis, keepdims=True)
    return top + jnp.log2(jnp.sum(jnp.exp2(t - top), axis=axis, keepdims=True))


def merged(ref):
    parts = ref[...]
    top = jnp.max(parts, axis=0)
    return top + jnp.log2(jnp.sum(jnp.exp2(parts - top[None]), axis=0))


def chunk(r):
    return pl.ds(r * 128, 128)


def at(place, which, rel, size):
    return lax.rem(place[which] + rel + size, size)


def blocks_of(parts):
    first, second = parts[:5], parts[5:]

    def of(five, far, near):
        if far < 3:
            return five[far].at[near]
        return five[3 + near // 2].at[near % 2]

    return (
        [[of(first, k, j) for k in range(Y)] for j in range(X)],
        [[of(second, j, k) for k in range(Y)] for j in range(X)],
    )


def partial_scores(place, data_ref, core, parts, q_ref, sq_ref):
    pieces = [at(place, 2, rel, Y) for rel in AROUND]
    lhs = jnp.concatenate([data_ref[p, core, n] for p in pieces for n in range(X)], axis=1)
    for h, blocks in enumerate(blocks_of(parts)):
        rhs = jnp.concatenate([jnp.concatenate([ref[...] for ref in row], axis=1) for row in blocks], axis=0)
        gram = lax.dot_general(lhs, rhs, (((1,), (1,)), ((), ())), preferred_element_type=F32) * (2.0 * UNIT)
        for j, rel in enumerate(AROUND):
            lanes = pl.ds(pl.multiple_of((h * X + at(place, 1, rel, X)) * 128, 128), 128)
            q_ref[:QUARTER, lanes] = gram[:, j * 128 : (j + 1) * 128]
    sq_ref[...] = squares(data_ref, [(p, core, n) for p in range(Y) for n in range(X)])


def theirs_kernel(place, data_ref, *refs):
    parts, (out_ref, sqn_ref, sq_ref) = refs[:10], refs[10:]
    partial_scores(place, data_ref, 1 - place[3], parts, out_ref, sq_ref)
    out_ref[:QUARTER, TALL:] = sq_ref[...]
    rows = []
    for blocks in blocks_of(parts):
        t = [squares(ref, [(slice(None), pl.ds(lane, 128)) for lane in range(0, SHARE, 128)]) for ref in blocks[0]]
        total = (t[0] + t[3]) + (t[1] + t[2])
        rows.append(jnp.sum(jnp.transpose(total), axis=0, keepdims=True))
    sqn_ref[...] = jnp.concatenate(rows, axis=0)
    out_ref[QUARTER:, :] = jnp.zeros((8, TALL + 128), F32)
    out_ref[QUARTER : QUARTER + 2, :128] = sqn_ref[...]


def theirs(place, data, parts):
    return pl.pallas_call(
        theirs_kernel,
        out_shape=(jax.ShapeDtypeStruct((QUARTER + 8, TALL + 128), F32), jax.ShapeDtypeStruct((2, 128), F32)),
        in_specs=[SMEM] + [VMEM] * 11,
        out_specs=(VMEM,) * 2,
        scratch_shapes=[pltpu.VMEM((QUARTER, 128), F32)],
        compiler_params=params(24),
        name="theirs",
    )(place, data, *parts)


def ours_kernel(place, data_ref, *refs):
    partial_scores(place, data_ref, place[3], refs[:10], refs[10], refs[11])


def ours(place, data, parts):
    return pl.pallas_call(
        ours_kernel,
        out_shape=(jax.ShapeDtypeStruct((QUARTER, TALL), F32), jax.ShapeDtypeStruct((QUARTER, 128), F32)),
        in_specs=[SMEM] + [VMEM] * 11,
        out_specs=(VMEM,) * 2,
        compiler_params=params(24),
        cost_estimate=pl.CostEstimate(flops=QUARTER * TALL * WIDTH, bytes_accessed=6 * 2**20, transcendentals=0),
        name="ours",
    )(place, data, *parts)


def score_kernel(mine_ref, sq_mine_ref, sqn_mine_ref, got_ref, q_ref, out_ref, sq_ref, sqn_ref, lse_ref):
    sq = jnp.sum(sq_mine_ref[...] + got_ref[:QUARTER, TALL:], axis=1, keepdims=True)
    sq_ref[...] = jnp.broadcast_to(sq, (QUARTER, 128))
    sqn_ref[...] = sqn_mine_ref[...] + got_ref[QUARTER : QUARTER + 2, :128]
    for r in range(CHUNKS):
        q = mine_ref[:, chunk(r)] + got_ref[:QUARTER, chunk(r)]
        q_ref[:, chunk(r)] = q
        lse_ref[pl.ds(r, 1), :] = lse(q - UNIT * sq_ref[...], 0)
    out_ref[...] = jnp.broadcast_to(lse_ref[...][None], (GROUP, CHUNKS, 128))


def score(mine, sq_mine, sqn_mine, got):
    return pl.pallas_call(
        score_kernel,
        out_shape=(
            jax.ShapeDtypeStruct((QUARTER, TALL), F32),
            jax.ShapeDtypeStruct((GROUP, CHUNKS, 128), F32),
            jax.ShapeDtypeStruct((QUARTER, 128), F32),
            jax.ShapeDtypeStruct((2, 128), F32),
        ),
        in_specs=[VMEM] * 4,
        out_specs=(VMEM,) * 4,
        scratch_shapes=[pltpu.VMEM((CHUNKS, 128), F32)],
        compiler_params=params(16),
        name="score",
    )(mine, sq_mine, sqn_mine, got)


def to_column(g):
    return jnp.concatenate([jnp.transpose(jnp.broadcast_to(g[r : r + 1], (128, 128))) for r in range(2)], axis=0)


def noise_kernel(q_ref, part_ref, out_ref, lse_ref, g_ref):
    g_ref[...] = to_column(-LOG2N - merged(part_ref))
    for r in range(CHUNKS):
        lse_ref[pl.ds(r, 1), :] = lse(q_ref[:, chunk(r)] + g_ref[...], 0)
    out_ref[...] = jnp.broadcast_to(lse_ref[...][None], (GROUP, CHUNKS, 128))


def noise_lse(q, parts):
    return pl.pallas_call(
        noise_kernel,
        out_shape=jax.ShapeDtypeStruct((GROUP, CHUNKS, 128), F32),
        in_specs=[VMEM] * 2,
        out_specs=VMEM,
        scratch_shapes=[pltpu.VMEM((CHUNKS, 128), F32), pltpu.VMEM((QUARTER, 128), F32)],
        compiler_params=params(16),
        name="noise_lse",
    )(q, parts)


def data_kernel(q_ref, part_ref, out_ref, f_ref, lane_ref):
    f_ref[...] = -LOG2N - merged(part_ref)
    row = data_row(q_ref, f_ref, lane_ref)
    out_ref[...] = jnp.broadcast_to(two_rows(row)[None], (Z, 8, 128))


def data_row(q_ref, f_ref, lane_ref):
    step = 32
    for start in range(0, QUARTER, step):
        rows = pl.ds(start, step)
        t = [q_ref[rows, chunk(r)] + f_ref[pl.ds(r, 1), :] for r in range(CHUNKS)]
        top = functools.reduce(jnp.maximum, t)
        lane_ref[rows, :] = top + jnp.log2(sum(jnp.exp2(part - top) for part in t))
    return lse(jnp.transpose(lane_ref[...]), 0)


def two_rows(*rows):
    halves = [half for row in rows for half in (row[:, :128], row[:, 128:])]
    return jnp.concatenate(halves + [jnp.zeros((8 - len(halves), 128), F32)], axis=0)


def data_lse(q, parts):
    return pl.pallas_call(
        data_kernel,
        out_shape=(jax.ShapeDtypeStruct((Z, 8, 128), F32), jax.ShapeDtypeStruct((CHUNKS, 128), F32)),
        in_specs=[VMEM] * 2,
        out_specs=(VMEM, VMEM),
        scratch_shapes=[pltpu.VMEM((QUARTER, 128), F32)],
        compiler_params=params(16),
        name="data_lse",
    )(q, parts)


def last_kernel(place, q_ref, part_ref, sq_ref, out_ref, f_ref, *refs):
    w_refs, lane_ref = refs[:X], refs[X]
    f_ref[...] = -LOG2N - merged(part_ref)
    tile = two_rows(data_row(q_ref, f_ref, lane_ref), jnp.transpose(sq_ref[...])[0:1, :])
    out_ref[...] = jnp.broadcast_to(tile[None], (Z * X, 8, 128))
    column = to_column(tile)
    for by in range(X):
        block = lax.rem(place[1] + by, X)
        for h in range(2):
            lanes = pl.ds(pl.multiple_of((h * X + block) * 128, 128), 128)
            w = jnp.exp2((q_ref[:, lanes] + f_ref[pl.ds(h * X + block, 1), :]) - column)
            w_refs[by][:, pl.ds(h * 128, 128)] = w.astype(BF16)


def last_lse(place, q, parts, sq):
    return pl.pallas_call(
        last_kernel,
        out_shape=(jax.ShapeDtypeStruct((Z * X, 8, 128), F32), jax.ShapeDtypeStruct((CHUNKS, 128), F32))
        + (jax.ShapeDtypeStruct((QUARTER, ROWS), BF16),) * X,
        in_specs=[SMEM] + [VMEM] * 3,
        out_specs=(VMEM,) * (2 + X),
        scratch_shapes=[pltpu.VMEM((QUARTER, 128), F32)],
        compiler_params=params(16),
        name="last_lse",
    )(place, q, parts, sq)


def scale_kernel(place, part_ref, *refs):
    w_refs, (w_ref, pot_ref) = refs[:X], refs[X:]
    z, x = place[0], place[1]
    for n in range(X):
        parts = jnp.stack([part_ref[k * X + n, 0:4, :] for k in range(Z)])
        top = jnp.max(parts, axis=0)
        total = top + jnp.log2(jnp.sum(jnp.exp2(parts - top[None]), axis=0))
        pot_ref[pl.ds(2 * n, 2), :] = (-LOG2N - total[0:2]) * (EPS / LOG2E) + parts[0, 2:4] * (1.0 / WIDTH)
    for by in range(X):
        n = lax.rem(x - by + X, X)
        parts = jnp.stack([part_ref[k * X + n] for k in range(Z)])
        top = jnp.max(parts, axis=0)
        total = top + jnp.log2(jnp.sum(jnp.exp2(parts - top[None]), axis=0))
        factor = jnp.exp2(part_ref[z * X + n] - total)
        factor = jnp.concatenate([factor[0:1], factor[1:2]], axis=1)
        lanes = pl.ds(pl.multiple_of(n * QUARTER, QUARTER), QUARTER)
        for h in range(2):
            w = jnp.transpose(w_refs[by][:, pl.ds(h * 128, 128)].astype(F32)) * factor
            w_ref[pl.ds(h * 128, 128), lanes] = w.astype(BF16)


def scale(place, parts, blocks):
    return pl.pallas_call(
        scale_kernel,
        out_shape=(jax.ShapeDtypeStruct((ROWS, COUNT), BF16), jax.ShapeDtypeStruct((2 * X, 128), F32)),
        in_specs=[SMEM] + [VMEM] * (1 + X),
        out_specs=(VMEM,) * 2,
        compiler_params=params(16),
        name="scale",
    )(place, parts, *blocks)


def transport_kernel(place, w_ref, got_ref, data_ref, own_ref, *out_refs):
    lhs = jnp.concatenate([w_ref[...], got_ref[...]], axis=1)
    for s in range(Y):
        y = at(place, 2, s, Y)
        rhs = []
        for core in (place[3], 1 - place[3]):
            for n in range(X):
                rhs.append(jnp.concatenate([data_ref[n, y, core, k] for k in range(X)], axis=1))
        total = jnp.dot(lhs, jnp.concatenate(rhs, axis=0), preferred_element_type=F32)
        if s:
            out_refs[s - 1][...] = total.astype(BF16)
        else:
            own_ref[...] = total


def transport(place, w, got, data):
    return pl.pallas_call(
        transport_kernel,
        out_shape=(jax.ShapeDtypeStruct((ROWS, SHARE), F32),)
        + (jax.ShapeDtypeStruct((ROWS, SHARE), BF16),) * (Y - 1),
        in_specs=[SMEM] + [VMEM] * 3,
        out_specs=(VMEM,) * Y,
        compiler_params=params(24),
        name="transport",
    )(place, w, got, data)


def body(noise, data):
    z, x, y, c = (lax.axis_index(a) for a in ("z", "x", "y", "core"))
    place = jnp.stack([z, x, y, c]).astype(jnp.int32)
    swapped = lax.all_to_all(data.reshape(X, QUARTER, SLICE), "x", 0, 0)
    noise_after, swapped = lax.optimization_barrier((noise, swapped))
    samples = lax.all_gather(swapped, ("z", "core")).reshape(Y, C, C, X, QUARTER, SLICE)
    samples, noise_parts = lax.optimization_barrier((samples, gather_noise(noise_after)))
    samples = lax.optimization_barrier(lax.dynamic_index_in_dim(samples, c, 1, False))
    data_all = lax.all_gather(samples, "x")
    given, sqn_mine = theirs(place, samples, noise_parts)
    got = shift(given, "core", 1)
    mine, sq_mine = ours(place, samples, noise_parts)
    q, rows, sq, sq_noise = score(mine, sq_mine, sqn_mine, got)
    for step in range(ITERS):
        if step:
            rows = noise_lse(q, columns)
        parts = lax.all_to_all(rows, ("x", "y", "core"), 0, 0)
        if step < ITERS - 1:
            columns, f = data_lse(q, parts)
            columns = lax.all_to_all(columns, "z", 0, 0)
    columns, f, *blocks = last_lse(place, q, parts, sq)
    blocks = [blocks[0]] + [shift(blocks[by], "x", by) for by in range(1, X)]
    columns = lax.all_to_all(columns, ("z", "x"), 0, 0)
    w, pot_g = scale(place, columns, blocks)
    target, *rest = transport(place, w, shift(w, "core", 1), data_all)
    for by in (2, 1, 3):
        target = target + shift(rest[by - 1], "y", by).astype(F32)
    velocity = (target - noise.astype(F32)).astype(BF16)
    own = lax.dynamic_index_in_dim(f.reshape(2, X, 128), x, 1, False)
    pot_f = (own * (EPS / LOG2E) + sq_noise / WIDTH).reshape(ROWS)
    return pot_f, pot_g.reshape(COUNT), velocity


def solution(mesh):
    fine = Mesh(mesh.devices.reshape(Z, X, Y, C), ("z", "x", "y", "core"))
    row, col = ("z", "x"), ("y", "core")
    return jax.shard_map(
        body,
        mesh=fine,
        in_specs=(P(row, col), P(col, row)),
        out_specs=(P(row), P(col), P(row, col)),
        check_vma=False,
    )
```

time: 206 us -> 200 us (0.971)
  waiting for transfers between devices: 63.2 us -> 40.2 us
  local copies, waits for them, and re-layouts: 10.2 us -> 20.6 us
  starting transfers between devices: 27.7 us -> 35 us
  Pallas kernels: 14.6 us -> 12.5 us
    all_gather x1, waiting for transfers between devices: 23.3 us -> 7.32 us  [body(): lax.all_gather(swapped, ('z', 'core')).reshape(Y, C, C, X, QUARTER, SLICE)]
    all_gather x1, waiting for transfers between devices: 12.3 us -> 0.01 us  [body(): data_all = lax.all_gather(samples, 'x')]
    ppermute x15 -> x22, starting transfers between devices: 23.8 us -> 31 us  [shift(): return lax.ppermute(x, axis, [(j, (j + by) % n) for j in range(n)])]
    unnamed x8 -> x36, local copies, waits for them, and re-layouts: 10.1 us -> 16.4 us
    ppermute x15 -> x22, waiting for transfers between devices: 26.9 us -> 32.8 us  [shift(): return lax.ppermute(x, axis, [(j, (j + by) % n) for j in range(n)])]
    pallas_call x1, Pallas kernels: 4.44 us -> 0.4 us  [score(): pl.pallas_call(score_kernel, out_shape=(jax.ShapeDtypeStruct((QUARTER, TA...]
    squeeze x0 -> x1, local copies, waits for them, and re-layouts: none -> 3.15 us  [body(): lax.dynamic_index_in_dim(samples, c, 1, False)]
  transfers between devices with their start and end apart: 18 -> 25, of which waited for: 8 -> 12; matrix products, arithmetic and copies ran while one was open for 0% -> 1% of each run, Pallas kernels for 6% -> 5%
where the time goes in v6:
time: 200 us; the launch traced here: 199 us
  blocking collectives  75.4 us (38%)
  waiting for transfers between devices  40.2 us (20%)
  starting transfers between devices  35 us (18%)
  local copies, waits for them, and re-layouts  20.6 us (10%)
  between operations  14.2 us (7%)
  Pallas kernels  12.5 us (6%)
    all_to_all x3, blocking collectives, body(): parts = lax.all_to_all(rows, ('x', 'y', 'core'), 0, 0)  41.3 us
    ppermute x22, waiting for transfers between devices, shift(): return lax.ppermute(x, axis, [(j, (j + by) % n) for j in range(n)])  32.8 us
    ppermute x22, starting transfers between devices, shift(): return lax.ppermute(x, axis, [(j, (j + by) % n) for j in range(n)])  31 us
    all_to_all x2, blocking collectives, body(): columns = lax.all_to_all(columns, 'z', 0, 0)  23.6 us
    unnamed x36, local copies, waits for them, and re-layouts  16.4 us
    all_to_all x1, blocking collectives, body(): swapped = lax.all_to_all(data.reshape(X, QUARTER, SLICE), 'x', 0, 0)  10.5 us
    all_gather x1, waiting for transfers between devices, body(): lax.all_gather(swapped, ('z', 'core')).reshape(Y, C, C, X, QUARTER, SLICE)  7.32 us
  transfers between devices with their start and end apart: 25, of which 12 were waited for; matrix products, arithmetic and copies ran while one was open for 1% of the time, Pallas kernels for 5%

profile of v6, /device:TPU:1, one launch (start us, length us, event | category | flops | bytes accessed | tf_op | source)
XLA Modules:
  0.0 199.5 jit_solution(17659289047094756069)
XLA Ops:
  7.2 10.5 %all_to_all.35 = bf16[4,256,128]{2,1,0:T(8,128)(2,1)} all-to-all(bf16[4,256,128]{2,1,0:T(8,128)(2,1)} %bitcast.31), channel_id=1, replica_groups=mesh['z'=8,'x'=4,'y'=4,'core'=2] {'x'}, dimensions={0} | all-to-all | bytes 524288 | tf_op jit(solution)/shard_map/all_to_all | solution.py:330
  19.1 2.4 %collective-permute-start.1 = (bf16[128,512]{1,0:T(8,128)(2,1)S(1)}, bf16[128,512]{1,0:T(8,128)(2,1)S(1)}, u32[]{:S(2)}, u32[]{:S(2)}) collective-permute-start(bf16[128,512]{1,0:T(8,128)(2,1)S(1)} %get-tuple-element.52), channel_id=1, source_target_pairs={{0,24},{8,0},{16,8},{24,16},{1,25},{9,1},{17,9},{25,17},{2,26},{10... | collective-permute-start | bytes 393224 | tf_op jit(solution)/shard_map/ppermute | solution.py:34
  24.3 2.5 %collective-permute-start.5 = (bf16[128,512]{1,0:T(8,128)(2,1)S(1)}, bf16[128,512]{1,0:T(8,128)(2,1)S(1)}, u32[]{:S(2)}, u32[]{:S(2)}) collective-permute-start(bf16[128,512]{1,0:T(8,128)(2,1)S(1)} %get-tuple-element.56), channel_id=1, source_target_pairs={{0,4},{2,6},{4,0},{6,2},{1,5},{3,7},{5,1},{7,3},{8,12},{10,14},{12... | collective-permute-start | bytes 393224 | tf_op jit(solution)/shard_map/ppermute | solution.py:34
  31.0 2.3 %collective-permute-start.7 = (bf16[4,128,512]{2,1,0:T(8,128)(2,1)S(1)}, bf16[4,128,512]{2,1,0:T(8,128)(2,1)S(1)}, u32[]{:S(2)}, u32[]{:S(2)}) collective-permute-start(bf16[4,128,512]{2,1,0:T(8,128)(2,1)S(1)} %pad_maximum_fusion.refs_0_), channel_id=1, source_target_pairs={{0,6},{2,0},{4,2},{6,4},{1,7},{3,1},{5,3},{7,5},{8,14},{10,8},{12,... | collective-permute-start | bytes 1572872 | tf_op jit(solution)/shard_map/ppermute | solution.py:34
  33.4 2.7 %collective-permute-start.9 = (bf16[4,128,512]{2,1,0:T(8,128)(2,1)S(1)}, bf16[4,128,512]{2,1,0:T(8,128)(2,1)S(1)}, u32[]{:S(2)}, u32[]{:S(2)}) collective-permute-start(bf16[4,128,512]{2,1,0:T(8,128)(2,1)S(1)} %pad_maximum_fusion.1.refs_5_), channel_id=1, source_target_pairs={{0,24},{8,0},{16,8},{24,16},{1,25},{9,1},{17,9},{25,17},{2,26},{10... | collective-permute-start | bytes 1572872 | tf_op jit(solution)/shard_map/ppermute | solution.py:34
  36.1 5.5 %collective-permute-done.6.refs_1_ = bf16[4,128,512]{2,1,0:T(8,128)(2,1)S(1)} collective-permute-done((bf16[4,128,512]{2,1,0:T(8,128)(2,1)S(1)}, bf16[4,128,512]{2,1,0:T(8,128)(2,1)S(1)}, u32[]{:S(2)}, u32[]{:S(2)}) %collective-permute-start.6) | collective-permute-done | bytes 524320 | tf_op jit(solution)/shard_map/ppermute | solution.py:34
  43.8 2.8 %collective-permute-start.11 = (bf16[2,128,512]{2,1,0:T(8,128)(2,1)S(1)}, bf16[2,128,512]{2,1,0:T(8,128)(2,1)S(1)}, u32[]{:S(2)}, u32[]{:S(2)}) collective-permute-start(bf16[2,128,512]{2,1,0:T(8,128)(2,1)S(1)} %slice.21), channel_id=1, source_target_pairs={{0,6},{2,0},{4,2},{6,4},{1,7},{3,1},{5,3},{7,5},{8,14},{10,8},{12,... | collective-permute-start | bytes 786440 | tf_op jit(solution)/shard_map/ppermute | solution.py:34
  51.6 2.6 %collective-permute-done.12.refs_8_ = bf16[2,128,512]{2,1,0:T(8,128)(2,1)S(1)} collective-permute-done((bf16[2,128,512]{2,1,0:T(8,128)(2,1)S(1)}, bf16[2,128,512]{2,1,0:T(8,128)(2,1)S(1)}, u32[]{:S(2)}, u32[]{:S(2)}) %collective-permute-start.12) | collective-permute-done | bytes 262176 | tf_op jit(solution)/shard_map/ppermute | solution.py:34
  55.6 7.3 %all-gather.5.cloned.1.call-done = bf16[64,256,128]{2,1,0:T(8,128)(2,1)} async-done(((bf16[4,256,128]{2,1,0:T(8,128)(2,1)}), bf16[64,256,128]{2,1,0:T(8,128)(2,1)}) %all-gather.5.cloned.1.call-update) | async-done | bytes 4194320 | tf_op jit(solution)/shard_map/all_gather | solution.py:332
  63.0 3.1 %dynamic-slice_bitcast_fusion.data_ref = bf16[4,2,4,256,128]{4,3,2,1,0:T(8,128)(2,1)} fusion(bf16[4,2,2,4,256,128]{5,4,3,2,1,0:T(8,128)(2,1)} %bitcast.28, s32[]{:T(128)S(6)} %select_n.8), kind=kLoop, calls=%fused_computation | loop fusion | bytes 4194308 | tf_op jit(solution)/shard_map/jit(dynamic_index_in_dim)/squeeze | solution.py:334
  76.7 3.0 %collective-permute-start.14 = (f32[264,1152]{1,0:T(8,128)S(1)}, f32[264,1152]{1,0:T(8,128)S(1)}, u32[]{:S(2)}, u32[]{:S(2)}) collective-permute-start(f32[264,1152]{1,0:T(8,128)S(1)} %get-tuple-element.78), channel_id=1, source_target_pairs={{0,1},{1,0},{2,3},{3,2},{4,5},{5,4},{6,7},{7,6},{8,9},{9,8},{10,11... | collective-permute-start | bytes 3649544 | tf_op jit(solution)/shard_map/ppermute | solution.py:34
  82.6 13.6 %all_to_all.36.part_ref = f32[32,8,128]{2,1,0:T(8,128)S(1)} all-to-all(f32[32,8,128]{2,1,0:T(8,128)S(1)} %get-tuple-element.80), channel_id=1, replica_groups=mesh['z'=8,'x'=4,'y'=4,'core'=2] {'x','y','core'}, dimensions={0} | all-to-all | bytes 262144 | tf_op jit(solution)/shard_map/all_to_all | solution.py:343
  97.0 14.3 %all_to_all.37.part_ref = f32[8,8,128]{2,1,0:T(8,128)S(1)} all-to-all(f32[8,8,128]{2,1,0:T(8,128)S(1)} %get-tuple-element.81), channel_id=1, replica_groups=mesh['z'=8,'x'=4,'y'=4,'core'=2] {'z'}, dimensions={0} | all-to-all | bytes 65536 | tf_op jit(solution)/shard_map/all_to_all | solution.py:346
  111.7 14.0 %all_to_all.38.part_ref = f32[32,8,128]{2,1,0:T(8,128)S(1)} all-to-all(f32[32,8,128]{2,1,0:T(8,128)S(1)} %noise_lse.2), channel_id=1, replica_groups=mesh['z'=8,'x'=4,'y'=4,'core'=2] {'x','y','core'}, dimensions={0} | all-to-all | bytes 262144 | tf_op jit(solution)/shard_map/all_to_all | solution.py:343
  126.5 9.2 %all_to_all.39.part_ref = f32[8,8,128]{2,1,0:T(8,128)S(1)} all-to-all(f32[8,8,128]{2,1,0:T(8,128)S(1)} %get-tuple-element.82), channel_id=1, replica_groups=mesh['z'=8,'x'=4,'y'=4,'core'=2] {'z'}, dimensions={0} | all-to-all | bytes 65536 | tf_op jit(solution)/shard_map/all_to_all | solution.py:346
  136.1 13.7 %all_to_all.40.part_ref = f32[32,8,128]{2,1,0:T(8,128)S(1)} all-to-all(f32[32,8,128]{2,1,0:T(8,128)S(1)} %noise_lse.3), channel_id=1, replica_groups=mesh['z'=8,'x'=4,'y'=4,'core'=2] {'x','y','core'}, dimensions={0} | all-to-all | bytes 262144 | tf_op jit(solution)/shard_map/all_to_all | solution.py:343
  151.4 3.9 %all-to-all-start.6 = ((f32[32,8,128]{2,1,0:T(8,128)}), f32[32,8,128]{2,1,0:T(8,128)S(1)}, u32[]{:S(2)}, u32[]{:S(2)}) async-start(f32[32,8,128]{2,1,0:T(8,128)} %get-tuple-element.86), calls=%async_computation.6 | async-start | bytes 262144 | tf_op jit(solution)/shard_map/all_to_all | solution.py:349
  156.5 2.4 %collective-permute-start.16 = (bf16[256,256]{1,0:T(8,128)(2,1)S(1)}, bf16[256,256]{1,0:T(8,128)(2,1)S(1)}, u32[]{:S(2)}, u32[]{:S(2)}) collective-permute-start(bf16[256,256]{1,0:T(8,128)(2,1)S(1)} %get-tuple-element.89), channel_id=1, source_target_pairs={{0,16},{8,24},{16,0},{24,8},{1,17},{9,25},{17,1},{25,9},{2,18},{10... | collective-permute-start | bytes 393224 | tf_op jit(solution)/shard_map/ppermute | solution.py:34
  160.1 2.5 %collective-permute-done.15.refs_1_ = bf16[256,256]{1,0:T(8,128)(2,1)S(1)} collective-permute-done((bf16[256,256]{1,0:T(8,128)(2,1)S(1)}, bf16[256,256]{1,0:T(8,128)(2,1)S(1)}, u32[]{:S(2)}, u32[]{:S(2)}) %collective-permute-start.15) | collective-permute-done | bytes 131104 | tf_op jit(solution)/shard_map/ppermute | solution.py:34
  162.5 3.9 %collective-permute-done.16.refs_2_ = bf16[256,256]{1,0:T(8,128)(2,1)S(1)} collective-permute-done((bf16[256,256]{1,0:T(8,128)(2,1)S(1)}, bf16[256,256]{1,0:T(8,128)(2,1)S(1)}, u32[]{:S(2)}, u32[]{:S(2)}) %collective-permute-start.16) | collective-permute-done | bytes 131104 | tf_op jit(solution)/shard_map/ppermute | solution.py:34
  170.4 3.4 %copy-done.1 = bf16[16,2,4,256,128]{4,3,2,1,0:T(8,128)(2,1)S(1)} copy-done((bf16[16,2,4,256,128]{4,3,2,1,0:T(8,128)(2,1)S(1)}, bf16[16,2,4,256,128]{4,3,2,1,0:T(8,128)(2,1)}, u32[]{:S(2)}) %copy-start.1) | copy-done | bytes 8388632
  173.7 2.9 %transport.1 = (f32[256,512]{1,0:T(8,128)S(1)}, bf16[256,512]{1,0:T(8,128)(2,1)S(1)}, bf16[256,512]{1,0:T(8,128)(2,1)S(1)}, bf16[256,512]{1,0:T(8,128)(2,1)S(1)}) custom-call(s32[4]{0:T(128)S(1)} %pad_add_fusion.place, bf16[256,1024]{1,0:T(8,128)(2,1)S(1)} %get-tuple-element.92.w_ref, bf16[256,1024]{1,0:T(8,128)(2,1)S(1)} %collective-permute-done.18.got_ref, ...), custom_call_target="tpu_custom_call" | custom-call | tf_op jit(solution)/shard_map/transport/pallas_call | solution.py:316
  179.7 4.5 %collective-permute-done.21 = bf16[256,512]{1,0:T(8,128)(2,1)S(1)} collective-permute-done((bf16[256,512]{1,0:T(8,128)(2,1)S(1)}, bf16[256,512]{1,0:T(8,128)(2,1)S(1)}, u32[]{:S(2)}, u32[]{:S(2)}) %collective-permute-start.21) | collective-permute-done | bytes 262176 | tf_op jit(solution)/shard_map/ppermute | solution.py:34
  184.2 7.5 %collective-permute-done.20 = bf16[256,512]{1,0:T(8,128)(2,1)S(1)} collective-permute-done((bf16[256,512]{1,0:T(8,128)(2,1)S(1)}, bf16[256,512]{1,0:T(8,128)(2,1)S(1)}, u32[]{:S(2)}, u32[]{:S(2)}) %collective-permute-start.20) | collective-permute-done | bytes 262176 | tf_op jit(solution)/shard_map/ppermute | solution.py:34
  (92 shorter events, 44.8 us)
Async XLA Ops:
  7.2 55.8 %all-gather.5.cloned.1.call-start = ((), (), s32[]{:S(2)}) async-start(), calls=%async_computation.7 | async-start | bytes 4456448 | tf_op jit(solution)/shard_map/all_gather | solution.py:332
  17.7 152.6 %all-gather.7.cloned.1.call-start = ((), (), s32[]{:S(2)}) async-start(), calls=%async_computation.8 | async-start | bytes 10485760 | tf_op jit(solution)/shard_map/all_gather | solution.py:335
  18.8 5.5 %collective-permute-start = (bf16[128,512]{1,0:T(8,128)(2,1)S(1)}, bf16[128,512]{1,0:T(8,128)(2,1)S(1)}, u32[]{:S(2)}, u32[]{:S(2)}) collective-permute-start(bf16[128,512]{1,0:T(8,128)(2,1)S(1)} %get-tuple-element.52), channel_id=1, source_target_pairs={{0,8},{8,16},{16,24},{24,0},{1,9},{9,17},{17,25},{25,1},{2,10},{10... | collective-permute-start | bytes 393224 | tf_op jit(solution)/shard_map/ppermute | solution.py:34
  19.1 7.7 %collective-permute-start.1 = (bf16[128,512]{1,0:T(8,128)(2,1)S(1)}, bf16[128,512]{1,0:T(8,128)(2,1)S(1)}, u32[]{:S(2)}, u32[]{:S(2)}) collective-permute-start(bf16[128,512]{1,0:T(8,128)(2,1)S(1)} %get-tuple-element.52), channel_id=1, source_target_pairs={{0,24},{8,0},{16,8},{24,16},{1,25},{9,1},{17,9},{25,17},{2,26},{10... | collective-permute-start | bytes 393224 | tf_op jit(solution)/shard_map/ppermute | solution.py:34
  21.5 6.4 %collective-permute-start.2 = (bf16[128,512]{1,0:T(8,128)(2,1)S(1)}, bf16[128,512]{1,0:T(8,128)(2,1)S(1)}, u32[]{:S(2)}, u32[]{:S(2)}) collective-permute-start(bf16[128,512]{1,0:T(8,128)(2,1)S(1)} %get-tuple-element.52), channel_id=1, source_target_pairs={{0,16},{8,24},{16,0},{24,8},{1,17},{9,25},{17,1},{25,9},{2,18},{10... | collective-permute-start | bytes 393224 | tf_op jit(solution)/shard_map/ppermute | solution.py:34
  21.5 6.4 %collective-permute-start.3 = (bf16[128,512]{1,0:T(8,128)(2,1)S(1)}, bf16[128,512]{1,0:T(8,128)(2,1)S(1)}, u32[]{:S(2)}, u32[]{:S(2)}) collective-permute-start(bf16[128,512]{1,0:T(8,128)(2,1)S(1)} %get-tuple-element.56), channel_id=1, source_target_pairs={{0,2},{2,4},{4,6},{6,0},{1,3},{3,5},{5,7},{7,1},{8,10},{10,12},{12... | collective-permute-start | bytes 393224 | tf_op jit(solution)/shard_map/ppermute | solution.py:34
  22.8 5.0 %collective-permute-start.4 = (bf16[128,512]{1,0:T(8,128)(2,1)S(1)}, bf16[128,512]{1,0:T(8,128)(2,1)S(1)}, u32[]{:S(2)}, u32[]{:S(2)}) collective-permute-start(bf16[128,512]{1,0:T(8,128)(2,1)S(1)} %get-tuple-element.56), channel_id=1, source_target_pairs={{0,6},{2,0},{4,2},{6,4},{1,7},{3,1},{5,3},{7,5},{8,14},{10,8},{12,... | collective-permute-start | bytes 393224 | tf_op jit(solution)/shard_map/ppermute | solution.py:34
  24.3 5.4 %collective-permute-start.5 = (bf16[128,512]{1,0:T(8,128)(2,1)S(1)}, bf16[128,512]{1,0:T(8,128)(2,1)S(1)}, u32[]{:S(2)}, u32[]{:S(2)}) collective-permute-start(bf16[128,512]{1,0:T(8,128)(2,1)S(1)} %get-tuple-element.56), channel_id=1, source_target_pairs={{0,4},{2,6},{4,0},{6,2},{1,5},{3,7},{5,1},{7,3},{8,12},{10,14},{12... | collective-permute-start | bytes 393224 | tf_op jit(solution)/shard_map/ppermute | solution.py:34
  29.7 11.9 %collective-permute-start.6 = (bf16[4,128,512]{2,1,0:T(8,128)(2,1)S(1)}, bf16[4,128,512]{2,1,0:T(8,128)(2,1)S(1)}, u32[]{:S(2)}, u32[]{:S(2)}) collective-permute-start(bf16[4,128,512]{2,1,0:T(8,128)(2,1)S(1)} %pad_maximum_fusion.refs_0_), channel_id=1, source_target_pairs={{0,2},{2,4},{4,6},{6,0},{1,3},{3,5},{5,7},{7,1},{8,10},{10,12},{12... | collective-permute-start | bytes 1572872 | tf_op jit(solution)/shard_map/ppermute | solution.py:34
  31.0 10.6 %collective-permute-start.7 = (bf16[4,128,512]{2,1,0:T(8,128)(2,1)S(1)}, bf16[4,128,512]{2,1,0:T(8,128)(2,1)S(1)}, u32[]{:S(2)}, u32[]{:S(2)}) collective-permute-start(bf16[4,128,512]{2,1,0:T(8,128)(2,1)S(1)} %pad_maximum_fusion.refs_0_), channel_id=1, source_target_pairs={{0,6},{2,0},{4,2},{6,4},{1,7},{3,1},{5,3},{7,5},{8,14},{10,8},{12,... | collective-permute-start | bytes 1572872 | tf_op jit(solution)/shard_map/ppermute | solution.py:34
  33.3 9.6 %collective-permute-start.8 = (bf16[4,128,512]{2,1,0:T(8,128)(2,1)S(1)}, bf16[4,128,512]{2,1,0:T(8,128)(2,1)S(1)}, u32[]{:S(2)}, u32[]{:S(2)}) collective-permute-start(bf16[4,128,512]{2,1,0:T(8,128)(2,1)S(1)} %pad_maximum_fusion.1.refs_5_), channel_id=1, source_target_pairs={{0,8},{8,16},{16,24},{24,0},{1,9},{9,17},{17,25},{25,1},{2,10},{10... | collective-permute-start | bytes 1572872 | tf_op jit(solution)/shard_map/ppermute | solution.py:34
  33.4 9.5 %collective-permute-start.9 = (bf16[4,128,512]{2,1,0:T(8,128)(2,1)S(1)}, bf16[4,128,512]{2,1,0:T(8,128)(2,1)S(1)}, u32[]{:S(2)}, u32[]{:S(2)}) collective-permute-start(bf16[4,128,512]{2,1,0:T(8,128)(2,1)S(1)} %pad_maximum_fusion.1.refs_5_), channel_id=1, source_target_pairs={{0,24},{8,0},{16,8},{24,16},{1,25},{9,1},{17,9},{25,17},{2,26},{10... | collective-permute-start | bytes 1572872 | tf_op jit(solution)/shard_map/ppermute | solution.py:34
  43.8 7.1 %collective-permute-start.10 = (bf16[2,128,512]{2,1,0:T(8,128)(2,1)S(1)}, bf16[2,128,512]{2,1,0:T(8,128)(2,1)S(1)}, u32[]{:S(2)}, u32[]{:S(2)}) collective-permute-start(bf16[2,128,512]{2,1,0:T(8,128)(2,1)S(1)} %slice.20), channel_id=1, source_target_pairs={{0,2},{2,4},{4,6},{6,0},{1,3},{3,5},{5,7},{7,1},{8,10},{10,12},{12... | collective-permute-start | bytes 786440 | tf_op jit(solution)/shard_map/ppermute | solution.py:34
  43.8 7.1 %collective-permute-start.11 = (bf16[2,128,512]{2,1,0:T(8,128)(2,1)S(1)}, bf16[2,128,512]{2,1,0:T(8,128)(2,1)S(1)}, u32[]{:S(2)}, u32[]{:S(2)}) collective-permute-start(bf16[2,128,512]{2,1,0:T(8,128)(2,1)S(1)} %slice.21), channel_id=1, source_target_pairs={{0,6},{2,0},{4,2},{6,4},{1,7},{3,1},{5,3},{7,5},{8,14},{10,8},{12,... | collective-permute-start | bytes 786440 | tf_op jit(solution)/shard_map/ppermute | solution.py:34
  47.4 6.8 %collective-permute-start.12 = (bf16[2,128,512]{2,1,0:T(8,128)(2,1)S(1)}, bf16[2,128,512]{2,1,0:T(8,128)(2,1)S(1)}, u32[]{:S(2)}, u32[]{:S(2)}) collective-permute-start(bf16[2,128,512]{2,1,0:T(8,128)(2,1)S(1)} %slice.22), channel_id=1, source_target_pairs={{0,8},{8,16},{16,24},{24,0},{1,9},{9,17},{17,25},{25,1},{2,10},{10... | collective-permute-start | bytes 786440 | tf_op jit(solution)/shard_map/ppermute | solution.py:34
  49.0 6.0 %collective-permute-start.13 = (bf16[2,128,512]{2,1,0:T(8,128)(2,1)S(1)}, bf16[2,128,512]{2,1,0:T(8,128)(2,1)S(1)}, u32[]{:S(2)}, u32[]{:S(2)}) collective-permute-start(bf16[2,128,512]{2,1,0:T(8,128)(2,1)S(1)} %slice.23), channel_id=1, source_target_pairs={{0,24},{8,0},{16,8},{24,16},{1,25},{9,1},{17,9},{25,17},{2,26},{10... | collective-permute-start | bytes 786440 | tf_op jit(solution)/shard_map/ppermute | solution.py:34
  76.7 5.6 %collective-permute-start.14 = (f32[264,1152]{1,0:T(8,128)S(1)}, f32[264,1152]{1,0:T(8,128)S(1)}, u32[]{:S(2)}, u32[]{:S(2)}) collective-permute-start(f32[264,1152]{1,0:T(8,128)S(1)} %get-tuple-element.78), channel_id=1, source_target_pairs={{0,1},{1,0},{2,3},{3,2},{4,5},{5,4},{6,7},{7,6},{8,9},{9,8},{10,11... | collective-permute-start | bytes 3649544 | tf_op jit(solution)/shard_map/ppermute | solution.py:34
  151.4 15.0 %all-to-all-start.6 = ((f32[32,8,128]{2,1,0:T(8,128)}), f32[32,8,128]{2,1,0:T(8,128)S(1)}, u32[]{:S(2)}, u32[]{:S(2)}) async-start(f32[32,8,128]{2,1,0:T(8,128)} %get-tuple-element.86), calls=%async_computation.6 | async-start | bytes 262144 | tf_op jit(solution)/shard_map/all_to_all | solution.py:349
  155.3 7.2 %collective-permute-start.15 = (bf16[256,256]{1,0:T(8,128)(2,1)S(1)}, bf16[256,256]{1,0:T(8,128)(2,1)S(1)}, u32[]{:S(2)}, u32[]{:S(2)}) collective-permute-start(bf16[256,256]{1,0:T(8,128)(2,1)S(1)} %get-tuple-element.88), channel_id=1, source_target_pairs={{0,8},{8,16},{16,24},{24,0},{1,9},{9,17},{17,25},{25,1},{2,10},{10... | collective-permute-start | bytes 393224 | tf_op jit(solution)/shard_map/ppermute | solution.py:34
  156.5 9.9 %collective-permute-start.16 = (bf16[256,256]{1,0:T(8,128)(2,1)S(1)}, bf16[256,256]{1,0:T(8,128)(2,1)S(1)}, u32[]{:S(2)}, u32[]{:S(2)}) collective-permute-start(bf16[256,256]{1,0:T(8,128)(2,1)S(1)} %get-tuple-element.89), channel_id=1, source_target_pairs={{0,16},{8,24},{16,0},{24,8},{1,17},{9,25},{17,1},{25,9},{2,18},{10... | collective-permute-start | bytes 393224 | tf_op jit(solution)/shard_map/ppermute | solution.py:34
  158.9 7.5 %collective-permute-start.17 = (bf16[256,256]{1,0:T(8,128)(2,1)S(1)}, bf16[256,256]{1,0:T(8,128)(2,1)S(1)}, u32[]{:S(2)}, u32[]{:S(2)}) collective-permute-start(bf16[256,256]{1,0:T(8,128)(2,1)S(1)} %get-tuple-element.90), channel_id=1, source_target_pairs={{0,24},{8,0},{16,8},{24,16},{1,25},{9,1},{17,9},{25,17},{2,26},{10... | collective-permute-start | bytes 393224 | tf_op jit(solution)/shard_map/ppermute | solution.py:34
  176.6 7.6 %collective-permute-start.21 = (bf16[256,512]{1,0:T(8,128)(2,1)S(1)}, bf16[256,512]{1,0:T(8,128)(2,1)S(1)}, u32[]{:S(2)}, u32[]{:S(2)}) collective-permute-start(bf16[256,512]{1,0:T(8,128)(2,1)S(1)} %get-tuple-element.96), channel_id=1, source_target_pairs={{0,6},{2,0},{4,2},{6,4},{1,7},{3,1},{5,3},{7,5},{8,14},{10,8},{12,... | collective-permute-start | bytes 786440 | tf_op jit(solution)/shard_map/ppermute | solution.py:34
  177.7 14.0 %collective-permute-start.20 = (bf16[256,512]{1,0:T(8,128)(2,1)S(1)}, bf16[256,512]{1,0:T(8,128)(2,1)S(1)}, u32[]{:S(2)}, u32[]{:S(2)}) collective-permute-start(bf16[256,512]{1,0:T(8,128)(2,1)S(1)} %get-tuple-element.95), channel_id=1, source_target_pairs={{0,2},{2,4},{4,6},{6,0},{1,3},{3,5},{5,7},{7,1},{8,10},{10,12},{12... | collective-permute-start | bytes 786440 | tf_op jit(solution)/shard_map/ppermute | solution.py:34
  178.2 13.6 %collective-permute-start.19 = (bf16[256,512]{1,0:T(8,128)(2,1)S(1)}, bf16[256,512]{1,0:T(8,128)(2,1)S(1)}, u32[]{:S(2)}, u32[]{:S(2)}) collective-permute-start(bf16[256,512]{1,0:T(8,128)(2,1)S(1)} %get-tuple-element.94), channel_id=1, source_target_pairs={{0,4},{2,6},{4,0},{6,2},{1,5},{3,7},{5,1},{7,3},{8,12},{10,14},{12... | collective-permute-start | bytes 786440 | tf_op jit(solution)/shard_map/ppermute | solution.py:34
  (19 other events, 44.3 us)
Sparse Core Ops, SparseCore 0:
  17.8 45.0 all-gather.4
  66.2 91.6 all-gather.6

commit v7 on v6

--- a/solution.py
+++ b/solution.py
@@ -100,11 +100,59 @@
     )
 
 
-def partial_scores(place, data_ref, core, parts, q_ref, sq_ref):
+def collect_kernel(*refs):
+    parts, (noise_ref, sqn_ref) = refs[:10], refs[10:]
+    rows = []
+    for h, blocks in enumerate(blocks_of(parts)):
+        for j, row in enumerate(blocks):
+            for k, ref in enumerate(row):
+                noise_ref[pl.ds((h * X + j) * CUT, CUT), pl.ds(k * SHARE, SHARE)] = ref[...]
+        t = [squares(ref, [(slice(None), pl.ds(lane, 128)) for lane in range(0, SHARE, 128)]) for ref in blocks[0]]
+        total = (t[0] + t[3]) + (t[1] + t[2])
+        rows.append(jnp.sum(jnp.transpose(total), axis=0, keepdims=True))
+    sqn_ref[...] = jnp.concatenate(rows, axis=0)
+
+
+def collect(parts):
+    return pl.pallas_call(
+        collect_kernel,
+        out_shape=(jax.ShapeDtypeStruct((TALL, WIDTH // C), BF16), jax.ShapeDtypeStruct((2, 128), F32)),
+        in_specs=[VMEM] * 10,
+        out_specs=(VMEM,) * 2,
+        compiler_params=params(16),
+        name="collect",
+    )(*parts)
+
+
+def pick_kernel(place, all_ref, far_ref, near_ref, sems):
+    copies = []
+    for y in range(Y):
+        for n, ref in enumerate((near_ref, far_ref)):
+            copies.append(pltpu.make_async_copy(all_ref.at[y, place[3]], ref.at[y], sems.at[n, y]))
+    for copy in copies:
+        copy.start()
+    for copy in copies:
+        copy.wait()
+
+
+def pick(place, samples):
+    half = jax.ShapeDtypeStruct((Y, C, X, QUARTER, SLICE), BF16)
+    return pl.pallas_call(
+        pick_kernel,
+        out_shape=(half, half),
+        in_specs=[SMEM, pl.BlockSpec(memory_space=pl.ANY)],
+        out_specs=(pl.BlockSpec(memory_space=pl.ANY), VMEM),
+        scratch_shapes=[pltpu.SemaphoreType.DMA((2, Y))],
+        compiler_params=params(47),
+        name="pick",
+    )(place, samples)
+
+
+def partial_scores(place, data_ref, core, noise_ref, q_ref, sq_ref):
     pieces = [at(place, 2, rel, Y) for rel in AROUND]
     lhs = jnp.concatenate([data_ref[p, core, n] for p in pieces for n in range(X)], axis=1)
-    for h, blocks in enumerate(blocks_of(parts)):
-        rhs = jnp.concatenate([jnp.concatenate([ref[...] for ref in row], axis=1) for row in blocks], axis=0)
+    for h in range(2):
+        rhs = noise_ref[pl.ds(h * X * CUT, X * CUT), :]
         gram = lax.dot_general(lhs, rhs, (((1,), (1,)), ((), ())), preferred_element_type=F32) * (2.0 * UNIT)
         for j, rel in enumerate(AROUND):
             lanes = pl.ds(pl.multiple_of((h * X + at(place, 1, rel, X)) * 128, 128), 128)
@@ -112,46 +160,39 @@
     sq_ref[...] = squares(data_ref, [(p, core, n) for p in range(Y) for n in range(X)])
 
 
-def theirs_kernel(place, data_ref, *refs):
-    parts, (out_ref, sqn_ref, sq_ref) = refs[:10], refs[10:]
-    partial_scores(place, data_ref, 1 - place[3], parts, out_ref, sq_ref)
+def theirs_kernel(place, data_ref, noise_ref, sqn_ref, out_ref, sq_ref):
+    partial_scores(place, data_ref, 1 - place[3], noise_ref, out_ref, sq_ref)
     out_ref[:QUARTER, TALL:] = sq_ref[...]
-    rows = []
-    for blocks in blocks_of(parts):
-        t = [squares(ref, [(slice(None), pl.ds(lane, 128)) for lane in range(0, SHARE, 128)]) for ref in blocks[0]]
-        total = (t[0] + t[3]) + (t[1] + t[2])
-        rows.append(jnp.sum(jnp.transpose(total), axis=0, keepdims=True))
-    sqn_ref[...] = jnp.concatenate(rows, axis=0)
     out_ref[QUARTER:, :] = jnp.zeros((8, TALL + 128), F32)
     out_ref[QUARTER : QUARTER + 2, :128] = sqn_ref[...]
 
 
-def theirs(place, data, parts):
+def theirs(place, data, noise, sqn):
     return pl.pallas_call(
         theirs_kernel,
-        out_shape=(jax.ShapeDtypeStruct((QUARTER + 8, TALL + 128), F32), jax.ShapeDtypeStruct((2, 128), F32)),
-        in_specs=[SMEM] + [VMEM] * 11,
-        out_specs=(VMEM,) * 2,
+        out_shape=jax.ShapeDtypeStruct((QUARTER + 8, TALL + 128), F32),
+        in_specs=[SMEM] + [VMEM] * 3,
+        out_specs=VMEM,
         scratch_shapes=[pltpu.VMEM((QUARTER, 128), F32)],
         compiler_params=params(24),
         name="theirs",
-    )(place, data, *parts)
-
-
-def ours_kernel(place, data_ref, *refs):
-    partial_scores(place, data_ref, place[3], refs[:10], refs[10], refs[11])
-
-
-def ours(place, data, parts):
+    )(place, data, noise, sqn)
+
+
+def ours_kernel(place, data_ref, noise_ref, q_ref, sq_ref):
+    partial_scores(place, data_ref, place[3], noise_ref, q_ref, sq_ref)
+
+
+def ours(place, data, noise):
     return pl.pallas_call(
         ours_kernel,
         out_shape=(jax.ShapeDtypeStruct((QUARTER, TALL), F32), jax.ShapeDtypeStruct((QUARTER, 128), F32)),
-        in_specs=[SMEM] + [VMEM] * 11,
+        in_specs=[SMEM] + [VMEM] * 2,
         out_specs=(VMEM,) * 2,
         compiler_params=params(24),
         cost_estimate=pl.CostEstimate(flops=QUARTER * TALL * WIDTH, bytes_accessed=6 * 2**20, transcendentals=0),
         name="ours",
-    )(place, data, *parts)
+    )(place, data, noise)
 
 
 def score_kernel(mine_ref, sq_mine_ref, sqn_mine_ref, got_ref, q_ref, out_ref, sq_ref, sqn_ref, lse_ref):
@@ -297,29 +338,32 @@
     )(place, parts, *blocks)
 
 
-def transport_kernel(place, w_ref, got_ref, data_ref, own_ref, *out_refs):
+def transport_kernel(pieces, place, w_ref, got_ref, data_ref, *out_refs):
     lhs = jnp.concatenate([w_ref[...], got_ref[...]], axis=1)
-    for s in range(Y):
+    for s, out_ref in zip(pieces, out_refs):
         y = at(place, 2, s, Y)
         rhs = []
         for core in (place[3], 1 - place[3]):
             for n in range(X):
                 rhs.append(jnp.concatenate([data_ref[n, y, core, k] for k in range(X)], axis=1))
         total = jnp.dot(lhs, jnp.concatenate(rhs, axis=0), preferred_element_type=F32)
-        if s:
-            out_refs[s - 1][...] = total.astype(BF16)
-        else:
-            own_ref[...] = total
-
-
-def transport(place, w, got, data):
-    return pl.pallas_call(
-        transport_kernel,
-        out_shape=(jax.ShapeDtypeStruct((ROWS, SHARE), F32),)
-        + (jax.ShapeDtypeStruct((ROWS, SHARE), BF16),) * (Y - 1),
+        out_ref[...] = total.astype(out_ref.dtype)
+
+
+def transport(place, w, got, data, pieces, hand_on):
+    kinds = [jax.ShapeDtypeStruct((ROWS, SHARE), BF16 if s else F32) for s in pieces]
+    if hand_on:
+        kinds.append(jax.ShapeDtypeStruct(data.shape, data.dtype))
+    return pl.pallas_call(
+        functools.partial(transport_kernel, pieces),
+        out_shape=kinds,
         in_specs=[SMEM] + [VMEM] * 3,
-        out_specs=(VMEM,) * Y,
+        out_specs=[VMEM] * len(kinds),
+        input_output_aliases={3: len(pieces)} if hand_on else {},
         compiler_params=params(24),
+        cost_estimate=pl.CostEstimate(
+            flops=2 * ROWS * COUNT * C * SHARE * len(pieces), bytes_accessed=2 * 2**20 * len(pieces), transcendentals=0
+        ),
         name="transport",
     )(place, w, got, data)
 
@@ -330,12 +374,11 @@
     swapped = lax.all_to_all(data.reshape(X, QUARTER, SLICE), "x", 0, 0)
     noise_after, swapped = lax.optimization_barrier((noise, swapped))
     samples = lax.all_gather(swapped, ("z", "core")).reshape(Y, C, C, X, QUARTER, SLICE)
-    samples, noise_parts = lax.optimization_barrier((samples, gather_noise(noise_after)))
-    samples = lax.optimization_barrier(lax.dynamic_index_in_dim(samples, c, 1, False))
-    data_all = lax.all_gather(samples, "x")
-    given, sqn_mine = theirs(place, samples, noise_parts)
-    got = shift(given, "core", 1)
-    mine, sq_mine = ours(place, samples, noise_parts)
+    samples, noise_all, sqn_mine = lax.optimization_barrier((samples, *collect(gather_noise(noise_after))))
+    far, near = pick(place, samples)
+    data_all = lax.all_gather(far, "x")
+    got = shift(theirs(place, near, noise_all, sqn_mine), "core", 1)
+    mine, sq_mine = ours(place, near, noise_all)
     q, rows, sq, sq_noise = score(mine, sq_mine, sqn_mine, got)
     for step in range(ITERS):
         if step:
@@ -347,10 +390,13 @@
     columns, f, *blocks = last_lse(place, q, parts, sq)
     blocks = [blocks[0]] + [shift(blocks[by], "x", by) for by in range(1, X)]
     columns = lax.all_to_all(columns, ("z", "x"), 0, 0)
+    data_all, blocks = lax.optimization_barrier((data_all, blocks))
     w, pot_g = scale(place, columns, blocks)
-    target, *rest = transport(place, w, shift(w, "core", 1), data_all)
-    for by in (2, 1, 3):
-        target = target + shift(rest[by - 1], "y", by).astype(F32)
+    got = shift(w, "core", 1)
+    *parts, data_all = transport(place, w, got, data_all, (2, 1, 3), True)
+    (target,) = transport(place, w, got, data_all, (0,), False)
+    for by, part in zip((2, 1, 3), parts):
+        target = target + shift(part, "y", by).astype(F32)
     velocity = (target - noise.astype(F32)).astype(BF16)
     own = lax.dynamic_index_in_dim(f.reshape(2, X, 128), x, 1, False)
     pot_f = (own * (EPS / LOG2E) + sq_noise / WIDTH).reshape(ROWS)

time: 200 us -> 201 us (level)
  local copies, waits for them, and re-layouts: 20.6 us -> 12.7 us
  Pallas kernels: 12.5 us -> 17.6 us
  waiting for transfers between devices: 40.2 us -> 45.1 us
    ppermute x22, waiting for transfers between devices: 32.8 us -> 44.2 us  [shift(): return lax.ppermute(x, axis, [(j, (j + by) % n) for j in range(n)])]
    unnamed x36 -> x10, local copies, waits for them, and re-layouts: 16.4 us -> 8.87 us
    all_gather x1, waiting for transfers between devices: 7.32 us -> 0.86 us  [body(): lax.all_gather(swapped, ('z', 'core')).reshape(Y, C, C, X, QUARTER, SLICE)]
    pallas_call x2 -> x5, Pallas kernels: 4.83 us -> 9.97 us  [the longest x2 3.58 us: transport(): pl.pallas_call(functools.partial(transport_kernel, pieces), out_shape=kin...]
    squeeze x1 -> x0, local copies, waits for them, and re-layouts: 3.15 us -> none  [body(): lax.dynamic_index_in_dim(samples, c, 1, False)]
    slice x4, local copies, waits for them, and re-layouts: 0.07 us -> 2.88 us  [halves(): return both_ways(forward[:cut], backward[cut:], axis)]
    all_to_all x3, blocking collectives: 41.3 us -> 39.2 us  [body(): parts = lax.all_to_all(rows, ('x', 'y', 'core'), 0, 0)]
  transfers between devices with their start and end apart: 25 -> 25, of which waited for: 12 -> 16; matrix products, arithmetic and copies ran while one was open for 1% -> 2% of each run, Pallas kernels for 5% -> 5%
where the time goes in v7:
time: 201 us
  blocking collectives  75 us (37%)
  waiting for transfers between devices  45.1 us (22%)
  starting transfers between devices  34.3 us (17%)
  Pallas kernels  17.6 us (9%)
  between operations  14.2 us (7%)
  local copies, waits for them, and re-layouts  12.7 us (6%)
    ppermute x22, waiting for transfers between devices, shift(): return lax.ppermute(x, axis, [(j, (j + by) % n) for j in range(n)])  44.2 us
    all_to_all x3, blocking collectives, body(): parts = lax.all_to_all(rows, ('x', 'y', 'core'), 0, 0)  39.2 us
    ppermute x22, starting transfers between devices, shift(): return lax.ppermute(x, axis, [(j, (j + by) % n) for j in range(n)])  30.4 us
    all_to_all x2, blocking collectives, body(): columns = lax.all_to_all(columns, 'z', 0, 0)  25.3 us
    all_to_all x1, blocking collectives, body(): swapped = lax.all_to_all(data.reshape(X, QUARTER, SLICE), 'x', 0, 0)  10.5 us
    unnamed x10, local copies, waits for them, and re-layouts  8.87 us
  transfers between devices with their start and end apart: 25, of which 16 were waited for; matrix products, arithmetic and copies ran while one was open for 2% of the time, Pallas kernels for 5%

profile of v7, /device:TPU:1, one launch (start us, length us, event | category | flops | bytes accessed | tf_op | source)
XLA Modules:
  0.0 200.6 jit_solution(6212463125648001769)
XLA Ops:
  7.2 10.5 %all_to_all.35 = bf16[4,256,128]{2,1,0:T(8,128)(2,1)} all-to-all(bf16[4,256,128]{2,1,0:T(8,128)(2,1)} %bitcast.29), channel_id=1, replica_groups=mesh['z'=8,'x'=4,'y'=4,'core'=2] {'x'}, dimensions={0} | all-to-all | bytes 524288 | tf_op jit(solution)/shard_map/all_to_all | solution.py:374
  18.8 3.0 %collective-permute-start.5 = (bf16[128,512]{1,0:T(8,128)(2,1)S(1)}, bf16[128,512]{1,0:T(8,128)(2,1)S(1)}, u32[]{:S(2)}, u32[]{:S(2)}) collective-permute-start(bf16[128,512]{1,0:T(8,128)(2,1)S(1)} %get-tuple-element.55), channel_id=1, source_target_pairs={{0,4},{2,6},{4,0},{6,2},{1,5},{3,7},{5,1},{7,3},{8,12},{10,14},{12... | collective-permute-start | bytes 393224 | tf_op jit(solution)/shard_map/ppermute | solution.py:34
  26.2 2.9 %collective-permute-done.3 = bf16[128,512]{1,0:T(8,128)(2,1)S(1)} collective-permute-done((bf16[128,512]{1,0:T(8,128)(2,1)S(1)}, bf16[128,512]{1,0:T(8,128)(2,1)S(1)}, u32[]{:S(2)}, u32[]{:S(2)}) %collective-permute-start.3) | collective-permute-done | bytes 131104 | tf_op jit(solution)/shard_map/ppermute | solution.py:34
  29.0 3.4 %collective-permute-done = bf16[128,512]{1,0:T(8,128)(2,1)S(1)} collective-permute-done((bf16[128,512]{1,0:T(8,128)(2,1)S(1)}, bf16[128,512]{1,0:T(8,128)(2,1)S(1)}, u32[]{:S(2)}, u32[]{:S(2)}) %collective-permute-start) | collective-permute-done | bytes 131104 | tf_op jit(solution)/shard_map/ppermute | solution.py:34
  36.2 6.8 %collective-permute-done.9.refs_7_ = bf16[4,128,512]{2,1,0:T(8,128)(2,1)S(1)} collective-permute-done((bf16[4,128,512]{2,1,0:T(8,128)(2,1)S(1)}, bf16[4,128,512]{2,1,0:T(8,128)(2,1)S(1)}, u32[]{:S(2)}, u32[]{:S(2)}) %collective-permute-start.9) | collective-permute-done | bytes 524320 | tf_op jit(solution)/shard_map/ppermute | solution.py:34
  44.3 2.6 %collective-permute-done.6.refs_1_ = bf16[4,128,512]{2,1,0:T(8,128)(2,1)S(1)} collective-permute-done((bf16[4,128,512]{2,1,0:T(8,128)(2,1)S(1)}, bf16[4,128,512]{2,1,0:T(8,128)(2,1)S(1)}, u32[]{:S(2)}, u32[]{:S(2)}) %collective-permute-start.6) | collective-permute-done | bytes 524320 | tf_op jit(solution)/shard_map/ppermute | solution.py:34
  53.0 2.4 %collective-permute-done.13.refs_9_ = bf16[2,128,512]{2,1,0:T(8,128)(2,1)S(1)} collective-permute-done((bf16[2,128,512]{2,1,0:T(8,128)(2,1)}, bf16[2,128,512]{2,1,0:T(8,128)(2,1)S(1)}, u32[]{:S(2)}, u32[]{:S(2)}) %collective-permute-start.13) | collective-permute-done | bytes 262176 | tf_op jit(solution)/shard_map/ppermute | solution.py:34
  55.4 3.1 %collective-permute-done.12.refs_8_ = bf16[2,128,512]{2,1,0:T(8,128)(2,1)} collective-permute-done((bf16[2,128,512]{2,1,0:T(8,128)(2,1)}, bf16[2,128,512]{2,1,0:T(8,128)(2,1)}, u32[]{:S(2)}, u32[]{:S(2)}) %collective-permute-start.12) | collective-permute-done | bytes 262176 | tf_op jit(solution)/shard_map/ppermute | solution.py:34
  63.2 2.9 %pick.1 = (bf16[4,2,4,256,128]{4,3,2,1,0:T(8,128)(2,1)S(1)}, bf16[4,2,4,256,128]{4,3,2,1,0:T(8,128)(2,1)S(1)}) custom-call(s32[4]{0:T(128)S(1)} %pad_add_fusion.place, bf16[4,2,2,4,256,128]{5,4,3,2,1,0:T(8,128)(2,1)} %bitcast.26), custom_call_target="tpu_custom_call" | custom-call | tf_op jit(solution)/shard_map/pick/pallas_call | solution.py:140
  71.6 5.2 %collective-permute-start.14 = (f32[264,1152]{1,0:T(8,128)S(1)}, f32[264,1152]{1,0:T(8,128)S(1)}, u32[]{:S(2)}, u32[]{:S(2)}) collective-permute-start(f32[264,1152]{1,0:T(8,128)S(1)} %theirs.1), channel_id=1, source_target_pairs={{0,1},{1,0},{2,3},{3,2},{4,5},{5,4},{6,7},{7,6},{8,9},{9,8},{10,11... | collective-permute-start | bytes 3649544 | tf_op jit(solution)/shard_map/ppermute | solution.py:34
  79.6 12.1 %all_to_all.36.part_ref = f32[32,8,128]{2,1,0:T(8,128)S(1)} all-to-all(f32[32,8,128]{2,1,0:T(8,128)S(1)} %get-tuple-element.72), channel_id=1, replica_groups=mesh['z'=8,'x'=4,'y'=4,'core'=2] {'x','y','core'}, dimensions={0} | all-to-all | bytes 262144 | tf_op jit(solution)/shard_map/all_to_all | solution.py:386
  92.6 16.1 %all_to_all.37.part_ref = f32[8,8,128]{2,1,0:T(8,128)S(1)} all-to-all(f32[8,8,128]{2,1,0:T(8,128)S(1)} %get-tuple-element.73), channel_id=1, replica_groups=mesh['z'=8,'x'=4,'y'=4,'core'=2] {'z'}, dimensions={0} | all-to-all | bytes 65536 | tf_op jit(solution)/shard_map/all_to_all | solution.py:389
  109.0 13.4 %all_to_all.38.part_ref = f32[32,8,128]{2,1,0:T(8,128)S(1)} all-to-all(f32[32,8,128]{2,1,0:T(8,128)S(1)} %noise_lse.2), channel_id=1, replica_groups=mesh['z'=8,'x'=4,'y'=4,'core'=2] {'x','y','core'}, dimensions={0} | all-to-all | bytes 262144 | tf_op jit(solution)/shard_map/all_to_all | solution.py:386
  123.2 9.2 %all_to_all.39.part_ref = f32[8,8,128]{2,1,0:T(8,128)S(1)} all-to-all(f32[8,8,128]{2,1,0:T(8,128)S(1)} %get-tuple-element.74), channel_id=1, replica_groups=mesh['z'=8,'x'=4,'y'=4,'core'=2] {'z'}, dimensions={0} | all-to-all | bytes 65536 | tf_op jit(solution)/shard_map/all_to_all | solution.py:389
  132.8 13.7 %all_to_all.40.part_ref = f32[32,8,128]{2,1,0:T(8,128)S(1)} all-to-all(f32[32,8,128]{2,1,0:T(8,128)S(1)} %noise_lse.3), channel_id=1, replica_groups=mesh['z'=8,'x'=4,'y'=4,'core'=2] {'x','y','core'}, dimensions={0} | all-to-all | bytes 262144 | tf_op jit(solution)/shard_map/all_to_all | solution.py:386
  148.1 3.9 %all-to-all-start.6 = ((f32[32,8,128]{2,1,0:T(8,128)}), f32[32,8,128]{2,1,0:T(8,128)S(1)}, u32[]{:S(2)}, u32[]{:S(2)}) async-start(f32[32,8,128]{2,1,0:T(8,128)} %get-tuple-element.78), calls=%async_computation.6 | async-start | bytes 262144 | tf_op jit(solution)/shard_map/all_to_all | solution.py:392
  153.2 2.4 %collective-permute-start.16 = (bf16[256,256]{1,0:T(8,128)(2,1)S(1)}, bf16[256,256]{1,0:T(8,128)(2,1)S(1)}, u32[]{:S(2)}, u32[]{:S(2)}) collective-permute-start(bf16[256,256]{1,0:T(8,128)(2,1)S(1)} %get-tuple-element.82), channel_id=1, source_target_pairs={{0,16},{8,24},{16,0},{24,8},{1,17},{9,25},{17,1},{25,9},{2,18},{10... | collective-permute-start | bytes 393224 | tf_op jit(solution)/shard_map/ppermute | solution.py:34
  156.8 6.1 %collective-permute-done.15.refs_1_ = bf16[256,256]{1,0:T(8,128)(2,1)S(1)} collective-permute-done((bf16[256,256]{1,0:T(8,128)(2,1)S(1)}, bf16[256,256]{1,0:T(8,128)(2,1)S(1)}, u32[]{:S(2)}, u32[]{:S(2)}) %collective-permute-start.15) | collective-permute-done | bytes 131104 | tf_op jit(solution)/shard_map/ppermute | solution.py:34
  162.9 5.1 %collective-permute-done.16.refs_2_ = bf16[256,256]{1,0:T(8,128)(2,1)S(1)} collective-permute-done((bf16[256,256]{1,0:T(8,128)(2,1)S(1)}, bf16[256,256]{1,0:T(8,128)(2,1)S(1)}, u32[]{:S(2)}, u32[]{:S(2)}) %collective-permute-start.16) | collective-permute-done | bytes 131104 | tf_op jit(solution)/shard_map/ppermute | solution.py:34
  171.5 3.4 %copy-done = bf16[16,2,4,256,128]{4,3,2,1,0:T(8,128)(2,1)S(1)} copy-done((bf16[16,2,4,256,128]{4,3,2,1,0:T(8,128)(2,1)S(1)}, bf16[16,2,4,256,128]{4,3,2,1,0:T(8,128)(2,1)}, u32[]{:S(2)}) %copy-start) | copy-done | bytes 8388632
  174.9 2.3 %transport.2 = (bf16[256,512]{1,0:T(8,128)(2,1)S(1)}, bf16[256,512]{1,0:T(8,128)(2,1)S(1)}, bf16[256,512]{1,0:T(8,128)(2,1)S(1)}, bf16[4,4,2,4,256,128]{5,4,3,2,1,0:T(8,128)(2,1)S(1)}) custom-call(s32[4]{0:T(128)S(1)} %pad_add_fusion.place, bf16[256,1024]{1,0:T(8,128)(2,1)S(1)} %get-tuple-element.89.w_ref, ...), custom_call_target="tpu_custom_call", output_to_operand_aliasing={{3}: (3, {})} | custom-call | flops 1610612736 | bytes 6291456 | tf_op jit(solution)/shard_map/transport/pallas_call | solution.py:357
  177.2 3.1 %collective-permute-start.19 = (bf16[256,512]{1,0:T(8,128)(2,1)S(1)}, bf16[256,512]{1,0:T(8,128)(2,1)S(1)}, u32[]{:S(2)}, u32[]{:S(2)}) collective-permute-start(bf16[256,512]{1,0:T(8,128)(2,1)S(1)} %get-tuple-element.92), channel_id=1, source_target_pairs={{0,4},{2,6},{4,0},{6,2},{1,5},{3,7},{5,1},{7,3},{8,12},{10,14},{12... | collective-permute-start | bytes 786440 | tf_op jit(solution)/shard_map/ppermute | solution.py:34
  180.7 2.4 %collective-permute-start.21 = (bf16[256,512]{1,0:T(8,128)(2,1)S(1)}, bf16[256,512]{1,0:T(8,128)(2,1)S(1)}, u32[]{:S(2)}, u32[]{:S(2)}) collective-permute-start(bf16[256,512]{1,0:T(8,128)(2,1)S(1)} %get-tuple-element.94), channel_id=1, source_target_pairs={{0,6},{2,0},{4,2},{6,4},{1,7},{3,1},{5,3},{7,5},{8,14},{10,8},{12,... | collective-permute-start | bytes 786440 | tf_op jit(solution)/shard_map/ppermute | solution.py:34
  186.6 6.3 %collective-permute-done.20 = bf16[256,512]{1,0:T(8,128)(2,1)S(1)} collective-permute-done((bf16[256,512]{1,0:T(8,128)(2,1)S(1)}, bf16[256,512]{1,0:T(8,128)(2,1)S(1)}, u32[]{:S(2)}, u32[]{:S(2)}) %collective-permute-start.20) | collective-permute-done | bytes 262176 | tf_op jit(solution)/shard_map/ppermute | solution.py:34
  (68 shorter events, 44.2 us)
Async XLA Ops:
  7.2 56.0 %all-gather.5.cloned.1.call-start = ((), (), s32[]{:S(2)}) async-start(), calls=%async_computation.7 | async-start | bytes 4456448 | tf_op jit(solution)/shard_map/all_gather | solution.py:376
  17.7 150.3 %all-gather.7.cloned.1.call-start = ((), (), s32[]{:S(2)}) async-start(), calls=%async_computation.8 | async-start | bytes 10485760 | tf_op jit(solution)/shard_map/all_gather | solution.py:379
  18.8 7.3 %collective-permute-start.5 = (bf16[128,512]{1,0:T(8,128)(2,1)S(1)}, bf16[128,512]{1,0:T(8,128)(2,1)S(1)}, u32[]{:S(2)}, u32[]{:S(2)}) collective-permute-start(bf16[128,512]{1,0:T(8,128)(2,1)S(1)} %get-tuple-element.55), channel_id=1, source_target_pairs={{0,4},{2,6},{4,0},{6,2},{1,5},{3,7},{5,1},{7,3},{8,12},{10,14},{12... | collective-permute-start | bytes 393224 | tf_op jit(solution)/shard_map/ppermute | solution.py:34
  21.8 4.4 %collective-permute-start.4 = (bf16[128,512]{1,0:T(8,128)(2,1)S(1)}, bf16[128,512]{1,0:T(8,128)(2,1)S(1)}, u32[]{:S(2)}, u32[]{:S(2)}) collective-permute-start(bf16[128,512]{1,0:T(8,128)(2,1)S(1)} %get-tuple-element.55), channel_id=1, source_target_pairs={{0,6},{2,0},{4,2},{6,4},{1,7},{3,1},{5,3},{7,5},{8,14},{10,8},{12,... | collective-permute-start | bytes 393224 | tf_op jit(solution)/shard_map/ppermute | solution.py:34
  22.6 6.4 %collective-permute-start.3 = (bf16[128,512]{1,0:T(8,128)(2,1)S(1)}, bf16[128,512]{1,0:T(8,128)(2,1)S(1)}, u32[]{:S(2)}, u32[]{:S(2)}) collective-permute-start(bf16[128,512]{1,0:T(8,128)(2,1)S(1)} %get-tuple-element.55), channel_id=1, source_target_pairs={{0,2},{2,4},{4,6},{6,0},{1,3},{3,5},{5,7},{7,1},{8,10},{10,12},{12... | collective-permute-start | bytes 393224 | tf_op jit(solution)/shard_map/ppermute | solution.py:34
  23.3 5.7 %collective-permute-start.2 = (bf16[128,512]{1,0:T(8,128)(2,1)S(1)}, bf16[128,512]{1,0:T(8,128)(2,1)S(1)}, u32[]{:S(2)}, u32[]{:S(2)}) collective-permute-start(bf16[128,512]{1,0:T(8,128)(2,1)S(1)} %get-tuple-element.51), channel_id=1, source_target_pairs={{0,16},{8,24},{16,0},{24,8},{1,17},{9,25},{17,1},{25,9},{2,18},{10... | collective-permute-start | bytes 393224 | tf_op jit(solution)/shard_map/ppermute | solution.py:34
  24.1 4.9 %collective-permute-start.1 = (bf16[128,512]{1,0:T(8,128)(2,1)S(1)}, bf16[128,512]{1,0:T(8,128)(2,1)S(1)}, u32[]{:S(2)}, u32[]{:S(2)}) collective-permute-start(bf16[128,512]{1,0:T(8,128)(2,1)S(1)} %get-tuple-element.51), channel_id=1, source_target_pairs={{0,24},{8,0},{16,8},{24,16},{1,25},{9,1},{17,9},{25,17},{2,26},{10... | collective-permute-start | bytes 393224 | tf_op jit(solution)/shard_map/ppermute | solution.py:34
  26.0 6.4 %collective-permute-start = (bf16[128,512]{1,0:T(8,128)(2,1)S(1)}, bf16[128,512]{1,0:T(8,128)(2,1)S(1)}, u32[]{:S(2)}, u32[]{:S(2)}) collective-permute-start(bf16[128,512]{1,0:T(8,128)(2,1)S(1)} %get-tuple-element.51), channel_id=1, source_target_pairs={{0,8},{8,16},{16,24},{24,0},{1,9},{9,17},{17,25},{25,1},{2,10},{10... | collective-permute-start | bytes 393224 | tf_op jit(solution)/shard_map/ppermute | solution.py:34
  32.5 10.5 %collective-permute-start.9 = (bf16[4,128,512]{2,1,0:T(8,128)(2,1)S(1)}, bf16[4,128,512]{2,1,0:T(8,128)(2,1)S(1)}, u32[]{:S(2)}, u32[]{:S(2)}) collective-permute-start(bf16[4,128,512]{2,1,0:T(8,128)(2,1)S(1)} %pad_maximum_fusion.1.refs_5_), channel_id=1, source_target_pairs={{0,24},{8,0},{16,8},{24,16},{1,25},{9,1},{17,9},{25,17},{2,26},{10... | collective-permute-start | bytes 1572872 | tf_op jit(solution)/shard_map/ppermute | solution.py:34
  32.6 11.7 %collective-permute-start.8 = (bf16[4,128,512]{2,1,0:T(8,128)(2,1)S(1)}, bf16[4,128,512]{2,1,0:T(8,128)(2,1)S(1)}, u32[]{:S(2)}, u32[]{:S(2)}) collective-permute-start(bf16[4,128,512]{2,1,0:T(8,128)(2,1)S(1)} %pad_maximum_fusion.1.refs_5_), channel_id=1, source_target_pairs={{0,8},{8,16},{16,24},{24,0},{1,9},{9,17},{17,25},{25,1},{2,10},{10... | collective-permute-start | bytes 1572872 | tf_op jit(solution)/shard_map/ppermute | solution.py:34
  34.1 10.1 %collective-permute-start.7 = (bf16[4,128,512]{2,1,0:T(8,128)(2,1)S(1)}, bf16[4,128,512]{2,1,0:T(8,128)(2,1)S(1)}, u32[]{:S(2)}, u32[]{:S(2)}) collective-permute-start(bf16[4,128,512]{2,1,0:T(8,128)(2,1)S(1)} %pad_maximum_fusion.refs_0_), channel_id=1, source_target_pairs={{0,6},{2,0},{4,2},{6,4},{1,7},{3,1},{5,3},{7,5},{8,14},{10,8},{12,... | collective-permute-start | bytes 1572872 | tf_op jit(solution)/shard_map/ppermute | solution.py:34
  36.2 10.6 %collective-permute-start.6 = (bf16[4,128,512]{2,1,0:T(8,128)(2,1)S(1)}, bf16[4,128,512]{2,1,0:T(8,128)(2,1)S(1)}, u32[]{:S(2)}, u32[]{:S(2)}) collective-permute-start(bf16[4,128,512]{2,1,0:T(8,128)(2,1)S(1)} %pad_maximum_fusion.refs_0_), channel_id=1, source_target_pairs={{0,2},{2,4},{4,6},{6,0},{1,3},{3,5},{5,7},{7,1},{8,10},{10,12},{12... | collective-permute-start | bytes 1572872 | tf_op jit(solution)/shard_map/ppermute | solution.py:34
  49.7 5.6 %collective-permute-start.13 = (bf16[2,128,512]{2,1,0:T(8,128)(2,1)}, bf16[2,128,512]{2,1,0:T(8,128)(2,1)S(1)}, u32[]{:S(2)}, u32[]{:S(2)}) collective-permute-start(bf16[2,128,512]{2,1,0:T(8,128)(2,1)} %slice.23), channel_id=1, source_target_pairs={{0,24},{8,0},{16,8},{24,16},{1,25},{9,1},{17,9},{25,17},{2,26},{10... | collective-permute-start | bytes 786440 | tf_op jit(solution)/shard_map/ppermute | solution.py:34
  51.4 7.0 %collective-permute-start.12 = (bf16[2,128,512]{2,1,0:T(8,128)(2,1)}, bf16[2,128,512]{2,1,0:T(8,128)(2,1)}, u32[]{:S(2)}, u32[]{:S(2)}) collective-permute-start(bf16[2,128,512]{2,1,0:T(8,128)(2,1)} %slice.22), channel_id=1, source_target_pairs={{0,8},{8,16},{16,24},{24,0},{1,9},{9,17},{17,25},{25,1},{2,10},{10... | collective-permute-start | bytes 786440 | tf_op jit(solution)/shard_map/ppermute | solution.py:34
  51.4 7.0 %collective-permute-start.11 = (bf16[2,128,512]{2,1,0:T(8,128)(2,1)}, bf16[2,128,512]{2,1,0:T(8,128)(2,1)}, u32[]{:S(2)}, u32[]{:S(2)}) collective-permute-start(bf16[2,128,512]{2,1,0:T(8,128)(2,1)} %slice.21), channel_id=1, source_target_pairs={{0,6},{2,0},{4,2},{6,4},{1,7},{3,1},{5,3},{7,5},{8,14},{10,8},{12,... | collective-permute-start | bytes 786440 | tf_op jit(solution)/shard_map/ppermute | solution.py:34
  51.7 7.0 %collective-permute-start.10 = (bf16[2,128,512]{2,1,0:T(8,128)(2,1)}, bf16[2,128,512]{2,1,0:T(8,128)(2,1)}, u32[]{:S(2)}, u32[]{:S(2)}) collective-permute-start(bf16[2,128,512]{2,1,0:T(8,128)(2,1)} %slice.20), channel_id=1, source_target_pairs={{0,2},{2,4},{4,6},{6,0},{1,3},{3,5},{5,7},{7,1},{8,10},{10,12},{12... | collective-permute-start | bytes 786440 | tf_op jit(solution)/shard_map/ppermute | solution.py:34
  71.6 7.7 %collective-permute-start.14 = (f32[264,1152]{1,0:T(8,128)S(1)}, f32[264,1152]{1,0:T(8,128)S(1)}, u32[]{:S(2)}, u32[]{:S(2)}) collective-permute-start(f32[264,1152]{1,0:T(8,128)S(1)} %theirs.1), channel_id=1, source_target_pairs={{0,1},{1,0},{2,3},{3,2},{4,5},{5,4},{6,7},{7,6},{8,9},{9,8},{10,11... | collective-permute-start | bytes 3649544 | tf_op jit(solution)/shard_map/ppermute | solution.py:34
  148.1 19.9 %all-to-all-start.6 = ((f32[32,8,128]{2,1,0:T(8,128)}), f32[32,8,128]{2,1,0:T(8,128)S(1)}, u32[]{:S(2)}, u32[]{:S(2)}) async-start(f32[32,8,128]{2,1,0:T(8,128)} %get-tuple-element.78), calls=%async_computation.6 | async-start | bytes 262144 | tf_op jit(solution)/shard_map/all_to_all | solution.py:392
  152.0 10.9 %collective-permute-start.15 = (bf16[256,256]{1,0:T(8,128)(2,1)S(1)}, bf16[256,256]{1,0:T(8,128)(2,1)S(1)}, u32[]{:S(2)}, u32[]{:S(2)}) collective-permute-start(bf16[256,256]{1,0:T(8,128)(2,1)S(1)} %get-tuple-element.81), channel_id=1, source_target_pairs={{0,8},{8,16},{16,24},{24,0},{1,9},{9,17},{17,25},{25,1},{2,10},{10... | collective-permute-start | bytes 393224 | tf_op jit(solution)/shard_map/ppermute | solution.py:34
  153.2 14.8 %collective-permute-start.16 = (bf16[256,256]{1,0:T(8,128)(2,1)S(1)}, bf16[256,256]{1,0:T(8,128)(2,1)S(1)}, u32[]{:S(2)}, u32[]{:S(2)}) collective-permute-start(bf16[256,256]{1,0:T(8,128)(2,1)S(1)} %get-tuple-element.82), channel_id=1, source_target_pairs={{0,16},{8,24},{16,0},{24,8},{1,17},{9,25},{17,1},{25,9},{2,18},{10... | collective-permute-start | bytes 393224 | tf_op jit(solution)/shard_map/ppermute | solution.py:34
  155.6 12.4 %collective-permute-start.17 = (bf16[256,256]{1,0:T(8,128)(2,1)S(1)}, bf16[256,256]{1,0:T(8,128)(2,1)S(1)}, u32[]{:S(2)}, u32[]{:S(2)}) collective-permute-start(bf16[256,256]{1,0:T(8,128)(2,1)S(1)} %get-tuple-element.83), channel_id=1, source_target_pairs={{0,24},{8,0},{16,8},{24,16},{1,25},{9,1},{17,9},{25,17},{2,26},{10... | collective-permute-start | bytes 393224 | tf_op jit(solution)/shard_map/ppermute | solution.py:34
  177.2 9.4 %collective-permute-start.19 = (bf16[256,512]{1,0:T(8,128)(2,1)S(1)}, bf16[256,512]{1,0:T(8,128)(2,1)S(1)}, u32[]{:S(2)}, u32[]{:S(2)}) collective-permute-start(bf16[256,512]{1,0:T(8,128)(2,1)S(1)} %get-tuple-element.92), channel_id=1, source_target_pairs={{0,4},{2,6},{4,0},{6,2},{1,5},{3,7},{5,1},{7,3},{8,12},{10,14},{12... | collective-permute-start | bytes 786440 | tf_op jit(solution)/shard_map/ppermute | solution.py:34
  180.4 12.5 %collective-permute-start.20 = (bf16[256,512]{1,0:T(8,128)(2,1)S(1)}, bf16[256,512]{1,0:T(8,128)(2,1)S(1)}, u32[]{:S(2)}, u32[]{:S(2)}) collective-permute-start(bf16[256,512]{1,0:T(8,128)(2,1)S(1)} %get-tuple-element.93), channel_id=1, source_target_pairs={{0,2},{2,4},{4,6},{6,0},{1,3},{3,5},{5,7},{7,1},{8,10},{10,12},{12... | collective-permute-start | bytes 786440 | tf_op jit(solution)/shard_map/ppermute | solution.py:34
  180.7 12.2 %collective-permute-start.21 = (bf16[256,512]{1,0:T(8,128)(2,1)S(1)}, bf16[256,512]{1,0:T(8,128)(2,1)S(1)}, u32[]{:S(2)}, u32[]{:S(2)}) collective-permute-start(bf16[256,512]{1,0:T(8,128)(2,1)S(1)} %get-tuple-element.94), channel_id=1, source_target_pairs={{0,6},{2,0},{4,2},{6,4},{1,7},{3,1},{5,3},{7,5},{8,14},{10,8},{12,... | collective-permute-start | bytes 786440 | tf_op jit(solution)/shard_map/ppermute | solution.py:34
  (6 other events, 20.3 us)
Sparse Core Ops, SparseCore 0:
  17.8 45.3 all-gather.4
  67.6 99.0 all-gather.6

commit v8 on v7

--- a/solution.py
+++ b/solution.py
@@ -143,7 +143,7 @@
         in_specs=[SMEM, pl.BlockSpec(memory_space=pl.ANY)],
         out_specs=(pl.BlockSpec(memory_space=pl.ANY), VMEM),
         scratch_shapes=[pltpu.SemaphoreType.DMA((2, Y))],
-        compiler_params=params(47),
+        compiler_params=params(16),
         name="pick",
     )(place, samples)
 
@@ -390,8 +390,8 @@
     columns, f, *blocks = last_lse(place, q, parts, sq)
     blocks = [blocks[0]] + [shift(blocks[by], "x", by) for by in range(1, X)]
     columns = lax.all_to_all(columns, ("z", "x"), 0, 0)
-    data_all, blocks = lax.optimization_barrier((data_all, blocks))
     w, pot_g = scale(place, columns, blocks)
+    data_all, pot_g = lax.optimization_barrier((data_all, pot_g))
     got = shift(w, "core", 1)
     *parts, data_all = transport(place, w, got, data_all, (2, 1, 3), True)
     (target,) = transport(place, w, got, data_all, (0,), False)

time: 201 us -> 201 us (level)
  local copies, waits for them, and re-layouts: 12.7 us -> 14.9 us
    unnamed x10 -> x12, local copies, waits for them, and re-layouts: 8.87 us -> 11.1 us
  transfers between devices with their start and end apart: 25 -> 25, of which waited for: 16 -> 16; matrix products, arithmetic and copies ran while one was open for 2% -> 2% of each run, Pallas kernels for 5% -> 6%
where the time goes in v8:
time: 201 us
  blocking collectives  75 us (37%)
  waiting for transfers between devices  45.5 us (23%)
  starting transfers between devices  33.9 us (17%)
  Pallas kernels  15.6 us (8%)
  local copies, waits for them, and re-layouts  14.9 us (7%)
  between operations  14.2 us (7%)
    ppermute x22, waiting for transfers between devices, shift(): return lax.ppermute(x, axis, [(j, (j + by) % n) for j in range(n)])  44.6 us
    all_to_all x3, blocking collectives, body(): parts = lax.all_to_all(rows, ('x', 'y', 'core'), 0, 0)  39.2 us
    ppermute x22, starting transfers between devices, shift(): return lax.ppermute(x, axis, [(j, (j + by) % n) for j in range(n)])  29.9 us
    all_to_all x2, blocking collectives, body(): columns = lax.all_to_all(columns, 'z', 0, 0)  25.3 us
    unnamed x12, local copies, waits for them, and re-layouts  11.1 us
    all_to_all x1, blocking collectives, body(): swapped = lax.all_to_all(data.reshape(X, QUARTER, SLICE), 'x', 0, 0)  10.5 us
  transfers between devices with their start and end apart: 25, of which 16 were waited for; matrix products, arithmetic and copies ran while one was open for 2% of the time, Pallas kernels for 6%

profile of v8, /device:TPU:1, one launch (start us, length us, event | category | flops | bytes accessed | tf_op | source)
XLA Modules:
  0.0 200.8 jit_solution(11014188354850297763)
XLA Ops:
  7.2 10.5 %all_to_all.35 = bf16[4,256,128]{2,1,0:T(8,128)(2,1)} all-to-all(bf16[4,256,128]{2,1,0:T(8,128)(2,1)} %bitcast.29), channel_id=1, replica_groups=mesh['z'=8,'x'=4,'y'=4,'core'=2] {'x'}, dimensions={0} | all-to-all | bytes 524288 | tf_op jit(solution)/shard_map/all_to_all | solution.py:374
  18.8 3.0 %collective-permute-start.5 = (bf16[128,512]{1,0:T(8,128)(2,1)S(1)}, bf16[128,512]{1,0:T(8,128)(2,1)S(1)}, u32[]{:S(2)}, u32[]{:S(2)}) collective-permute-start(bf16[128,512]{1,0:T(8,128)(2,1)S(1)} %get-tuple-element.52), channel_id=1, source_target_pairs={{0,4},{2,6},{4,0},{6,2},{1,5},{3,7},{5,1},{7,3},{8,12},{10,14},{12... | collective-permute-start | bytes 393224 | tf_op jit(solution)/shard_map/ppermute | solution.py:34
  26.2 2.9 %collective-permute-done.3 = bf16[128,512]{1,0:T(8,128)(2,1)S(1)} collective-permute-done((bf16[128,512]{1,0:T(8,128)(2,1)S(1)}, bf16[128,512]{1,0:T(8,128)(2,1)S(1)}, u32[]{:S(2)}, u32[]{:S(2)}) %collective-permute-start.3) | collective-permute-done | bytes 131104 | tf_op jit(solution)/shard_map/ppermute | solution.py:34
  29.0 3.4 %collective-permute-done = bf16[128,512]{1,0:T(8,128)(2,1)S(1)} collective-permute-done((bf16[128,512]{1,0:T(8,128)(2,1)S(1)}, bf16[128,512]{1,0:T(8,128)(2,1)S(1)}, u32[]{:S(2)}, u32[]{:S(2)}) %collective-permute-start) | collective-permute-done | bytes 131104 | tf_op jit(solution)/shard_map/ppermute | solution.py:34
  36.2 6.8 %collective-permute-done.9.refs_7_ = bf16[4,128,512]{2,1,0:T(8,128)(2,1)S(1)} collective-permute-done((bf16[4,128,512]{2,1,0:T(8,128)(2,1)S(1)}, bf16[4,128,512]{2,1,0:T(8,128)(2,1)S(1)}, u32[]{:S(2)}, u32[]{:S(2)}) %collective-permute-start.9) | collective-permute-done | bytes 524320 | tf_op jit(solution)/shard_map/ppermute | solution.py:34
  44.3 2.6 %collective-permute-done.6.refs_1_ = bf16[4,128,512]{2,1,0:T(8,128)(2,1)S(1)} collective-permute-done((bf16[4,128,512]{2,1,0:T(8,128)(2,1)S(1)}, bf16[4,128,512]{2,1,0:T(8,128)(2,1)S(1)}, u32[]{:S(2)}, u32[]{:S(2)}) %collective-permute-start.6) | collective-permute-done | bytes 524320 | tf_op jit(solution)/shard_map/ppermute | solution.py:34
  53.0 2.4 %collective-permute-done.13.refs_9_ = bf16[2,128,512]{2,1,0:T(8,128)(2,1)S(1)} collective-permute-done((bf16[2,128,512]{2,1,0:T(8,128)(2,1)}, bf16[2,128,512]{2,1,0:T(8,128)(2,1)S(1)}, u32[]{:S(2)}, u32[]{:S(2)}) %collective-permute-start.13) | collective-permute-done | bytes 262176 | tf_op jit(solution)/shard_map/ppermute | solution.py:34
  55.4 3.1 %collective-permute-done.12.refs_8_ = bf16[2,128,512]{2,1,0:T(8,128)(2,1)} collective-permute-done((bf16[2,128,512]{2,1,0:T(8,128)(2,1)}, bf16[2,128,512]{2,1,0:T(8,128)(2,1)}, u32[]{:S(2)}, u32[]{:S(2)}) %collective-permute-start.12) | collective-permute-done | bytes 262176 | tf_op jit(solution)/shard_map/ppermute | solution.py:34
  63.2 2.2 %copy-done.3 = bf16[64,256,128]{2,1,0:T(8,128)(2,1)S(1)} copy-done((bf16[64,256,128]{2,1,0:T(8,128)(2,1)S(1)}, bf16[64,256,128]{2,1,0:T(8,128)(2,1)}, u32[]{:S(2)}) %copy-start.3) | copy-done | bytes 4194328
  67.7 2.2 %copy-done.2 = bf16[1024,2048]{1,0:T(8,128)(2,1)S(1)} copy-done((bf16[1024,2048]{1,0:T(8,128)(2,1)S(1)}, bf16[1024,2048]{1,0:T(8,128)(2,1)}, u32[]{:S(2)}) %copy-start.2) | copy-done | bytes 4194328
  71.7 5.3 %collective-permute-start.14 = (f32[264,1152]{1,0:T(8,128)S(1)}, f32[264,1152]{1,0:T(8,128)S(1)}, u32[]{:S(2)}, u32[]{:S(2)}) collective-permute-start(f32[264,1152]{1,0:T(8,128)S(1)} %theirs.1), channel_id=1, source_target_pairs={{0,1},{1,0},{2,3},{3,2},{4,5},{5,4},{6,7},{7,6},{8,9},{9,8},{10,11... | collective-permute-start | bytes 3649544 | tf_op jit(solution)/shard_map/ppermute | solution.py:34
  80.0 12.1 %all_to_all.36.part_ref = f32[32,8,128]{2,1,0:T(8,128)S(1)} all-to-all(f32[32,8,128]{2,1,0:T(8,128)S(1)} %get-tuple-element.69), channel_id=1, replica_groups=mesh['z'=8,'x'=4,'y'=4,'core'=2] {'x','y','core'}, dimensions={0} | all-to-all | bytes 262144 | tf_op jit(solution)/shard_map/all_to_all | solution.py:386
  92.9 16.1 %all_to_all.37.part_ref = f32[8,8,128]{2,1,0:T(8,128)S(1)} all-to-all(f32[8,8,128]{2,1,0:T(8,128)S(1)} %get-tuple-element.70), channel_id=1, replica_groups=mesh['z'=8,'x'=4,'y'=4,'core'=2] {'z'}, dimensions={0} | all-to-all | bytes 65536 | tf_op jit(solution)/shard_map/all_to_all | solution.py:389
  109.4 13.4 %all_to_all.38.part_ref = f32[32,8,128]{2,1,0:T(8,128)S(1)} all-to-all(f32[32,8,128]{2,1,0:T(8,128)S(1)} %noise_lse.2), channel_id=1, replica_groups=mesh['z'=8,'x'=4,'y'=4,'core'=2] {'x','y','core'}, dimensions={0} | all-to-all | bytes 262144 | tf_op jit(solution)/shard_map/all_to_all | solution.py:386
  123.6 9.2 %all_to_all.39.part_ref = f32[8,8,128]{2,1,0:T(8,128)S(1)} all-to-all(f32[8,8,128]{2,1,0:T(8,128)S(1)} %get-tuple-element.71), channel_id=1, replica_groups=mesh['z'=8,'x'=4,'y'=4,'core'=2] {'z'}, dimensions={0} | all-to-all | bytes 65536 | tf_op jit(solution)/shard_map/all_to_all | solution.py:389
  133.2 13.7 %all_to_all.40.part_ref = f32[32,8,128]{2,1,0:T(8,128)S(1)} all-to-all(f32[32,8,128]{2,1,0:T(8,128)S(1)} %noise_lse.3), channel_id=1, replica_groups=mesh['z'=8,'x'=4,'y'=4,'core'=2] {'x','y','core'}, dimensions={0} | all-to-all | bytes 262144 | tf_op jit(solution)/shard_map/all_to_all | solution.py:386
  148.5 3.9 %all-to-all-start.6 = ((f32[32,8,128]{2,1,0:T(8,128)}), f32[32,8,128]{2,1,0:T(8,128)S(1)}, u32[]{:S(2)}, u32[]{:S(2)}) async-start(f32[32,8,128]{2,1,0:T(8,128)} %get-tuple-element.76), calls=%async_computation.6 | async-start | bytes 262144 | tf_op jit(solution)/shard_map/all_to_all | solution.py:392
  153.5 2.4 %collective-permute-start.16 = (bf16[256,256]{1,0:T(8,128)(2,1)S(1)}, bf16[256,256]{1,0:T(8,128)(2,1)S(1)}, u32[]{:S(2)}, u32[]{:S(2)}) collective-permute-start(bf16[256,256]{1,0:T(8,128)(2,1)S(1)} %get-tuple-element.79), channel_id=1, source_target_pairs={{0,16},{8,24},{16,0},{24,8},{1,17},{9,25},{17,1},{25,9},{2,18},{10... | collective-permute-start | bytes 393224 | tf_op jit(solution)/shard_map/ppermute | solution.py:34
  157.1 6.1 %collective-permute-done.15.refs_1_ = bf16[256,256]{1,0:T(8,128)(2,1)S(1)} collective-permute-done((bf16[256,256]{1,0:T(8,128)(2,1)S(1)}, bf16[256,256]{1,0:T(8,128)(2,1)S(1)}, u32[]{:S(2)}, u32[]{:S(2)}) %collective-permute-start.15) | collective-permute-done | bytes 131104 | tf_op jit(solution)/shard_map/ppermute | solution.py:34
  163.2 5.1 %collective-permute-done.16.refs_2_ = bf16[256,256]{1,0:T(8,128)(2,1)S(1)} collective-permute-done((bf16[256,256]{1,0:T(8,128)(2,1)S(1)}, bf16[256,256]{1,0:T(8,128)(2,1)S(1)}, u32[]{:S(2)}, u32[]{:S(2)}) %collective-permute-start.16) | collective-permute-done | bytes 131104 | tf_op jit(solution)/shard_map/ppermute | solution.py:34
  171.9 3.4 %copy-done = bf16[16,2,4,256,128]{4,3,2,1,0:T(8,128)(2,1)S(1)} copy-done((bf16[16,2,4,256,128]{4,3,2,1,0:T(8,128)(2,1)S(1)}, bf16[16,2,4,256,128]{4,3,2,1,0:T(8,128)(2,1)}, u32[]{:S(2)}) %copy-start) | copy-done | bytes 8388632
  175.3 2.3 %transport.2 = (bf16[256,512]{1,0:T(8,128)(2,1)S(1)}, bf16[256,512]{1,0:T(8,128)(2,1)S(1)}, bf16[256,512]{1,0:T(8,128)(2,1)S(1)}, bf16[4,4,2,4,256,128]{5,4,3,2,1,0:T(8,128)(2,1)S(1)}) custom-call(s32[4]{0:T(128)S(1)} %pad_add_fusion.place, bf16[256,1024]{1,0:T(8,128)(2,1)S(1)} %get-tuple-element.83.w_ref, ...), custom_call_target="tpu_custom_call", output_to_operand_aliasing={{3}: (3, {})} | custom-call | flops 1610612736 | bytes 6291456 | tf_op jit(solution)/shard_map/transport/pallas_call | solution.py:357
  177.6 2.5 %collective-permute-start.19 = (bf16[256,512]{1,0:T(8,128)(2,1)S(1)}, bf16[256,512]{1,0:T(8,128)(2,1)S(1)}, u32[]{:S(2)}, u32[]{:S(2)}) collective-permute-start(bf16[256,512]{1,0:T(8,128)(2,1)S(1)} %get-tuple-element.86), channel_id=1, source_target_pairs={{0,4},{2,6},{4,0},{6,2},{1,5},{3,7},{5,1},{7,3},{8,12},{10,14},{12... | collective-permute-start | bytes 786440 | tf_op jit(solution)/shard_map/ppermute | solution.py:34
  186.7 6.3 %collective-permute-done.20 = bf16[256,512]{1,0:T(8,128)(2,1)S(1)} collective-permute-done((bf16[256,512]{1,0:T(8,128)(2,1)S(1)}, bf16[256,512]{1,0:T(8,128)(2,1)S(1)}, u32[]{:S(2)}, u32[]{:S(2)}) %collective-permute-start.20) | collective-permute-done | bytes 262176 | tf_op jit(solution)/shard_map/ppermute | solution.py:34
  (70 shorter events, 45.7 us)
Async XLA Ops:
  7.2 56.0 %all-gather.5.cloned.1.call-start = ((), (), s32[]{:S(2)}) async-start(), calls=%async_computation.7 | async-start | bytes 4456448 | tf_op jit(solution)/shard_map/all_gather | solution.py:376
  17.7 152.6 %all-gather.7.cloned.1.call-start = ((), (), s32[]{:S(2)}) async-start(), calls=%async_computation.8 | async-start | bytes 10485760 | tf_op jit(solution)/shard_map/all_gather | solution.py:379
  18.8 7.3 %collective-permute-start.5 = (bf16[128,512]{1,0:T(8,128)(2,1)S(1)}, bf16[128,512]{1,0:T(8,128)(2,1)S(1)}, u32[]{:S(2)}, u32[]{:S(2)}) collective-permute-start(bf16[128,512]{1,0:T(8,128)(2,1)S(1)} %get-tuple-element.52), channel_id=1, source_target_pairs={{0,4},{2,6},{4,0},{6,2},{1,5},{3,7},{5,1},{7,3},{8,12},{10,14},{12... | collective-permute-start | bytes 393224 | tf_op jit(solution)/shard_map/ppermute | solution.py:34
  21.8 4.4 %collective-permute-start.4 = (bf16[128,512]{1,0:T(8,128)(2,1)S(1)}, bf16[128,512]{1,0:T(8,128)(2,1)S(1)}, u32[]{:S(2)}, u32[]{:S(2)}) collective-permute-start(bf16[128,512]{1,0:T(8,128)(2,1)S(1)} %get-tuple-element.52), channel_id=1, source_target_pairs={{0,6},{2,0},{4,2},{6,4},{1,7},{3,1},{5,3},{7,5},{8,14},{10,8},{12,... | collective-permute-start | bytes 393224 | tf_op jit(solution)/shard_map/ppermute | solution.py:34
  22.6 6.4 %collective-permute-start.3 = (bf16[128,512]{1,0:T(8,128)(2,1)S(1)}, bf16[128,512]{1,0:T(8,128)(2,1)S(1)}, u32[]{:S(2)}, u32[]{:S(2)}) collective-permute-start(bf16[128,512]{1,0:T(8,128)(2,1)S(1)} %get-tuple-element.52), channel_id=1, source_target_pairs={{0,2},{2,4},{4,6},{6,0},{1,3},{3,5},{5,7},{7,1},{8,10},{10,12},{12... | collective-permute-start | bytes 393224 | tf_op jit(solution)/shard_map/ppermute | solution.py:34
  23.3 5.7 %collective-permute-start.2 = (bf16[128,512]{1,0:T(8,128)(2,1)S(1)}, bf16[128,512]{1,0:T(8,128)(2,1)S(1)}, u32[]{:S(2)}, u32[]{:S(2)}) collective-permute-start(bf16[128,512]{1,0:T(8,128)(2,1)S(1)} %get-tuple-element.48), channel_id=1, source_target_pairs={{0,16},{8,24},{16,0},{24,8},{1,17},{9,25},{17,1},{25,9},{2,18},{10... | collective-permute-start | bytes 393224 | tf_op jit(solution)/shard_map/ppermute | solution.py:34
  24.1 4.9 %collective-permute-start.1 = (bf16[128,512]{1,0:T(8,128)(2,1)S(1)}, bf16[128,512]{1,0:T(8,128)(2,1)S(1)}, u32[]{:S(2)}, u32[]{:S(2)}) collective-permute-start(bf16[128,512]{1,0:T(8,128)(2,1)S(1)} %get-tuple-element.48), channel_id=1, source_target_pairs={{0,24},{8,0},{16,8},{24,16},{1,25},{9,1},{17,9},{25,17},{2,26},{10... | collective-permute-start | bytes 393224 | tf_op jit(solution)/shard_map/ppermute | solution.py:34
  26.0 6.4 %collective-permute-start = (bf16[128,512]{1,0:T(8,128)(2,1)S(1)}, bf16[128,512]{1,0:T(8,128)(2,1)S(1)}, u32[]{:S(2)}, u32[]{:S(2)}) collective-permute-start(bf16[128,512]{1,0:T(8,128)(2,1)S(1)} %get-tuple-element.48), channel_id=1, source_target_pairs={{0,8},{8,16},{16,24},{24,0},{1,9},{9,17},{17,25},{25,1},{2,10},{10... | collective-permute-start | bytes 393224 | tf_op jit(solution)/shard_map/ppermute | solution.py:34
  32.5 10.5 %collective-permute-start.9 = (bf16[4,128,512]{2,1,0:T(8,128)(2,1)S(1)}, bf16[4,128,512]{2,1,0:T(8,128)(2,1)S(1)}, u32[]{:S(2)}, u32[]{:S(2)}) collective-permute-start(bf16[4,128,512]{2,1,0:T(8,128)(2,1)S(1)} %pad_maximum_fusion.1.refs_5_), channel_id=1, source_target_pairs={{0,24},{8,0},{16,8},{24,16},{1,25},{9,1},{17,9},{25,17},{2,26},{10... | collective-permute-start | bytes 1572872 | tf_op jit(solution)/shard_map/ppermute | solution.py:34
  32.6 11.7 %collective-permute-start.8 = (bf16[4,128,512]{2,1,0:T(8,128)(2,1)S(1)}, bf16[4,128,512]{2,1,0:T(8,128)(2,1)S(1)}, u32[]{:S(2)}, u32[]{:S(2)}) collective-permute-start(bf16[4,128,512]{2,1,0:T(8,128)(2,1)S(1)} %pad_maximum_fusion.1.refs_5_), channel_id=1, source_target_pairs={{0,8},{8,16},{16,24},{24,0},{1,9},{9,17},{17,25},{25,1},{2,10},{10... | collective-permute-start | bytes 1572872 | tf_op jit(solution)/shard_map/ppermute | solution.py:34
  34.1 10.1 %collective-permute-start.7 = (bf16[4,128,512]{2,1,0:T(8,128)(2,1)S(1)}, bf16[4,128,512]{2,1,0:T(8,128)(2,1)S(1)}, u32[]{:S(2)}, u32[]{:S(2)}) collective-permute-start(bf16[4,128,512]{2,1,0:T(8,128)(2,1)S(1)} %pad_maximum_fusion.refs_0_), channel_id=1, source_target_pairs={{0,6},{2,0},{4,2},{6,4},{1,7},{3,1},{5,3},{7,5},{8,14},{10,8},{12,... | collective-permute-start | bytes 1572872 | tf_op jit(solution)/shard_map/ppermute | solution.py:34
  36.2 10.6 %collective-permute-start.6 = (bf16[4,128,512]{2,1,0:T(8,128)(2,1)S(1)}, bf16[4,128,512]{2,1,0:T(8,128)(2,1)S(1)}, u32[]{:S(2)}, u32[]{:S(2)}) collective-permute-start(bf16[4,128,512]{2,1,0:T(8,128)(2,1)S(1)} %pad_maximum_fusion.refs_0_), channel_id=1, source_target_pairs={{0,2},{2,4},{4,6},{6,0},{1,3},{3,5},{5,7},{7,1},{8,10},{10,12},{12... | collective-permute-start | bytes 1572872 | tf_op jit(solution)/shard_map/ppermute | solution.py:34
  49.7 5.6 %collective-permute-start.13 = (bf16[2,128,512]{2,1,0:T(8,128)(2,1)}, bf16[2,128,512]{2,1,0:T(8,128)(2,1)S(1)}, u32[]{:S(2)}, u32[]{:S(2)}) collective-permute-start(bf16[2,128,512]{2,1,0:T(8,128)(2,1)} %slice.23), channel_id=1, source_target_pairs={{0,24},{8,0},{16,8},{24,16},{1,25},{9,1},{17,9},{25,17},{2,26},{10... | collective-permute-start | bytes 786440 | tf_op jit(solution)/shard_map/ppermute | solution.py:34
  51.4 7.0 %collective-permute-start.12 = (bf16[2,128,512]{2,1,0:T(8,128)(2,1)}, bf16[2,128,512]{2,1,0:T(8,128)(2,1)}, u32[]{:S(2)}, u32[]{:S(2)}) collective-permute-start(bf16[2,128,512]{2,1,0:T(8,128)(2,1)} %slice.22), channel_id=1, source_target_pairs={{0,8},{8,16},{16,24},{24,0},{1,9},{9,17},{17,25},{25,1},{2,10},{10... | collective-permute-start | bytes 786440 | tf_op jit(solution)/shard_map/ppermute | solution.py:34
  51.4 7.0 %collective-permute-start.11 = (bf16[2,128,512]{2,1,0:T(8,128)(2,1)}, bf16[2,128,512]{2,1,0:T(8,128)(2,1)}, u32[]{:S(2)}, u32[]{:S(2)}) collective-permute-start(bf16[2,128,512]{2,1,0:T(8,128)(2,1)} %slice.21), channel_id=1, source_target_pairs={{0,6},{2,0},{4,2},{6,4},{1,7},{3,1},{5,3},{7,5},{8,14},{10,8},{12,... | collective-permute-start | bytes 786440 | tf_op jit(solution)/shard_map/ppermute | solution.py:34
  51.7 7.0 %collective-permute-start.10 = (bf16[2,128,512]{2,1,0:T(8,128)(2,1)}, bf16[2,128,512]{2,1,0:T(8,128)(2,1)}, u32[]{:S(2)}, u32[]{:S(2)}) collective-permute-start(bf16[2,128,512]{2,1,0:T(8,128)(2,1)} %slice.20), channel_id=1, source_target_pairs={{0,2},{2,4},{4,6},{6,0},{1,3},{3,5},{5,7},{7,1},{8,10},{10,12},{12... | collective-permute-start | bytes 786440 | tf_op jit(solution)/shard_map/ppermute | solution.py:34
  71.7 7.9 %collective-permute-start.14 = (f32[264,1152]{1,0:T(8,128)S(1)}, f32[264,1152]{1,0:T(8,128)S(1)}, u32[]{:S(2)}, u32[]{:S(2)}) collective-permute-start(f32[264,1152]{1,0:T(8,128)S(1)} %theirs.1), channel_id=1, source_target_pairs={{0,1},{1,0},{2,3},{3,2},{4,5},{5,4},{6,7},{7,6},{8,9},{9,8},{10,11... | collective-permute-start | bytes 3649544 | tf_op jit(solution)/shard_map/ppermute | solution.py:34
  148.5 19.9 %all-to-all-start.6 = ((f32[32,8,128]{2,1,0:T(8,128)}), f32[32,8,128]{2,1,0:T(8,128)S(1)}, u32[]{:S(2)}, u32[]{:S(2)}) async-start(f32[32,8,128]{2,1,0:T(8,128)} %get-tuple-element.76), calls=%async_computation.6 | async-start | bytes 262144 | tf_op jit(solution)/shard_map/all_to_all | solution.py:392
  152.3 10.9 %collective-permute-start.15 = (bf16[256,256]{1,0:T(8,128)(2,1)S(1)}, bf16[256,256]{1,0:T(8,128)(2,1)S(1)}, u32[]{:S(2)}, u32[]{:S(2)}) collective-permute-start(bf16[256,256]{1,0:T(8,128)(2,1)S(1)} %get-tuple-element.78), channel_id=1, source_target_pairs={{0,8},{8,16},{16,24},{24,0},{1,9},{9,17},{17,25},{25,1},{2,10},{10... | collective-permute-start | bytes 393224 | tf_op jit(solution)/shard_map/ppermute | solution.py:34
  153.5 14.8 %collective-permute-start.16 = (bf16[256,256]{1,0:T(8,128)(2,1)S(1)}, bf16[256,256]{1,0:T(8,128)(2,1)S(1)}, u32[]{:S(2)}, u32[]{:S(2)}) collective-permute-start(bf16[256,256]{1,0:T(8,128)(2,1)S(1)} %get-tuple-element.79), channel_id=1, source_target_pairs={{0,16},{8,24},{16,0},{24,8},{1,17},{9,25},{17,1},{25,9},{2,18},{10... | collective-permute-start | bytes 393224 | tf_op jit(solution)/shard_map/ppermute | solution.py:34
  156.0 12.4 %collective-permute-start.17 = (bf16[256,256]{1,0:T(8,128)(2,1)S(1)}, bf16[256,256]{1,0:T(8,128)(2,1)S(1)}, u32[]{:S(2)}, u32[]{:S(2)}) collective-permute-start(bf16[256,256]{1,0:T(8,128)(2,1)S(1)} %get-tuple-element.80), channel_id=1, source_target_pairs={{0,24},{8,0},{16,8},{24,16},{1,25},{9,1},{17,9},{25,17},{2,26},{10... | collective-permute-start | bytes 393224 | tf_op jit(solution)/shard_map/ppermute | solution.py:34
  177.6 9.1 %collective-permute-start.19 = (bf16[256,512]{1,0:T(8,128)(2,1)S(1)}, bf16[256,512]{1,0:T(8,128)(2,1)S(1)}, u32[]{:S(2)}, u32[]{:S(2)}) collective-permute-start(bf16[256,512]{1,0:T(8,128)(2,1)S(1)} %get-tuple-element.86), channel_id=1, source_target_pairs={{0,4},{2,6},{4,0},{6,2},{1,5},{3,7},{5,1},{7,3},{8,12},{10,14},{12... | collective-permute-start | bytes 786440 | tf_op jit(solution)/shard_map/ppermute | solution.py:34
  180.1 12.9 %collective-permute-start.20 = (bf16[256,512]{1,0:T(8,128)(2,1)S(1)}, bf16[256,512]{1,0:T(8,128)(2,1)S(1)}, u32[]{:S(2)}, u32[]{:S(2)}) collective-permute-start(bf16[256,512]{1,0:T(8,128)(2,1)S(1)} %get-tuple-element.87), channel_id=1, source_target_pairs={{0,2},{2,4},{4,6},{6,0},{1,3},{3,5},{5,7},{7,1},{8,10},{10,12},{12... | collective-permute-start | bytes 786440 | tf_op jit(solution)/shard_map/ppermute | solution.py:34
  180.6 12.4 %collective-permute-start.21 = (bf16[256,512]{1,0:T(8,128)(2,1)S(1)}, bf16[256,512]{1,0:T(8,128)(2,1)S(1)}, u32[]{:S(2)}, u32[]{:S(2)}) collective-permute-start(bf16[256,512]{1,0:T(8,128)(2,1)S(1)} %get-tuple-element.88), channel_id=1, source_target_pairs={{0,6},{2,0},{4,2},{6,4},{1,7},{3,1},{5,3},{7,5},{8,14},{10,8},{12,... | collective-permute-start | bytes 786440 | tf_op jit(solution)/shard_map/ppermute | solution.py:34
  (7 other events, 22.9 us)
Sparse Core Ops, SparseCore 0:
  17.8 45.3 all-gather.4
  67.8 99.2 all-gather.6

commit v9 on v8

--- a/solution.py
+++ b/solution.py
@@ -124,11 +124,13 @@
     )(*parts)
 
 
-def pick_kernel(place, all_ref, far_ref, near_ref, sems):
+def pick_kernel(place, all_ref, far_ref, side_ref, near_ref, sems):
     copies = []
     for y in range(Y):
-        for n, ref in enumerate((near_ref, far_ref)):
-            copies.append(pltpu.make_async_copy(all_ref.at[y, place[3]], ref.at[y], sems.at[n, y]))
+        own = all_ref.at[y, place[3]]
+        copies.append(pltpu.make_async_copy(own, near_ref.at[y], sems.at[0, y]))
+        copies.append(pltpu.make_async_copy(own.at[:, : X - 1], far_ref.at[y], sems.at[1, y]))
+        copies.append(pltpu.make_async_copy(own.at[:, X - 1], side_ref.at[y], sems.at[2, y]))
     for copy in copies:
         copy.start()
     for copy in copies:
@@ -136,13 +138,16 @@
 
 
 def pick(place, samples):
-    half = jax.ShapeDtypeStruct((Y, C, X, QUARTER, SLICE), BF16)
     return pl.pallas_call(
         pick_kernel,
-        out_shape=(half, half),
+        out_shape=(
+            jax.ShapeDtypeStruct((Y, C, X - 1, QUARTER, SLICE), BF16),
+            jax.ShapeDtypeStruct((Y, C, QUARTER, SLICE), BF16),
+            jax.ShapeDtypeStruct((Y, C, X, QUARTER, SLICE), BF16),
+        ),
         in_specs=[SMEM, pl.BlockSpec(memory_space=pl.ANY)],
-        out_specs=(pl.BlockSpec(memory_space=pl.ANY), VMEM),
-        scratch_shapes=[pltpu.SemaphoreType.DMA((2, Y))],
+        out_specs=(pl.BlockSpec(memory_space=pl.ANY), pl.BlockSpec(memory_space=pl.ANY), VMEM),
+        scratch_shapes=[pltpu.SemaphoreType.DMA((3, Y))],
         compiler_params=params(16),
         name="pick",
     )(place, samples)
@@ -195,7 +200,8 @@
     )(place, data, noise)
 
 
-def score_kernel(mine_ref, sq_mine_ref, sqn_mine_ref, got_ref, q_ref, out_ref, sq_ref, sqn_ref, lse_ref):
+def score_kernel(place, mine_ref, sq_mine_ref, sqn_mine_ref, got_ref, q_ref, out_ref, sq_ref, sqn_ref, *refs):
+    block_refs, lse_ref = refs[:X], refs[X]
     sq = jnp.sum(sq_mine_ref[...] + got_ref[:QUARTER, TALL:], axis=1, keepdims=True)
     sq_ref[...] = jnp.broadcast_to(sq, (QUARTER, 128))
     sqn_ref[...] = sqn_mine_ref[...] + got_ref[QUARTER : QUARTER + 2, :128]
@@ -204,9 +210,13 @@
         q_ref[:, chunk(r)] = q
         lse_ref[pl.ds(r, 1), :] = lse(q - UNIT * sq_ref[...], 0)
     out_ref[...] = jnp.broadcast_to(lse_ref[...][None], (GROUP, CHUNKS, 128))
-
-
-def score(mine, sq_mine, sqn_mine, got):
+    for rel, ref in zip(AROUND, block_refs):
+        for h in range(2):
+            lanes = pl.ds(pl.multiple_of((h * X + at(place, 1, -rel, X)) * 128, 128), 128)
+            ref[:, chunk(h)] = q_ref[:, lanes]
+
+
+def score(place, mine, sq_mine, sqn_mine, got):
     return pl.pallas_call(
         score_kernel,
         out_shape=(
@@ -214,13 +224,14 @@
             jax.ShapeDtypeStruct((GROUP, CHUNKS, 128), F32),
             jax.ShapeDtypeStruct((QUARTER, 128), F32),
             jax.ShapeDtypeStruct((2, 128), F32),
-        ),
-        in_specs=[VMEM] * 4,
-        out_specs=(VMEM,) * 4,
+        )
+        + (jax.ShapeDtypeStruct((QUARTER, ROWS), F32),) * X,
+        in_specs=[SMEM] + [VMEM] * 4,
+        out_specs=(VMEM,) * (4 + X),
         scratch_shapes=[pltpu.VMEM((CHUNKS, 128), F32)],
         compiler_params=params(16),
         name="score",
-    )(mine, sq_mine, sqn_mine, got)
+    )(place, mine, sq_mine, sqn_mine, got)
 
 
 def to_column(g):
@@ -279,93 +290,83 @@
     )(q, parts)
 
 
-def last_kernel(place, q_ref, part_ref, sq_ref, out_ref, f_ref, *refs):
-    w_refs, lane_ref = refs[:X], refs[X]
+def last_kernel(q_ref, part_ref, sq_ref, out_ref, f_ref, lane_ref):
     f_ref[...] = -LOG2N - merged(part_ref)
     tile = two_rows(data_row(q_ref, f_ref, lane_ref), jnp.transpose(sq_ref[...])[0:1, :])
     out_ref[...] = jnp.broadcast_to(tile[None], (Z * X, 8, 128))
-    column = to_column(tile)
-    for by in range(X):
-        block = lax.rem(place[1] + by, X)
-        for h in range(2):
-            lanes = pl.ds(pl.multiple_of((h * X + block) * 128, 128), 128)
-            w = jnp.exp2((q_ref[:, lanes] + f_ref[pl.ds(h * X + block, 1), :]) - column)
-            w_refs[by][:, pl.ds(h * 128, 128)] = w.astype(BF16)
-
-
-def last_lse(place, q, parts, sq):
+
+
+def last_lse(q, parts, sq):
     return pl.pallas_call(
         last_kernel,
-        out_shape=(jax.ShapeDtypeStruct((Z * X, 8, 128), F32), jax.ShapeDtypeStruct((CHUNKS, 128), F32))
-        + (jax.ShapeDtypeStruct((QUARTER, ROWS), BF16),) * X,
-        in_specs=[SMEM] + [VMEM] * 3,
-        out_specs=(VMEM,) * (2 + X),
+        out_shape=(jax.ShapeDtypeStruct((Z * X, 8, 128), F32), jax.ShapeDtypeStruct((CHUNKS, 128), F32)),
+        in_specs=[VMEM] * 3,
+        out_specs=(VMEM,) * 2,
         scratch_shapes=[pltpu.VMEM((QUARTER, 128), F32)],
         compiler_params=params(16),
         name="last_lse",
-    )(place, q, parts, sq)
-
-
-def scale_kernel(place, part_ref, *refs):
-    w_refs, (w_ref, pot_ref) = refs[:X], refs[X:]
-    z, x = place[0], place[1]
+    )(q, parts, sq)
+
+
+def weigh_kernel(place, part_ref, f_ref, *refs):
+    q_refs, (w_ref, pot_ref) = refs[:X], refs[X:]
     for n in range(X):
         parts = jnp.stack([part_ref[k * X + n, 0:4, :] for k in range(Z)])
         top = jnp.max(parts, axis=0)
         total = top + jnp.log2(jnp.sum(jnp.exp2(parts - top[None]), axis=0))
         pot_ref[pl.ds(2 * n, 2), :] = (-LOG2N - total[0:2]) * (EPS / LOG2E) + parts[0, 2:4] * (1.0 / WIDTH)
-    for by in range(X):
-        n = lax.rem(x - by + X, X)
+    for j, rel in enumerate(AROUND):
+        n = at(place, 1, rel, X)
         parts = jnp.stack([part_ref[k * X + n] for k in range(Z)])
         top = jnp.max(parts, axis=0)
-        total = top + jnp.log2(jnp.sum(jnp.exp2(parts - top[None]), axis=0))
-        factor = jnp.exp2(part_ref[z * X + n] - total)
-        factor = jnp.concatenate([factor[0:1], factor[1:2]], axis=1)
-        lanes = pl.ds(pl.multiple_of(n * QUARTER, QUARTER), QUARTER)
+        column = to_column(top + jnp.log2(jnp.sum(jnp.exp2(parts - top[None]), axis=0)))
         for h in range(2):
-            w = jnp.transpose(w_refs[by][:, pl.ds(h * 128, 128)].astype(F32)) * factor
-            w_ref[pl.ds(h * 128, 128), lanes] = w.astype(BF16)
-
-
-def scale(place, parts, blocks):
-    return pl.pallas_call(
-        scale_kernel,
+            f = f_ref[pl.ds(h * X + place[1], 1), :]
+            w = jnp.exp2((q_refs[j][:, chunk(h)] + f) - column)
+            w_ref[pl.ds(h * 128, 128), pl.ds(j * QUARTER, QUARTER)] = jnp.transpose(w).astype(BF16)
+
+
+def weigh(place, parts, f, blocks):
+    return pl.pallas_call(
+        weigh_kernel,
         out_shape=(jax.ShapeDtypeStruct((ROWS, COUNT), BF16), jax.ShapeDtypeStruct((2 * X, 128), F32)),
-        in_specs=[SMEM] + [VMEM] * (1 + X),
+        in_specs=[SMEM] + [VMEM] * (2 + X),
         out_specs=(VMEM,) * 2,
         compiler_params=params(16),
-        name="scale",
-    )(place, parts, *blocks)
-
-
-def transport_kernel(pieces, place, w_ref, got_ref, data_ref, *out_refs):
+        name="weigh",
+    )(place, parts, f, *blocks)
+
+
+def transport_kernel(pieces, place, w_ref, got_ref, *refs):
+    side_refs, data_ref, out_refs = refs[:X], refs[X], refs[X + 1 :]
     lhs = jnp.concatenate([w_ref[...], got_ref[...]], axis=1)
     for s, out_ref in zip(pieces, out_refs):
         y = at(place, 2, s, Y)
         rhs = []
         for core in (place[3], 1 - place[3]):
-            for n in range(X):
-                rhs.append(jnp.concatenate([data_ref[n, y, core, k] for k in range(X)], axis=1))
+            for rel, side_ref in zip(AROUND, side_refs):
+                n = at(place, 1, rel, X)
+                rhs.append(jnp.concatenate([data_ref[n, y, core, k] for k in range(X - 1)] + [side_ref[y, core]], axis=1))
         total = jnp.dot(lhs, jnp.concatenate(rhs, axis=0), preferred_element_type=F32)
         out_ref[...] = total.astype(out_ref.dtype)
 
 
-def transport(place, w, got, data, pieces, hand_on):
+def transport(place, w, got, sides, data, pieces, hand_on):
     kinds = [jax.ShapeDtypeStruct((ROWS, SHARE), BF16 if s else F32) for s in pieces]
     if hand_on:
         kinds.append(jax.ShapeDtypeStruct(data.shape, data.dtype))
     return pl.pallas_call(
         functools.partial(transport_kernel, pieces),
         out_shape=kinds,
-        in_specs=[SMEM] + [VMEM] * 3,
+        in_specs=[SMEM] + [VMEM] * (3 + X),
         out_specs=[VMEM] * len(kinds),
-        input_output_aliases={3: len(pieces)} if hand_on else {},
+        input_output_aliases={3 + X: len(pieces)} if hand_on else {},
         compiler_params=params(24),
         cost_estimate=pl.CostEstimate(
             flops=2 * ROWS * COUNT * C * SHARE * len(pieces), bytes_accessed=2 * 2**20 * len(pieces), transcendentals=0
         ),
         name="transport",
-    )(place, w, got, data)
+    )(place, w, got, *sides, data)
 
 
 def body(noise, data):
@@ -375,26 +376,29 @@
     noise_after, swapped = lax.optimization_barrier((noise, swapped))
     samples = lax.all_gather(swapped, ("z", "core")).reshape(Y, C, C, X, QUARTER, SLICE)
     samples, noise_all, sqn_mine = lax.optimization_barrier((samples, *collect(gather_noise(noise_after))))
-    far, near = pick(place, samples)
+    far, side, near = pick(place, samples)
     data_all = lax.all_gather(far, "x")
+    sides = around(side, "x")
     got = shift(theirs(place, near, noise_all, sqn_mine), "core", 1)
     mine, sq_mine = ours(place, near, noise_all)
-    q, rows, sq, sq_noise = score(mine, sq_mine, sqn_mine, got)
+    q, rows, sq, sq_noise, *blocks = score(place, mine, sq_mine, sqn_mine, got)
+    blocks = [blocks[0]] + [shift(block, "x", by) for block, by in zip(blocks[1:], (1, -1, 2))]
     for step in range(ITERS):
+        if step == 1:
+            columns, sides = lax.optimization_barrier((columns, sides))
         if step:
             rows = noise_lse(q, columns)
         parts = lax.all_to_all(rows, ("x", "y", "core"), 0, 0)
         if step < ITERS - 1:
             columns, f = data_lse(q, parts)
             columns = lax.all_to_all(columns, "z", 0, 0)
-    columns, f, *blocks = last_lse(place, q, parts, sq)
-    blocks = [blocks[0]] + [shift(blocks[by], "x", by) for by in range(1, X)]
+    columns, f = last_lse(q, parts, sq)
+    data_all, columns = lax.optimization_barrier((data_all, columns))
     columns = lax.all_to_all(columns, ("z", "x"), 0, 0)
-    w, pot_g = scale(place, columns, blocks)
-    data_all, pot_g = lax.optimization_barrier((data_all, pot_g))
+    w, pot_g = weigh(place, columns, f, blocks)
     got = shift(w, "core", 1)
-    *parts, data_all = transport(place, w, got, data_all, (2, 1, 3), True)
-    (target,) = transport(place, w, got, data_all, (0,), False)
+    *parts, data_all = transport(place, w, got, sides, data_all, (2, 1, 3), True)
+    (target,) = transport(place, w, got, sides, data_all, (0,), False)
     for by, part in zip((2, 1, 3), parts):
         target = target + shift(part, "y", by).astype(F32)
     velocity = (target - noise.astype(F32)).astype(BF16)

time: 201 us -> 227 us (1.13)
  starting transfers between devices: 33.9 us -> 54.2 us
  waiting for transfers between devices: 45.5 us -> 49.8 us
  Pallas kernels: 15.6 us -> 19.5 us
  blocking collectives: 75 us -> 72.7 us
    all_to_all x2 -> x1, blocking collectives: 25.3 us -> 9.23 us  [body(): columns = lax.all_to_all(columns, 'z', 0, 0)]
    ppermute x22 -> x25, waiting for transfers between devices: 44.6 us -> 28.6 us  [shift(): return lax.ppermute(x, axis, [(j, (j + by) % n) for j in range(n)])]
    all_to_all x3 -> x2, blocking collectives: 39.2 us -> 53 us  [body(): parts = lax.all_to_all(rows, ('x', 'y', 'core'), 0, 0)]
    all_to_all x0 -> x2, starting transfers between devices: none -> 12.1 us  [the longest x1 7.43 us: body(): columns = lax.all_to_all(columns, 'z', 0, 0)]
    all_to_all x0 -> x2, waiting for transfers between devices: none -> 10.3 us  [the longest x1 6.85 us: body(): columns = lax.all_to_all(columns, 'z', 0, 0)]
    ppermute x22 -> x25, starting transfers between devices: 29.9 us -> 37.9 us  [shift(): return lax.ppermute(x, axis, [(j, (j + by) % n) for j in range(n)])]
    all_to_all x1, waiting for transfers between devices: 0.01 us -> 6.59 us  [body(): columns = lax.all_to_all(columns, ('z', 'x'), 0, 0)]
    all_gather x1, waiting for transfers between devices: 0.84 us -> 4.23 us  [body(): lax.all_gather(swapped, ('z', 'core')).reshape(Y, C, C, X, QUARTER, SLICE)]
  transfers between devices with their start and end apart: 25 -> 30, of which waited for: 16 -> 14; matrix products, arithmetic and copies ran while one was open for 2% -> 2% of each run, Pallas kernels for 6% -> 6%
where the time goes in v9:
time: 227 us; the launch traced here: 226 us
  blocking collectives  72.7 us (32%)
  starting transfers between devices  54.2 us (24%)
  waiting for transfers between devices  49.8 us (22%)
  Pallas kernels  19.5 us (9%)
  local copies, waits for them, and re-layouts  14.3 us (6%)
  between operations  14.2 us (6%)
    all_to_all x2, blocking collectives, body(): parts = lax.all_to_all(rows, ('x', 'y', 'core'), 0, 0)  53 us
    ppermute x25, starting transfers between devices, shift(): return lax.ppermute(x, axis, [(j, (j + by) % n) for j in range(n)])  37.9 us
    ppermute x25, waiting for transfers between devices, shift(): return lax.ppermute(x, axis, [(j, (j + by) % n) for j in range(n)])  28.6 us
    all_to_all x1, blocking collectives, body(): swapped = lax.all_to_all(data.reshape(X, QUARTER, SLICE), 'x', 0, 0)  10.5 us
    unnamed x14, local copies, waits for them, and re-layouts  10.4 us
    all_to_all x1, blocking collectives, body(): columns = lax.all_to_all(columns, 'z', 0, 0)  9.23 us
    all_to_all x1, starting transfers between devices, body(): columns = lax.all_to_all(columns, 'z', 0, 0)  7.43 us
    all_to_all x1, waiting for transfers between devices, body(): columns = lax.all_to_all(columns, 'z', 0, 0)  6.85 us
  transfers between devices with their start and end apart: 30, of which 14 were waited for; matrix products, arithmetic and copies ran while one was open for 2% of the time, Pallas kernels for 6%

profile of v9, /device:TPU:1, one launch (start us, length us, event | category | flops | bytes accessed | tf_op | source)
XLA Modules:
  0.0 226.2 jit_solution(15681550926467405087)
XLA Ops:
  7.2 10.5 %all_to_all.35 = bf16[4,256,128]{2,1,0:T(8,128)(2,1)} all-to-all(bf16[4,256,128]{2,1,0:T(8,128)(2,1)} %bitcast.29), channel_id=1, replica_groups=mesh['z'=8,'x'=4,'y'=4,'core'=2] {'x'}, dimensions={0} | all-to-all | bytes 524288 | tf_op jit(solution)/shard_map/all_to_all | solution.py:375
  19.1 2.4 %collective-permute-start.1 = (bf16[128,512]{1,0:T(8,128)(2,1)S(1)}, bf16[128,512]{1,0:T(8,128)(2,1)S(1)}, u32[]{:S(2)}, u32[]{:S(2)}) collective-permute-start(bf16[128,512]{1,0:T(8,128)(2,1)S(1)} %get-tuple-element.54), channel_id=1, source_target_pairs={{0,24},{8,0},{16,8},{24,16},{1,25},{9,1},{17,9},{25,17},{2,26},{10... | collective-permute-start | bytes 393224 | tf_op jit(solution)/shard_map/ppermute | solution.py:34
  24.3 2.5 %collective-permute-start.5 = (bf16[128,512]{1,0:T(8,128)(2,1)S(1)}, bf16[128,512]{1,0:T(8,128)(2,1)S(1)}, u32[]{:S(2)}, u32[]{:S(2)}) collective-permute-start(bf16[128,512]{1,0:T(8,128)(2,1)S(1)} %get-tuple-element.58), channel_id=1, source_target_pairs={{0,4},{2,6},{4,0},{6,2},{1,5},{3,7},{5,1},{7,3},{8,12},{10,14},{12... | collective-permute-start | bytes 393224 | tf_op jit(solution)/shard_map/ppermute | solution.py:34
  33.4 2.7 %collective-permute-start.9 = (bf16[4,128,512]{2,1,0:T(8,128)(2,1)S(1)}, bf16[4,128,512]{2,1,0:T(8,128)(2,1)S(1)}, u32[]{:S(2)}, u32[]{:S(2)}) collective-permute-start(bf16[4,128,512]{2,1,0:T(8,128)(2,1)S(1)} %pad_maximum_fusion.1.refs_5_), channel_id=1, source_target_pairs={{0,24},{8,0},{16,8},{24,16},{1,25},{9,1},{17,9},{25,17},{2,26},{10... | collective-permute-start | bytes 1572872 | tf_op jit(solution)/shard_map/ppermute | solution.py:34
  36.1 5.5 %collective-permute-done.6.refs_1_ = bf16[4,128,512]{2,1,0:T(8,128)(2,1)S(1)} collective-permute-done((bf16[4,128,512]{2,1,0:T(8,128)(2,1)S(1)}, bf16[4,128,512]{2,1,0:T(8,128)(2,1)S(1)}, u32[]{:S(2)}, u32[]{:S(2)}) %collective-permute-start.6) | collective-permute-done | bytes 524320 | tf_op jit(solution)/shard_map/ppermute | solution.py:34
  44.4 2.7 %collective-permute-start.11 = (bf16[2,128,512]{2,1,0:T(8,128)(2,1)}, bf16[2,128,512]{2,1,0:T(8,128)(2,1)}, u32[]{:S(2)}, u32[]{:S(2)}) collective-permute-start(bf16[2,128,512]{2,1,0:T(8,128)(2,1)} %slice.21), channel_id=1, source_target_pairs={{0,6},{2,0},{4,2},{6,4},{1,7},{3,1},{5,3},{7,5},{8,14},{10,8},{12,... | collective-permute-start | bytes 786440 | tf_op jit(solution)/shard_map/ppermute | solution.py:34
  51.2 3.6 %collective-permute-done.12.refs_8_ = bf16[2,128,512]{2,1,0:T(8,128)(2,1)} collective-permute-done((bf16[2,128,512]{2,1,0:T(8,128)(2,1)}, bf16[2,128,512]{2,1,0:T(8,128)(2,1)}, u32[]{:S(2)}, u32[]{:S(2)}) %collective-permute-start.12) | collective-permute-done | bytes 262176 | tf_op jit(solution)/shard_map/ppermute | solution.py:34
  58.7 4.2 %all-gather.5.cloned.1.call-done = bf16[64,256,128]{2,1,0:T(8,128)(2,1)} async-done(((bf16[4,256,128]{2,1,0:T(8,128)(2,1)}), bf16[64,256,128]{2,1,0:T(8,128)(2,1)}) %all-gather.5.cloned.1.call-update) | async-done | bytes 4194320 | tf_op jit(solution)/shard_map/all_gather | solution.py:377
  72.0 6.5 %collective-permute-start.14 = (f32[264,1152]{1,0:T(8,128)S(1)}, f32[264,1152]{1,0:T(8,128)S(1)}, u32[]{:S(2)}, u32[]{:S(2)}) collective-permute-start(f32[264,1152]{1,0:T(8,128)S(1)} %theirs.1), channel_id=1, source_target_pairs={{0,1},{1,0},{2,3},{3,2},{4,5},{5,4},{6,7},{7,6},{8,9},{9,8},{10,11... | collective-permute-start | bytes 3649544 | tf_op jit(solution)/shard_map/ppermute | solution.py:34
  78.6 2.7 %collective-permute-start.16 = (bf16[4,2,256,128]{3,2,1,0:T(8,128)(2,1)S(1)}, bf16[4,2,256,128]{3,2,1,0:T(8,128)(2,1)}, u32[]{:S(2)}, u32[]{:S(2)}) collective-permute-start(bf16[4,2,256,128]{3,2,1,0:T(8,128)(2,1)S(1)} %get-tuple-element.92.refs_0_), channel_id=1, source_target_pairs={{0,24},{8,0},{16,8},{24,16},{1,25},{9,1},{17,9},{25,17},{2,26},{10... | collective-permute-start | bytes 1572872 | tf_op jit(solution)/shard_map/ppermute | solution.py:34
  85.6 35.9 %all_to_all.36.part_ref = f32[32,8,128]{2,1,0:T(8,128)S(1)} all-to-all(f32[32,8,128]{2,1,0:T(8,128)S(1)} %get-tuple-element.75), channel_id=1, replica_groups=mesh['z'=8,'x'=4,'y'=4,'core'=2] {'x','y','core'}, dimensions={0} | all-to-all | bytes 262144 | tf_op jit(solution)/shard_map/all_to_all | solution.py:391
  122.5 7.4 %all-to-all-start.2 = ((f32[8,8,128]{2,1,0:T(8,128)}), f32[8,8,128]{2,1,0:T(8,128)S(1)}, u32[]{:S(2)}, u32[]{:S(2)}) async-start(f32[8,8,128]{2,1,0:T(8,128)} %get-tuple-element.76), calls=%async_computation.2 | async-start | bytes 65536 | tf_op jit(solution)/shard_map/all_to_all | solution.py:394
  129.9 6.8 %all-to-all-done.2.part_ref = f32[8,8,128]{2,1,0:T(8,128)S(1)} async-done(((f32[8,8,128]{2,1,0:T(8,128)}), f32[8,8,128]{2,1,0:T(8,128)S(1)}, u32[]{:S(2)}, u32[]{:S(2)}) %all-to-all-start.2) | async-done | bytes 32800 | tf_op jit(solution)/shard_map/all_to_all | solution.py:394
  137.1 17.1 %all_to_all.37.part_ref = f32[32,8,128]{2,1,0:T(8,128)S(1)} all-to-all(f32[32,8,128]{2,1,0:T(8,128)S(1)} %noise_lse.2), channel_id=1, replica_groups=mesh['z'=8,'x'=4,'y'=4,'core'=2] {'x','y','core'}, dimensions={0} | all-to-all | bytes 262144 | tf_op jit(solution)/shard_map/all_to_all | solution.py:391
  155.0 9.2 %all_to_all.38.part_ref = f32[8,8,128]{2,1,0:T(8,128)S(1)} all-to-all(f32[8,8,128]{2,1,0:T(8,128)S(1)} %get-tuple-element.79), channel_id=1, replica_groups=mesh['z'=8,'x'=4,'y'=4,'core'=2] {'z'}, dimensions={0} | all-to-all | bytes 65536 | tf_op jit(solution)/shard_map/all_to_all | solution.py:394
  165.3 4.7 %all-to-all-start.5 = ((f32[32,8,128]{2,1,0:T(8,128)}), f32[32,8,128]{2,1,0:T(8,128)S(1)}, u32[]{:S(2)}, u32[]{:S(2)}) async-start(f32[32,8,128]{2,1,0:T(8,128)} %noise_lse.3), calls=%async_computation.5 | async-start | bytes 262144 | tf_op jit(solution)/shard_map/all_to_all | solution.py:391
  174.5 3.5 %all-to-all-done.5.part_ref = f32[32,8,128]{2,1,0:T(8,128)S(1)} async-done(((f32[32,8,128]{2,1,0:T(8,128)}), f32[32,8,128]{2,1,0:T(8,128)S(1)}, u32[]{:S(2)}, u32[]{:S(2)}) %all-to-all-start.5) | async-done | bytes 131104 | tf_op jit(solution)/shard_map/all_to_all | solution.py:391
  179.0 4.1 %all-to-all-start.6 = ((f32[32,8,128]{2,1,0:T(8,128)}), f32[32,8,128]{2,1,0:T(8,128)S(1)}, u32[]{:S(2)}, u32[]{:S(2)}) async-start(f32[32,8,128]{2,1,0:T(8,128)} %get-tuple-element.85), calls=%async_computation.6 | async-start | bytes 262144 | tf_op jit(solution)/shard_map/all_to_all | solution.py:397
  183.1 3.3 %collective-permute-done.20.refs_3_ = f32[256,256]{1,0:T(8,128)S(1)} collective-permute-done((f32[256,256]{1,0:T(8,128)}, f32[256,256]{1,0:T(8,128)S(1)}, u32[]{:S(2)}, u32[]{:S(2)}) %collective-permute-start.20) | collective-permute-done | bytes 262176 | tf_op jit(solution)/shard_map/ppermute | solution.py:34
  186.3 6.6 %all-to-all-done.6.part_ref = f32[32,8,128]{2,1,0:T(8,128)S(1)} async-done(((f32[32,8,128]{2,1,0:T(8,128)}), f32[32,8,128]{2,1,0:T(8,128)S(1)}, u32[]{:S(2)}, u32[]{:S(2)}) %all-to-all-start.6) | async-done | bytes 131104 | tf_op jit(solution)/shard_map/all_to_all | solution.py:397
  197.7 2.8 %copy-done = bf16[16,2,3,256,128]{4,3,2,1,0:T(8,128)(2,1)S(1)} copy-done((bf16[16,2,3,256,128]{4,3,2,1,0:T(8,128)(2,1)S(1)}, bf16[16,2,3,256,128]{4,3,2,1,0:T(8,128)(2,1)}, u32[]{:S(2)}) %copy-start) | copy-done | bytes 6291480
  200.4 3.0 %transport.2 = (bf16[256,512]{1,0:T(8,128)(2,1)S(1)}, bf16[256,512]{1,0:T(8,128)(2,1)S(1)}, bf16[256,512]{1,0:T(8,128)(2,1)S(1)}, bf16[4,4,2,3,256,128]{5,4,3,2,1,0:T(8,128)(2,1)S(1)}) custom-call(s32[4]{0:T(128)S(1)} %pad_add_fusion.place, bf16[256,1024]{1,0:T(8,128)(2,1)S(1)} %get-tuple-element.91.w_ref, ...), custom_call_target="tpu_custom_call", output_to_operand_aliasing={{3}: (7, {})} | custom-call | flops 1610612736 | bytes 6291456 | tf_op jit(solution)/shard_map/transport/pallas_call | solution.py:358
  208.3 2.7 %collective-permute-done.24 = bf16[256,512]{1,0:T(8,128)(2,1)S(1)} collective-permute-done((bf16[256,512]{1,0:T(8,128)(2,1)S(1)}, bf16[256,512]{1,0:T(8,128)(2,1)S(1)}, u32[]{:S(2)}, u32[]{:S(2)}) %collective-permute-start.24) | collective-permute-done | bytes 262176 | tf_op jit(solution)/shard_map/ppermute | solution.py:34
  211.0 7.5 %collective-permute-done.23 = bf16[256,512]{1,0:T(8,128)(2,1)S(1)} collective-permute-done((bf16[256,512]{1,0:T(8,128)(2,1)S(1)}, bf16[256,512]{1,0:T(8,128)(2,1)S(1)}, u32[]{:S(2)}, u32[]{:S(2)}) %collective-permute-start.23) | collective-permute-done | bytes 262176 | tf_op jit(solution)/shard_map/ppermute | solution.py:34
  (80 shorter events, 54.2 us)
Async XLA Ops:
  7.2 55.8 %all-gather.5.cloned.1.call-start = ((), (), s32[]{:S(2)}) async-start(), calls=%async_computation.7 | async-start | bytes 4456448 | tf_op jit(solution)/shard_map/all_gather | solution.py:377
  17.7 161.2 %all-gather.7.cloned.1.call-start = ((), (), s32[]{:S(2)}) async-start(), calls=%async_computation.8 | async-start | bytes 7864320 | tf_op jit(solution)/shard_map/all_gather | solution.py:380
  19.1 7.7 %collective-permute-start.1 = (bf16[128,512]{1,0:T(8,128)(2,1)S(1)}, bf16[128,512]{1,0:T(8,128)(2,1)S(1)}, u32[]{:S(2)}, u32[]{:S(2)}) collective-permute-start(bf16[128,512]{1,0:T(8,128)(2,1)S(1)} %get-tuple-element.54), channel_id=1, source_target_pairs={{0,24},{8,0},{16,8},{24,16},{1,25},{9,1},{17,9},{25,17},{2,26},{10... | collective-permute-start | bytes 393224 | tf_op jit(solution)/shard_map/ppermute | solution.py:34
  21.5 6.4 %collective-permute-start.2 = (bf16[128,512]{1,0:T(8,128)(2,1)S(1)}, bf16[128,512]{1,0:T(8,128)(2,1)S(1)}, u32[]{:S(2)}, u32[]{:S(2)}) collective-permute-start(bf16[128,512]{1,0:T(8,128)(2,1)S(1)} %get-tuple-element.54), channel_id=1, source_target_pairs={{0,16},{8,24},{16,0},{24,8},{1,17},{9,25},{17,1},{25,9},{2,18},{10... | collective-permute-start | bytes 393224 | tf_op jit(solution)/shard_map/ppermute | solution.py:34
  29.7 11.9 %collective-permute-start.6 = (bf16[4,128,512]{2,1,0:T(8,128)(2,1)S(1)}, bf16[4,128,512]{2,1,0:T(8,128)(2,1)S(1)}, u32[]{:S(2)}, u32[]{:S(2)}) collective-permute-start(bf16[4,128,512]{2,1,0:T(8,128)(2,1)S(1)} %pad_maximum_fusion.refs_0_), channel_id=1, source_target_pairs={{0,2},{2,4},{4,6},{6,0},{1,3},{3,5},{5,7},{7,1},{8,10},{10,12},{12... | collective-permute-start | bytes 1572872 | tf_op jit(solution)/shard_map/ppermute | solution.py:34
  31.0 10.6 %collective-permute-start.7 = (bf16[4,128,512]{2,1,0:T(8,128)(2,1)S(1)}, bf16[4,128,512]{2,1,0:T(8,128)(2,1)S(1)}, u32[]{:S(2)}, u32[]{:S(2)}) collective-permute-start(bf16[4,128,512]{2,1,0:T(8,128)(2,1)S(1)} %pad_maximum_fusion.refs_0_), channel_id=1, source_target_pairs={{0,6},{2,0},{4,2},{6,4},{1,7},{3,1},{5,3},{7,5},{8,14},{10,8},{12,... | collective-permute-start | bytes 1572872 | tf_op jit(solution)/shard_map/ppermute | solution.py:34
  33.3 9.6 %collective-permute-start.8 = (bf16[4,128,512]{2,1,0:T(8,128)(2,1)S(1)}, bf16[4,128,512]{2,1,0:T(8,128)(2,1)S(1)}, u32[]{:S(2)}, u32[]{:S(2)}) collective-permute-start(bf16[4,128,512]{2,1,0:T(8,128)(2,1)S(1)} %pad_maximum_fusion.1.refs_5_), channel_id=1, source_target_pairs={{0,8},{8,16},{16,24},{24,0},{1,9},{9,17},{17,25},{25,1},{2,10},{10... | collective-permute-start | bytes 1572872 | tf_op jit(solution)/shard_map/ppermute | solution.py:34
  33.4 9.5 %collective-permute-start.9 = (bf16[4,128,512]{2,1,0:T(8,128)(2,1)S(1)}, bf16[4,128,512]{2,1,0:T(8,128)(2,1)S(1)}, u32[]{:S(2)}, u32[]{:S(2)}) collective-permute-start(bf16[4,128,512]{2,1,0:T(8,128)(2,1)S(1)} %pad_maximum_fusion.1.refs_5_), channel_id=1, source_target_pairs={{0,24},{8,0},{16,8},{24,16},{1,25},{9,1},{17,9},{25,17},{2,26},{10... | collective-permute-start | bytes 1572872 | tf_op jit(solution)/shard_map/ppermute | solution.py:34
  43.6 7.6 %collective-permute-start.10 = (bf16[2,128,512]{2,1,0:T(8,128)(2,1)}, bf16[2,128,512]{2,1,0:T(8,128)(2,1)S(1)}, u32[]{:S(2)}, u32[]{:S(2)}) collective-permute-start(bf16[2,128,512]{2,1,0:T(8,128)(2,1)} %slice.20), channel_id=1, source_target_pairs={{0,2},{2,4},{4,6},{6,0},{1,3},{3,5},{5,7},{7,1},{8,10},{10,12},{12... | collective-permute-start | bytes 786440 | tf_op jit(solution)/shard_map/ppermute | solution.py:34
  44.4 6.9 %collective-permute-start.11 = (bf16[2,128,512]{2,1,0:T(8,128)(2,1)}, bf16[2,128,512]{2,1,0:T(8,128)(2,1)}, u32[]{:S(2)}, u32[]{:S(2)}) collective-permute-start(bf16[2,128,512]{2,1,0:T(8,128)(2,1)} %slice.21), channel_id=1, source_target_pairs={{0,6},{2,0},{4,2},{6,4},{1,7},{3,1},{5,3},{7,5},{8,14},{10,8},{12,... | collective-permute-start | bytes 786440 | tf_op jit(solution)/shard_map/ppermute | solution.py:34
  47.7 7.0 %collective-permute-start.12 = (bf16[2,128,512]{2,1,0:T(8,128)(2,1)}, bf16[2,128,512]{2,1,0:T(8,128)(2,1)}, u32[]{:S(2)}, u32[]{:S(2)}) collective-permute-start(bf16[2,128,512]{2,1,0:T(8,128)(2,1)} %slice.22), channel_id=1, source_target_pairs={{0,8},{8,16},{16,24},{24,0},{1,9},{9,17},{17,25},{25,1},{2,10},{10... | collective-permute-start | bytes 786440 | tf_op jit(solution)/shard_map/ppermute | solution.py:34
  72.0 11.8 %collective-permute-start.14 = (f32[264,1152]{1,0:T(8,128)S(1)}, f32[264,1152]{1,0:T(8,128)S(1)}, u32[]{:S(2)}, u32[]{:S(2)}) collective-permute-start(f32[264,1152]{1,0:T(8,128)S(1)} %theirs.1), channel_id=1, source_target_pairs={{0,1},{1,0},{2,3},{3,2},{4,5},{5,4},{6,7},{7,6},{8,9},{9,8},{10,11... | collective-permute-start | bytes 3649544 | tf_op jit(solution)/shard_map/ppermute | solution.py:34
  78.5 51.4 %collective-permute-start.15 = (bf16[4,2,256,128]{3,2,1,0:T(8,128)(2,1)S(1)}, bf16[4,2,256,128]{3,2,1,0:T(8,128)(2,1)S(1)}, u32[]{:S(2)}, u32[]{:S(2)}) collective-permute-start(bf16[4,2,256,128]{3,2,1,0:T(8,128)(2,1)S(1)} %get-tuple-element.92.refs_0_), channel_id=1, source_target_pairs={{0,8},{8,16},{16,24},{24,0},{1,9},{9,17},{17,25},{25,1},{2,10},{10... | collective-permute-start | bytes 1572872 | tf_op jit(solution)/shard_map/ppermute | solution.py:34
  78.6 51.3 %collective-permute-start.16 = (bf16[4,2,256,128]{3,2,1,0:T(8,128)(2,1)S(1)}, bf16[4,2,256,128]{3,2,1,0:T(8,128)(2,1)}, u32[]{:S(2)}, u32[]{:S(2)}) collective-permute-start(bf16[4,2,256,128]{3,2,1,0:T(8,128)(2,1)S(1)} %get-tuple-element.92.refs_0_), channel_id=1, source_target_pairs={{0,24},{8,0},{16,8},{24,16},{1,25},{9,1},{17,9},{25,17},{2,26},{10... | collective-permute-start | bytes 1572872 | tf_op jit(solution)/shard_map/ppermute | solution.py:34
  81.2 48.7 %collective-permute-start.17 = (bf16[4,2,256,128]{3,2,1,0:T(8,128)(2,1)S(1)}, bf16[4,2,256,128]{3,2,1,0:T(8,128)(2,1)}, u32[]{:S(2)}, u32[]{:S(2)}) collective-permute-start(bf16[4,2,256,128]{3,2,1,0:T(8,128)(2,1)S(1)} %get-tuple-element.92.refs_0_), channel_id=1, source_target_pairs={{0,16},{8,24},{16,0},{24,8},{1,17},{9,25},{17,1},{25,9},{2,18},{10... | collective-permute-start | bytes 1572872 | tf_op jit(solution)/shard_map/ppermute | solution.py:34
  122.5 14.3 %all-to-all-start.2 = ((f32[8,8,128]{2,1,0:T(8,128)}), f32[8,8,128]{2,1,0:T(8,128)S(1)}, u32[]{:S(2)}, u32[]{:S(2)}) async-start(f32[8,8,128]{2,1,0:T(8,128)} %get-tuple-element.76), calls=%async_computation.2 | async-start | bytes 65536 | tf_op jit(solution)/shard_map/all_to_all | solution.py:394
  165.3 12.7 %all-to-all-start.5 = ((f32[32,8,128]{2,1,0:T(8,128)}), f32[32,8,128]{2,1,0:T(8,128)S(1)}, u32[]{:S(2)}, u32[]{:S(2)}) async-start(f32[32,8,128]{2,1,0:T(8,128)} %noise_lse.3), calls=%async_computation.5 | async-start | bytes 262144 | tf_op jit(solution)/shard_map/all_to_all | solution.py:391
  170.0 13.1 %collective-permute-start.18 = (f32[256,256]{1,0:T(8,128)}, f32[256,256]{1,0:T(8,128)S(1)}, u32[]{:S(2)}, u32[]{:S(2)}) collective-permute-start(f32[256,256]{1,0:T(8,128)} %get-tuple-element.87), channel_id=1, source_target_pairs={{0,8},{8,16},{16,24},{24,0},{1,9},{9,17},{17,25},{25,1},{2,10},{10... | collective-permute-start | bytes 786440 | tf_op jit(solution)/shard_map/ppermute | solution.py:34
  171.5 11.6 %collective-permute-start.19 = (f32[256,256]{1,0:T(8,128)}, f32[256,256]{1,0:T(8,128)S(1)}, u32[]{:S(2)}, u32[]{:S(2)}) collective-permute-start(f32[256,256]{1,0:T(8,128)} %get-tuple-element.88), channel_id=1, source_target_pairs={{0,24},{8,0},{16,8},{24,16},{1,25},{9,1},{17,9},{25,17},{2,26},{10... | collective-permute-start | bytes 786440 | tf_op jit(solution)/shard_map/ppermute | solution.py:34
  172.8 13.5 %collective-permute-start.20 = (f32[256,256]{1,0:T(8,128)}, f32[256,256]{1,0:T(8,128)S(1)}, u32[]{:S(2)}, u32[]{:S(2)}) collective-permute-start(f32[256,256]{1,0:T(8,128)} %copy-done.5), channel_id=1, source_target_pairs={{0,16},{8,24},{16,0},{24,8},{1,17},{9,25},{17,1},{25,9},{2,18},{10... | collective-permute-start | bytes 786440 | tf_op jit(solution)/shard_map/ppermute | solution.py:34
  179.0 14.0 %all-to-all-start.6 = ((f32[32,8,128]{2,1,0:T(8,128)}), f32[32,8,128]{2,1,0:T(8,128)S(1)}, u32[]{:S(2)}, u32[]{:S(2)}) async-start(f32[32,8,128]{2,1,0:T(8,128)} %get-tuple-element.85), calls=%async_computation.6 | async-start | bytes 262144 | tf_op jit(solution)/shard_map/all_to_all | solution.py:397
  203.5 7.6 %collective-permute-start.24 = (bf16[256,512]{1,0:T(8,128)(2,1)S(1)}, bf16[256,512]{1,0:T(8,128)(2,1)S(1)}, u32[]{:S(2)}, u32[]{:S(2)}) collective-permute-start(bf16[256,512]{1,0:T(8,128)(2,1)S(1)} %get-tuple-element.100), channel_id=1, source_target_pairs={{0,6},{2,0},{4,2},{6,4},{1,7},{3,1},{5,3},{7,5},{8,14},{10,8},{12,... | collective-permute-start | bytes 786440 | tf_op jit(solution)/shard_map/ppermute | solution.py:34
  204.5 14.0 %collective-permute-start.23 = (bf16[256,512]{1,0:T(8,128)(2,1)S(1)}, bf16[256,512]{1,0:T(8,128)(2,1)S(1)}, u32[]{:S(2)}, u32[]{:S(2)}) collective-permute-start(bf16[256,512]{1,0:T(8,128)(2,1)S(1)} %get-tuple-element.99), channel_id=1, source_target_pairs={{0,2},{2,4},{4,6},{6,0},{1,3},{3,5},{5,7},{7,1},{8,10},{10,12},{12... | collective-permute-start | bytes 786440 | tf_op jit(solution)/shard_map/ppermute | solution.py:34
  205.0 13.5 %collective-permute-start.22 = (bf16[256,512]{1,0:T(8,128)(2,1)S(1)}, bf16[256,512]{1,0:T(8,128)(2,1)S(1)}, u32[]{:S(2)}, u32[]{:S(2)}) collective-permute-start(bf16[256,512]{1,0:T(8,128)(2,1)S(1)} %get-tuple-element.98), channel_id=1, source_target_pairs={{0,4},{2,6},{4,0},{6,2},{1,5},{3,7},{5,1},{7,3},{8,12},{10,14},{12... | collective-permute-start | bytes 786440 | tf_op jit(solution)/shard_map/ppermute | solution.py:34
  (13 other events, 138.3 us)
Sparse Core Ops, SparseCore 0:
  17.8 45.0 all-gather.4
  68.0 90.5 all-gather.6

commit v10 on v9

--- a/solution.py
+++ b/solution.py
@@ -124,13 +124,11 @@
     )(*parts)
 
 
-def pick_kernel(place, all_ref, far_ref, side_ref, near_ref, sems):
+def pick_kernel(place, all_ref, far_ref, near_ref, sems):
     copies = []
     for y in range(Y):
-        own = all_ref.at[y, place[3]]
-        copies.append(pltpu.make_async_copy(own, near_ref.at[y], sems.at[0, y]))
-        copies.append(pltpu.make_async_copy(own.at[:, : X - 1], far_ref.at[y], sems.at[1, y]))
-        copies.append(pltpu.make_async_copy(own.at[:, X - 1], side_ref.at[y], sems.at[2, y]))
+        for n, ref in enumerate((near_ref, far_ref)):
+            copies.append(pltpu.make_async_copy(all_ref.at[y, place[3]], ref.at[y], sems.at[n, y]))
     for copy in copies:
         copy.start()
     for copy in copies:
@@ -138,16 +136,13 @@
 
 
 def pick(place, samples):
+    half = jax.ShapeDtypeStruct((Y, C, X, QUARTER, SLICE), BF16)
     return pl.pallas_call(
         pick_kernel,
-        out_shape=(
-            jax.ShapeDtypeStruct((Y, C, X - 1, QUARTER, SLICE), BF16),
-            jax.ShapeDtypeStruct((Y, C, QUARTER, SLICE), BF16),
-            jax.ShapeDtypeStruct((Y, C, X, QUARTER, SLICE), BF16),
-        ),
+        out_shape=(half, half),
         in_specs=[SMEM, pl.BlockSpec(memory_space=pl.ANY)],
-        out_specs=(pl.BlockSpec(memory_space=pl.ANY), pl.BlockSpec(memory_space=pl.ANY), VMEM),
-        scratch_shapes=[pltpu.SemaphoreType.DMA((3, Y))],
+        out_specs=(pl.BlockSpec(memory_space=pl.ANY), VMEM),
+        scratch_shapes=[pltpu.SemaphoreType.DMA((2, Y))],
         compiler_params=params(16),
         name="pick",
     )(place, samples)
@@ -337,36 +332,41 @@
     )(place, parts, f, *blocks)
 
 
-def transport_kernel(pieces, place, w_ref, got_ref, *refs):
-    side_refs, data_ref, out_refs = refs[:X], refs[X], refs[X + 1 :]
+def transport_kernel(pieces, place, w_ref, got_ref, data_ref, *refs):
+    out_refs, (buffer_ref, sems) = refs[:-2], refs[-2:]
+    copies = []
+    for i, s in enumerate(pieces):
+        for j, rel in enumerate(AROUND):
+            for k in range(C):
+                block = data_ref.at[at(place, 1, rel, X), at(place, 2, s, Y), at(place, 3, k, C)]
+                copies.append(pltpu.make_async_copy(block, buffer_ref.at[i, k, j], sems.at[i, k, j]))
+    for copy in copies:
+        copy.start()
     lhs = jnp.concatenate([w_ref[...], got_ref[...]], axis=1)
-    for s, out_ref in zip(pieces, out_refs):
-        y = at(place, 2, s, Y)
-        rhs = []
-        for core in (place[3], 1 - place[3]):
-            for rel, side_ref in zip(AROUND, side_refs):
-                n = at(place, 1, rel, X)
-                rhs.append(jnp.concatenate([data_ref[n, y, core, k] for k in range(X - 1)] + [side_ref[y, core]], axis=1))
+    for i, out_ref in enumerate(out_refs):
+        for copy in copies[i * X * C : (i + 1) * X * C]:
+            copy.wait()
+        rhs = [jnp.concatenate([buffer_ref[i, k, j, n] for n in range(X)], axis=1) for k in range(C) for j in range(X)]
         total = jnp.dot(lhs, jnp.concatenate(rhs, axis=0), preferred_element_type=F32)
         out_ref[...] = total.astype(out_ref.dtype)
 
 
-def transport(place, w, got, sides, data, pieces, hand_on):
-    kinds = [jax.ShapeDtypeStruct((ROWS, SHARE), BF16 if s else F32) for s in pieces]
-    if hand_on:
-        kinds.append(jax.ShapeDtypeStruct(data.shape, data.dtype))
+def transport(place, w, got, data, pieces):
     return pl.pallas_call(
         functools.partial(transport_kernel, pieces),
-        out_shape=kinds,
-        in_specs=[SMEM] + [VMEM] * (3 + X),
-        out_specs=[VMEM] * len(kinds),
-        input_output_aliases={3 + X: len(pieces)} if hand_on else {},
-        compiler_params=params(24),
+        out_shape=[jax.ShapeDtypeStruct((ROWS, SHARE), BF16 if s else F32) for s in pieces],
+        in_specs=[SMEM] + [VMEM] * 2 + [pl.BlockSpec(memory_space=pl.ANY)],
+        out_specs=[VMEM] * len(pieces),
+        scratch_shapes=[
+            pltpu.VMEM((len(pieces), C, X, X, QUARTER, SLICE), BF16),
+            pltpu.SemaphoreType.DMA((len(pieces), C, X)),
+        ],
+        compiler_params=params(53),
         cost_estimate=pl.CostEstimate(
             flops=2 * ROWS * COUNT * C * SHARE * len(pieces), bytes_accessed=2 * 2**20 * len(pieces), transcendentals=0
         ),
         name="transport",
-    )(place, w, got, *sides, data)
+    )(place, w, got, data)
 
 
 def body(noise, data):
@@ -376,16 +376,13 @@
     noise_after, swapped = lax.optimization_barrier((noise, swapped))
     samples = lax.all_gather(swapped, ("z", "core")).reshape(Y, C, C, X, QUARTER, SLICE)
     samples, noise_all, sqn_mine = lax.optimization_barrier((samples, *collect(gather_noise(noise_after))))
-    far, side, near = pick(place, samples)
+    far, near = pick(place, samples)
     data_all = lax.all_gather(far, "x")
-    sides = around(side, "x")
     got = shift(theirs(place, near, noise_all, sqn_mine), "core", 1)
     mine, sq_mine = ours(place, near, noise_all)
     q, rows, sq, sq_noise, *blocks = score(place, mine, sq_mine, sqn_mine, got)
     blocks = [blocks[0]] + [shift(block, "x", by) for block, by in zip(blocks[1:], (1, -1, 2))]
     for step in range(ITERS):
-        if step == 1:
-            columns, sides = lax.optimization_barrier((columns, sides))
         if step:
             rows = noise_lse(q, columns)
         parts = lax.all_to_all(rows, ("x", "y", "core"), 0, 0)
@@ -393,12 +390,12 @@
             columns, f = data_lse(q, parts)
             columns = lax.all_to_all(columns, "z", 0, 0)
     columns, f = last_lse(q, parts, sq)
-    data_all, columns = lax.optimization_barrier((data_all, columns))
     columns = lax.all_to_all(columns, ("z", "x"), 0, 0)
     w, pot_g = weigh(place, columns, f, blocks)
     got = shift(w, "core", 1)
-    *parts, data_all = transport(place, w, got, sides, data_all, (2, 1, 3), True)
-    (target,) = transport(place, w, got, sides, data_all, (0,), False)
+    data_all, pot_g = lax.optimization_barrier((data_all, pot_g))
+    parts = [part for pieces in ((2,), (1, 3)) for part in transport(place, w, got, data_all, pieces)]
+    (target,) = transport(place, w, got, data_all, (0,))
     for by, part in zip((2, 1, 3), parts):
         target = target + shift(part, "y", by).astype(F32)
     velocity = (target - noise.astype(F32)).astype(BF16)

time: 227 us -> 204 us (0.90)
  blocking collectives: 72.7 us -> 61.8 us
  starting transfers between devices: 54.2 us -> 45 us
  waiting for transfers between devices: 49.8 us -> 43.8 us
  Pallas kernels: 19.5 us -> 24.2 us
    all_to_all x2, blocking collectives: 53 us -> 28.7 us  [body(): parts = lax.all_to_all(rows, ('x', 'y', 'core'), 0, 0)]
    all_to_all x1 -> x2, blocking collectives: 9.23 us -> 22.6 us  [body(): columns = lax.all_to_all(columns, 'z', 0, 0)]
    all_to_all x1 -> x0, starting transfers between devices: 7.43 us -> none  [body(): columns = lax.all_to_all(columns, 'z', 0, 0)]
    all_to_all x1 -> x0, waiting for transfers between devices: 6.85 us -> none  [body(): columns = lax.all_to_all(columns, 'z', 0, 0)]
    all_to_all x1, waiting for transfers between devices: 6.59 us -> 0.35 us  [body(): columns = lax.all_to_all(columns, ('z', 'x'), 0, 0)]
    pallas_call x3 -> x4, Pallas kernels: 6.53 us -> 12.1 us  [the longest x3 11.2 us: transport(): pl.pallas_call(functools.partial(transport_kernel, pieces), out_shape=[ja...]
    ppermute x25 -> x22, waiting for transfers between devices: 28.6 us -> 31.6 us  [shift(): return lax.ppermute(x, axis, [(j, (j + by) % n) for j in range(n)])]
    all_gather x1, waiting for transfers between devices: 0.01 us -> 2.41 us  [body(): data_all = lax.all_gather(far, 'x')]
  transfers between devices with their start and end apart: 30 -> 26, of which waited for: 14 -> 15; matrix products, arithmetic and copies ran while one was open for 2% -> 2% of each run, Pallas kernels for 6% -> 10%
where the time goes in v10:
time: 204 us; the launch traced here: 203 us
  blocking collectives  61.8 us (30%)
  starting transfers between devices  45 us (22%)
  waiting for transfers between devices  43.8 us (21%)
  Pallas kernels  24.2 us (12%)
  between operations  14.2 us (7%)
  local copies, waits for them, and re-layouts  12.4 us (6%)
    ppermute x22, starting transfers between devices, shift(): return lax.ppermute(x, axis, [(j, (j + by) % n) for j in range(n)])  36.4 us
    ppermute x22, waiting for transfers between devices, shift(): return lax.ppermute(x, axis, [(j, (j + by) % n) for j in range(n)])  31.6 us
    all_to_all x2, blocking collectives, body(): parts = lax.all_to_all(rows, ('x', 'y', 'core'), 0, 0)  28.7 us
    all_to_all x2, blocking collectives, body(): columns = lax.all_to_all(columns, 'z', 0, 0)  22.6 us
    pallas_call x3, Pallas kernels, transport(): pl.pallas_call(functools.partial(transport_kernel, pieces), out_shape=[ja...  11.2 us
    all_to_all x1, blocking collectives, body(): swapped = lax.all_to_all(data.reshape(X, QUARTER, SLICE), 'x', 0, 0)  10.5 us
    unnamed x14, local copies, waits for them, and re-layouts  8.54 us
    all_to_all x1, waiting for transfers between devices, body(): parts = lax.all_to_all(rows, ('x', 'y', 'core'), 0, 0)  4.89 us
  transfers between devices with their start and end apart: 26, of which 15 were waited for; matrix products, arithmetic and copies ran while one was open for 2% of the time, Pallas kernels for 10%

profile of v10, /device:TPU:1, one launch (start us, length us, event | category | flops | bytes accessed | tf_op | source)
XLA Modules:
  0.0 203.1 jit_solution(1426444740213544080)
XLA Ops:
  7.2 10.5 %all_to_all.35 = bf16[4,256,128]{2,1,0:T(8,128)(2,1)} all-to-all(bf16[4,256,128]{2,1,0:T(8,128)(2,1)} %bitcast.31), channel_id=1, replica_groups=mesh['z'=8,'x'=4,'y'=4,'core'=2] {'x'}, dimensions={0} | all-to-all | bytes 524288 | tf_op jit(solution)/shard_map/all_to_all | solution.py:375
  19.1 2.4 %collective-permute-start.1 = (bf16[128,512]{1,0:T(8,128)(2,1)S(1)}, bf16[128,512]{1,0:T(8,128)(2,1)S(1)}, u32[]{:S(2)}, u32[]{:S(2)}) collective-permute-start(bf16[128,512]{1,0:T(8,128)(2,1)S(1)} %get-tuple-element.46), channel_id=1, source_target_pairs={{0,24},{8,0},{16,8},{24,16},{1,25},{9,1},{17,9},{25,17},{2,26},{10... | collective-permute-start | bytes 393224 | tf_op jit(solution)/shard_map/ppermute | solution.py:34
  24.3 2.5 %collective-permute-start.5 = (bf16[128,512]{1,0:T(8,128)(2,1)S(1)}, bf16[128,512]{1,0:T(8,128)(2,1)S(1)}, u32[]{:S(2)}, u32[]{:S(2)}) collective-permute-start(bf16[128,512]{1,0:T(8,128)(2,1)S(1)} %get-tuple-element.50), channel_id=1, source_target_pairs={{0,4},{2,6},{4,0},{6,2},{1,5},{3,7},{5,1},{7,3},{8,12},{10,14},{12... | collective-permute-start | bytes 393224 | tf_op jit(solution)/shard_map/ppermute | solution.py:34
  36.1 3.0 %collective-permute-done.8.refs_6_ = bf16[4,128,512]{2,1,0:T(8,128)(2,1)S(1)} collective-permute-done((bf16[4,128,512]{2,1,0:T(8,128)(2,1)S(1)}, bf16[4,128,512]{2,1,0:T(8,128)(2,1)S(1)}, u32[]{:S(2)}, u32[]{:S(2)}) %collective-permute-start.8) | collective-permute-done | bytes 524320 | tf_op jit(solution)/shard_map/ppermute | solution.py:34
  39.4 3.5 %collective-permute-done.6.refs_1_ = bf16[4,128,512]{2,1,0:T(8,128)(2,1)S(1)} collective-permute-done((bf16[4,128,512]{2,1,0:T(8,128)(2,1)S(1)}, bf16[4,128,512]{2,1,0:T(8,128)(2,1)S(1)}, u32[]{:S(2)}, u32[]{:S(2)}) %collective-permute-start.6) | collective-permute-done | bytes 524320 | tf_op jit(solution)/shard_map/ppermute | solution.py:34
  48.5 2.7 %collective-permute-start.13 = (bf16[2,128,512]{2,1,0:T(8,128)(2,1)}, bf16[2,128,512]{2,1,0:T(8,128)(2,1)}, u32[]{:S(2)}, u32[]{:S(2)}) collective-permute-start(bf16[2,128,512]{2,1,0:T(8,128)(2,1)} %slice.23), channel_id=1, source_target_pairs={{0,24},{8,0},{16,8},{24,16},{1,25},{9,1},{17,9},{25,17},{2,26},{10... | collective-permute-start | bytes 786440 | tf_op jit(solution)/shard_map/ppermute | solution.py:34
  52.2 2.6 %collective-permute-done.12.refs_8_ = bf16[2,128,512]{2,1,0:T(8,128)(2,1)} collective-permute-done((bf16[2,128,512]{2,1,0:T(8,128)(2,1)}, bf16[2,128,512]{2,1,0:T(8,128)(2,1)}, u32[]{:S(2)}, u32[]{:S(2)}) %collective-permute-start.12) | collective-permute-done | bytes 262176 | tf_op jit(solution)/shard_map/ppermute | solution.py:34
  58.5 4.5 %all-gather.5.cloned.1.call-done = bf16[64,256,128]{2,1,0:T(8,128)(2,1)} async-done(((bf16[4,256,128]{2,1,0:T(8,128)(2,1)}), bf16[64,256,128]{2,1,0:T(8,128)(2,1)}) %all-gather.5.cloned.1.call-update) | async-done | bytes 4194320 | tf_op jit(solution)/shard_map/all_gather | solution.py:377
  71.5 5.5 %collective-permute-start.14 = (f32[264,1152]{1,0:T(8,128)S(1)}, f32[264,1152]{1,0:T(8,128)S(1)}, u32[]{:S(2)}, u32[]{:S(2)}) collective-permute-start(f32[264,1152]{1,0:T(8,128)S(1)} %theirs.1), channel_id=1, source_target_pairs={{0,1},{1,0},{2,3},{3,2},{4,5},{5,4},{6,7},{7,6},{8,9},{9,8},{10,11... | collective-permute-start | bytes 3649544 | tf_op jit(solution)/shard_map/ppermute | solution.py:34
  80.6 15.2 %all_to_all.36.part_ref = f32[32,8,128]{2,1,0:T(8,128)S(1)} all-to-all(f32[32,8,128]{2,1,0:T(8,128)S(1)} %get-tuple-element.67), channel_id=1, replica_groups=mesh['z'=8,'x'=4,'y'=4,'core'=2] {'x','y','core'}, dimensions={0} | all-to-all | bytes 262144 | tf_op jit(solution)/shard_map/all_to_all | solution.py:388
  96.7 13.4 %all_to_all.37.part_ref = f32[8,8,128]{2,1,0:T(8,128)S(1)} all-to-all(f32[8,8,128]{2,1,0:T(8,128)S(1)} %get-tuple-element.68), channel_id=1, replica_groups=mesh['z'=8,'x'=4,'y'=4,'core'=2] {'z'}, dimensions={0} | all-to-all | bytes 65536 | tf_op jit(solution)/shard_map/all_to_all | solution.py:391
  110.4 13.4 %all_to_all.38.part_ref = f32[32,8,128]{2,1,0:T(8,128)S(1)} all-to-all(f32[32,8,128]{2,1,0:T(8,128)S(1)} %noise_lse.2), channel_id=1, replica_groups=mesh['z'=8,'x'=4,'y'=4,'core'=2] {'x','y','core'}, dimensions={0} | all-to-all | bytes 262144 | tf_op jit(solution)/shard_map/all_to_all | solution.py:388
  124.7 9.2 %all_to_all.39.part_ref = f32[8,8,128]{2,1,0:T(8,128)S(1)} all-to-all(f32[8,8,128]{2,1,0:T(8,128)S(1)} %get-tuple-element.69), channel_id=1, replica_groups=mesh['z'=8,'x'=4,'y'=4,'core'=2] {'z'}, dimensions={0} | all-to-all | bytes 65536 | tf_op jit(solution)/shard_map/all_to_all | solution.py:391
  135.0 4.7 %all-to-all-start.5 = ((f32[32,8,128]{2,1,0:T(8,128)}), f32[32,8,128]{2,1,0:T(8,128)S(1)}, u32[]{:S(2)}, u32[]{:S(2)}) async-start(f32[32,8,128]{2,1,0:T(8,128)} %noise_lse.3), calls=%async_computation.5 | async-start | bytes 262144 | tf_op jit(solution)/shard_map/all_to_all | solution.py:388
  144.1 4.9 %all-to-all-done.5.part_ref = f32[32,8,128]{2,1,0:T(8,128)S(1)} async-done(((f32[32,8,128]{2,1,0:T(8,128)}), f32[32,8,128]{2,1,0:T(8,128)S(1)}, u32[]{:S(2)}, u32[]{:S(2)}) %all-to-all-start.5) | async-done | bytes 131104 | tf_op jit(solution)/shard_map/all_to_all | solution.py:388
  150.1 3.9 %all-to-all-start.6 = ((f32[32,8,128]{2,1,0:T(8,128)}), f32[32,8,128]{2,1,0:T(8,128)S(1)}, u32[]{:S(2)}, u32[]{:S(2)}) async-start(f32[32,8,128]{2,1,0:T(8,128)} %get-tuple-element.74), calls=%async_computation.6 | async-start | bytes 262144 | tf_op jit(solution)/shard_map/all_to_all | solution.py:393
  153.9 3.0 %collective-permute-done.15.refs_1_ = f32[256,256]{1,0:T(8,128)S(1)} collective-permute-done((f32[256,256]{1,0:T(8,128)S(1)}, f32[256,256]{1,0:T(8,128)S(1)}, u32[]{:S(2)}, u32[]{:S(2)}) %collective-permute-start.15) | collective-permute-done | bytes 262176 | tf_op jit(solution)/shard_map/ppermute | solution.py:34
  157.0 13.3 %collective-permute-done.17.refs_3_ = f32[256,256]{1,0:T(8,128)S(1)} collective-permute-done((f32[256,256]{1,0:T(8,128)S(1)}, f32[256,256]{1,0:T(8,128)S(1)}, u32[]{:S(2)}, u32[]{:S(2)}) %collective-permute-start.17) | collective-permute-done | bytes 262176 | tf_op jit(solution)/shard_map/ppermute | solution.py:34
  173.1 2.4 %all-gather.7.cloned.1.call-done = bf16[16,2,4,256,128]{4,3,2,1,0:T(8,128)(2,1)} async-done(((bf16[4,2,4,256,128]{4,3,2,1,0:T(8,128)(2,1)}), bf16[16,2,4,256,128]{4,3,2,1,0:T(8,128)(2,1)}) %all-gather.7.cloned.1.call-update) | async-done | bytes 8388624 | tf_op jit(solution)/shard_map/all_gather | solution.py:380
  176.3 3.3 %transport.4 = bf16[256,512]{1,0:T(8,128)(2,1)S(1)} custom-call(s32[4]{0:T(128)S(1)} %pad_add_fusion.place, bf16[256,1024]{1,0:T(8,128)(2,1)S(1)} %get-tuple-element.81.w_ref, bf16[256,1024]{1,0:T(8,128)(2,1)} %copy-done.5, bf16[4,4,2,4,256,128]{5,4,3,2,1,0:T(8,128)(2,1)} %bitcast.26), custom_call_target="tpu_custom_call" | custom-call | flops 536870912 | bytes 2097152 | tf_op jit(solution)/shard_map/transport/pallas_call | solution.py:355
  179.7 3.0 %collective-permute-start.19 = (bf16[256,512]{1,0:T(8,128)(2,1)S(1)}, bf16[256,512]{1,0:T(8,128)(2,1)S(1)}, u32[]{:S(2)}, u32[]{:S(2)}) collective-permute-start(bf16[256,512]{1,0:T(8,128)(2,1)S(1)} %transport.4), channel_id=1, source_target_pairs={{0,4},{2,6},{4,0},{6,2},{1,5},{3,7},{5,1},{7,3},{8,12},{10,14},{12... | collective-permute-start | bytes 786440 | tf_op jit(solution)/shard_map/ppermute | solution.py:34
  182.7 4.3 %transport.5 = (bf16[256,512]{1,0:T(8,128)(2,1)S(1)}, bf16[256,512]{1,0:T(8,128)(2,1)S(1)}) custom-call(s32[4]{0:T(128)S(1)} %pad_add_fusion.place, bf16[256,1024]{1,0:T(8,128)(2,1)} %copy-done.2, bf16[256,1024]{1,0:T(8,128)(2,1)} %copy-done.5, bf16[4,4,2,4,256,128]{5,4,3,2,1,0:T(8,128)(2,1)} %bitcast.27), custom_call_target="tpu_custom_call" | custom-call | flops 1073741824 | bytes 4194304 | tf_op jit(solution)/shard_map/transport/pallas_call | solution.py:355
  187.4 2.4 %collective-permute-start.21 = (bf16[256,512]{1,0:T(8,128)(2,1)S(1)}, bf16[256,512]{1,0:T(8,128)(2,1)S(1)}, u32[]{:S(2)}, u32[]{:S(2)}) collective-permute-start(bf16[256,512]{1,0:T(8,128)(2,1)S(1)} %get-tuple-element.84), channel_id=1, source_target_pairs={{0,6},{2,0},{4,2},{6,4},{1,7},{3,1},{5,3},{7,5},{8,14},{10,8},{12,... | collective-permute-start | bytes 786440 | tf_op jit(solution)/shard_map/ppermute | solution.py:34
  190.3 3.5 %transport.3 = f32[256,512]{1,0:T(8,128)S(1)} custom-call(s32[4]{0:T(128)S(1)} %pad_add_fusion.place, bf16[256,1024]{1,0:T(8,128)(2,1)} %copy-done.2, bf16[256,1024]{1,0:T(8,128)(2,1)} %copy-done.5, bf16[4,4,2,4,256,128]{5,4,3,2,1,0:T(8,128)(2,1)} %bitcast.28), custom_call_target="tpu_custom_call" | custom-call | flops 536870912 | bytes 2097152 | tf_op jit(solution)/shard_map/transport/pallas_call | solution.py:355
  (74 shorter events, 51.7 us)
Async XLA Ops:
  7.2 55.8 %all-gather.5.cloned.1.call-start = ((), (), s32[]{:S(2)}) async-start(), calls=%async_computation.7 | async-start | bytes 4456448 | tf_op jit(solution)/shard_map/all_gather | solution.py:377
  17.7 157.8 %all-gather.7.cloned.1.call-start = ((), (), s32[]{:S(2)}) async-start(), calls=%async_computation.8 | async-start | bytes 10485760 | tf_op jit(solution)/shard_map/all_gather | solution.py:380
  18.8 5.5 %collective-permute-start = (bf16[128,512]{1,0:T(8,128)(2,1)S(1)}, bf16[128,512]{1,0:T(8,128)(2,1)S(1)}, u32[]{:S(2)}, u32[]{:S(2)}) collective-permute-start(bf16[128,512]{1,0:T(8,128)(2,1)S(1)} %get-tuple-element.46), channel_id=1, source_target_pairs={{0,8},{8,16},{16,24},{24,0},{1,9},{9,17},{17,25},{25,1},{2,10},{10... | collective-permute-start | bytes 393224 | tf_op jit(solution)/shard_map/ppermute | solution.py:34
  19.1 7.7 %collective-permute-start.1 = (bf16[128,512]{1,0:T(8,128)(2,1)S(1)}, bf16[128,512]{1,0:T(8,128)(2,1)S(1)}, u32[]{:S(2)}, u32[]{:S(2)}) collective-permute-start(bf16[128,512]{1,0:T(8,128)(2,1)S(1)} %get-tuple-element.46), channel_id=1, source_target_pairs={{0,24},{8,0},{16,8},{24,16},{1,25},{9,1},{17,9},{25,17},{2,26},{10... | collective-permute-start | bytes 393224 | tf_op jit(solution)/shard_map/ppermute | solution.py:34
  21.5 6.4 %collective-permute-start.2 = (bf16[128,512]{1,0:T(8,128)(2,1)S(1)}, bf16[128,512]{1,0:T(8,128)(2,1)S(1)}, u32[]{:S(2)}, u32[]{:S(2)}) collective-permute-start(bf16[128,512]{1,0:T(8,128)(2,1)S(1)} %get-tuple-element.46), channel_id=1, source_target_pairs={{0,16},{8,24},{16,0},{24,8},{1,17},{9,25},{17,1},{25,9},{2,18},{10... | collective-permute-start | bytes 393224 | tf_op jit(solution)/shard_map/ppermute | solution.py:34
  21.5 6.4 %collective-permute-start.3 = (bf16[128,512]{1,0:T(8,128)(2,1)S(1)}, bf16[128,512]{1,0:T(8,128)(2,1)S(1)}, u32[]{:S(2)}, u32[]{:S(2)}) collective-permute-start(bf16[128,512]{1,0:T(8,128)(2,1)S(1)} %get-tuple-element.50), channel_id=1, source_target_pairs={{0,2},{2,4},{4,6},{6,0},{1,3},{3,5},{5,7},{7,1},{8,10},{10,12},{12... | collective-permute-start | bytes 393224 | tf_op jit(solution)/shard_map/ppermute | solution.py:34
  24.3 5.4 %collective-permute-start.5 = (bf16[128,512]{1,0:T(8,128)(2,1)S(1)}, bf16[128,512]{1,0:T(8,128)(2,1)S(1)}, u32[]{:S(2)}, u32[]{:S(2)}) collective-permute-start(bf16[128,512]{1,0:T(8,128)(2,1)S(1)} %get-tuple-element.50), channel_id=1, source_target_pairs={{0,4},{2,6},{4,0},{6,2},{1,5},{3,7},{5,1},{7,3},{8,12},{10,14},{12... | collective-permute-start | bytes 393224 | tf_op jit(solution)/shard_map/ppermute | solution.py:34
  29.7 9.3 %collective-permute-start.8 = (bf16[4,128,512]{2,1,0:T(8,128)(2,1)S(1)}, bf16[4,128,512]{2,1,0:T(8,128)(2,1)S(1)}, u32[]{:S(2)}, u32[]{:S(2)}) collective-permute-start(bf16[4,128,512]{2,1,0:T(8,128)(2,1)S(1)} %pad_maximum_fusion.1.refs_5_), channel_id=1, source_target_pairs={{0,8},{8,16},{16,24},{24,0},{1,9},{9,17},{17,25},{25,1},{2,10},{10... | collective-permute-start | bytes 1572872 | tf_op jit(solution)/shard_map/ppermute | solution.py:34
  30.4 9.0 %collective-permute-start.9 = (bf16[4,128,512]{2,1,0:T(8,128)(2,1)S(1)}, bf16[4,128,512]{2,1,0:T(8,128)(2,1)S(1)}, u32[]{:S(2)}, u32[]{:S(2)}) collective-permute-start(bf16[4,128,512]{2,1,0:T(8,128)(2,1)S(1)} %pad_maximum_fusion.1.refs_5_), channel_id=1, source_target_pairs={{0,24},{8,0},{16,8},{24,16},{1,25},{9,1},{17,9},{25,17},{2,26},{10... | collective-permute-start | bytes 1572872 | tf_op jit(solution)/shard_map/ppermute | solution.py:34
  32.6 10.3 %collective-permute-start.6 = (bf16[4,128,512]{2,1,0:T(8,128)(2,1)S(1)}, bf16[4,128,512]{2,1,0:T(8,128)(2,1)S(1)}, u32[]{:S(2)}, u32[]{:S(2)}) collective-permute-start(bf16[4,128,512]{2,1,0:T(8,128)(2,1)S(1)} %pad_maximum_fusion.refs_0_), channel_id=1, source_target_pairs={{0,2},{2,4},{4,6},{6,0},{1,3},{3,5},{5,7},{7,1},{8,10},{10,12},{12... | collective-permute-start | bytes 1572872 | tf_op jit(solution)/shard_map/ppermute | solution.py:34
  33.8 9.1 %collective-permute-start.7 = (bf16[4,128,512]{2,1,0:T(8,128)(2,1)S(1)}, bf16[4,128,512]{2,1,0:T(8,128)(2,1)S(1)}, u32[]{:S(2)}, u32[]{:S(2)}) collective-permute-start(bf16[4,128,512]{2,1,0:T(8,128)(2,1)S(1)} %pad_maximum_fusion.refs_0_), channel_id=1, source_target_pairs={{0,6},{2,0},{4,2},{6,4},{1,7},{3,1},{5,3},{7,5},{8,14},{10,8},{12,... | collective-permute-start | bytes 1572872 | tf_op jit(solution)/shard_map/ppermute | solution.py:34
  43.6 8.6 %collective-permute-start.10 = (bf16[2,128,512]{2,1,0:T(8,128)(2,1)}, bf16[2,128,512]{2,1,0:T(8,128)(2,1)S(1)}, u32[]{:S(2)}, u32[]{:S(2)}) collective-permute-start(bf16[2,128,512]{2,1,0:T(8,128)(2,1)} %slice.20), channel_id=1, source_target_pairs={{0,2},{2,4},{4,6},{6,0},{1,3},{3,5},{5,7},{7,1},{8,10},{10,12},{12... | collective-permute-start | bytes 786440 | tf_op jit(solution)/shard_map/ppermute | solution.py:34
  45.4 6.8 %collective-permute-start.11 = (bf16[2,128,512]{2,1,0:T(8,128)(2,1)}, bf16[2,128,512]{2,1,0:T(8,128)(2,1)}, u32[]{:S(2)}, u32[]{:S(2)}) collective-permute-start(bf16[2,128,512]{2,1,0:T(8,128)(2,1)} %slice.21), channel_id=1, source_target_pairs={{0,6},{2,0},{4,2},{6,4},{1,7},{3,1},{5,3},{7,5},{8,14},{10,8},{12,... | collective-permute-start | bytes 786440 | tf_op jit(solution)/shard_map/ppermute | solution.py:34
  47.8 7.0 %collective-permute-start.12 = (bf16[2,128,512]{2,1,0:T(8,128)(2,1)}, bf16[2,128,512]{2,1,0:T(8,128)(2,1)}, u32[]{:S(2)}, u32[]{:S(2)}) collective-permute-start(bf16[2,128,512]{2,1,0:T(8,128)(2,1)} %slice.22), channel_id=1, source_target_pairs={{0,8},{8,16},{16,24},{24,0},{1,9},{9,17},{17,25},{25,1},{2,10},{10... | collective-permute-start | bytes 786440 | tf_op jit(solution)/shard_map/ppermute | solution.py:34
  48.5 6.3 %collective-permute-start.13 = (bf16[2,128,512]{2,1,0:T(8,128)(2,1)}, bf16[2,128,512]{2,1,0:T(8,128)(2,1)}, u32[]{:S(2)}, u32[]{:S(2)}) collective-permute-start(bf16[2,128,512]{2,1,0:T(8,128)(2,1)} %slice.23), channel_id=1, source_target_pairs={{0,24},{8,0},{16,8},{24,16},{1,25},{9,1},{17,9},{25,17},{2,26},{10... | collective-permute-start | bytes 786440 | tf_op jit(solution)/shard_map/ppermute | solution.py:34
  71.5 8.0 %collective-permute-start.14 = (f32[264,1152]{1,0:T(8,128)S(1)}, f32[264,1152]{1,0:T(8,128)S(1)}, u32[]{:S(2)}, u32[]{:S(2)}) collective-permute-start(f32[264,1152]{1,0:T(8,128)S(1)} %theirs.1), channel_id=1, source_target_pairs={{0,1},{1,0},{2,3},{3,2},{4,5},{5,4},{6,7},{7,6},{8,9},{9,8},{10,11... | collective-permute-start | bytes 3649544 | tf_op jit(solution)/shard_map/ppermute | solution.py:34
  135.0 14.1 %all-to-all-start.5 = ((f32[32,8,128]{2,1,0:T(8,128)}), f32[32,8,128]{2,1,0:T(8,128)S(1)}, u32[]{:S(2)}, u32[]{:S(2)}) async-start(f32[32,8,128]{2,1,0:T(8,128)} %noise_lse.3), calls=%async_computation.5 | async-start | bytes 262144 | tf_op jit(solution)/shard_map/all_to_all | solution.py:388
  139.7 17.3 %collective-permute-start.15 = (f32[256,256]{1,0:T(8,128)S(1)}, f32[256,256]{1,0:T(8,128)S(1)}, u32[]{:S(2)}, u32[]{:S(2)}) collective-permute-start(f32[256,256]{1,0:T(8,128)S(1)} %get-tuple-element.76), channel_id=1, source_target_pairs={{0,8},{8,16},{16,24},{24,0},{1,9},{9,17},{17,25},{25,1},{2,10},{10... | collective-permute-start | bytes 786440 | tf_op jit(solution)/shard_map/ppermute | solution.py:34
  141.1 15.8 %collective-permute-start.16 = (f32[256,256]{1,0:T(8,128)S(1)}, f32[256,256]{1,0:T(8,128)S(1)}, u32[]{:S(2)}, u32[]{:S(2)}) collective-permute-start(f32[256,256]{1,0:T(8,128)S(1)} %get-tuple-element.77), channel_id=1, source_target_pairs={{0,24},{8,0},{16,8},{24,16},{1,25},{9,1},{17,9},{25,17},{2,26},{10... | collective-permute-start | bytes 786440 | tf_op jit(solution)/shard_map/ppermute | solution.py:34
  142.5 27.7 %collective-permute-start.17 = (f32[256,256]{1,0:T(8,128)S(1)}, f32[256,256]{1,0:T(8,128)S(1)}, u32[]{:S(2)}, u32[]{:S(2)}) collective-permute-start(f32[256,256]{1,0:T(8,128)S(1)} %get-tuple-element.78), channel_id=1, source_target_pairs={{0,16},{8,24},{16,0},{24,8},{1,17},{9,25},{17,1},{25,9},{2,18},{10... | collective-permute-start | bytes 786440 | tf_op jit(solution)/shard_map/ppermute | solution.py:34
  150.1 20.5 %all-to-all-start.6 = ((f32[32,8,128]{2,1,0:T(8,128)}), f32[32,8,128]{2,1,0:T(8,128)S(1)}, u32[]{:S(2)}, u32[]{:S(2)}) async-start(f32[32,8,128]{2,1,0:T(8,128)} %get-tuple-element.74), calls=%async_computation.6 | async-start | bytes 262144 | tf_op jit(solution)/shard_map/all_to_all | solution.py:393
  179.7 14.2 %collective-permute-start.19 = (bf16[256,512]{1,0:T(8,128)(2,1)S(1)}, bf16[256,512]{1,0:T(8,128)(2,1)S(1)}, u32[]{:S(2)}, u32[]{:S(2)}) collective-permute-start(bf16[256,512]{1,0:T(8,128)(2,1)S(1)} %transport.4), channel_id=1, source_target_pairs={{0,4},{2,6},{4,0},{6,2},{1,5},{3,7},{5,1},{7,3},{8,12},{10,14},{12... | collective-permute-start | bytes 786440 | tf_op jit(solution)/shard_map/ppermute | solution.py:34
  187.0 8.4 %collective-permute-start.20 = (bf16[256,512]{1,0:T(8,128)(2,1)S(1)}, bf16[256,512]{1,0:T(8,128)(2,1)S(1)}, u32[]{:S(2)}, u32[]{:S(2)}) collective-permute-start(bf16[256,512]{1,0:T(8,128)(2,1)S(1)} %get-tuple-element.83), channel_id=1, source_target_pairs={{0,2},{2,4},{4,6},{6,0},{1,3},{3,5},{5,7},{7,1},{8,10},{10,12},{12... | collective-permute-start | bytes 786440 | tf_op jit(solution)/shard_map/ppermute | solution.py:34
  187.4 8.0 %collective-permute-start.21 = (bf16[256,512]{1,0:T(8,128)(2,1)S(1)}, bf16[256,512]{1,0:T(8,128)(2,1)S(1)}, u32[]{:S(2)}, u32[]{:S(2)}) collective-permute-start(bf16[256,512]{1,0:T(8,128)(2,1)S(1)} %get-tuple-element.84), channel_id=1, source_target_pairs={{0,6},{2,0},{4,2},{6,4},{1,7},{3,1},{5,3},{7,5},{8,14},{10,8},{12,... | collective-permute-start | bytes 786440 | tf_op jit(solution)/shard_map/ppermute | solution.py:34
  (9 other events, 29.5 us)
Sparse Core Ops, SparseCore 0:
  17.8 45.0 all-gather.4
  67.5 107.9 all-gather.6

commit v11 on v8

--- a/solution.py
+++ b/solution.py
@@ -86,6 +86,10 @@
     return lax.rem(place[which] + rel + size, size)
 
 
+def from_x(x, n):
+    return lax.rem(x - n + X, X) if not isinstance(x, int) else (x - n) % X
+
+
 def blocks_of(parts):
     first, second = parts[:5], parts[5:]
 
@@ -124,11 +128,8 @@
     )(*parts)
 
 
-def pick_kernel(place, all_ref, far_ref, near_ref, sems):
-    copies = []
-    for y in range(Y):
-        for n, ref in enumerate((near_ref, far_ref)):
-            copies.append(pltpu.make_async_copy(all_ref.at[y, place[3]], ref.at[y], sems.at[n, y]))
+def pick_kernel(place, all_ref, out_ref, sems):
+    copies = [pltpu.make_async_copy(all_ref.at[y, place[3]], out_ref.at[y], sems.at[y]) for y in range(Y)]
     for copy in copies:
         copy.start()
     for copy in copies:
@@ -136,21 +137,36 @@
 
 
 def pick(place, samples):
-    half = jax.ShapeDtypeStruct((Y, C, X, QUARTER, SLICE), BF16)
     return pl.pallas_call(
         pick_kernel,
-        out_shape=(half, half),
+        out_shape=jax.ShapeDtypeStruct((Y, C, X, QUARTER, SLICE), BF16),
         in_specs=[SMEM, pl.BlockSpec(memory_space=pl.ANY)],
-        out_specs=(pl.BlockSpec(memory_space=pl.ANY), VMEM),
-        scratch_shapes=[pltpu.SemaphoreType.DMA((2, Y))],
-        compiler_params=params(16),
+        out_specs=pl.BlockSpec(memory_space=pl.ANY),
+        scratch_shapes=[pltpu.SemaphoreType.DMA((Y,))],
+        compiler_params=params(53),
         name="pick",
     )(place, samples)
 
 
+def deal_kernel(place, data_ref, *out_refs):
+    for by, ref in enumerate(out_refs):
+        ref[...] = data_ref[at(place, 1, by, X)]
+
+
+def deal(place, data):
+    return pl.pallas_call(
+        deal_kernel,
+        out_shape=(jax.ShapeDtypeStruct((QUARTER, SLICE), BF16),) * X,
+        in_specs=[SMEM, VMEM],
+        out_specs=(VMEM,) * X,
+        compiler_params=params(16),
+        name="deal",
+    )(place, data.reshape(X, QUARTER, SLICE))
+
+
 def partial_scores(place, data_ref, core, noise_ref, q_ref, sq_ref):
     pieces = [at(place, 2, rel, Y) for rel in AROUND]
-    lhs = jnp.concatenate([data_ref[p, core, n] for p in pieces for n in range(X)], axis=1)
+    lhs = jnp.concatenate([data_ref[p, core, from_x(place[1], n)] for p in pieces for n in range(X)], axis=1)
     for h in range(2):
         rhs = noise_ref[pl.ds(h * X * CUT, X * CUT), :]
         gram = lax.dot_general(lhs, rhs, (((1,), (1,)), ((), ())), preferred_element_type=F32) * (2.0 * UNIT)
@@ -345,7 +361,7 @@
         rhs = []
         for core in (place[3], 1 - place[3]):
             for n in range(X):
-                rhs.append(jnp.concatenate([data_ref[n, y, core, k] for k in range(X)], axis=1))
+                rhs.append(jnp.concatenate([data_ref[n, y, core, from_x(n, k)] for k in range(X)], axis=1))
         total = jnp.dot(lhs, jnp.concatenate(rhs, axis=0), preferred_element_type=F32)
         out_ref[...] = total.astype(out_ref.dtype)
 
@@ -371,14 +387,15 @@
 def body(noise, data):
     z, x, y, c = (lax.axis_index(a) for a in ("z", "x", "y", "core"))
     place = jnp.stack([z, x, y, c]).astype(jnp.int32)
-    swapped = lax.all_to_all(data.reshape(X, QUARTER, SLICE), "x", 0, 0)
+    dealt = deal(place, data)
+    swapped = jnp.stack([dealt[0]] + [shift(dealt[by], "x", by) for by in range(1, X)])
     noise_after, swapped = lax.optimization_barrier((noise, swapped))
     samples = lax.all_gather(swapped, ("z", "core")).reshape(Y, C, C, X, QUARTER, SLICE)
     samples, noise_all, sqn_mine = lax.optimization_barrier((samples, *collect(gather_noise(noise_after))))
-    far, near = pick(place, samples)
-    data_all = lax.all_gather(far, "x")
-    got = shift(theirs(place, near, noise_all, sqn_mine), "core", 1)
-    mine, sq_mine = ours(place, near, noise_all)
+    samples = pick(place, samples)
+    data_all = lax.all_gather(samples, "x")
+    got = shift(theirs(place, samples, noise_all, sqn_mine), "core", 1)
+    mine, sq_mine = ours(place, samples, noise_all)
     q, rows, sq, sq_noise = score(mine, sq_mine, sqn_mine, got)
     for step in range(ITERS):
         if step:
@@ -393,9 +410,10 @@
     w, pot_g = scale(place, columns, blocks)
     data_all, pot_g = lax.optimization_barrier((data_all, pot_g))
     got = shift(w, "core", 1)
-    *parts, data_all = transport(place, w, got, data_all, (2, 1, 3), True)
+    opposite, data_all = transport(place, w, got, data_all, (2,), True)
+    up, down, data_all = transport(place, w, got, data_all, (1, 3), True)
     (target,) = transport(place, w, got, data_all, (0,), False)
-    for by, part in zip((2, 1, 3), parts):
+    for by, part in zip((2, 1, 3), (opposite, up, down)):
         target = target + shift(part, "y", by).astype(F32)
     velocity = (target - noise.astype(F32)).astype(BF16)
     own = lax.dynamic_index_in_dim(f.reshape(2, X, 128), x, 1, False)

time: 201 us -> 257 us (1.28)
  Pallas kernels: 15.6 us -> 80.1 us
  blocking collectives: 75 us -> 64.2 us
  waiting for transfers between devices: 45.5 us -> 49.2 us
  local copies, waits for them, and re-layouts: 14.9 us -> 11.2 us
    pallas_call x1 -> x2, Pallas kernels: 0.92 us -> 65.8 us  [the longest x1 65.2 us: pick(): pl.pallas_call(pick_kernel, out_shape=jax.ShapeDtypeStruct((Y, C, X, QUAR...]
    all_to_all x1 -> x0, blocking collectives: 10.5 us -> none  [body(): swapped = lax.all_to_all(data.reshape(X, QUARTER, SLICE), 'x', 0, 0)]
    all_gather x1, waiting for transfers between devices: 0.84 us -> 8.12 us  [body(): lax.all_gather(swapped, ('z', 'core')).reshape(Y, C, C, X, QUARTER, SLICE)]
    all_to_all x2, blocking collectives: 25.3 us -> 20.1 us  [body(): columns = lax.all_to_all(columns, 'z', 0, 0)]
    all_to_all x3, blocking collectives: 39.2 us -> 44.1 us  [body(): parts = lax.all_to_all(rows, ('x', 'y', 'core'), 0, 0)]
    ppermute x22 -> x25, waiting for transfers between devices: 44.6 us -> 41.1 us  [shift(): return lax.ppermute(x, axis, [(j, (j + by) % n) for j in range(n)])]
    slice x4, local copies, waits for them, and re-layouts: 2.89 us -> 0.07 us  [halves(): return both_ways(forward[:cut], backward[cut:], axis)]
    ppermute x22 -> x25, starting transfers between devices: 29.9 us -> 31.5 us  [shift(): return lax.ppermute(x, axis, [(j, (j + by) % n) for j in range(n)])]
  transfers between devices with their start and end apart: 25 -> 28, of which waited for: 16 -> 19; matrix products, arithmetic and copies ran while one was open for 2% -> 1% of each run, Pallas kernels for 6% -> 5%
where the time goes in v11:
time: 257 us
  Pallas kernels  80.1 us (31%)
  blocking collectives  64.2 us (25%)
  waiting for transfers between devices  49.2 us (19%)
  starting transfers between devices  35.4 us (14%)
  between operations  14.2 us (6%)
  local copies, waits for them, and re-layouts  11.2 us (4%)
    pallas_call x1, Pallas kernels, pick(): pl.pallas_call(pick_kernel, out_shape=jax.ShapeDtypeStruct((Y, C, X, QUAR...  65.2 us
    all_to_all x3, blocking collectives, body(): parts = lax.all_to_all(rows, ('x', 'y', 'core'), 0, 0)  44.1 us
    ppermute x25, waiting for transfers between devices, shift(): return lax.ppermute(x, axis, [(j, (j + by) % n) for j in range(n)])  41.1 us
    ppermute x25, starting transfers between devices, shift(): return lax.ppermute(x, axis, [(j, (j + by) % n) for j in range(n)])  31.5 us
    all_to_all x2, blocking collectives, body(): columns = lax.all_to_all(columns, 'z', 0, 0)  20.1 us
    unnamed x12, local copies, waits for them, and re-layouts  10.1 us
    all_gather x1, waiting for transfers between devices, body(): lax.all_gather(swapped, ('z', 'core')).reshape(Y, C, C, X, QUARTER, SLICE)  8.12 us
  transfers between devices with their start and end apart: 28, of which 19 were waited for; matrix products, arithmetic and copies ran while one was open for 1% of the time, Pallas kernels for 5%

profile of v11, /device:TPU:1, one launch (start us, length us, event | category | flops | bytes accessed | tf_op | source)
XLA Modules:
  0.0 256.8 jit_solution(1696934837853554438)
XLA Ops:
  8.8 2.1 collective-permute-start
  10.9 2.5 collective-permute-start.1
  18.6 3.2 %collective-permute-start.8 = (bf16[128,512]{1,0:T(8,128)(2,1)S(1)}, bf16[128,512]{1,0:T(8,128)(2,1)S(1)}, u32[]{:S(2)}, u32[]{:S(2)}) collective-permute-start(bf16[128,512]{1,0:T(8,128)(2,1)S(1)} %get-tuple-element.59), channel_id=1, source_target_pairs={{0,4},{2,6},{4,0},{6,2},{1,5},{3,7},{5,1},{7,3},{8,12},{10,14},{12... | collective-permute-start | bytes 393224 | tf_op jit(solution)/shard_map/ppermute | solution.py:34
  30.1 2.0 collective-permute-done.3
  35.4 7.1 %collective-permute-done.12.refs_7_ = bf16[4,128,512]{2,1,0:T(8,128)(2,1)S(1)} collective-permute-done((bf16[4,128,512]{2,1,0:T(8,128)(2,1)S(1)}, bf16[4,128,512]{2,1,0:T(8,128)(2,1)S(1)}, u32[]{:S(2)}, u32[]{:S(2)}) %collective-permute-start.12) | collective-permute-done | bytes 524320 | tf_op jit(solution)/shard_map/ppermute | solution.py:34
  44.3 2.3 collective-permute-start.16
  50.0 3.4 %collective-permute-done.15.refs_8_ = bf16[2,128,512]{2,1,0:T(8,128)(2,1)S(1)} collective-permute-done((bf16[2,128,512]{2,1,0:T(8,128)(2,1)S(1)}, bf16[2,128,512]{2,1,0:T(8,128)(2,1)S(1)}, u32[]{:S(2)}, u32[]{:S(2)}) %collective-permute-start.15) | collective-permute-done | bytes 262176 | tf_op jit(solution)/shard_map/ppermute | solution.py:34
  54.1 2.0 copy-done.2
  56.1 8.1 %all-gather.5.cloned.1.call-done = bf16[64,256,128]{2,1,0:T(8,128)(2,1)} async-done(((bf16[4,256,128]{2,1,0:T(8,128)(2,1)}), bf16[64,256,128]{2,1,0:T(8,128)(2,1)}) %all-gather.5.cloned.1.call-update) | async-done | bytes 4194320 | tf_op jit(solution)/shard_map/all_gather | solution.py:393
  64.3 65.2 %pick.1.data_ref = bf16[4,2,4,256,128]{4,3,2,1,0:T(8,128)(2,1)} custom-call(s32[4]{0:T(128)S(1)} %pad_add_fusion.place, bf16[4,2,2,4,256,128]{5,4,3,2,1,0:T(8,128)(2,1)} %bitcast.32), custom_call_target="tpu_custom_call" | custom-call | tf_op jit(solution)/shard_map/pick/pallas_call | solution.py:140
  131.1 2.2 copy-done.3
  138.6 16.4 %all_to_all.30.part_ref = f32[32,8,128]{2,1,0:T(8,128)S(1)} all-to-all(f32[32,8,128]{2,1,0:T(8,128)S(1)} %get-tuple-element.75), channel_id=1, replica_groups=mesh['z'=8,'x'=4,'y'=4,'core'=2] {'x','y','core'}, dimensions={0} | all-to-all | bytes 262144 | tf_op jit(solution)/shard_map/all_to_all | solution.py:403
  155.8 10.9 %all_to_all.31.part_ref = f32[8,8,128]{2,1,0:T(8,128)S(1)} all-to-all(f32[8,8,128]{2,1,0:T(8,128)S(1)} %get-tuple-element.76), channel_id=1, replica_groups=mesh['z'=8,'x'=4,'y'=4,'core'=2] {'z'}, dimensions={0} | all-to-all | bytes 65536 | tf_op jit(solution)/shard_map/all_to_all | solution.py:406
  167.0 14.0 %all_to_all.32.part_ref = f32[32,8,128]{2,1,0:T(8,128)S(1)} all-to-all(f32[32,8,128]{2,1,0:T(8,128)S(1)} %noise_lse.2), channel_id=1, replica_groups=mesh['z'=8,'x'=4,'y'=4,'core'=2] {'x','y','core'}, dimensions={0} | all-to-all | bytes 262144 | tf_op jit(solution)/shard_map/all_to_all | solution.py:403
  181.8 9.2 %all_to_all.33.part_ref = f32[8,8,128]{2,1,0:T(8,128)S(1)} all-to-all(f32[8,8,128]{2,1,0:T(8,128)S(1)} %get-tuple-element.77), channel_id=1, replica_groups=mesh['z'=8,'x'=4,'y'=4,'core'=2] {'z'}, dimensions={0} | all-to-all | bytes 65536 | tf_op jit(solution)/shard_map/all_to_all | solution.py:406
  191.4 13.7 %all_to_all.34.part_ref = f32[32,8,128]{2,1,0:T(8,128)S(1)} all-to-all(f32[32,8,128]{2,1,0:T(8,128)S(1)} %noise_lse.3), channel_id=1, replica_groups=mesh['z'=8,'x'=4,'y'=4,'core'=2] {'x','y','core'}, dimensions={0} | all-to-all | bytes 262144 | tf_op jit(solution)/shard_map/all_to_all | solution.py:403
  206.7 3.9 %all-to-all-start.5 = ((f32[32,8,128]{2,1,0:T(8,128)}), f32[32,8,128]{2,1,0:T(8,128)S(1)}, u32[]{:S(2)}, u32[]{:S(2)}) async-start(f32[32,8,128]{2,1,0:T(8,128)} %get-tuple-element.81), calls=%async_computation.5 | async-start | bytes 262144 | tf_op jit(solution)/shard_map/all_to_all | solution.py:409
  211.8 2.4 collective-permute-start.19
  215.4 6.1 %collective-permute-done.18.refs_1_ = bf16[256,256]{1,0:T(8,128)(2,1)S(1)} collective-permute-done((bf16[256,256]{1,0:T(8,128)(2,1)S(1)}, bf16[256,256]{1,0:T(8,128)(2,1)S(1)}, u32[]{:S(2)}, u32[]{:S(2)}) %collective-permute-start.18) | collective-permute-done | bytes 131104 | tf_op jit(solution)/shard_map/ppermute | solution.py:34
  221.5 4.0 %collective-permute-done.19.refs_2_ = bf16[256,256]{1,0:T(8,128)(2,1)S(1)} collective-permute-done((bf16[256,256]{1,0:T(8,128)(2,1)S(1)}, bf16[256,256]{1,0:T(8,128)(2,1)S(1)}, u32[]{:S(2)}, u32[]{:S(2)}) %collective-permute-start.19) | collective-permute-done | bytes 131104 | tf_op jit(solution)/shard_map/ppermute | solution.py:34
  229.0 3.4 %copy-done = bf16[16,2,4,256,128]{4,3,2,1,0:T(8,128)(2,1)S(1)} copy-done((bf16[16,2,4,256,128]{4,3,2,1,0:T(8,128)(2,1)S(1)}, bf16[16,2,4,256,128]{4,3,2,1,0:T(8,128)(2,1)}, u32[]{:S(2)}) %copy-start) | copy-done | bytes 8388632
  233.6 3.0 %collective-permute-start.22 = (bf16[256,512]{1,0:T(8,128)(2,1)S(1)}, bf16[256,512]{1,0:T(8,128)(2,1)S(1)}, u32[]{:S(2)}, u32[]{:S(2)}) collective-permute-start(bf16[256,512]{1,0:T(8,128)(2,1)S(1)} %get-tuple-element.92), channel_id=1, source_target_pairs={{0,4},{2,6},{4,0},{6,2},{1,5},{3,7},{5,1},{7,3},{8,12},{10,14},{12... | collective-permute-start | bytes 786440 | tf_op jit(solution)/shard_map/ppermute | solution.py:34
  238.9 2.4 collective-permute-start.24
  243.1 6.0 %collective-permute-done.23 = bf16[256,512]{1,0:T(8,128)(2,1)S(1)} collective-permute-done((bf16[256,512]{1,0:T(8,128)(2,1)S(1)}, bf16[256,512]{1,0:T(8,128)(2,1)S(1)}, u32[]{:S(2)}, u32[]{:S(2)}) %collective-permute-start.23) | collective-permute-done | bytes 262176 | tf_op jit(solution)/shard_map/ppermute | solution.py:34
  (78 shorter events, 47.0 us)
Async XLA Ops:
  7.2 57.1 %all-gather.5.cloned.1.call-start = ((), (), s32[]{:S(2)}) async-start(), calls=%async_computation.6 | async-start | bytes 4456448 | tf_op jit(solution)/shard_map/all_gather | solution.py:393
  8.8 5.7 %collective-permute-start = (bf16[256,128]{1,0:T(8,128)(2,1)S(1)}, bf16[256,128]{1,0:T(8,128)(2,1)S(1)}, u32[]{:S(2)}, u32[]{:S(2)}) collective-permute-start(bf16[256,128]{1,0:T(8,128)(2,1)S(1)} %get-tuple-element.50), channel_id=1, source_target_pairs={{0,8},{8,16},{16,24},{24,0},{1,9},{9,17},{17,25},{25,1},{2,10},{10... | collective-permute-start | bytes 196616 | tf_op jit(solution)/shard_map/ppermute | solution.py:34
  10.9 5.1 %collective-permute-start.1 = (bf16[256,128]{1,0:T(8,128)(2,1)S(1)}, bf16[256,128]{1,0:T(8,128)(2,1)S(1)}, u32[]{:S(2)}, u32[]{:S(2)}) collective-permute-start(bf16[256,128]{1,0:T(8,128)(2,1)S(1)} %get-tuple-element.51), channel_id=1, source_target_pairs={{0,16},{8,24},{16,0},{24,8},{1,17},{9,25},{17,1},{25,9},{2,18},{10... | collective-permute-start | bytes 196616 | tf_op jit(solution)/shard_map/ppermute | solution.py:34
  17.6 209.9 %all-gather.7.cloned.1.call-start = ((), (), s32[]{:S(2)}) async-start(), calls=%async_computation.7 | async-start | bytes 10485760 | tf_op jit(solution)/shard_map/all_gather | solution.py:396
  18.6 6.9 %collective-permute-start.8 = (bf16[128,512]{1,0:T(8,128)(2,1)S(1)}, bf16[128,512]{1,0:T(8,128)(2,1)S(1)}, u32[]{:S(2)}, u32[]{:S(2)}) collective-permute-start(bf16[128,512]{1,0:T(8,128)(2,1)S(1)} %get-tuple-element.59), channel_id=1, source_target_pairs={{0,4},{2,6},{4,0},{6,2},{1,5},{3,7},{5,1},{7,3},{8,12},{10,14},{12... | collective-permute-start | bytes 393224 | tf_op jit(solution)/shard_map/ppermute | solution.py:34
  22.6 6.0 %collective-permute-start.6 = (bf16[128,512]{1,0:T(8,128)(2,1)S(1)}, bf16[128,512]{1,0:T(8,128)(2,1)S(1)}, u32[]{:S(2)}, u32[]{:S(2)}) collective-permute-start(bf16[128,512]{1,0:T(8,128)(2,1)S(1)} %get-tuple-element.59), channel_id=1, source_target_pairs={{0,2},{2,4},{4,6},{6,0},{1,3},{3,5},{5,7},{7,1},{8,10},{10,12},{12... | collective-permute-start | bytes 393224 | tf_op jit(solution)/shard_map/ppermute | solution.py:34
  23.3 5.3 %collective-permute-start.5 = (bf16[128,512]{1,0:T(8,128)(2,1)S(1)}, bf16[128,512]{1,0:T(8,128)(2,1)S(1)}, u32[]{:S(2)}, u32[]{:S(2)}) collective-permute-start(bf16[128,512]{1,0:T(8,128)(2,1)S(1)} %get-tuple-element.55), channel_id=1, source_target_pairs={{0,16},{8,24},{16,0},{24,8},{1,17},{9,25},{17,1},{25,9},{2,18},{10... | collective-permute-start | bytes 393224 | tf_op jit(solution)/shard_map/ppermute | solution.py:34
  24.3 5.7 %collective-permute-start.4 = (bf16[128,512]{1,0:T(8,128)(2,1)S(1)}, bf16[128,512]{1,0:T(8,128)(2,1)S(1)}, u32[]{:S(2)}, u32[]{:S(2)}) collective-permute-start(bf16[128,512]{1,0:T(8,128)(2,1)S(1)} %get-tuple-element.55), channel_id=1, source_target_pairs={{0,24},{8,0},{16,8},{24,16},{1,25},{9,1},{17,9},{25,17},{2,26},{10... | collective-permute-start | bytes 393224 | tf_op jit(solution)/shard_map/ppermute | solution.py:34
  25.5 6.7 %collective-permute-start.3 = (bf16[128,512]{1,0:T(8,128)(2,1)S(1)}, bf16[128,512]{1,0:T(8,128)(2,1)S(1)}, u32[]{:S(2)}, u32[]{:S(2)}) collective-permute-start(bf16[128,512]{1,0:T(8,128)(2,1)S(1)} %get-tuple-element.55), channel_id=1, source_target_pairs={{0,8},{8,16},{16,24},{24,0},{1,9},{9,17},{17,25},{25,1},{2,10},{10... | collective-permute-start | bytes 393224 | tf_op jit(solution)/shard_map/ppermute | solution.py:34
  32.2 10.3 %collective-permute-start.12 = (bf16[4,128,512]{2,1,0:T(8,128)(2,1)S(1)}, bf16[4,128,512]{2,1,0:T(8,128)(2,1)S(1)}, u32[]{:S(2)}, u32[]{:S(2)}) collective-permute-start(bf16[4,128,512]{2,1,0:T(8,128)(2,1)S(1)} %pad_maximum_fusion.1.refs_5_), channel_id=1, source_target_pairs={{0,24},{8,0},{16,8},{24,16},{1,25},{9,1},{17,9},{25,17},{2,26},{10... | collective-permute-start | bytes 1572872 | tf_op jit(solution)/shard_map/ppermute | solution.py:34
  32.4 10.4 %collective-permute-start.11 = (bf16[4,128,512]{2,1,0:T(8,128)(2,1)S(1)}, bf16[4,128,512]{2,1,0:T(8,128)(2,1)S(1)}, u32[]{:S(2)}, u32[]{:S(2)}) collective-permute-start(bf16[4,128,512]{2,1,0:T(8,128)(2,1)S(1)} %pad_maximum_fusion.1.refs_5_), channel_id=1, source_target_pairs={{0,8},{8,16},{16,24},{24,0},{1,9},{9,17},{17,25},{25,1},{2,10},{10... | collective-permute-start | bytes 1572872 | tf_op jit(solution)/shard_map/ppermute | solution.py:34
  33.8 9.7 %collective-permute-start.10 = (bf16[4,128,512]{2,1,0:T(8,128)(2,1)S(1)}, bf16[4,128,512]{2,1,0:T(8,128)(2,1)S(1)}, u32[]{:S(2)}, u32[]{:S(2)}) collective-permute-start(bf16[4,128,512]{2,1,0:T(8,128)(2,1)S(1)} %pad_maximum_fusion.refs_0_), channel_id=1, source_target_pairs={{0,6},{2,0},{4,2},{6,4},{1,7},{3,1},{5,3},{7,5},{8,14},{10,8},{12,... | collective-permute-start | bytes 1572872 | tf_op jit(solution)/shard_map/ppermute | solution.py:34
  34.7 9.5 %collective-permute-start.9 = (bf16[4,128,512]{2,1,0:T(8,128)(2,1)S(1)}, bf16[4,128,512]{2,1,0:T(8,128)(2,1)S(1)}, u32[]{:S(2)}, u32[]{:S(2)}) collective-permute-start(bf16[4,128,512]{2,1,0:T(8,128)(2,1)S(1)} %pad_maximum_fusion.refs_0_), channel_id=1, source_target_pairs={{0,2},{2,4},{4,6},{6,0},{1,3},{3,5},{5,7},{7,1},{8,10},{10,12},{12... | collective-permute-start | bytes 1572872 | tf_op jit(solution)/shard_map/ppermute | solution.py:34
  44.3 5.7 %collective-permute-start.16 = (bf16[2,128,512]{2,1,0:T(8,128)(2,1)S(1)}, bf16[2,128,512]{2,1,0:T(8,128)(2,1)S(1)}, u32[]{:S(2)}, u32[]{:S(2)}) collective-permute-start(bf16[2,128,512]{2,1,0:T(8,128)(2,1)S(1)} %slice.23), channel_id=1, source_target_pairs={{0,24},{8,0},{16,8},{24,16},{1,25},{9,1},{17,9},{25,17},{2,26},{10... | collective-permute-start | bytes 786440 | tf_op jit(solution)/shard_map/ppermute | solution.py:34
  46.6 6.8 %collective-permute-start.15 = (bf16[2,128,512]{2,1,0:T(8,128)(2,1)S(1)}, bf16[2,128,512]{2,1,0:T(8,128)(2,1)S(1)}, u32[]{:S(2)}, u32[]{:S(2)}) collective-permute-start(bf16[2,128,512]{2,1,0:T(8,128)(2,1)S(1)} %slice.22), channel_id=1, source_target_pairs={{0,8},{8,16},{16,24},{24,0},{1,9},{9,17},{17,25},{25,1},{2,10},{10... | collective-permute-start | bytes 786440 | tf_op jit(solution)/shard_map/ppermute | solution.py:34
  46.6 6.8 %collective-permute-start.14 = (bf16[2,128,512]{2,1,0:T(8,128)(2,1)S(1)}, bf16[2,128,512]{2,1,0:T(8,128)(2,1)S(1)}, u32[]{:S(2)}, u32[]{:S(2)}) collective-permute-start(bf16[2,128,512]{2,1,0:T(8,128)(2,1)S(1)} %slice.21), channel_id=1, source_target_pairs={{0,6},{2,0},{4,2},{6,4},{1,7},{3,1},{5,3},{7,5},{8,14},{10,8},{12,... | collective-permute-start | bytes 786440 | tf_op jit(solution)/shard_map/ppermute | solution.py:34
  46.8 6.8 %collective-permute-start.13 = (bf16[2,128,512]{2,1,0:T(8,128)(2,1)S(1)}, bf16[2,128,512]{2,1,0:T(8,128)(2,1)S(1)}, u32[]{:S(2)}, u32[]{:S(2)}) collective-permute-start(bf16[2,128,512]{2,1,0:T(8,128)(2,1)S(1)} %slice.20), channel_id=1, source_target_pairs={{0,2},{2,4},{4,6},{6,0},{1,3},{3,5},{5,7},{7,1},{8,10},{10,12},{12... | collective-permute-start | bytes 786440 | tf_op jit(solution)/shard_map/ppermute | solution.py:34
  206.7 18.7 %all-to-all-start.5 = ((f32[32,8,128]{2,1,0:T(8,128)}), f32[32,8,128]{2,1,0:T(8,128)S(1)}, u32[]{:S(2)}, u32[]{:S(2)}) async-start(f32[32,8,128]{2,1,0:T(8,128)} %get-tuple-element.81), calls=%async_computation.5 | async-start | bytes 262144 | tf_op jit(solution)/shard_map/all_to_all | solution.py:409
  210.6 10.9 %collective-permute-start.18 = (bf16[256,256]{1,0:T(8,128)(2,1)S(1)}, bf16[256,256]{1,0:T(8,128)(2,1)S(1)}, u32[]{:S(2)}, u32[]{:S(2)}) collective-permute-start(bf16[256,256]{1,0:T(8,128)(2,1)S(1)} %get-tuple-element.83), channel_id=1, source_target_pairs={{0,8},{8,16},{16,24},{24,0},{1,9},{9,17},{17,25},{25,1},{2,10},{10... | collective-permute-start | bytes 393224 | tf_op jit(solution)/shard_map/ppermute | solution.py:34
  211.8 13.7 %collective-permute-start.19 = (bf16[256,256]{1,0:T(8,128)(2,1)S(1)}, bf16[256,256]{1,0:T(8,128)(2,1)S(1)}, u32[]{:S(2)}, u32[]{:S(2)}) collective-permute-start(bf16[256,256]{1,0:T(8,128)(2,1)S(1)} %get-tuple-element.84), channel_id=1, source_target_pairs={{0,16},{8,24},{16,0},{24,8},{1,17},{9,25},{17,1},{25,9},{2,18},{10... | collective-permute-start | bytes 393224 | tf_op jit(solution)/shard_map/ppermute | solution.py:34
  214.2 11.3 %collective-permute-start.20 = (bf16[256,256]{1,0:T(8,128)(2,1)S(1)}, bf16[256,256]{1,0:T(8,128)(2,1)S(1)}, u32[]{:S(2)}, u32[]{:S(2)}) collective-permute-start(bf16[256,256]{1,0:T(8,128)(2,1)S(1)} %get-tuple-element.85), channel_id=1, source_target_pairs={{0,24},{8,0},{16,8},{24,16},{1,25},{9,1},{17,9},{25,17},{2,26},{10... | collective-permute-start | bytes 393224 | tf_op jit(solution)/shard_map/ppermute | solution.py:34
  233.6 9.5 %collective-permute-start.22 = (bf16[256,512]{1,0:T(8,128)(2,1)S(1)}, bf16[256,512]{1,0:T(8,128)(2,1)S(1)}, u32[]{:S(2)}, u32[]{:S(2)}) collective-permute-start(bf16[256,512]{1,0:T(8,128)(2,1)S(1)} %get-tuple-element.92), channel_id=1, source_target_pairs={{0,4},{2,6},{4,0},{6,2},{1,5},{3,7},{5,1},{7,3},{8,12},{10,14},{12... | collective-permute-start | bytes 786440 | tf_op jit(solution)/shard_map/ppermute | solution.py:34
  238.5 10.6 %collective-permute-start.23 = (bf16[256,512]{1,0:T(8,128)(2,1)S(1)}, bf16[256,512]{1,0:T(8,128)(2,1)S(1)}, u32[]{:S(2)}, u32[]{:S(2)}) collective-permute-start(bf16[256,512]{1,0:T(8,128)(2,1)S(1)} %get-tuple-element.93), channel_id=1, source_target_pairs={{0,2},{2,4},{4,6},{6,0},{1,3},{3,5},{5,7},{7,1},{8,10},{10,12},{12... | collective-permute-start | bytes 786440 | tf_op jit(solution)/shard_map/ppermute | solution.py:34
  238.9 10.2 %collective-permute-start.24 = (bf16[256,512]{1,0:T(8,128)(2,1)S(1)}, bf16[256,512]{1,0:T(8,128)(2,1)S(1)}, u32[]{:S(2)}, u32[]{:S(2)}) collective-permute-start(bf16[256,512]{1,0:T(8,128)(2,1)S(1)} %get-tuple-element.94), channel_id=1, source_target_pairs={{0,6},{2,0},{4,2},{6,4},{1,7},{3,1},{5,3},{7,5},{8,14},{10,8},{12,... | collective-permute-start | bytes 786440 | tf_op jit(solution)/shard_map/ppermute | solution.py:34
  (10 other events, 30.8 us)
Sparse Core Ops, SparseCore 0:
  17.7 46.5 all-gather.4
  129.6 93.3 all-gather.6

commit v12 on v11

--- a/solution.py
+++ b/solution.py
@@ -128,21 +128,26 @@
     )(*parts)
 
 
-def pick_kernel(place, all_ref, out_ref, sems):
-    copies = [pltpu.make_async_copy(all_ref.at[y, place[3]], out_ref.at[y], sems.at[y]) for y in range(Y)]
-    for copy in copies:
+def pick_kernel(place, all_ref, out_ref, buffer_ref, sems):
+    ins = [pltpu.make_async_copy(all_ref.at[y, place[3]], buffer_ref.at[y], sems.at[0, y]) for y in range(Y)]
+    outs = [pltpu.make_async_copy(buffer_ref.at[y], out_ref.at[y], sems.at[1, y]) for y in range(Y)]
+    for copy in ins:
         copy.start()
-    for copy in copies:
+    for y in range(Y):
+        ins[y].wait()
+        outs[y].start()
+    for copy in outs:
         copy.wait()
 
 
 def pick(place, samples):
+    half = (Y, C, X, QUARTER, SLICE)
     return pl.pallas_call(
         pick_kernel,
-        out_shape=jax.ShapeDtypeStruct((Y, C, X, QUARTER, SLICE), BF16),
+        out_shape=jax.ShapeDtypeStruct(half, BF16),
         in_specs=[SMEM, pl.BlockSpec(memory_space=pl.ANY)],
         out_specs=pl.BlockSpec(memory_space=pl.ANY),
-        scratch_shapes=[pltpu.SemaphoreType.DMA((Y,))],
+        scratch_shapes=[pltpu.VMEM(half, BF16), pltpu.SemaphoreType.DMA((2, Y))],
         compiler_params=params(53),
         name="pick",
     )(place, samples)

time: 257 us -> 195 us (0.76)
  Pallas kernels: 80.1 us -> 17.9 us
    pallas_call x1, Pallas kernels: 65.2 us -> 2.96 us  [pick(): pl.pallas_call(pick_kernel, out_shape=jax.ShapeDtypeStruct(half, BF16), i...]
  transfers between devices with their start and end apart: 28 -> 28, of which waited for: 19 -> 19; matrix products, arithmetic and copies ran while one was open for 1% -> 1% of each run, Pallas kernels for 5% -> 7%
where the time goes in v12:
time: 195 us
  blocking collectives  64.2 us (33%)
  waiting for transfers between devices  49.2 us (25%)
  starting transfers between devices  35.4 us (18%)
  Pallas kernels  17.9 us (9%)
  between operations  14.2 us (7%)
  local copies, waits for them, and re-layouts  11.2 us (6%)
  other arithmetic  2.39 us (1%)
    all_to_all x3, blocking collectives, body(): parts = lax.all_to_all(rows, ('x', 'y', 'core'), 0, 0)  44.1 us
    ppermute x25, waiting for transfers between devices, shift(): return lax.ppermute(x, axis, [(j, (j + by) % n) for j in range(n)])  41.1 us
    ppermute x25, starting transfers between devices, shift(): return lax.ppermute(x, axis, [(j, (j + by) % n) for j in range(n)])  31.5 us
    all_to_all x2, blocking collectives, body(): columns = lax.all_to_all(columns, 'z', 0, 0)  20.1 us
    unnamed x12, local copies, waits for them, and re-layouts  10.1 us
    all_gather x1, waiting for transfers between devices, body(): lax.all_gather(swapped, ('z', 'core')).reshape(Y, C, C, X, QUARTER, SLICE)  8.12 us
    pallas_call x3, Pallas kernels, transport(): pl.pallas_call(functools.partial(transport_kernel, pieces), out_shape=kin...  4.34 us
  transfers between devices with their start and end apart: 28, of which 19 were waited for; matrix products, arithmetic and copies ran while one was open for 1% of the time, Pallas kernels for 7%

profile of v12, /device:TPU:1, one launch (start us, length us, event | category | flops | bytes accessed | tf_op | source)
XLA Modules:
  0.0 194.5 jit_solution(5974691936055483037)
XLA Ops:
  8.8 2.1 %collective-permute-start = (bf16[256,128]{1,0:T(8,128)(2,1)S(1)}, bf16[256,128]{1,0:T(8,128)(2,1)S(1)}, u32[]{:S(2)}, u32[]{:S(2)}) collective-permute-start(bf16[256,128]{1,0:T(8,128)(2,1)S(1)} %get-tuple-element.50), channel_id=1, source_target_pairs={{0,8},{8,16},{16,24},{24,0},{1,9},{9,17},{17,25},{25,1},{2,10},{10... | collective-permute-start | bytes 196616 | tf_op jit(solution)/shard_map/ppermute | solution.py:34
  10.9 2.5 %collective-permute-start.1 = (bf16[256,128]{1,0:T(8,128)(2,1)S(1)}, bf16[256,128]{1,0:T(8,128)(2,1)S(1)}, u32[]{:S(2)}, u32[]{:S(2)}) collective-permute-start(bf16[256,128]{1,0:T(8,128)(2,1)S(1)} %get-tuple-element.51), channel_id=1, source_target_pairs={{0,16},{8,24},{16,0},{24,8},{1,17},{9,25},{17,1},{25,9},{2,18},{10... | collective-permute-start | bytes 196616 | tf_op jit(solution)/shard_map/ppermute | solution.py:34
  18.6 3.2 %collective-permute-start.8 = (bf16[128,512]{1,0:T(8,128)(2,1)S(1)}, bf16[128,512]{1,0:T(8,128)(2,1)S(1)}, u32[]{:S(2)}, u32[]{:S(2)}) collective-permute-start(bf16[128,512]{1,0:T(8,128)(2,1)S(1)} %get-tuple-element.59), channel_id=1, source_target_pairs={{0,4},{2,6},{4,0},{6,2},{1,5},{3,7},{5,1},{7,3},{8,12},{10,14},{12... | collective-permute-start | bytes 393224 | tf_op jit(solution)/shard_map/ppermute | solution.py:34
  30.1 2.0 %collective-permute-done.3 = bf16[128,512]{1,0:T(8,128)(2,1)S(1)} collective-permute-done((bf16[128,512]{1,0:T(8,128)(2,1)S(1)}, bf16[128,512]{1,0:T(8,128)(2,1)S(1)}, u32[]{:S(2)}, u32[]{:S(2)}) %collective-permute-start.3) | collective-permute-done | bytes 131104 | tf_op jit(solution)/shard_map/ppermute | solution.py:34
  35.4 7.1 %collective-permute-done.12.refs_7_ = bf16[4,128,512]{2,1,0:T(8,128)(2,1)S(1)} collective-permute-done((bf16[4,128,512]{2,1,0:T(8,128)(2,1)S(1)}, bf16[4,128,512]{2,1,0:T(8,128)(2,1)S(1)}, u32[]{:S(2)}, u32[]{:S(2)}) %collective-permute-start.12) | collective-permute-done | bytes 524320 | tf_op jit(solution)/shard_map/ppermute | solution.py:34
  44.3 2.3 %collective-permute-start.16 = (bf16[2,128,512]{2,1,0:T(8,128)(2,1)S(1)}, bf16[2,128,512]{2,1,0:T(8,128)(2,1)S(1)}, u32[]{:S(2)}, u32[]{:S(2)}) collective-permute-start(bf16[2,128,512]{2,1,0:T(8,128)(2,1)S(1)} %slice.23), channel_id=1, source_target_pairs={{0,24},{8,0},{16,8},{24,16},{1,25},{9,1},{17,9},{25,17},{2,26},{10... | collective-permute-start | bytes 786440 | tf_op jit(solution)/shard_map/ppermute | solution.py:34
  50.0 3.4 %collective-permute-done.15.refs_8_ = bf16[2,128,512]{2,1,0:T(8,128)(2,1)S(1)} collective-permute-done((bf16[2,128,512]{2,1,0:T(8,128)(2,1)S(1)}, bf16[2,128,512]{2,1,0:T(8,128)(2,1)S(1)}, u32[]{:S(2)}, u32[]{:S(2)}) %collective-permute-start.15) | collective-permute-done | bytes 262176 | tf_op jit(solution)/shard_map/ppermute | solution.py:34
  54.1 2.0 %copy-done.2 = bf16[1024,2048]{1,0:T(8,128)(2,1)} copy-done((bf16[1024,2048]{1,0:T(8,128)(2,1)}, bf16[1024,2048]{1,0:T(8,128)(2,1)S(1)}, u32[]{:S(2)}) %copy-start.2) | copy-done | bytes 4194328
  56.1 8.1 %all-gather.5.cloned.1.call-done = bf16[64,256,128]{2,1,0:T(8,128)(2,1)} async-done(((bf16[4,256,128]{2,1,0:T(8,128)(2,1)}), bf16[64,256,128]{2,1,0:T(8,128)(2,1)}) %all-gather.5.cloned.1.call-update) | async-done | bytes 4194320 | tf_op jit(solution)/shard_map/all_gather | solution.py:398
  64.3 3.0 %pick.1.data_ref = bf16[4,2,4,256,128]{4,3,2,1,0:T(8,128)(2,1)} custom-call(s32[4]{0:T(128)S(1)} %pad_add_fusion.place, bf16[4,2,2,4,256,128]{5,4,3,2,1,0:T(8,128)(2,1)} %bitcast.32), custom_call_target="tpu_custom_call" | custom-call | tf_op jit(solution)/shard_map/pick/pallas_call | solution.py:145
  68.8 2.2 %copy-done.3 = bf16[1024,2048]{1,0:T(8,128)(2,1)S(1)} copy-done((bf16[1024,2048]{1,0:T(8,128)(2,1)S(1)}, bf16[1024,2048]{1,0:T(8,128)(2,1)}, u32[]{:S(2)}) %copy-start.3) | copy-done | bytes 4194328
  76.3 16.4 %all_to_all.30.part_ref = f32[32,8,128]{2,1,0:T(8,128)S(1)} all-to-all(f32[32,8,128]{2,1,0:T(8,128)S(1)} %get-tuple-element.75), channel_id=1, replica_groups=mesh['z'=8,'x'=4,'y'=4,'core'=2] {'x','y','core'}, dimensions={0} | all-to-all | bytes 262144 | tf_op jit(solution)/shard_map/all_to_all | solution.py:408
  93.5 10.9 %all_to_all.31.part_ref = f32[8,8,128]{2,1,0:T(8,128)S(1)} all-to-all(f32[8,8,128]{2,1,0:T(8,128)S(1)} %get-tuple-element.76), channel_id=1, replica_groups=mesh['z'=8,'x'=4,'y'=4,'core'=2] {'z'}, dimensions={0} | all-to-all | bytes 65536 | tf_op jit(solution)/shard_map/all_to_all | solution.py:411
  104.8 14.0 %all_to_all.32.part_ref = f32[32,8,128]{2,1,0:T(8,128)S(1)} all-to-all(f32[32,8,128]{2,1,0:T(8,128)S(1)} %noise_lse.2), channel_id=1, replica_groups=mesh['z'=8,'x'=4,'y'=4,'core'=2] {'x','y','core'}, dimensions={0} | all-to-all | bytes 262144 | tf_op jit(solution)/shard_map/all_to_all | solution.py:408
  119.6 9.2 %all_to_all.33.part_ref = f32[8,8,128]{2,1,0:T(8,128)S(1)} all-to-all(f32[8,8,128]{2,1,0:T(8,128)S(1)} %get-tuple-element.77), channel_id=1, replica_groups=mesh['z'=8,'x'=4,'y'=4,'core'=2] {'z'}, dimensions={0} | all-to-all | bytes 65536 | tf_op jit(solution)/shard_map/all_to_all | solution.py:411
  129.2 13.7 %all_to_all.34.part_ref = f32[32,8,128]{2,1,0:T(8,128)S(1)} all-to-all(f32[32,8,128]{2,1,0:T(8,128)S(1)} %noise_lse.3), channel_id=1, replica_groups=mesh['z'=8,'x'=4,'y'=4,'core'=2] {'x','y','core'}, dimensions={0} | all-to-all | bytes 262144 | tf_op jit(solution)/shard_map/all_to_all | solution.py:408
  144.5 3.9 %all-to-all-start.5 = ((f32[32,8,128]{2,1,0:T(8,128)}), f32[32,8,128]{2,1,0:T(8,128)S(1)}, u32[]{:S(2)}, u32[]{:S(2)}) async-start(f32[32,8,128]{2,1,0:T(8,128)} %get-tuple-element.81), calls=%async_computation.5 | async-start | bytes 262144 | tf_op jit(solution)/shard_map/all_to_all | solution.py:414
  149.5 2.4 %collective-permute-start.19 = (bf16[256,256]{1,0:T(8,128)(2,1)S(1)}, bf16[256,256]{1,0:T(8,128)(2,1)S(1)}, u32[]{:S(2)}, u32[]{:S(2)}) collective-permute-start(bf16[256,256]{1,0:T(8,128)(2,1)S(1)} %get-tuple-element.84), channel_id=1, source_target_pairs={{0,16},{8,24},{16,0},{24,8},{1,17},{9,25},{17,1},{25,9},{2,18},{10... | collective-permute-start | bytes 393224 | tf_op jit(solution)/shard_map/ppermute | solution.py:34
  153.1 6.1 %collective-permute-done.18.refs_1_ = bf16[256,256]{1,0:T(8,128)(2,1)S(1)} collective-permute-done((bf16[256,256]{1,0:T(8,128)(2,1)S(1)}, bf16[256,256]{1,0:T(8,128)(2,1)S(1)}, u32[]{:S(2)}, u32[]{:S(2)}) %collective-permute-start.18) | collective-permute-done | bytes 131104 | tf_op jit(solution)/shard_map/ppermute | solution.py:34
  159.2 4.0 %collective-permute-done.19.refs_2_ = bf16[256,256]{1,0:T(8,128)(2,1)S(1)} collective-permute-done((bf16[256,256]{1,0:T(8,128)(2,1)S(1)}, bf16[256,256]{1,0:T(8,128)(2,1)S(1)}, u32[]{:S(2)}, u32[]{:S(2)}) %collective-permute-start.19) | collective-permute-done | bytes 131104 | tf_op jit(solution)/shard_map/ppermute | solution.py:34
  166.7 3.4 %copy-done = bf16[16,2,4,256,128]{4,3,2,1,0:T(8,128)(2,1)S(1)} copy-done((bf16[16,2,4,256,128]{4,3,2,1,0:T(8,128)(2,1)S(1)}, bf16[16,2,4,256,128]{4,3,2,1,0:T(8,128)(2,1)}, u32[]{:S(2)}) %copy-start) | copy-done | bytes 8388632
  171.4 3.0 %collective-permute-start.22 = (bf16[256,512]{1,0:T(8,128)(2,1)S(1)}, bf16[256,512]{1,0:T(8,128)(2,1)S(1)}, u32[]{:S(2)}, u32[]{:S(2)}) collective-permute-start(bf16[256,512]{1,0:T(8,128)(2,1)S(1)} %get-tuple-element.92), channel_id=1, source_target_pairs={{0,4},{2,6},{4,0},{6,2},{1,5},{3,7},{5,1},{7,3},{8,12},{10,14},{12... | collective-permute-start | bytes 786440 | tf_op jit(solution)/shard_map/ppermute | solution.py:34
  176.6 2.4 %collective-permute-start.24 = (bf16[256,512]{1,0:T(8,128)(2,1)S(1)}, bf16[256,512]{1,0:T(8,128)(2,1)S(1)}, u32[]{:S(2)}, u32[]{:S(2)}) collective-permute-start(bf16[256,512]{1,0:T(8,128)(2,1)S(1)} %get-tuple-element.94), channel_id=1, source_target_pairs={{0,6},{2,0},{4,2},{6,4},{1,7},{3,1},{5,3},{7,5},{8,14},{10,8},{12,... | collective-permute-start | bytes 786440 | tf_op jit(solution)/shard_map/ppermute | solution.py:34
  180.8 6.0 %collective-permute-done.23 = bf16[256,512]{1,0:T(8,128)(2,1)S(1)} collective-permute-done((bf16[256,512]{1,0:T(8,128)(2,1)S(1)}, bf16[256,512]{1,0:T(8,128)(2,1)S(1)}, u32[]{:S(2)}, u32[]{:S(2)}) %collective-permute-start.23) | collective-permute-done | bytes 262176 | tf_op jit(solution)/shard_map/ppermute | solution.py:34
  (78 shorter events, 47.0 us)
Async XLA Ops:
  7.2 57.1 %all-gather.5.cloned.1.call-start = ((), (), s32[]{:S(2)}) async-start(), calls=%async_computation.6 | async-start | bytes 4456448 | tf_op jit(solution)/shard_map/all_gather | solution.py:398
  8.8 5.7 %collective-permute-start = (bf16[256,128]{1,0:T(8,128)(2,1)S(1)}, bf16[256,128]{1,0:T(8,128)(2,1)S(1)}, u32[]{:S(2)}, u32[]{:S(2)}) collective-permute-start(bf16[256,128]{1,0:T(8,128)(2,1)S(1)} %get-tuple-element.50), channel_id=1, source_target_pairs={{0,8},{8,16},{16,24},{24,0},{1,9},{9,17},{17,25},{25,1},{2,10},{10... | collective-permute-start | bytes 196616 | tf_op jit(solution)/shard_map/ppermute | solution.py:34
  10.9 5.1 %collective-permute-start.1 = (bf16[256,128]{1,0:T(8,128)(2,1)S(1)}, bf16[256,128]{1,0:T(8,128)(2,1)S(1)}, u32[]{:S(2)}, u32[]{:S(2)}) collective-permute-start(bf16[256,128]{1,0:T(8,128)(2,1)S(1)} %get-tuple-element.51), channel_id=1, source_target_pairs={{0,16},{8,24},{16,0},{24,8},{1,17},{9,25},{17,1},{25,9},{2,18},{10... | collective-permute-start | bytes 196616 | tf_op jit(solution)/shard_map/ppermute | solution.py:34
  17.6 147.6 %all-gather.7.cloned.1.call-start = ((), (), s32[]{:S(2)}) async-start(), calls=%async_computation.7 | async-start | bytes 10485760 | tf_op jit(solution)/shard_map/all_gather | solution.py:401
  18.6 6.9 %collective-permute-start.8 = (bf16[128,512]{1,0:T(8,128)(2,1)S(1)}, bf16[128,512]{1,0:T(8,128)(2,1)S(1)}, u32[]{:S(2)}, u32[]{:S(2)}) collective-permute-start(bf16[128,512]{1,0:T(8,128)(2,1)S(1)} %get-tuple-element.59), channel_id=1, source_target_pairs={{0,4},{2,6},{4,0},{6,2},{1,5},{3,7},{5,1},{7,3},{8,12},{10,14},{12... | collective-permute-start | bytes 393224 | tf_op jit(solution)/shard_map/ppermute | solution.py:34
  22.6 6.0 %collective-permute-start.6 = (bf16[128,512]{1,0:T(8,128)(2,1)S(1)}, bf16[128,512]{1,0:T(8,128)(2,1)S(1)}, u32[]{:S(2)}, u32[]{:S(2)}) collective-permute-start(bf16[128,512]{1,0:T(8,128)(2,1)S(1)} %get-tuple-element.59), channel_id=1, source_target_pairs={{0,2},{2,4},{4,6},{6,0},{1,3},{3,5},{5,7},{7,1},{8,10},{10,12},{12... | collective-permute-start | bytes 393224 | tf_op jit(solution)/shard_map/ppermute | solution.py:34
  23.3 5.3 %collective-permute-start.5 = (bf16[128,512]{1,0:T(8,128)(2,1)S(1)}, bf16[128,512]{1,0:T(8,128)(2,1)S(1)}, u32[]{:S(2)}, u32[]{:S(2)}) collective-permute-start(bf16[128,512]{1,0:T(8,128)(2,1)S(1)} %get-tuple-element.55), channel_id=1, source_target_pairs={{0,16},{8,24},{16,0},{24,8},{1,17},{9,25},{17,1},{25,9},{2,18},{10... | collective-permute-start | bytes 393224 | tf_op jit(solution)/shard_map/ppermute | solution.py:34
  24.3 5.7 %collective-permute-start.4 = (bf16[128,512]{1,0:T(8,128)(2,1)S(1)}, bf16[128,512]{1,0:T(8,128)(2,1)S(1)}, u32[]{:S(2)}, u32[]{:S(2)}) collective-permute-start(bf16[128,512]{1,0:T(8,128)(2,1)S(1)} %get-tuple-element.55), channel_id=1, source_target_pairs={{0,24},{8,0},{16,8},{24,16},{1,25},{9,1},{17,9},{25,17},{2,26},{10... | collective-permute-start | bytes 393224 | tf_op jit(solution)/shard_map/ppermute | solution.py:34
  25.5 6.7 %collective-permute-start.3 = (bf16[128,512]{1,0:T(8,128)(2,1)S(1)}, bf16[128,512]{1,0:T(8,128)(2,1)S(1)}, u32[]{:S(2)}, u32[]{:S(2)}) collective-permute-start(bf16[128,512]{1,0:T(8,128)(2,1)S(1)} %get-tuple-element.55), channel_id=1, source_target_pairs={{0,8},{8,16},{16,24},{24,0},{1,9},{9,17},{17,25},{25,1},{2,10},{10... | collective-permute-start | bytes 393224 | tf_op jit(solution)/shard_map/ppermute | solution.py:34
  32.2 10.3 %collective-permute-start.12 = (bf16[4,128,512]{2,1,0:T(8,128)(2,1)S(1)}, bf16[4,128,512]{2,1,0:T(8,128)(2,1)S(1)}, u32[]{:S(2)}, u32[]{:S(2)}) collective-permute-start(bf16[4,128,512]{2,1,0:T(8,128)(2,1)S(1)} %pad_maximum_fusion.1.refs_5_), channel_id=1, source_target_pairs={{0,24},{8,0},{16,8},{24,16},{1,25},{9,1},{17,9},{25,17},{2,26},{10... | collective-permute-start | bytes 1572872 | tf_op jit(solution)/shard_map/ppermute | solution.py:34
  32.4 10.4 %collective-permute-start.11 = (bf16[4,128,512]{2,1,0:T(8,128)(2,1)S(1)}, bf16[4,128,512]{2,1,0:T(8,128)(2,1)S(1)}, u32[]{:S(2)}, u32[]{:S(2)}) collective-permute-start(bf16[4,128,512]{2,1,0:T(8,128)(2,1)S(1)} %pad_maximum_fusion.1.refs_5_), channel_id=1, source_target_pairs={{0,8},{8,16},{16,24},{24,0},{1,9},{9,17},{17,25},{25,1},{2,10},{10... | collective-permute-start | bytes 1572872 | tf_op jit(solution)/shard_map/ppermute | solution.py:34
  33.8 9.7 %collective-permute-start.10 = (bf16[4,128,512]{2,1,0:T(8,128)(2,1)S(1)}, bf16[4,128,512]{2,1,0:T(8,128)(2,1)S(1)}, u32[]{:S(2)}, u32[]{:S(2)}) collective-permute-start(bf16[4,128,512]{2,1,0:T(8,128)(2,1)S(1)} %pad_maximum_fusion.refs_0_), channel_id=1, source_target_pairs={{0,6},{2,0},{4,2},{6,4},{1,7},{3,1},{5,3},{7,5},{8,14},{10,8},{12,... | collective-permute-start | bytes 1572872 | tf_op jit(solution)/shard_map/ppermute | solution.py:34
  34.7 9.5 %collective-permute-start.9 = (bf16[4,128,512]{2,1,0:T(8,128)(2,1)S(1)}, bf16[4,128,512]{2,1,0:T(8,128)(2,1)S(1)}, u32[]{:S(2)}, u32[]{:S(2)}) collective-permute-start(bf16[4,128,512]{2,1,0:T(8,128)(2,1)S(1)} %pad_maximum_fusion.refs_0_), channel_id=1, source_target_pairs={{0,2},{2,4},{4,6},{6,0},{1,3},{3,5},{5,7},{7,1},{8,10},{10,12},{12... | collective-permute-start | bytes 1572872 | tf_op jit(solution)/shard_map/ppermute | solution.py:34
  44.3 5.7 %collective-permute-start.16 = (bf16[2,128,512]{2,1,0:T(8,128)(2,1)S(1)}, bf16[2,128,512]{2,1,0:T(8,128)(2,1)S(1)}, u32[]{:S(2)}, u32[]{:S(2)}) collective-permute-start(bf16[2,128,512]{2,1,0:T(8,128)(2,1)S(1)} %slice.23), channel_id=1, source_target_pairs={{0,24},{8,0},{16,8},{24,16},{1,25},{9,1},{17,9},{25,17},{2,26},{10... | collective-permute-start | bytes 786440 | tf_op jit(solution)/shard_map/ppermute | solution.py:34
  46.6 6.8 %collective-permute-start.15 = (bf16[2,128,512]{2,1,0:T(8,128)(2,1)S(1)}, bf16[2,128,512]{2,1,0:T(8,128)(2,1)S(1)}, u32[]{:S(2)}, u32[]{:S(2)}) collective-permute-start(bf16[2,128,512]{2,1,0:T(8,128)(2,1)S(1)} %slice.22), channel_id=1, source_target_pairs={{0,8},{8,16},{16,24},{24,0},{1,9},{9,17},{17,25},{25,1},{2,10},{10... | collective-permute-start | bytes 786440 | tf_op jit(solution)/shard_map/ppermute | solution.py:34
  46.6 6.8 %collective-permute-start.14 = (bf16[2,128,512]{2,1,0:T(8,128)(2,1)S(1)}, bf16[2,128,512]{2,1,0:T(8,128)(2,1)S(1)}, u32[]{:S(2)}, u32[]{:S(2)}) collective-permute-start(bf16[2,128,512]{2,1,0:T(8,128)(2,1)S(1)} %slice.21), channel_id=1, source_target_pairs={{0,6},{2,0},{4,2},{6,4},{1,7},{3,1},{5,3},{7,5},{8,14},{10,8},{12,... | collective-permute-start | bytes 786440 | tf_op jit(solution)/shard_map/ppermute | solution.py:34
  46.8 6.8 %collective-permute-start.13 = (bf16[2,128,512]{2,1,0:T(8,128)(2,1)S(1)}, bf16[2,128,512]{2,1,0:T(8,128)(2,1)S(1)}, u32[]{:S(2)}, u32[]{:S(2)}) collective-permute-start(bf16[2,128,512]{2,1,0:T(8,128)(2,1)S(1)} %slice.20), channel_id=1, source_target_pairs={{0,2},{2,4},{4,6},{6,0},{1,3},{3,5},{5,7},{7,1},{8,10},{10,12},{12... | collective-permute-start | bytes 786440 | tf_op jit(solution)/shard_map/ppermute | solution.py:34
  144.5 18.7 %all-to-all-start.5 = ((f32[32,8,128]{2,1,0:T(8,128)}), f32[32,8,128]{2,1,0:T(8,128)S(1)}, u32[]{:S(2)}, u32[]{:S(2)}) async-start(f32[32,8,128]{2,1,0:T(8,128)} %get-tuple-element.81), calls=%async_computation.5 | async-start | bytes 262144 | tf_op jit(solution)/shard_map/all_to_all | solution.py:414
  148.3 10.9 %collective-permute-start.18 = (bf16[256,256]{1,0:T(8,128)(2,1)S(1)}, bf16[256,256]{1,0:T(8,128)(2,1)S(1)}, u32[]{:S(2)}, u32[]{:S(2)}) collective-permute-start(bf16[256,256]{1,0:T(8,128)(2,1)S(1)} %get-tuple-element.83), channel_id=1, source_target_pairs={{0,8},{8,16},{16,24},{24,0},{1,9},{9,17},{17,25},{25,1},{2,10},{10... | collective-permute-start | bytes 393224 | tf_op jit(solution)/shard_map/ppermute | solution.py:34
  149.5 13.7 %collective-permute-start.19 = (bf16[256,256]{1,0:T(8,128)(2,1)S(1)}, bf16[256,256]{1,0:T(8,128)(2,1)S(1)}, u32[]{:S(2)}, u32[]{:S(2)}) collective-permute-start(bf16[256,256]{1,0:T(8,128)(2,1)S(1)} %get-tuple-element.84), channel_id=1, source_target_pairs={{0,16},{8,24},{16,0},{24,8},{1,17},{9,25},{17,1},{25,9},{2,18},{10... | collective-permute-start | bytes 393224 | tf_op jit(solution)/shard_map/ppermute | solution.py:34
  151.9 11.3 %collective-permute-start.20 = (bf16[256,256]{1,0:T(8,128)(2,1)S(1)}, bf16[256,256]{1,0:T(8,128)(2,1)S(1)}, u32[]{:S(2)}, u32[]{:S(2)}) collective-permute-start(bf16[256,256]{1,0:T(8,128)(2,1)S(1)} %get-tuple-element.85), channel_id=1, source_target_pairs={{0,24},{8,0},{16,8},{24,16},{1,25},{9,1},{17,9},{25,17},{2,26},{10... | collective-permute-start | bytes 393224 | tf_op jit(solution)/shard_map/ppermute | solution.py:34
  171.4 9.5 %collective-permute-start.22 = (bf16[256,512]{1,0:T(8,128)(2,1)S(1)}, bf16[256,512]{1,0:T(8,128)(2,1)S(1)}, u32[]{:S(2)}, u32[]{:S(2)}) collective-permute-start(bf16[256,512]{1,0:T(8,128)(2,1)S(1)} %get-tuple-element.92), channel_id=1, source_target_pairs={{0,4},{2,6},{4,0},{6,2},{1,5},{3,7},{5,1},{7,3},{8,12},{10,14},{12... | collective-permute-start | bytes 786440 | tf_op jit(solution)/shard_map/ppermute | solution.py:34
  176.2 10.6 %collective-permute-start.23 = (bf16[256,512]{1,0:T(8,128)(2,1)S(1)}, bf16[256,512]{1,0:T(8,128)(2,1)S(1)}, u32[]{:S(2)}, u32[]{:S(2)}) collective-permute-start(bf16[256,512]{1,0:T(8,128)(2,1)S(1)} %get-tuple-element.93), channel_id=1, source_target_pairs={{0,2},{2,4},{4,6},{6,0},{1,3},{3,5},{5,7},{7,1},{8,10},{10,12},{12... | collective-permute-start | bytes 786440 | tf_op jit(solution)/shard_map/ppermute | solution.py:34
  176.6 10.2 %collective-permute-start.24 = (bf16[256,512]{1,0:T(8,128)(2,1)S(1)}, bf16[256,512]{1,0:T(8,128)(2,1)S(1)}, u32[]{:S(2)}, u32[]{:S(2)}) collective-permute-start(bf16[256,512]{1,0:T(8,128)(2,1)S(1)} %get-tuple-element.94), channel_id=1, source_target_pairs={{0,6},{2,0},{4,2},{6,4},{1,7},{3,1},{5,3},{7,5},{8,14},{10,8},{12,... | collective-permute-start | bytes 786440 | tf_op jit(solution)/shard_map/ppermute | solution.py:34
  (10 other events, 30.8 us)
Sparse Core Ops, SparseCore 0:
  17.7 46.5 all-gather.4
  67.4 93.3 all-gather.6

commit v13 on v12

--- a/solution.py
+++ b/solution.py
@@ -300,75 +300,68 @@
     )(q, parts)
 
 
-def last_kernel(place, q_ref, part_ref, sq_ref, out_ref, f_ref, *refs):
-    w_refs, lane_ref = refs[:X], refs[X]
+def last_kernel(q_ref, part_ref, sq_ref, out_ref, f_ref, w_ref, lane_ref):
     f_ref[...] = -LOG2N - merged(part_ref)
     tile = two_rows(data_row(q_ref, f_ref, lane_ref), jnp.transpose(sq_ref[...])[0:1, :])
     out_ref[...] = jnp.broadcast_to(tile[None], (Z * X, 8, 128))
     column = to_column(tile)
-    for by in range(X):
-        block = lax.rem(place[1] + by, X)
-        for h in range(2):
-            lanes = pl.ds(pl.multiple_of((h * X + block) * 128, 128), 128)
-            w = jnp.exp2((q_ref[:, lanes] + f_ref[pl.ds(h * X + block, 1), :]) - column)
-            w_refs[by][:, pl.ds(h * 128, 128)] = w.astype(BF16)
-
-
-def last_lse(place, q, parts, sq):
+    for r in range(CHUNKS):
+        w = jnp.exp2((q_ref[:, chunk(r)] + f_ref[pl.ds(r, 1), :]) - column)
+        w_ref[r % X, :, chunk(r // X)] = w.astype(BF16)
+
+
+def last_lse(q, parts, sq):
     return pl.pallas_call(
         last_kernel,
-        out_shape=(jax.ShapeDtypeStruct((Z * X, 8, 128), F32), jax.ShapeDtypeStruct((CHUNKS, 128), F32))
-        + (jax.ShapeDtypeStruct((QUARTER, ROWS), BF16),) * X,
-        in_specs=[SMEM] + [VMEM] * 3,
-        out_specs=(VMEM,) * (2 + X),
+        out_shape=(
+            jax.ShapeDtypeStruct((Z * X, 8, 128), F32),
+            jax.ShapeDtypeStruct((CHUNKS, 128), F32),
+            jax.ShapeDtypeStruct((X, QUARTER, ROWS), BF16),
+        ),
+        in_specs=[VMEM] * 3,
+        out_specs=(VMEM,) * 3,
         scratch_shapes=[pltpu.VMEM((QUARTER, 128), F32)],
         compiler_params=params(16),
         name="last_lse",
-    )(place, q, parts, sq)
-
-
-def scale_kernel(place, part_ref, *refs):
-    w_refs, (w_ref, pot_ref) = refs[:X], refs[X:]
-    z, x = place[0], place[1]
+    )(q, parts, sq)
+
+
+def scale_kernel(place, part_ref, block_ref, w_ref, pot_ref):
     for n in range(X):
-        parts = jnp.stack([part_ref[k * X + n, 0:4, :] for k in range(Z)])
+        parts = jnp.stack([part_ref[k * X + n] for k in range(Z)])
         top = jnp.max(parts, axis=0)
         total = top + jnp.log2(jnp.sum(jnp.exp2(parts - top[None]), axis=0))
         pot_ref[pl.ds(2 * n, 2), :] = (-LOG2N - total[0:2]) * (EPS / LOG2E) + parts[0, 2:4] * (1.0 / WIDTH)
-    for by in range(X):
-        n = lax.rem(x - by + X, X)
-        parts = jnp.stack([part_ref[k * X + n] for k in range(Z)])
-        top = jnp.max(parts, axis=0)
-        total = top + jnp.log2(jnp.sum(jnp.exp2(parts - top[None]), axis=0))
-        factor = jnp.exp2(part_ref[z * X + n] - total)
+        factor = jnp.exp2(part_ref[place[0] * X + n] - total)
         factor = jnp.concatenate([factor[0:1], factor[1:2]], axis=1)
-        lanes = pl.ds(pl.multiple_of(n * QUARTER, QUARTER), QUARTER)
         for h in range(2):
-            w = jnp.transpose(w_refs[by][:, pl.ds(h * 128, 128)].astype(F32)) * factor
-            w_ref[pl.ds(h * 128, 128), lanes] = w.astype(BF16)
+            w = jnp.transpose(block_ref[n, :, chunk(h)].astype(F32)) * factor
+            w_ref[pl.ds(h * 128, 128), pl.ds(n * QUARTER, QUARTER)] = w.astype(BF16)
 
 
 def scale(place, parts, blocks):
     return pl.pallas_call(
         scale_kernel,
         out_shape=(jax.ShapeDtypeStruct((ROWS, COUNT), BF16), jax.ShapeDtypeStruct((2 * X, 128), F32)),
-        in_specs=[SMEM] + [VMEM] * (1 + X),
+        in_specs=[SMEM] + [VMEM] * 2,
         out_specs=(VMEM,) * 2,
         compiler_params=params(16),
         name="scale",
-    )(place, parts, *blocks)
+    )(place, parts, blocks)
+
+
+def rows_of(place, data_ref, s, core):
+    y = at(place, 2, s, Y)
+    return jnp.concatenate(
+        [jnp.concatenate([data_ref[n, y, core, from_x(n, k)] for k in range(X)], axis=1) for n in range(X)], axis=0
+    )
 
 
 def transport_kernel(pieces, place, w_ref, got_ref, data_ref, *out_refs):
     lhs = jnp.concatenate([w_ref[...], got_ref[...]], axis=1)
     for s, out_ref in zip(pieces, out_refs):
-        y = at(place, 2, s, Y)
-        rhs = []
-        for core in (place[3], 1 - place[3]):
-            for n in range(X):
-                rhs.append(jnp.concatenate([data_ref[n, y, core, from_x(n, k)] for k in range(X)], axis=1))
-        total = jnp.dot(lhs, jnp.concatenate(rhs, axis=0), preferred_element_type=F32)
-        out_ref[...] = total.astype(out_ref.dtype)
+        rhs = jnp.concatenate([rows_of(place, data_ref, s, core) for core in (place[3], 1 - place[3])], axis=0)
+        out_ref[...] = jnp.dot(lhs, rhs, preferred_element_type=F32).astype(out_ref.dtype)
 
 
 def transport(place, w, got, data, pieces, hand_on):
@@ -409,8 +402,8 @@
         if step < ITERS - 1:
             columns, f = data_lse(q, parts)
             columns = lax.all_to_all(columns, "z", 0, 0)
-    columns, f, *blocks = last_lse(place, q, parts, sq)
-    blocks = [blocks[0]] + [shift(blocks[by], "x", by) for by in range(1, X)]
+    columns, f, blocks = last_lse(q, parts, sq)
+    blocks = lax.all_to_all(blocks, "x", 0, 0)
     columns = lax.all_to_all(columns, ("z", "x"), 0, 0)
     w, pot_g = scale(place, columns, blocks)
     data_all, pot_g = lax.optimization_barrier((data_all, pot_g))

time: 195 us -> 200 us (1.026)
  blocking collectives: 64.2 us -> 87.3 us
  starting transfers between devices: 35.4 us -> 26 us
  waiting for transfers between devices: 49.2 us -> 41.9 us
    all_to_all x0 -> x2, blocking collectives: none -> 23.2 us  [the longest x1 12.8 us: body(): columns = lax.all_to_all(columns, ('z', 'x'), 0, 0)]
    ppermute x25 -> x22, waiting for transfers between devices: 41.1 us -> 33.7 us  [shift(): return lax.ppermute(x, axis, [(j, (j + by) % n) for j in range(n)])]
    ppermute x25 -> x22, starting transfers between devices: 31.5 us -> 25.9 us  [shift(): return lax.ppermute(x, axis, [(j, (j + by) % n) for j in range(n)])]
    all_to_all x1 -> x0, starting transfers between devices: 3.86 us -> none  [body(): columns = lax.all_to_all(columns, ('z', 'x'), 0, 0)]
  transfers between devices with their start and end apart: 28 -> 24, of which waited for: 19 -> 18; matrix products, arithmetic and copies ran while one was open for 1% -> 1% of each run, Pallas kernels for 7% -> 6%
where the time goes in v13:
time: 200 us
  blocking collectives  87.3 us (44%)
  waiting for transfers between devices  41.9 us (21%)
  starting transfers between devices  26 us (13%)
  Pallas kernels  16.8 us (8%)
  between operations  14.2 us (7%)
  local copies, waits for them, and re-layouts  11.2 us (6%)
  other arithmetic  2.39 us (1%)
    all_to_all x3, blocking collectives, body(): parts = lax.all_to_all(rows, ('x', 'y', 'core'), 0, 0)  44.1 us
    ppermute x22, waiting for transfers between devices, shift(): return lax.ppermute(x, axis, [(j, (j + by) % n) for j in range(n)])  33.7 us
    ppermute x22, starting transfers between devices, shift(): return lax.ppermute(x, axis, [(j, (j + by) % n) for j in range(n)])  25.9 us
    all_to_all x2, blocking collectives, body(): columns = lax.all_to_all(columns, 'z', 0, 0)  20 us
    all_to_all x1, blocking collectives, body(): columns = lax.all_to_all(columns, ('z', 'x'), 0, 0)  12.8 us
    all_to_all x1, blocking collectives, body(): blocks = lax.all_to_all(blocks, 'x', 0, 0)  10.4 us
    unnamed x12, local copies, waits for them, and re-layouts  10.1 us
    all_gather x1, waiting for transfers between devices, body(): lax.all_gather(swapped, ('z', 'core')).reshape(Y, C, C, X, QUARTER, SLICE)  8.15 us
  transfers between devices with their start and end apart: 24, of which 18 were waited for; matrix products, arithmetic and copies ran while one was open for 1% of the time, Pallas kernels for 6%

profile of v13, /device:TPU:1, one launch (start us, length us, event | category | flops | bytes accessed | tf_op | source)
XLA Modules:
  0.0 199.8 jit_solution(12042520156220595249)
XLA Ops:
  8.8 2.1 %collective-permute-start = (bf16[256,128]{1,0:T(8,128)(2,1)S(1)}, bf16[256,128]{1,0:T(8,128)(2,1)S(1)}, u32[]{:S(2)}, u32[]{:S(2)}) collective-permute-start(bf16[256,128]{1,0:T(8,128)(2,1)S(1)} %get-tuple-element.47), channel_id=1, source_target_pairs={{0,8},{8,16},{16,24},{24,0},{1,9},{9,17},{17,25},{25,1},{2,10},{10... | collective-permute-start | bytes 196616 | tf_op jit(solution)/shard_map/ppermute | solution.py:34
  10.9 2.5 %collective-permute-start.1 = (bf16[256,128]{1,0:T(8,128)(2,1)S(1)}, bf16[256,128]{1,0:T(8,128)(2,1)S(1)}, u32[]{:S(2)}, u32[]{:S(2)}) collective-permute-start(bf16[256,128]{1,0:T(8,128)(2,1)S(1)} %get-tuple-element.48), channel_id=1, source_target_pairs={{0,16},{8,24},{16,0},{24,8},{1,17},{9,25},{17,1},{25,9},{2,18},{10... | collective-permute-start | bytes 196616 | tf_op jit(solution)/shard_map/ppermute | solution.py:34
  18.6 3.2 %collective-permute-start.8 = (bf16[128,512]{1,0:T(8,128)(2,1)S(1)}, bf16[128,512]{1,0:T(8,128)(2,1)S(1)}, u32[]{:S(2)}, u32[]{:S(2)}) collective-permute-start(bf16[128,512]{1,0:T(8,128)(2,1)S(1)} %get-tuple-element.56), channel_id=1, source_target_pairs={{0,4},{2,6},{4,0},{6,2},{1,5},{3,7},{5,1},{7,3},{8,12},{10,14},{12... | collective-permute-start | bytes 393224 | tf_op jit(solution)/shard_map/ppermute | solution.py:34
  30.1 2.0 %collective-permute-done.3 = bf16[128,512]{1,0:T(8,128)(2,1)S(1)} collective-permute-done((bf16[128,512]{1,0:T(8,128)(2,1)S(1)}, bf16[128,512]{1,0:T(8,128)(2,1)S(1)}, u32[]{:S(2)}, u32[]{:S(2)}) %collective-permute-start.3) | collective-permute-done | bytes 131104 | tf_op jit(solution)/shard_map/ppermute | solution.py:34
  35.4 7.1 %collective-permute-done.12.refs_7_ = bf16[4,128,512]{2,1,0:T(8,128)(2,1)S(1)} collective-permute-done((bf16[4,128,512]{2,1,0:T(8,128)(2,1)S(1)}, bf16[4,128,512]{2,1,0:T(8,128)(2,1)S(1)}, u32[]{:S(2)}, u32[]{:S(2)}) %collective-permute-start.12) | collective-permute-done | bytes 524320 | tf_op jit(solution)/shard_map/ppermute | solution.py:34
  44.3 2.3 %collective-permute-start.16 = (bf16[2,128,512]{2,1,0:T(8,128)(2,1)S(1)}, bf16[2,128,512]{2,1,0:T(8,128)(2,1)S(1)}, u32[]{:S(2)}, u32[]{:S(2)}) collective-permute-start(bf16[2,128,512]{2,1,0:T(8,128)(2,1)S(1)} %slice.23), channel_id=1, source_target_pairs={{0,24},{8,0},{16,8},{24,16},{1,25},{9,1},{17,9},{25,17},{2,26},{10... | collective-permute-start | bytes 786440 | tf_op jit(solution)/shard_map/ppermute | solution.py:34
  48.1 1.9 collective-permute-done.16.refs_9_
  50.0 3.4 %collective-permute-done.15.refs_8_ = bf16[2,128,512]{2,1,0:T(8,128)(2,1)S(1)} collective-permute-done((bf16[2,128,512]{2,1,0:T(8,128)(2,1)S(1)}, bf16[2,128,512]{2,1,0:T(8,128)(2,1)S(1)}, u32[]{:S(2)}, u32[]{:S(2)}) %collective-permute-start.15) | collective-permute-done | bytes 262176 | tf_op jit(solution)/shard_map/ppermute | solution.py:34
  54.1 2.0 %copy-done.2 = bf16[1024,2048]{1,0:T(8,128)(2,1)} copy-done((bf16[1024,2048]{1,0:T(8,128)(2,1)}, bf16[1024,2048]{1,0:T(8,128)(2,1)S(1)}, u32[]{:S(2)}) %copy-start.2) | copy-done | bytes 4194328
  56.1 8.1 %all-gather.5.cloned.1.call-done = bf16[64,256,128]{2,1,0:T(8,128)(2,1)} async-done(((bf16[4,256,128]{2,1,0:T(8,128)(2,1)}), bf16[64,256,128]{2,1,0:T(8,128)(2,1)}) %all-gather.5.cloned.1.call-update) | async-done | bytes 4194320 | tf_op jit(solution)/shard_map/all_gather | solution.py:391
  64.3 3.0 %pick.1.data_ref = bf16[4,2,4,256,128]{4,3,2,1,0:T(8,128)(2,1)} custom-call(s32[4]{0:T(128)S(1)} %pad_add_fusion.place, bf16[4,2,2,4,256,128]{5,4,3,2,1,0:T(8,128)(2,1)} %bitcast.32), custom_call_target="tpu_custom_call" | custom-call | tf_op jit(solution)/shard_map/pick/pallas_call | solution.py:145
  68.8 2.2 %copy-done.3 = bf16[1024,2048]{1,0:T(8,128)(2,1)S(1)} copy-done((bf16[1024,2048]{1,0:T(8,128)(2,1)S(1)}, bf16[1024,2048]{1,0:T(8,128)(2,1)}, u32[]{:S(2)}) %copy-start.3) | copy-done | bytes 4194328
  73.3 1.9 ours.1
  76.3 16.4 %all_to_all.35.part_ref = f32[32,8,128]{2,1,0:T(8,128)S(1)} all-to-all(f32[32,8,128]{2,1,0:T(8,128)S(1)} %get-tuple-element.72), channel_id=1, replica_groups=mesh['z'=8,'x'=4,'y'=4,'core'=2] {'x','y','core'}, dimensions={0} | all-to-all | bytes 262144 | tf_op jit(solution)/shard_map/all_to_all | solution.py:401
  93.5 10.8 %all_to_all.36.part_ref = f32[8,8,128]{2,1,0:T(8,128)S(1)} all-to-all(f32[8,8,128]{2,1,0:T(8,128)S(1)} %get-tuple-element.73), channel_id=1, replica_groups=mesh['z'=8,'x'=4,'y'=4,'core'=2] {'z'}, dimensions={0} | all-to-all | bytes 65536 | tf_op jit(solution)/shard_map/all_to_all | solution.py:404
  104.7 14.0 %all_to_all.37.part_ref = f32[32,8,128]{2,1,0:T(8,128)S(1)} all-to-all(f32[32,8,128]{2,1,0:T(8,128)S(1)} %noise_lse.2), channel_id=1, replica_groups=mesh['z'=8,'x'=4,'y'=4,'core'=2] {'x','y','core'}, dimensions={0} | all-to-all | bytes 262144 | tf_op jit(solution)/shard_map/all_to_all | solution.py:401
  119.5 9.2 %all_to_all.38.part_ref = f32[8,8,128]{2,1,0:T(8,128)S(1)} all-to-all(f32[8,8,128]{2,1,0:T(8,128)S(1)} %get-tuple-element.74), channel_id=1, replica_groups=mesh['z'=8,'x'=4,'y'=4,'core'=2] {'z'}, dimensions={0} | all-to-all | bytes 65536 | tf_op jit(solution)/shard_map/all_to_all | solution.py:404
  129.1 13.7 %all_to_all.39.part_ref = f32[32,8,128]{2,1,0:T(8,128)S(1)} all-to-all(f32[32,8,128]{2,1,0:T(8,128)S(1)} %noise_lse.3), channel_id=1, replica_groups=mesh['z'=8,'x'=4,'y'=4,'core'=2] {'x','y','core'}, dimensions={0} | all-to-all | bytes 262144 | tf_op jit(solution)/shard_map/all_to_all | solution.py:401
  143.4 12.8 %all_to_all.40.part_ref = f32[32,8,128]{2,1,0:T(8,128)S(1)} all-to-all(f32[32,8,128]{2,1,0:T(8,128)S(1)} %get-tuple-element.78), channel_id=1, replica_groups=mesh['z'=8,'x'=4,'y'=4,'core'=2] {'z','x'}, dimensions={0} | all-to-all | bytes 262144 | tf_op jit(solution)/shard_map/all_to_all | solution.py:407
  156.2 10.4 %all_to_all.41.block_ref = bf16[4,256,256]{2,1,0:T(8,128)(2,1)S(1)} all-to-all(bf16[4,256,256]{2,1,0:T(8,128)(2,1)S(1)} %get-tuple-element.79), channel_id=1, replica_groups=mesh['z'=8,'x'=4,'y'=4,'core'=2] {'x'}, dimensions={0} | all-to-all | bytes 1048576 | tf_op jit(solution)/shard_map/all_to_all | solution.py:406
  167.9 2.6 %collective-permute-start.18 = (bf16[256,1024]{1,0:T(8,128)(2,1)S(1)}, bf16[256,1024]{1,0:T(8,128)(2,1)S(1)}, u32[]{:S(2)}, u32[]{:S(2)}) collective-permute-start(bf16[256,1024]{1,0:T(8,128)(2,1)S(1)} %get-tuple-element.82.w_ref), channel_id=1, source_target_pairs={{0,1},{1,0},{2,3},{3,2},{4,5},{5,4},{6,7},{7,6},{8,9},{9,8},{10,11... | collective-permute-start | bytes 1572872 | tf_op jit(solution)/shard_map/ppermute | solution.py:34
  172.0 3.4 %copy-done = bf16[16,2,4,256,128]{4,3,2,1,0:T(8,128)(2,1)S(1)} copy-done((bf16[16,2,4,256,128]{4,3,2,1,0:T(8,128)(2,1)S(1)}, bf16[16,2,4,256,128]{4,3,2,1,0:T(8,128)(2,1)}, u32[]{:S(2)}) %copy-start) | copy-done | bytes 8388632
  183.4 2.4 %collective-permute-done.19 = bf16[256,512]{1,0:T(8,128)(2,1)S(1)} collective-permute-done((bf16[256,512]{1,0:T(8,128)(2,1)S(1)}, bf16[256,512]{1,0:T(8,128)(2,1)S(1)}, u32[]{:S(2)}, u32[]{:S(2)}) %collective-permute-start.19) | collective-permute-done | bytes 262176 | tf_op jit(solution)/shard_map/ppermute | solution.py:34
  185.8 6.3 %collective-permute-done.20 = bf16[256,512]{1,0:T(8,128)(2,1)S(1)} collective-permute-done((bf16[256,512]{1,0:T(8,128)(2,1)S(1)}, bf16[256,512]{1,0:T(8,128)(2,1)S(1)}, u32[]{:S(2)}, u32[]{:S(2)}) %collective-permute-start.20) | collective-permute-done | bytes 262176 | tf_op jit(solution)/shard_map/ppermute | solution.py:34
  (72 shorter events, 41.8 us)
Async XLA Ops:
  7.2 57.1 %all-gather.5.cloned.1.call-start = ((), (), s32[]{:S(2)}) async-start(), calls=%async_computation.7 | async-start | bytes 4456448 | tf_op jit(solution)/shard_map/all_gather | solution.py:391
  8.8 5.7 %collective-permute-start = (bf16[256,128]{1,0:T(8,128)(2,1)S(1)}, bf16[256,128]{1,0:T(8,128)(2,1)S(1)}, u32[]{:S(2)}, u32[]{:S(2)}) collective-permute-start(bf16[256,128]{1,0:T(8,128)(2,1)S(1)} %get-tuple-element.47), channel_id=1, source_target_pairs={{0,8},{8,16},{16,24},{24,0},{1,9},{9,17},{17,25},{25,1},{2,10},{10... | collective-permute-start | bytes 196616 | tf_op jit(solution)/shard_map/ppermute | solution.py:34
  10.9 5.1 %collective-permute-start.1 = (bf16[256,128]{1,0:T(8,128)(2,1)S(1)}, bf16[256,128]{1,0:T(8,128)(2,1)S(1)}, u32[]{:S(2)}, u32[]{:S(2)}) collective-permute-start(bf16[256,128]{1,0:T(8,128)(2,1)S(1)} %get-tuple-element.48), channel_id=1, source_target_pairs={{0,16},{8,24},{16,0},{24,8},{1,17},{9,25},{17,1},{25,9},{2,18},{10... | collective-permute-start | bytes 196616 | tf_op jit(solution)/shard_map/ppermute | solution.py:34
  13.4 3.4 %collective-permute-start.2 = (bf16[256,128]{1,0:T(8,128)(2,1)S(1)}, bf16[256,128]{1,0:T(8,128)(2,1)S(1)}, u32[]{:S(2)}, u32[]{:S(2)}) collective-permute-start(bf16[256,128]{1,0:T(8,128)(2,1)S(1)} %get-tuple-element.49), channel_id=1, source_target_pairs={{0,24},{8,0},{16,8},{24,16},{1,25},{9,1},{17,9},{25,17},{2,26},{10... | collective-permute-start | bytes 196616 | tf_op jit(solution)/shard_map/ppermute | solution.py:34
  17.6 152.9 %all-gather.7.cloned.1.call-start = ((), (), s32[]{:S(2)}) async-start(), calls=%async_computation.8 | async-start | bytes 10485760 | tf_op jit(solution)/shard_map/all_gather | solution.py:394
  18.6 6.9 %collective-permute-start.8 = (bf16[128,512]{1,0:T(8,128)(2,1)S(1)}, bf16[128,512]{1,0:T(8,128)(2,1)S(1)}, u32[]{:S(2)}, u32[]{:S(2)}) collective-permute-start(bf16[128,512]{1,0:T(8,128)(2,1)S(1)} %get-tuple-element.56), channel_id=1, source_target_pairs={{0,4},{2,6},{4,0},{6,2},{1,5},{3,7},{5,1},{7,3},{8,12},{10,14},{12... | collective-permute-start | bytes 393224 | tf_op jit(solution)/shard_map/ppermute | solution.py:34
  21.8 4.9 %collective-permute-start.7 = (bf16[128,512]{1,0:T(8,128)(2,1)S(1)}, bf16[128,512]{1,0:T(8,128)(2,1)S(1)}, u32[]{:S(2)}, u32[]{:S(2)}) collective-permute-start(bf16[128,512]{1,0:T(8,128)(2,1)S(1)} %get-tuple-element.56), channel_id=1, source_target_pairs={{0,6},{2,0},{4,2},{6,4},{1,7},{3,1},{5,3},{7,5},{8,14},{10,8},{12,... | collective-permute-start | bytes 393224 | tf_op jit(solution)/shard_map/ppermute | solution.py:34
  22.6 6.0 %collective-permute-start.6 = (bf16[128,512]{1,0:T(8,128)(2,1)S(1)}, bf16[128,512]{1,0:T(8,128)(2,1)S(1)}, u32[]{:S(2)}, u32[]{:S(2)}) collective-permute-start(bf16[128,512]{1,0:T(8,128)(2,1)S(1)} %get-tuple-element.56), channel_id=1, source_target_pairs={{0,2},{2,4},{4,6},{6,0},{1,3},{3,5},{5,7},{7,1},{8,10},{10,12},{12... | collective-permute-start | bytes 393224 | tf_op jit(solution)/shard_map/ppermute | solution.py:34
  23.3 5.3 %collective-permute-start.5 = (bf16[128,512]{1,0:T(8,128)(2,1)S(1)}, bf16[128,512]{1,0:T(8,128)(2,1)S(1)}, u32[]{:S(2)}, u32[]{:S(2)}) collective-permute-start(bf16[128,512]{1,0:T(8,128)(2,1)S(1)} %get-tuple-element.52), channel_id=1, source_target_pairs={{0,16},{8,24},{16,0},{24,8},{1,17},{9,25},{17,1},{25,9},{2,18},{10... | collective-permute-start | bytes 393224 | tf_op jit(solution)/shard_map/ppermute | solution.py:34
  24.3 5.7 %collective-permute-start.4 = (bf16[128,512]{1,0:T(8,128)(2,1)S(1)}, bf16[128,512]{1,0:T(8,128)(2,1)S(1)}, u32[]{:S(2)}, u32[]{:S(2)}) collective-permute-start(bf16[128,512]{1,0:T(8,128)(2,1)S(1)} %get-tuple-element.52), channel_id=1, source_target_pairs={{0,24},{8,0},{16,8},{24,16},{1,25},{9,1},{17,9},{25,17},{2,26},{10... | collective-permute-start | bytes 393224 | tf_op jit(solution)/shard_map/ppermute | solution.py:34
  25.5 6.7 %collective-permute-start.3 = (bf16[128,512]{1,0:T(8,128)(2,1)S(1)}, bf16[128,512]{1,0:T(8,128)(2,1)S(1)}, u32[]{:S(2)}, u32[]{:S(2)}) collective-permute-start(bf16[128,512]{1,0:T(8,128)(2,1)S(1)} %get-tuple-element.52), channel_id=1, source_target_pairs={{0,8},{8,16},{16,24},{24,0},{1,9},{9,17},{17,25},{25,1},{2,10},{10... | collective-permute-start | bytes 393224 | tf_op jit(solution)/shard_map/ppermute | solution.py:34
  32.2 10.3 %collective-permute-start.12 = (bf16[4,128,512]{2,1,0:T(8,128)(2,1)S(1)}, bf16[4,128,512]{2,1,0:T(8,128)(2,1)S(1)}, u32[]{:S(2)}, u32[]{:S(2)}) collective-permute-start(bf16[4,128,512]{2,1,0:T(8,128)(2,1)S(1)} %pad_maximum_fusion.1.refs_5_), channel_id=1, source_target_pairs={{0,24},{8,0},{16,8},{24,16},{1,25},{9,1},{17,9},{25,17},{2,26},{10... | collective-permute-start | bytes 1572872 | tf_op jit(solution)/shard_map/ppermute | solution.py:34
  32.4 10.4 %collective-permute-start.11 = (bf16[4,128,512]{2,1,0:T(8,128)(2,1)S(1)}, bf16[4,128,512]{2,1,0:T(8,128)(2,1)S(1)}, u32[]{:S(2)}, u32[]{:S(2)}) collective-permute-start(bf16[4,128,512]{2,1,0:T(8,128)(2,1)S(1)} %pad_maximum_fusion.1.refs_5_), channel_id=1, source_target_pairs={{0,8},{8,16},{16,24},{24,0},{1,9},{9,17},{17,25},{25,1},{2,10},{10... | collective-permute-start | bytes 1572872 | tf_op jit(solution)/shard_map/ppermute | solution.py:34
  33.8 9.7 %collective-permute-start.10 = (bf16[4,128,512]{2,1,0:T(8,128)(2,1)S(1)}, bf16[4,128,512]{2,1,0:T(8,128)(2,1)S(1)}, u32[]{:S(2)}, u32[]{:S(2)}) collective-permute-start(bf16[4,128,512]{2,1,0:T(8,128)(2,1)S(1)} %pad_maximum_fusion.refs_0_), channel_id=1, source_target_pairs={{0,6},{2,0},{4,2},{6,4},{1,7},{3,1},{5,3},{7,5},{8,14},{10,8},{12,... | collective-permute-start | bytes 1572872 | tf_op jit(solution)/shard_map/ppermute | solution.py:34
  34.7 9.5 %collective-permute-start.9 = (bf16[4,128,512]{2,1,0:T(8,128)(2,1)S(1)}, bf16[4,128,512]{2,1,0:T(8,128)(2,1)S(1)}, u32[]{:S(2)}, u32[]{:S(2)}) collective-permute-start(bf16[4,128,512]{2,1,0:T(8,128)(2,1)S(1)} %pad_maximum_fusion.refs_0_), channel_id=1, source_target_pairs={{0,2},{2,4},{4,6},{6,0},{1,3},{3,5},{5,7},{7,1},{8,10},{10,12},{12... | collective-permute-start | bytes 1572872 | tf_op jit(solution)/shard_map/ppermute | solution.py:34
  44.3 5.7 %collective-permute-start.16 = (bf16[2,128,512]{2,1,0:T(8,128)(2,1)S(1)}, bf16[2,128,512]{2,1,0:T(8,128)(2,1)S(1)}, u32[]{:S(2)}, u32[]{:S(2)}) collective-permute-start(bf16[2,128,512]{2,1,0:T(8,128)(2,1)S(1)} %slice.23), channel_id=1, source_target_pairs={{0,24},{8,0},{16,8},{24,16},{1,25},{9,1},{17,9},{25,17},{2,26},{10... | collective-permute-start | bytes 786440 | tf_op jit(solution)/shard_map/ppermute | solution.py:34
  46.6 6.8 %collective-permute-start.15 = (bf16[2,128,512]{2,1,0:T(8,128)(2,1)S(1)}, bf16[2,128,512]{2,1,0:T(8,128)(2,1)S(1)}, u32[]{:S(2)}, u32[]{:S(2)}) collective-permute-start(bf16[2,128,512]{2,1,0:T(8,128)(2,1)S(1)} %slice.22), channel_id=1, source_target_pairs={{0,8},{8,16},{16,24},{24,0},{1,9},{9,17},{17,25},{25,1},{2,10},{10... | collective-permute-start | bytes 786440 | tf_op jit(solution)/shard_map/ppermute | solution.py:34
  46.6 6.8 %collective-permute-start.14 = (bf16[2,128,512]{2,1,0:T(8,128)(2,1)S(1)}, bf16[2,128,512]{2,1,0:T(8,128)(2,1)S(1)}, u32[]{:S(2)}, u32[]{:S(2)}) collective-permute-start(bf16[2,128,512]{2,1,0:T(8,128)(2,1)S(1)} %slice.21), channel_id=1, source_target_pairs={{0,6},{2,0},{4,2},{6,4},{1,7},{3,1},{5,3},{7,5},{8,14},{10,8},{12,... | collective-permute-start | bytes 786440 | tf_op jit(solution)/shard_map/ppermute | solution.py:34
  46.8 6.8 %collective-permute-start.13 = (bf16[2,128,512]{2,1,0:T(8,128)(2,1)S(1)}, bf16[2,128,512]{2,1,0:T(8,128)(2,1)S(1)}, u32[]{:S(2)}, u32[]{:S(2)}) collective-permute-start(bf16[2,128,512]{2,1,0:T(8,128)(2,1)S(1)} %slice.20), channel_id=1, source_target_pairs={{0,2},{2,4},{4,6},{6,0},{1,3},{3,5},{5,7},{7,1},{8,10},{10,12},{12... | collective-permute-start | bytes 786440 | tf_op jit(solution)/shard_map/ppermute | solution.py:34
  72.9 3.0 %collective-permute-start.17 = (f32[264,1152]{1,0:T(8,128)S(1)}, f32[264,1152]{1,0:T(8,128)S(1)}, u32[]{:S(2)}, u32[]{:S(2)}) collective-permute-start(f32[264,1152]{1,0:T(8,128)S(1)} %theirs.1), channel_id=1, source_target_pairs={{0,1},{1,0},{2,3},{3,2},{4,5},{5,4},{6,7},{7,6},{8,9},{9,8},{10,11... | collective-permute-start | bytes 3649544 | tf_op jit(solution)/shard_map/ppermute | solution.py:34
  167.9 4.1 %collective-permute-start.18 = (bf16[256,1024]{1,0:T(8,128)(2,1)S(1)}, bf16[256,1024]{1,0:T(8,128)(2,1)S(1)}, u32[]{:S(2)}, u32[]{:S(2)}) collective-permute-start(bf16[256,1024]{1,0:T(8,128)(2,1)S(1)} %get-tuple-element.82.w_ref), channel_id=1, source_target_pairs={{0,1},{1,0},{2,3},{3,2},{4,5},{5,4},{6,7},{7,6},{8,9},{9,8},{10,11... | collective-permute-start | bytes 1572872 | tf_op jit(solution)/shard_map/ppermute | solution.py:34
  176.6 9.2 %collective-permute-start.19 = (bf16[256,512]{1,0:T(8,128)(2,1)S(1)}, bf16[256,512]{1,0:T(8,128)(2,1)S(1)}, u32[]{:S(2)}, u32[]{:S(2)}) collective-permute-start(bf16[256,512]{1,0:T(8,128)(2,1)S(1)} %get-tuple-element.86), channel_id=1, source_target_pairs={{0,4},{2,6},{4,0},{6,2},{1,5},{3,7},{5,1},{7,3},{8,12},{10,14},{12... | collective-permute-start | bytes 786440 | tf_op jit(solution)/shard_map/ppermute | solution.py:34
  178.6 13.5 %collective-permute-start.20 = (bf16[256,512]{1,0:T(8,128)(2,1)S(1)}, bf16[256,512]{1,0:T(8,128)(2,1)S(1)}, u32[]{:S(2)}, u32[]{:S(2)}) collective-permute-start(bf16[256,512]{1,0:T(8,128)(2,1)S(1)} %get-tuple-element.87), channel_id=1, source_target_pairs={{0,2},{2,4},{4,6},{6,0},{1,3},{3,5},{5,7},{7,1},{8,10},{10,12},{12... | collective-permute-start | bytes 786440 | tf_op jit(solution)/shard_map/ppermute | solution.py:34
  180.3 11.8 %collective-permute-start.21 = (bf16[256,512]{1,0:T(8,128)(2,1)S(1)}, bf16[256,512]{1,0:T(8,128)(2,1)S(1)}, u32[]{:S(2)}, u32[]{:S(2)}) collective-permute-start(bf16[256,512]{1,0:T(8,128)(2,1)S(1)} %get-tuple-element.88), channel_id=1, source_target_pairs={{0,6},{2,0},{4,2},{6,4},{1,7},{3,1},{5,3},{7,5},{8,14},{10,8},{12,... | collective-permute-start | bytes 786440 | tf_op jit(solution)/shard_map/ppermute | solution.py:34
  (6 other events, 20.1 us)
Sparse Core Ops, SparseCore 0:
  17.7 46.5 all-gather.4
  67.4 90.1 all-gather.6

commit v14 on v11

--- a/solution.py
+++ b/solution.py
@@ -128,21 +128,29 @@
     )(*parts)
 
 
-def pick_kernel(place, all_ref, out_ref, sems):
-    copies = [pltpu.make_async_copy(all_ref.at[y, place[3]], out_ref.at[y], sems.at[y]) for y in range(Y)]
-    for copy in copies:
+def pick_kernel(place, all_ref, far_ref, near_ref, buffer_ref, sems):
+    ins, outs = [], []
+    for s in range(Y):
+        ins.append(pltpu.make_async_copy(all_ref.at[at(place, 2, s, Y), place[3]], buffer_ref.at[s], sems.at[0, s]))
+        out = far_ref.at[s - 1] if s else near_ref
+        outs.append(pltpu.make_async_copy(buffer_ref.at[s], out, sems.at[1, s]))
+    for copy in ins:
         copy.start()
-    for copy in copies:
+    for s in range(Y):
+        ins[s].wait()
+        outs[s].start()
+    for copy in outs:
         copy.wait()
 
 
 def pick(place, samples):
+    part = (C, X, QUARTER, SLICE)
     return pl.pallas_call(
         pick_kernel,
-        out_shape=jax.ShapeDtypeStruct((Y, C, X, QUARTER, SLICE), BF16),
+        out_shape=(jax.ShapeDtypeStruct((Y - 1, *part), BF16), jax.ShapeDtypeStruct(part, BF16)),
         in_specs=[SMEM, pl.BlockSpec(memory_space=pl.ANY)],
-        out_specs=pl.BlockSpec(memory_space=pl.ANY),
-        scratch_shapes=[pltpu.SemaphoreType.DMA((Y,))],
+        out_specs=(pl.BlockSpec(memory_space=pl.ANY),) * 2,
+        scratch_shapes=[pltpu.VMEM((Y, *part), BF16), pltpu.SemaphoreType.DMA((2, Y))],
         compiler_params=params(53),
         name="pick",
     )(place, samples)
@@ -164,51 +172,52 @@
     )(place, data.reshape(X, QUARTER, SLICE))
 
 
-def partial_scores(place, data_ref, core, noise_ref, q_ref, sq_ref):
-    pieces = [at(place, 2, rel, Y) for rel in AROUND]
-    lhs = jnp.concatenate([data_ref[p, core, from_x(place[1], n)] for p in pieces for n in range(X)], axis=1)
+def partial_scores(place, far_ref, near_ref, core, noise_ref, q_ref, sq_ref):
+    pieces = [far_ref.at[rel % Y - 1] if rel else near_ref for rel in AROUND]
+    lhs = jnp.concatenate([piece[core, from_x(place[1], n)] for piece in pieces for n in range(X)], axis=1)
     for h in range(2):
         rhs = noise_ref[pl.ds(h * X * CUT, X * CUT), :]
         gram = lax.dot_general(lhs, rhs, (((1,), (1,)), ((), ())), preferred_element_type=F32) * (2.0 * UNIT)
         for j, rel in enumerate(AROUND):
             lanes = pl.ds(pl.multiple_of((h * X + at(place, 1, rel, X)) * 128, 128), 128)
             q_ref[:QUARTER, lanes] = gram[:, j * 128 : (j + 1) * 128]
-    sq_ref[...] = squares(data_ref, [(p, core, n) for p in range(Y) for n in range(X)])
-
-
-def theirs_kernel(place, data_ref, noise_ref, sqn_ref, out_ref, sq_ref):
-    partial_scores(place, data_ref, 1 - place[3], noise_ref, out_ref, sq_ref)
+    total = [squares(piece, [(core, n) for n in range(X)]) for piece in pieces]
+    sq_ref[...] = (total[0] + total[3]) + (total[1] + total[2])
+
+
+def theirs_kernel(place, far_ref, near_ref, noise_ref, sqn_ref, out_ref, sq_ref):
+    partial_scores(place, far_ref, near_ref, 1 - place[3], noise_ref, out_ref, sq_ref)
     out_ref[:QUARTER, TALL:] = sq_ref[...]
     out_ref[QUARTER:, :] = jnp.zeros((8, TALL + 128), F32)
     out_ref[QUARTER : QUARTER + 2, :128] = sqn_ref[...]
 
 
-def theirs(place, data, noise, sqn):
+def theirs(place, far, near, noise, sqn):
     return pl.pallas_call(
         theirs_kernel,
         out_shape=jax.ShapeDtypeStruct((QUARTER + 8, TALL + 128), F32),
-        in_specs=[SMEM] + [VMEM] * 3,
+        in_specs=[SMEM] + [VMEM] * 4,
         out_specs=VMEM,
         scratch_shapes=[pltpu.VMEM((QUARTER, 128), F32)],
         compiler_params=params(24),
         name="theirs",
-    )(place, data, noise, sqn)
-
-
-def ours_kernel(place, data_ref, noise_ref, q_ref, sq_ref):
-    partial_scores(place, data_ref, place[3], noise_ref, q_ref, sq_ref)
-
-
-def ours(place, data, noise):
+    )(place, far, near, noise, sqn)
+
+
+def ours_kernel(place, far_ref, near_ref, noise_ref, q_ref, sq_ref):
+    partial_scores(place, far_ref, near_ref, place[3], noise_ref, q_ref, sq_ref)
+
+
+def ours(place, far, near, noise):
     return pl.pallas_call(
         ours_kernel,
         out_shape=(jax.ShapeDtypeStruct((QUARTER, TALL), F32), jax.ShapeDtypeStruct((QUARTER, 128), F32)),
-        in_specs=[SMEM] + [VMEM] * 2,
+        in_specs=[SMEM] + [VMEM] * 3,
         out_specs=(VMEM,) * 2,
         compiler_params=params(24),
         cost_estimate=pl.CostEstimate(flops=QUARTER * TALL * WIDTH, bytes_accessed=6 * 2**20, transcendentals=0),
         name="ours",
-    )(place, data, noise)
+    )(place, far, near, noise)
 
 
 def score_kernel(mine_ref, sq_mine_ref, sqn_mine_ref, got_ref, q_ref, out_ref, sq_ref, sqn_ref, lse_ref):
@@ -357,17 +366,16 @@
 def transport_kernel(pieces, place, w_ref, got_ref, data_ref, *out_refs):
     lhs = jnp.concatenate([w_ref[...], got_ref[...]], axis=1)
     for s, out_ref in zip(pieces, out_refs):
-        y = at(place, 2, s, Y)
         rhs = []
         for core in (place[3], 1 - place[3]):
             for n in range(X):
-                rhs.append(jnp.concatenate([data_ref[n, y, core, from_x(n, k)] for k in range(X)], axis=1))
+                rhs.append(jnp.concatenate([data_ref[n, s - 1, core, from_x(n, k)] for k in range(X)], axis=1))
         total = jnp.dot(lhs, jnp.concatenate(rhs, axis=0), preferred_element_type=F32)
         out_ref[...] = total.astype(out_ref.dtype)
 
 
 def transport(place, w, got, data, pieces, hand_on):
-    kinds = [jax.ShapeDtypeStruct((ROWS, SHARE), BF16 if s else F32) for s in pieces]
+    kinds = [jax.ShapeDtypeStruct((ROWS, SHARE), BF16) for _ in pieces]
     if hand_on:
         kinds.append(jax.ShapeDtypeStruct(data.shape, data.dtype))
     return pl.pallas_call(
@@ -384,6 +392,55 @@
     )(place, w, got, data)
 
 
+def near_scale_kernel(place, part_ref, *refs):
+    blocks, out_ref = refs[:X], refs[X]
+    parts = jnp.stack([part_ref[k * X + place[1]] for k in range(Z)])
+    top = jnp.max(parts, axis=0)
+    total = top + jnp.log2(jnp.sum(jnp.exp2(parts - top[None]), axis=0))
+    column = to_column(jnp.exp2(part_ref[place[0] * X + place[1]] - total))
+    for by in range(X):
+        for h in range(2):
+            out_ref[by, :, chunk(h)] = (blocks[by][:, chunk(h)].astype(F32) * column).astype(BF16)
+
+
+def near_scale(place, parts, blocks):
+    return pl.pallas_call(
+        near_scale_kernel,
+        out_shape=jax.ShapeDtypeStruct((X, QUARTER, ROWS), BF16),
+        in_specs=[SMEM] + [VMEM] * (1 + X),
+        out_specs=VMEM,
+        compiler_params=params(16),
+        name="near_scale",
+    )(place, parts, *blocks)
+
+
+def near_kernel(place, w_ref, got_ref, data_ref, own_ref, *out_refs):
+    rhs = [
+        jnp.concatenate([data_ref[core, from_x(place[1], k)] for k in range(X)], axis=1)
+        for core in (place[3], 1 - place[3])
+    ]
+    rhs = jnp.concatenate(rhs, axis=0)
+    for by in range(X):
+        lhs = jnp.concatenate([w_ref[by], got_ref[by]], axis=0)
+        total = lax.dot_general(lhs, rhs, (((0,), (0,)), ((), ())), preferred_element_type=F32)
+        if by:
+            out_refs[by - 1][...] = total.astype(BF16)
+        else:
+            own_ref[...] = total
+
+
+def near_transport(place, w, got, data):
+    return pl.pallas_call(
+        near_kernel,
+        out_shape=(jax.ShapeDtypeStruct((ROWS, SHARE), F32),)
+        + (jax.ShapeDtypeStruct((ROWS, SHARE), BF16),) * (X - 1),
+        in_specs=[SMEM] + [VMEM] * 3,
+        out_specs=(VMEM,) * X,
+        compiler_params=params(16),
+        name="near",
+    )(place, w, got, data)
+
+
 def body(noise, data):
     z, x, y, c = (lax.axis_index(a) for a in ("z", "x", "y", "core"))
     place = jnp.stack([z, x, y, c]).astype(jnp.int32)
@@ -392,10 +449,10 @@
     noise_after, swapped = lax.optimization_barrier((noise, swapped))
     samples = lax.all_gather(swapped, ("z", "core")).reshape(Y, C, C, X, QUARTER, SLICE)
     samples, noise_all, sqn_mine = lax.optimization_barrier((samples, *collect(gather_noise(noise_after))))
-    samples = pick(place, samples)
-    data_all = lax.all_gather(samples, "x")
-    got = shift(theirs(place, samples, noise_all, sqn_mine), "core", 1)
-    mine, sq_mine = ours(place, samples, noise_all)
+    far, near = pick(place, samples)
+    data_all = lax.all_gather(far, "x")
+    got = shift(theirs(place, far, near, noise_all, sqn_mine), "core", 1)
+    mine, sq_mine = ours(place, far, near, noise_all)
     q, rows, sq, sq_noise = score(mine, sq_mine, sqn_mine, got)
     for step in range(ITERS):
         if step:
@@ -405,16 +462,20 @@
             columns, f = data_lse(q, parts)
             columns = lax.all_to_all(columns, "z", 0, 0)
     columns, f, *blocks = last_lse(place, q, parts, sq)
-    blocks = [blocks[0]] + [shift(blocks[by], "x", by) for by in range(1, X)]
+    given, blocks = blocks, [blocks[0]] + [shift(blocks[by], "x", by) for by in range(1, X)]
     columns = lax.all_to_all(columns, ("z", "x"), 0, 0)
     w, pot_g = scale(place, columns, blocks)
     data_all, pot_g = lax.optimization_barrier((data_all, pot_g))
     got = shift(w, "core", 1)
     opposite, data_all = transport(place, w, got, data_all, (2,), True)
-    up, down, data_all = transport(place, w, got, data_all, (1, 3), True)
-    (target,) = transport(place, w, got, data_all, (0,), False)
+    up, down = transport(place, w, got, data_all, (1, 3), False)
+    near_w = near_scale(place, columns, given)
+    near_w, opposite = lax.optimization_barrier((near_w, opposite))
+    target, *rest = near_transport(place, near_w, shift(near_w, "core", 1), near)
     for by, part in zip((2, 1, 3), (opposite, up, down)):
         target = target + shift(part, "y", by).astype(F32)
+    for by, part in zip((2, 1, 3), (rest[1], rest[0], rest[2])):
+        target = target + shift(part, "x", by).astype(F32)
     velocity = (target - noise.astype(F32)).astype(BF16)
     own = lax.dynamic_index_in_dim(f.reshape(2, X, 128), x, 1, False)
     pot_f = (own * (EPS / LOG2E) + sq_noise / WIDTH).reshape(ROWS)

time: 257 us -> 202 us (0.79); the launches traced: 257 us -> 199 us
  Pallas kernels: 80.1 us -> 18.7 us
  starting transfers between devices: 35.4 us -> 41.6 us
  waiting for transfers between devices: 49.2 us -> 43.6 us
  blocking collectives: 64.2 us -> 66.9 us
    pallas_call x1 -> x3, Pallas kernels: 65.2 us -> 5.01 us  [the longest x1 2.98 us: pick(): pl.pallas_call(pick_kernel, out_shape=(jax.ShapeDtypeStruct((Y - 1, *part...]
    ppermute x25 -> x29, starting transfers between devices: 31.5 us -> 37.3 us  [shift(): return lax.ppermute(x, axis, [(j, (j + by) % n) for j in range(n)])]
    ppermute x25 -> x29, waiting for transfers between devices: 41.1 us -> 35.8 us  [shift(): return lax.ppermute(x, axis, [(j, (j + by) % n) for j in range(n)])]
    all_to_all x2, blocking collectives: 20.1 us -> 24.3 us  [body(): columns = lax.all_to_all(columns, 'z', 0, 0)]
    unnamed x12 -> x10, local copies, waits for them, and re-layouts: 10.1 us -> 9.39 us
  transfers between devices with their start and end apart: 28 -> 32, of which waited for: 19 -> 18; matrix products, arithmetic and copies ran while one was open for 1% -> 1% of each run, Pallas kernels for 5% -> 7%
where the time goes in v14:
time: 202 us; the launch traced here: 199 us
  blocking collectives  66.9 us (33%)
  waiting for transfers between devices  43.6 us (22%)
  starting transfers between devices  41.6 us (21%)
  Pallas kernels  18.7 us (9%)
  between operations  14.3 us (7%)
  local copies, waits for them, and re-layouts  10.5 us (5%)
  other arithmetic  3.46 us (2%)
    all_to_all x3, blocking collectives, body(): parts = lax.all_to_all(rows, ('x', 'y', 'core'), 0, 0)  42.5 us
    ppermute x29, starting transfers between devices, shift(): return lax.ppermute(x, axis, [(j, (j + by) % n) for j in range(n)])  37.3 us
    ppermute x29, waiting for transfers between devices, shift(): return lax.ppermute(x, axis, [(j, (j + by) % n) for j in range(n)])  35.8 us
    all_to_all x2, blocking collectives, body(): columns = lax.all_to_all(columns, 'z', 0, 0)  24.3 us
    unnamed x10, local copies, waits for them, and re-layouts  9.39 us
    all_gather x1, waiting for transfers between devices, body(): lax.all_gather(swapped, ('z', 'core')).reshape(Y, C, C, X, QUARTER, SLICE)  7.82 us
    all_to_all x1, starting transfers between devices, body(): columns = lax.all_to_all(columns, ('z', 'x'), 0, 0)  4.26 us
  transfers between devices with their start and end apart: 32, of which 18 were waited for; matrix products, arithmetic and copies ran while one was open for 1% of the time, Pallas kernels for 7%

profile of v14, /device:TPU:1, one launch (start us, length us, event | category | flops | bytes accessed | tf_op | source)
XLA Modules:
  0.0 199.0 jit_solution(8066665920811111584)
XLA Ops:
  8.8 3.4 %collective-permute-start.2 = (bf16[256,128]{1,0:T(8,128)(2,1)S(1)}, bf16[256,128]{1,0:T(8,128)(2,1)S(1)}, u32[]{:S(2)}, u32[]{:S(2)}) collective-permute-start(bf16[256,128]{1,0:T(8,128)(2,1)S(1)} %get-tuple-element.59), channel_id=1, source_target_pairs={{0,24},{8,0},{16,8},{24,16},{1,25},{9,1},{17,9},{25,17},{2,26},{10... | collective-permute-start | bytes 196616 | tf_op jit(solution)/shard_map/ppermute | solution.py:34
  13.5 3.3 %collective-permute-done.1 = bf16[256,128]{1,0:T(8,128)(2,1)S(1)} collective-permute-done((bf16[256,128]{1,0:T(8,128)(2,1)S(1)}, bf16[256,128]{1,0:T(8,128)(2,1)S(1)}, u32[]{:S(2)}, u32[]{:S(2)}) %collective-permute-start.1) | collective-permute-done | bytes 65568 | tf_op jit(solution)/shard_map/ppermute | solution.py:34
  19.4 2.7 %collective-permute-start.4 = (bf16[128,512]{1,0:T(8,128)(2,1)S(1)}, bf16[128,512]{1,0:T(8,128)(2,1)S(1)}, u32[]{:S(2)}, u32[]{:S(2)}) collective-permute-start(bf16[128,512]{1,0:T(8,128)(2,1)S(1)} %get-tuple-element.62), channel_id=1, source_target_pairs={{0,24},{8,0},{16,8},{24,16},{1,25},{9,1},{17,9},{25,17},{2,26},{10... | collective-permute-start | bytes 393224 | tf_op jit(solution)/shard_map/ppermute | solution.py:34
  28.2 2.7 %collective-permute-done.8 = bf16[128,512]{1,0:T(8,128)(2,1)S(1)} collective-permute-done((bf16[128,512]{1,0:T(8,128)(2,1)S(1)}, bf16[128,512]{1,0:T(8,128)(2,1)S(1)}, u32[]{:S(2)}, u32[]{:S(2)}) %collective-permute-start.8) | collective-permute-done | bytes 131104 | tf_op jit(solution)/shard_map/ppermute | solution.py:34
  31.5 2.3 %collective-permute-start.10 = (bf16[4,128,512]{2,1,0:T(8,128)(2,1)S(1)}, bf16[4,128,512]{2,1,0:T(8,128)(2,1)S(1)}, u32[]{:S(2)}, u32[]{:S(2)}) collective-permute-start(bf16[4,128,512]{2,1,0:T(8,128)(2,1)S(1)} %pad_maximum_fusion.refs_0_), channel_id=1, source_target_pairs={{0,6},{2,0},{4,2},{6,4},{1,7},{3,1},{5,3},{7,5},{8,14},{10,8},{12,... | collective-permute-start | bytes 1572872 | tf_op jit(solution)/shard_map/ppermute | solution.py:34
  34.0 2.7 %collective-permute-start.12 = (bf16[4,128,512]{2,1,0:T(8,128)(2,1)S(1)}, bf16[4,128,512]{2,1,0:T(8,128)(2,1)S(1)}, u32[]{:S(2)}, u32[]{:S(2)}) collective-permute-start(bf16[4,128,512]{2,1,0:T(8,128)(2,1)S(1)} %pad_maximum_fusion.1.refs_5_), channel_id=1, source_target_pairs={{0,24},{8,0},{16,8},{24,16},{1,25},{9,1},{17,9},{25,17},{2,26},{10... | collective-permute-start | bytes 1572872 | tf_op jit(solution)/shard_map/ppermute | solution.py:34
  36.6 4.3 %collective-permute-done.9.refs_1_ = bf16[4,128,512]{2,1,0:T(8,128)(2,1)S(1)} collective-permute-done((bf16[4,128,512]{2,1,0:T(8,128)(2,1)S(1)}, bf16[4,128,512]{2,1,0:T(8,128)(2,1)S(1)}, u32[]{:S(2)}, u32[]{:S(2)}) %collective-permute-start.9) | collective-permute-done | bytes 524320 | tf_op jit(solution)/shard_map/ppermute | solution.py:34
  41.2 2.2 %collective-permute-done.11.refs_6_ = bf16[4,128,512]{2,1,0:T(8,128)(2,1)S(1)} collective-permute-done((bf16[4,128,512]{2,1,0:T(8,128)(2,1)S(1)}, bf16[4,128,512]{2,1,0:T(8,128)(2,1)S(1)}, u32[]{:S(2)}, u32[]{:S(2)}) %collective-permute-start.11) | collective-permute-done | bytes 524320 | tf_op jit(solution)/shard_map/ppermute | solution.py:34
  43.6 2.7 %collective-permute-start.14 = (bf16[2,128,512]{2,1,0:T(8,128)(2,1)S(1)}, bf16[2,128,512]{2,1,0:T(8,128)(2,1)S(1)}, u32[]{:S(2)}, u32[]{:S(2)}) collective-permute-start(bf16[2,128,512]{2,1,0:T(8,128)(2,1)S(1)} %slice.21), channel_id=1, source_target_pairs={{0,6},{2,0},{4,2},{6,4},{1,7},{3,1},{5,3},{7,5},{8,14},{10,8},{12,... | collective-permute-start | bytes 786440 | tf_op jit(solution)/shard_map/ppermute | solution.py:34
  50.4 2.9 %collective-permute-done.15.refs_8_ = bf16[2,128,512]{2,1,0:T(8,128)(2,1)S(1)} collective-permute-done((bf16[2,128,512]{2,1,0:T(8,128)(2,1)S(1)}, bf16[2,128,512]{2,1,0:T(8,128)(2,1)S(1)}, u32[]{:S(2)}, u32[]{:S(2)}) %collective-permute-start.15) | collective-permute-done | bytes 262176 | tf_op jit(solution)/shard_map/ppermute | solution.py:34
  55.9 7.8 %all-gather.5.cloned.1.call-done = bf16[64,256,128]{2,1,0:T(8,128)(2,1)} async-done(((bf16[4,256,128]{2,1,0:T(8,128)(2,1)}), bf16[64,256,128]{2,1,0:T(8,128)(2,1)}) %all-gather.5.cloned.1.call-update) | async-done | bytes 4194320 | tf_op jit(solution)/shard_map/all_gather | solution.py:450
  63.7 3.0 %pick.1 = (bf16[3,2,4,256,128]{4,3,2,1,0:T(8,128)(2,1)}, bf16[2,4,256,128]{3,2,1,0:T(8,128)(2,1)S(1)}) custom-call(s32[4]{0:T(128)S(1)} %pad_add_fusion.place, bf16[4,2,2,4,256,128]{5,4,3,2,1,0:T(8,128)(2,1)} %bitcast.32), custom_call_target="tpu_custom_call" | custom-call | tf_op jit(solution)/shard_map/pick/pallas_call | solution.py:148
  75.6 16.4 %all_to_all.30.part_ref = f32[32,8,128]{2,1,0:T(8,128)S(1)} all-to-all(f32[32,8,128]{2,1,0:T(8,128)S(1)} %get-tuple-element.84), channel_id=1, replica_groups=mesh['z'=8,'x'=4,'y'=4,'core'=2] {'x','y','core'}, dimensions={0} | all-to-all | bytes 262144 | tf_op jit(solution)/shard_map/all_to_all | solution.py:460
  92.8 15.1 %all_to_all.31.part_ref = f32[8,8,128]{2,1,0:T(8,128)S(1)} all-to-all(f32[8,8,128]{2,1,0:T(8,128)S(1)} %get-tuple-element.85), channel_id=1, replica_groups=mesh['z'=8,'x'=4,'y'=4,'core'=2] {'z'}, dimensions={0} | all-to-all | bytes 65536 | tf_op jit(solution)/shard_map/all_to_all | solution.py:463
  108.3 14.0 %all_to_all.32.part_ref = f32[32,8,128]{2,1,0:T(8,128)S(1)} all-to-all(f32[32,8,128]{2,1,0:T(8,128)S(1)} %noise_lse.2), channel_id=1, replica_groups=mesh['z'=8,'x'=4,'y'=4,'core'=2] {'x','y','core'}, dimensions={0} | all-to-all | bytes 262144 | tf_op jit(solution)/shard_map/all_to_all | solution.py:460
  123.0 9.2 %all_to_all.33.part_ref = f32[8,8,128]{2,1,0:T(8,128)S(1)} all-to-all(f32[8,8,128]{2,1,0:T(8,128)S(1)} %get-tuple-element.86), channel_id=1, replica_groups=mesh['z'=8,'x'=4,'y'=4,'core'=2] {'z'}, dimensions={0} | all-to-all | bytes 65536 | tf_op jit(solution)/shard_map/all_to_all | solution.py:463
  132.6 12.2 %all_to_all.34.part_ref = f32[32,8,128]{2,1,0:T(8,128)S(1)} all-to-all(f32[32,8,128]{2,1,0:T(8,128)S(1)} %noise_lse.3), channel_id=1, replica_groups=mesh['z'=8,'x'=4,'y'=4,'core'=2] {'x','y','core'}, dimensions={0} | all-to-all | bytes 262144 | tf_op jit(solution)/shard_map/all_to_all | solution.py:460
  146.4 4.3 %all-to-all-start.5 = ((f32[32,8,128]{2,1,0:T(8,128)}), f32[32,8,128]{2,1,0:T(8,128)S(1)}, u32[]{:S(2)}, u32[]{:S(2)}) async-start(f32[32,8,128]{2,1,0:T(8,128)} %get-tuple-element.90), calls=%async_computation.5 | async-start | bytes 262144 | tf_op jit(solution)/shard_map/all_to_all | solution.py:466
  152.0 2.4 %collective-permute-start.19 = (bf16[256,256]{1,0:T(8,128)(2,1)S(1)}, bf16[256,256]{1,0:T(8,128)(2,1)S(1)}, u32[]{:S(2)}, u32[]{:S(2)}) collective-permute-start(bf16[256,256]{1,0:T(8,128)(2,1)S(1)} %get-tuple-element.93.refs_2_), channel_id=1, source_target_pairs={{0,16},{8,24},{16,0},{24,8},{1,17},{9,25},{17,1},{25,9},{2,18},{10... | collective-permute-start | bytes 393224 | tf_op jit(solution)/shard_map/ppermute | solution.py:34
  157.1 4.5 %collective-permute-done.19.refs_2_ = bf16[256,256]{1,0:T(8,128)(2,1)S(1)} collective-permute-done((bf16[256,256]{1,0:T(8,128)(2,1)S(1)}, bf16[256,256]{1,0:T(8,128)(2,1)S(1)}, u32[]{:S(2)}, u32[]{:S(2)}) %collective-permute-start.19) | collective-permute-done | bytes 131104 | tf_op jit(solution)/shard_map/ppermute | solution.py:34
  165.9 2.8 %copy-done = bf16[12,2,4,256,128]{4,3,2,1,0:T(8,128)(2,1)S(1)} copy-done((bf16[12,2,4,256,128]{4,3,2,1,0:T(8,128)(2,1)S(1)}, bf16[12,2,4,256,128]{4,3,2,1,0:T(8,128)(2,1)}, u32[]{:S(2)}) %copy-start) | copy-done | bytes 6291480
  177.7 2.6 %collective-permute-done.25 = bf16[256,512]{1,0:T(8,128)(2,1)S(1)} collective-permute-done((bf16[256,512]{1,0:T(8,128)(2,1)S(1)}, bf16[256,512]{1,0:T(8,128)(2,1)S(1)}, u32[]{:S(2)}, u32[]{:S(2)}) %collective-permute-start.25) | collective-permute-done | bytes 262176 | tf_op jit(solution)/shard_map/ppermute | solution.py:34
  182.9 4.8 %collective-permute-done.24 = bf16[256,512]{1,0:T(8,128)(2,1)S(1)} collective-permute-done((bf16[256,512]{1,0:T(8,128)(2,1)S(1)}, bf16[256,512]{1,0:T(8,128)(2,1)S(1)}, u32[]{:S(2)}, u32[]{:S(2)}) %collective-permute-start.24) | collective-permute-done | bytes 262176 | tf_op jit(solution)/shard_map/ppermute | solution.py:34
  187.7 2.6 %collective-permute-done.26 = bf16[256,512]{1,0:T(8,128)(2,1)S(1)} collective-permute-done((bf16[256,512]{1,0:T(8,128)(2,1)S(1)}, bf16[256,512]{1,0:T(8,128)(2,1)S(1)}, u32[]{:S(2)}, u32[]{:S(2)}) %collective-permute-start.26) | collective-permute-done | bytes 262176 | tf_op jit(solution)/shard_map/ppermute | solution.py:34
  (85 shorter events, 54.1 us)
Async XLA Ops:
  7.2 56.5 %all-gather.5.cloned.1.call-start = ((), (), s32[]{:S(2)}) async-start(), calls=%async_computation.6 | async-start | bytes 4456448 | tf_op jit(solution)/shard_map/all_gather | solution.py:450
  18.3 146.9 %all-gather.7.cloned.1.call-start = ((), (), s32[]{:S(2)}) async-start(), calls=%async_computation.7 | async-start | bytes 7864320 | tf_op jit(solution)/shard_map/all_gather | solution.py:453
  19.3 5.8 %collective-permute-start.3 = (bf16[128,512]{1,0:T(8,128)(2,1)S(1)}, bf16[128,512]{1,0:T(8,128)(2,1)S(1)}, u32[]{:S(2)}, u32[]{:S(2)}) collective-permute-start(bf16[128,512]{1,0:T(8,128)(2,1)S(1)} %get-tuple-element.62), channel_id=1, source_target_pairs={{0,8},{8,16},{16,24},{24,0},{1,9},{9,17},{17,25},{25,1},{2,10},{10... | collective-permute-start | bytes 393224 | tf_op jit(solution)/shard_map/ppermute | solution.py:34
  19.4 7.9 %collective-permute-start.4 = (bf16[128,512]{1,0:T(8,128)(2,1)S(1)}, bf16[128,512]{1,0:T(8,128)(2,1)S(1)}, u32[]{:S(2)}, u32[]{:S(2)}) collective-permute-start(bf16[128,512]{1,0:T(8,128)(2,1)S(1)} %get-tuple-element.62), channel_id=1, source_target_pairs={{0,24},{8,0},{16,8},{24,16},{1,25},{9,1},{17,9},{25,17},{2,26},{10... | collective-permute-start | bytes 393224 | tf_op jit(solution)/shard_map/ppermute | solution.py:34
  22.1 6.1 %collective-permute-start.5 = (bf16[128,512]{1,0:T(8,128)(2,1)S(1)}, bf16[128,512]{1,0:T(8,128)(2,1)S(1)}, u32[]{:S(2)}, u32[]{:S(2)}) collective-permute-start(bf16[128,512]{1,0:T(8,128)(2,1)S(1)} %get-tuple-element.62), channel_id=1, source_target_pairs={{0,16},{8,24},{16,0},{24,8},{1,17},{9,25},{17,1},{25,9},{2,18},{10... | collective-permute-start | bytes 393224 | tf_op jit(solution)/shard_map/ppermute | solution.py:34
  22.4 5.8 %collective-permute-start.6 = (bf16[128,512]{1,0:T(8,128)(2,1)S(1)}, bf16[128,512]{1,0:T(8,128)(2,1)S(1)}, u32[]{:S(2)}, u32[]{:S(2)}) collective-permute-start(bf16[128,512]{1,0:T(8,128)(2,1)S(1)} %get-tuple-element.66), channel_id=1, source_target_pairs={{0,2},{2,4},{4,6},{6,0},{1,3},{3,5},{5,7},{7,1},{8,10},{10,12},{12... | collective-permute-start | bytes 393224 | tf_op jit(solution)/shard_map/ppermute | solution.py:34
  30.9 10.0 %collective-permute-start.9 = (bf16[4,128,512]{2,1,0:T(8,128)(2,1)S(1)}, bf16[4,128,512]{2,1,0:T(8,128)(2,1)S(1)}, u32[]{:S(2)}, u32[]{:S(2)}) collective-permute-start(bf16[4,128,512]{2,1,0:T(8,128)(2,1)S(1)} %pad_maximum_fusion.refs_0_), channel_id=1, source_target_pairs={{0,2},{2,4},{4,6},{6,0},{1,3},{3,5},{5,7},{7,1},{8,10},{10,12},{12... | collective-permute-start | bytes 1572872 | tf_op jit(solution)/shard_map/ppermute | solution.py:34
  31.5 9.7 %collective-permute-start.10 = (bf16[4,128,512]{2,1,0:T(8,128)(2,1)S(1)}, bf16[4,128,512]{2,1,0:T(8,128)(2,1)S(1)}, u32[]{:S(2)}, u32[]{:S(2)}) collective-permute-start(bf16[4,128,512]{2,1,0:T(8,128)(2,1)S(1)} %pad_maximum_fusion.refs_0_), channel_id=1, source_target_pairs={{0,6},{2,0},{4,2},{6,4},{1,7},{3,1},{5,3},{7,5},{8,14},{10,8},{12,... | collective-permute-start | bytes 1572872 | tf_op jit(solution)/shard_map/ppermute | solution.py:34
  33.9 9.6 %collective-permute-start.11 = (bf16[4,128,512]{2,1,0:T(8,128)(2,1)S(1)}, bf16[4,128,512]{2,1,0:T(8,128)(2,1)S(1)}, u32[]{:S(2)}, u32[]{:S(2)}) collective-permute-start(bf16[4,128,512]{2,1,0:T(8,128)(2,1)S(1)} %pad_maximum_fusion.1.refs_5_), channel_id=1, source_target_pairs={{0,8},{8,16},{16,24},{24,0},{1,9},{9,17},{17,25},{25,1},{2,10},{10... | collective-permute-start | bytes 1572872 | tf_op jit(solution)/shard_map/ppermute | solution.py:34
  34.0 9.5 %collective-permute-start.12 = (bf16[4,128,512]{2,1,0:T(8,128)(2,1)S(1)}, bf16[4,128,512]{2,1,0:T(8,128)(2,1)S(1)}, u32[]{:S(2)}, u32[]{:S(2)}) collective-permute-start(bf16[4,128,512]{2,1,0:T(8,128)(2,1)S(1)} %pad_maximum_fusion.1.refs_5_), channel_id=1, source_target_pairs={{0,24},{8,0},{16,8},{24,16},{1,25},{9,1},{17,9},{25,17},{2,26},{10... | collective-permute-start | bytes 1572872 | tf_op jit(solution)/shard_map/ppermute | solution.py:34
  43.5 6.9 %collective-permute-start.13 = (bf16[2,128,512]{2,1,0:T(8,128)(2,1)S(1)}, bf16[2,128,512]{2,1,0:T(8,128)(2,1)S(1)}, u32[]{:S(2)}, u32[]{:S(2)}) collective-permute-start(bf16[2,128,512]{2,1,0:T(8,128)(2,1)S(1)} %slice.20), channel_id=1, source_target_pairs={{0,2},{2,4},{4,6},{6,0},{1,3},{3,5},{5,7},{7,1},{8,10},{10,12},{12... | collective-permute-start | bytes 786440 | tf_op jit(solution)/shard_map/ppermute | solution.py:34
  43.6 6.8 %collective-permute-start.14 = (bf16[2,128,512]{2,1,0:T(8,128)(2,1)S(1)}, bf16[2,128,512]{2,1,0:T(8,128)(2,1)S(1)}, u32[]{:S(2)}, u32[]{:S(2)}) collective-permute-start(bf16[2,128,512]{2,1,0:T(8,128)(2,1)S(1)} %slice.21), channel_id=1, source_target_pairs={{0,6},{2,0},{4,2},{6,4},{1,7},{3,1},{5,3},{7,5},{8,14},{10,8},{12,... | collective-permute-start | bytes 786440 | tf_op jit(solution)/shard_map/ppermute | solution.py:34
  46.4 6.9 %collective-permute-start.15 = (bf16[2,128,512]{2,1,0:T(8,128)(2,1)S(1)}, bf16[2,128,512]{2,1,0:T(8,128)(2,1)S(1)}, u32[]{:S(2)}, u32[]{:S(2)}) collective-permute-start(bf16[2,128,512]{2,1,0:T(8,128)(2,1)S(1)} %slice.22), channel_id=1, source_target_pairs={{0,8},{8,16},{16,24},{24,0},{1,9},{9,17},{17,25},{25,1},{2,10},{10... | collective-permute-start | bytes 786440 | tf_op jit(solution)/shard_map/ppermute | solution.py:34
  47.3 6.0 %collective-permute-start.16 = (bf16[2,128,512]{2,1,0:T(8,128)(2,1)S(1)}, bf16[2,128,512]{2,1,0:T(8,128)(2,1)S(1)}, u32[]{:S(2)}, u32[]{:S(2)}) collective-permute-start(bf16[2,128,512]{2,1,0:T(8,128)(2,1)S(1)} %slice.23), channel_id=1, source_target_pairs={{0,24},{8,0},{16,8},{24,16},{1,25},{9,1},{17,9},{25,17},{2,26},{10... | collective-permute-start | bytes 786440 | tf_op jit(solution)/shard_map/ppermute | solution.py:34
  146.4 15.2 %all-to-all-start.5 = ((f32[32,8,128]{2,1,0:T(8,128)}), f32[32,8,128]{2,1,0:T(8,128)S(1)}, u32[]{:S(2)}, u32[]{:S(2)}) async-start(f32[32,8,128]{2,1,0:T(8,128)} %get-tuple-element.90), calls=%async_computation.5 | async-start | bytes 262144 | tf_op jit(solution)/shard_map/all_to_all | solution.py:466
  150.7 6.4 %collective-permute-start.18 = (bf16[256,256]{1,0:T(8,128)(2,1)S(1)}, bf16[256,256]{1,0:T(8,128)(2,1)S(1)}, u32[]{:S(2)}, u32[]{:S(2)}) collective-permute-start(bf16[256,256]{1,0:T(8,128)(2,1)S(1)} %get-tuple-element.92.refs_1_), channel_id=1, source_target_pairs={{0,8},{8,16},{16,24},{24,0},{1,9},{9,17},{17,25},{25,1},{2,10},{10... | collective-permute-start | bytes 393224 | tf_op jit(solution)/shard_map/ppermute | solution.py:34
  152.0 9.6 %collective-permute-start.19 = (bf16[256,256]{1,0:T(8,128)(2,1)S(1)}, bf16[256,256]{1,0:T(8,128)(2,1)S(1)}, u32[]{:S(2)}, u32[]{:S(2)}) collective-permute-start(bf16[256,256]{1,0:T(8,128)(2,1)S(1)} %get-tuple-element.93.refs_2_), channel_id=1, source_target_pairs={{0,16},{8,24},{16,0},{24,8},{1,17},{9,25},{17,1},{25,9},{2,18},{10... | collective-permute-start | bytes 393224 | tf_op jit(solution)/shard_map/ppermute | solution.py:34
  154.4 7.2 %collective-permute-start.20 = (bf16[256,256]{1,0:T(8,128)(2,1)S(1)}, bf16[256,256]{1,0:T(8,128)(2,1)S(1)}, u32[]{:S(2)}, u32[]{:S(2)}) collective-permute-start(bf16[256,256]{1,0:T(8,128)(2,1)S(1)} %get-tuple-element.94.refs_3_), channel_id=1, source_target_pairs={{0,24},{8,0},{16,8},{24,16},{1,25},{9,1},{17,9},{25,17},{2,26},{10... | collective-permute-start | bytes 393224 | tf_op jit(solution)/shard_map/ppermute | solution.py:34
  172.5 7.8 %collective-permute-start.25 = (bf16[256,512]{1,0:T(8,128)(2,1)S(1)}, bf16[256,512]{1,0:T(8,128)(2,1)S(1)}, u32[]{:S(2)}, u32[]{:S(2)}) collective-permute-start(bf16[256,512]{1,0:T(8,128)(2,1)S(1)} %get-tuple-element.105), channel_id=1, source_target_pairs={{0,6},{2,0},{4,2},{6,4},{1,7},{3,1},{5,3},{7,5},{8,14},{10,8},{12,... | collective-permute-start | bytes 786440 | tf_op jit(solution)/shard_map/ppermute | solution.py:34
  173.4 14.3 %collective-permute-start.24 = (bf16[256,512]{1,0:T(8,128)(2,1)S(1)}, bf16[256,512]{1,0:T(8,128)(2,1)S(1)}, u32[]{:S(2)}, u32[]{:S(2)}) collective-permute-start(bf16[256,512]{1,0:T(8,128)(2,1)S(1)} %get-tuple-element.104), channel_id=1, source_target_pairs={{0,2},{2,4},{4,6},{6,0},{1,3},{3,5},{5,7},{7,1},{8,10},{10,12},{12... | collective-permute-start | bytes 786440 | tf_op jit(solution)/shard_map/ppermute | solution.py:34
  174.0 13.6 %collective-permute-start.23 = (bf16[256,512]{1,0:T(8,128)(2,1)S(1)}, bf16[256,512]{1,0:T(8,128)(2,1)S(1)}, u32[]{:S(2)}, u32[]{:S(2)}) collective-permute-start(bf16[256,512]{1,0:T(8,128)(2,1)S(1)} %get-tuple-element.102), channel_id=1, source_target_pairs={{0,4},{2,6},{4,0},{6,2},{1,5},{3,7},{5,1},{7,3},{8,12},{10,14},{12... | collective-permute-start | bytes 786440 | tf_op jit(solution)/shard_map/ppermute | solution.py:34
  175.9 11.7 %collective-permute-start.28 = (bf16[256,512]{1,0:T(8,128)(2,1)S(1)}, bf16[256,512]{1,0:T(8,128)(2,1)S(1)}, u32[]{:S(2)}, u32[]{:S(2)}) collective-permute-start(bf16[256,512]{1,0:T(8,128)(2,1)S(1)} %get-tuple-element.108), channel_id=1, source_target_pairs={{0,24},{8,0},{16,8},{24,16},{1,25},{9,1},{17,9},{25,17},{2,26},{10... | collective-permute-start | bytes 786440 | tf_op jit(solution)/shard_map/ppermute | solution.py:34
  177.7 9.9 %collective-permute-start.27 = (bf16[256,512]{1,0:T(8,128)(2,1)S(1)}, bf16[256,512]{1,0:T(8,128)(2,1)S(1)}, u32[]{:S(2)}, u32[]{:S(2)}) collective-permute-start(bf16[256,512]{1,0:T(8,128)(2,1)S(1)} %get-tuple-element.107), channel_id=1, source_target_pairs={{0,8},{8,16},{16,24},{24,0},{1,9},{9,17},{17,25},{25,1},{2,10},{10... | collective-permute-start | bytes 786440 | tf_op jit(solution)/shard_map/ppermute | solution.py:34
  180.3 9.9 %collective-permute-start.26 = (bf16[256,512]{1,0:T(8,128)(2,1)S(1)}, bf16[256,512]{1,0:T(8,128)(2,1)S(1)}, u32[]{:S(2)}, u32[]{:S(2)}) collective-permute-start(bf16[256,512]{1,0:T(8,128)(2,1)S(1)} %get-tuple-element.106), channel_id=1, source_target_pairs={{0,16},{8,24},{16,0},{24,8},{1,17},{9,25},{17,1},{25,9},{2,18},{10... | collective-permute-start | bytes 786440 | tf_op jit(solution)/shard_map/ppermute | solution.py:34
  (13 other events, 44.4 us)
Sparse Core Ops, SparseCore 0:
  18.4 45.2 all-gather.4
  66.8 73.8 all-gather.6

commit v15 on v12

--- a/solution.py
+++ b/solution.py
@@ -48,7 +48,8 @@
 
 
 def around(block, axis):
-    return [block, shift(block, axis, 1), shift(block, axis, -1), shift(block, axis, 2)]
+    far = shift(block, axis, 2)
+    return [block, shift(block, axis, 1), shift(block, axis, -1), far]
 
 
 def gather_noise(noise):
@@ -335,7 +336,7 @@
         top = jnp.max(parts, axis=0)
         total = top + jnp.log2(jnp.sum(jnp.exp2(parts - top[None]), axis=0))
         pot_ref[pl.ds(2 * n, 2), :] = (-LOG2N - total[0:2]) * (EPS / LOG2E) + parts[0, 2:4] * (1.0 / WIDTH)
-    for by in range(X):
+    for w_ref_by, by in zip(w_refs, (0, 2, 1, 3)):
         n = lax.rem(x - by + X, X)
         parts = jnp.stack([part_ref[k * X + n] for k in range(Z)])
         top = jnp.max(parts, axis=0)
@@ -344,7 +345,7 @@
         factor = jnp.concatenate([factor[0:1], factor[1:2]], axis=1)
         lanes = pl.ds(pl.multiple_of(n * QUARTER, QUARTER), QUARTER)
         for h in range(2):
-            w = jnp.transpose(w_refs[by][:, pl.ds(h * 128, 128)].astype(F32)) * factor
+            w = jnp.transpose(w_ref_by[:, pl.ds(h * 128, 128)].astype(F32)) * factor
             w_ref[pl.ds(h * 128, 128), lanes] = w.astype(BF16)
 
 
@@ -410,7 +411,7 @@
             columns, f = data_lse(q, parts)
             columns = lax.all_to_all(columns, "z", 0, 0)
     columns, f, *blocks = last_lse(place, q, parts, sq)
-    blocks = [blocks[0]] + [shift(blocks[by], "x", by) for by in range(1, X)]
+    blocks = [blocks[0]] + [shift(blocks[by], "x", by) for by in (2, 1, 3)]
     columns = lax.all_to_all(columns, ("z", "x"), 0, 0)
     w, pot_g = scale(place, columns, blocks)
     data_all, pot_g = lax.optimization_barrier((data_all, pot_g))

time: 195 us -> 195 us (level)
  no operation moved by 1% of the time
where the time goes in v15:
time: 195 us; the launch traced here: 194 us
  blocking collectives  64.2 us (33%)
  waiting for transfers between devices  48.5 us (25%)
  starting transfers between devices  35.8 us (18%)
  Pallas kernels  17.9 us (9%)
  between operations  14.2 us (7%)
  local copies, waits for them, and re-layouts  11.2 us (6%)
  other arithmetic  2.39 us (1%)
    all_to_all x3, blocking collectives, body(): parts = lax.all_to_all(rows, ('x', 'y', 'core'), 0, 0)  44.1 us
    ppermute x25, waiting for transfers between devices, shift(): return lax.ppermute(x, axis, [(j, (j + by) % n) for j in range(n)])  40.4 us
    ppermute x25, starting transfers between devices, shift(): return lax.ppermute(x, axis, [(j, (j + by) % n) for j in range(n)])  31.9 us
    all_to_all x2, blocking collectives, body(): columns = lax.all_to_all(columns, 'z', 0, 0)  20.1 us
    unnamed x12, local copies, waits for them, and re-layouts  10.1 us
    all_gather x1, waiting for transfers between devices, body(): lax.all_gather(swapped, ('z', 'core')).reshape(Y, C, C, X, QUARTER, SLICE)  8.12 us
    pallas_call x3, Pallas kernels, transport(): pl.pallas_call(functools.partial(transport_kernel, pieces), out_shape=kin...  4.35 us
  transfers between devices with their start and end apart: 28, of which 19 were waited for; matrix products, arithmetic and copies ran while one was open for 1% of the time, Pallas kernels for 7%

profile of v15, /device:TPU:1, one launch (start us, length us, event | category | flops | bytes accessed | tf_op | source)
XLA Modules:
  0.0 194.3 jit_solution(17456212413170277180)
XLA Ops:
  8.8 2.1 %collective-permute-start = (bf16[256,128]{1,0:T(8,128)(2,1)S(1)}, bf16[256,128]{1,0:T(8,128)(2,1)S(1)}, u32[]{:S(2)}, u32[]{:S(2)}) collective-permute-start(bf16[256,128]{1,0:T(8,128)(2,1)S(1)} %get-tuple-element.50), channel_id=1, source_target_pairs={{0,8},{8,16},{16,24},{24,0},{1,9},{9,17},{17,25},{25,1},{2,10},{10... | collective-permute-start | bytes 196616 | tf_op jit(solution)/shard_map/ppermute | solution.py:34
  10.9 2.5 %collective-permute-start.1 = (bf16[256,128]{1,0:T(8,128)(2,1)S(1)}, bf16[256,128]{1,0:T(8,128)(2,1)S(1)}, u32[]{:S(2)}, u32[]{:S(2)}) collective-permute-start(bf16[256,128]{1,0:T(8,128)(2,1)S(1)} %get-tuple-element.51), channel_id=1, source_target_pairs={{0,16},{8,24},{16,0},{24,8},{1,17},{9,25},{17,1},{25,9},{2,18},{10... | collective-permute-start | bytes 196616 | tf_op jit(solution)/shard_map/ppermute | solution.py:34
  18.6 3.2 %collective-permute-start.8 = (bf16[128,512]{1,0:T(8,128)(2,1)S(1)}, bf16[128,512]{1,0:T(8,128)(2,1)S(1)}, u32[]{:S(2)}, u32[]{:S(2)}) collective-permute-start(bf16[128,512]{1,0:T(8,128)(2,1)S(1)} %get-tuple-element.59), channel_id=1, source_target_pairs={{0,4},{2,6},{4,0},{6,2},{1,5},{3,7},{5,1},{7,3},{8,12},{10,14},{12... | collective-permute-start | bytes 393224 | tf_op jit(solution)/shard_map/ppermute | solution.py:34
  35.4 7.1 %collective-permute-done.12.refs_7_ = bf16[4,128,512]{2,1,0:T(8,128)(2,1)S(1)} collective-permute-done((bf16[4,128,512]{2,1,0:T(8,128)(2,1)S(1)}, bf16[4,128,512]{2,1,0:T(8,128)(2,1)S(1)}, u32[]{:S(2)}, u32[]{:S(2)}) %collective-permute-start.12) | collective-permute-done | bytes 524320 | tf_op jit(solution)/shard_map/ppermute | solution.py:34
  44.3 2.3 %collective-permute-start.16 = (bf16[2,128,512]{2,1,0:T(8,128)(2,1)S(1)}, bf16[2,128,512]{2,1,0:T(8,128)(2,1)S(1)}, u32[]{:S(2)}, u32[]{:S(2)}) collective-permute-start(bf16[2,128,512]{2,1,0:T(8,128)(2,1)S(1)} %slice.23), channel_id=1, source_target_pairs={{0,24},{8,0},{16,8},{24,16},{1,25},{9,1},{17,9},{25,17},{2,26},{10... | collective-permute-start | bytes 786440 | tf_op jit(solution)/shard_map/ppermute | solution.py:34
  50.0 3.4 %collective-permute-done.15.refs_8_ = bf16[2,128,512]{2,1,0:T(8,128)(2,1)S(1)} collective-permute-done((bf16[2,128,512]{2,1,0:T(8,128)(2,1)S(1)}, bf16[2,128,512]{2,1,0:T(8,128)(2,1)S(1)}, u32[]{:S(2)}, u32[]{:S(2)}) %collective-permute-start.15) | collective-permute-done | bytes 262176 | tf_op jit(solution)/shard_map/ppermute | solution.py:34
  54.1 2.0 %copy-done.2 = bf16[1024,2048]{1,0:T(8,128)(2,1)} copy-done((bf16[1024,2048]{1,0:T(8,128)(2,1)}, bf16[1024,2048]{1,0:T(8,128)(2,1)S(1)}, u32[]{:S(2)}) %copy-start.2) | copy-done | bytes 4194328
  56.1 8.1 %all-gather.5.cloned.1.call-done = bf16[64,256,128]{2,1,0:T(8,128)(2,1)} async-done(((bf16[4,256,128]{2,1,0:T(8,128)(2,1)}), bf16[64,256,128]{2,1,0:T(8,128)(2,1)}) %all-gather.5.cloned.1.call-update) | async-done | bytes 4194320 | tf_op jit(solution)/shard_map/all_gather | solution.py:399
  64.3 3.0 %pick.1.data_ref = bf16[4,2,4,256,128]{4,3,2,1,0:T(8,128)(2,1)} custom-call(s32[4]{0:T(128)S(1)} %pad_add_fusion.place, bf16[4,2,2,4,256,128]{5,4,3,2,1,0:T(8,128)(2,1)} %bitcast.32), custom_call_target="tpu_custom_call" | custom-call | tf_op jit(solution)/shard_map/pick/pallas_call | solution.py:146
  68.8 2.2 %copy-done.3 = bf16[1024,2048]{1,0:T(8,128)(2,1)S(1)} copy-done((bf16[1024,2048]{1,0:T(8,128)(2,1)S(1)}, bf16[1024,2048]{1,0:T(8,128)(2,1)}, u32[]{:S(2)}) %copy-start.3) | copy-done | bytes 4194328
  76.3 16.4 %all_to_all.30.part_ref = f32[32,8,128]{2,1,0:T(8,128)S(1)} all-to-all(f32[32,8,128]{2,1,0:T(8,128)S(1)} %get-tuple-element.75), channel_id=1, replica_groups=mesh['z'=8,'x'=4,'y'=4,'core'=2] {'x','y','core'}, dimensions={0} | all-to-all | bytes 262144 | tf_op jit(solution)/shard_map/all_to_all | solution.py:409
  93.5 10.9 %all_to_all.31.part_ref = f32[8,8,128]{2,1,0:T(8,128)S(1)} all-to-all(f32[8,8,128]{2,1,0:T(8,128)S(1)} %get-tuple-element.76), channel_id=1, replica_groups=mesh['z'=8,'x'=4,'y'=4,'core'=2] {'z'}, dimensions={0} | all-to-all | bytes 65536 | tf_op jit(solution)/shard_map/all_to_all | solution.py:412
  104.8 14.0 %all_to_all.32.part_ref = f32[32,8,128]{2,1,0:T(8,128)S(1)} all-to-all(f32[32,8,128]{2,1,0:T(8,128)S(1)} %noise_lse.2), channel_id=1, replica_groups=mesh['z'=8,'x'=4,'y'=4,'core'=2] {'x','y','core'}, dimensions={0} | all-to-all | bytes 262144 | tf_op jit(solution)/shard_map/all_to_all | solution.py:409
  119.6 9.2 %all_to_all.33.part_ref = f32[8,8,128]{2,1,0:T(8,128)S(1)} all-to-all(f32[8,8,128]{2,1,0:T(8,128)S(1)} %get-tuple-element.77), channel_id=1, replica_groups=mesh['z'=8,'x'=4,'y'=4,'core'=2] {'z'}, dimensions={0} | all-to-all | bytes 65536 | tf_op jit(solution)/shard_map/all_to_all | solution.py:412
  129.2 13.7 %all_to_all.34.part_ref = f32[32,8,128]{2,1,0:T(8,128)S(1)} all-to-all(f32[32,8,128]{2,1,0:T(8,128)S(1)} %noise_lse.3), channel_id=1, replica_groups=mesh['z'=8,'x'=4,'y'=4,'core'=2] {'x','y','core'}, dimensions={0} | all-to-all | bytes 262144 | tf_op jit(solution)/shard_map/all_to_all | solution.py:409
  144.5 3.9 %all-to-all-start.5 = ((f32[32,8,128]{2,1,0:T(8,128)}), f32[32,8,128]{2,1,0:T(8,128)S(1)}, u32[]{:S(2)}, u32[]{:S(2)}) async-start(f32[32,8,128]{2,1,0:T(8,128)} %get-tuple-element.81), calls=%async_computation.5 | async-start | bytes 262144 | tf_op jit(solution)/shard_map/all_to_all | solution.py:415
  148.3 2.7 %collective-permute-start.18 = (bf16[256,256]{1,0:T(8,128)(2,1)S(1)}, bf16[256,256]{1,0:T(8,128)(2,1)S(1)}, u32[]{:S(2)}, u32[]{:S(2)}) collective-permute-start(bf16[256,256]{1,0:T(8,128)(2,1)S(1)} %get-tuple-element.83), channel_id=1, source_target_pairs={{0,16},{8,24},{16,0},{24,8},{1,17},{9,25},{17,1},{25,9},{2,18},{10... | collective-permute-start | bytes 393224 | tf_op jit(solution)/shard_map/ppermute | solution.py:34
  151.3 2.4 %collective-permute-start.20 = (bf16[256,256]{1,0:T(8,128)(2,1)S(1)}, bf16[256,256]{1,0:T(8,128)(2,1)S(1)}, u32[]{:S(2)}, u32[]{:S(2)}) collective-permute-start(bf16[256,256]{1,0:T(8,128)(2,1)S(1)} %get-tuple-element.85), channel_id=1, source_target_pairs={{0,24},{8,0},{16,8},{24,16},{1,25},{9,1},{17,9},{25,17},{2,26},{10... | collective-permute-start | bytes 393224 | tf_op jit(solution)/shard_map/ppermute | solution.py:34
  153.7 5.7 %collective-permute-done.18.refs_1_ = bf16[256,256]{1,0:T(8,128)(2,1)S(1)} collective-permute-done((bf16[256,256]{1,0:T(8,128)(2,1)S(1)}, bf16[256,256]{1,0:T(8,128)(2,1)S(1)}, u32[]{:S(2)}, u32[]{:S(2)}) %collective-permute-start.18) | collective-permute-done | bytes 131104 | tf_op jit(solution)/shard_map/ppermute | solution.py:34
  159.4 3.7 %collective-permute-done.19.refs_2_ = bf16[256,256]{1,0:T(8,128)(2,1)S(1)} collective-permute-done((bf16[256,256]{1,0:T(8,128)(2,1)S(1)}, bf16[256,256]{1,0:T(8,128)(2,1)S(1)}, u32[]{:S(2)}, u32[]{:S(2)}) %collective-permute-start.19) | collective-permute-done | bytes 131104 | tf_op jit(solution)/shard_map/ppermute | solution.py:34
  166.5 3.4 %copy-done = bf16[16,2,4,256,128]{4,3,2,1,0:T(8,128)(2,1)S(1)} copy-done((bf16[16,2,4,256,128]{4,3,2,1,0:T(8,128)(2,1)S(1)}, bf16[16,2,4,256,128]{4,3,2,1,0:T(8,128)(2,1)}, u32[]{:S(2)}) %copy-start) | copy-done | bytes 8388632
  171.1 3.0 %collective-permute-start.22 = (bf16[256,512]{1,0:T(8,128)(2,1)S(1)}, bf16[256,512]{1,0:T(8,128)(2,1)S(1)}, u32[]{:S(2)}, u32[]{:S(2)}) collective-permute-start(bf16[256,512]{1,0:T(8,128)(2,1)S(1)} %get-tuple-element.92), channel_id=1, source_target_pairs={{0,4},{2,6},{4,0},{6,2},{1,5},{3,7},{5,1},{7,3},{8,12},{10,14},{12... | collective-permute-start | bytes 786440 | tf_op jit(solution)/shard_map/ppermute | solution.py:34
  176.4 2.4 %collective-permute-start.24 = (bf16[256,512]{1,0:T(8,128)(2,1)S(1)}, bf16[256,512]{1,0:T(8,128)(2,1)S(1)}, u32[]{:S(2)}, u32[]{:S(2)}) collective-permute-start(bf16[256,512]{1,0:T(8,128)(2,1)S(1)} %get-tuple-element.94), channel_id=1, source_target_pairs={{0,6},{2,0},{4,2},{6,4},{1,7},{3,1},{5,3},{7,5},{8,14},{10,8},{12,... | collective-permute-start | bytes 786440 | tf_op jit(solution)/shard_map/ppermute | solution.py:34
  180.6 6.0 %collective-permute-done.23 = bf16[256,512]{1,0:T(8,128)(2,1)S(1)} collective-permute-done((bf16[256,512]{1,0:T(8,128)(2,1)S(1)}, bf16[256,512]{1,0:T(8,128)(2,1)S(1)}, u32[]{:S(2)}, u32[]{:S(2)}) %collective-permute-start.23) | collective-permute-done | bytes 262176 | tf_op jit(solution)/shard_map/ppermute | solution.py:34
  (78 shorter events, 46.8 us)
Async XLA Ops:
  7.2 57.1 %all-gather.5.cloned.1.call-start = ((), (), s32[]{:S(2)}) async-start(), calls=%async_computation.6 | async-start | bytes 4456448 | tf_op jit(solution)/shard_map/all_gather | solution.py:399
  8.8 5.7 %collective-permute-start = (bf16[256,128]{1,0:T(8,128)(2,1)S(1)}, bf16[256,128]{1,0:T(8,128)(2,1)S(1)}, u32[]{:S(2)}, u32[]{:S(2)}) collective-permute-start(bf16[256,128]{1,0:T(8,128)(2,1)S(1)} %get-tuple-element.50), channel_id=1, source_target_pairs={{0,8},{8,16},{16,24},{24,0},{1,9},{9,17},{17,25},{25,1},{2,10},{10... | collective-permute-start | bytes 196616 | tf_op jit(solution)/shard_map/ppermute | solution.py:34
  10.9 5.1 %collective-permute-start.1 = (bf16[256,128]{1,0:T(8,128)(2,1)S(1)}, bf16[256,128]{1,0:T(8,128)(2,1)S(1)}, u32[]{:S(2)}, u32[]{:S(2)}) collective-permute-start(bf16[256,128]{1,0:T(8,128)(2,1)S(1)} %get-tuple-element.51), channel_id=1, source_target_pairs={{0,16},{8,24},{16,0},{24,8},{1,17},{9,25},{17,1},{25,9},{2,18},{10... | collective-permute-start | bytes 196616 | tf_op jit(solution)/shard_map/ppermute | solution.py:34
  17.6 147.4 %all-gather.7.cloned.1.call-start = ((), (), s32[]{:S(2)}) async-start(), calls=%async_computation.7 | async-start | bytes 10485760 | tf_op jit(solution)/shard_map/all_gather | solution.py:402
  18.6 6.9 %collective-permute-start.8 = (bf16[128,512]{1,0:T(8,128)(2,1)S(1)}, bf16[128,512]{1,0:T(8,128)(2,1)S(1)}, u32[]{:S(2)}, u32[]{:S(2)}) collective-permute-start(bf16[128,512]{1,0:T(8,128)(2,1)S(1)} %get-tuple-element.59), channel_id=1, source_target_pairs={{0,4},{2,6},{4,0},{6,2},{1,5},{3,7},{5,1},{7,3},{8,12},{10,14},{12... | collective-permute-start | bytes 393224 | tf_op jit(solution)/shard_map/ppermute | solution.py:34
  22.6 6.0 %collective-permute-start.6 = (bf16[128,512]{1,0:T(8,128)(2,1)S(1)}, bf16[128,512]{1,0:T(8,128)(2,1)S(1)}, u32[]{:S(2)}, u32[]{:S(2)}) collective-permute-start(bf16[128,512]{1,0:T(8,128)(2,1)S(1)} %get-tuple-element.59), channel_id=1, source_target_pairs={{0,2},{2,4},{4,6},{6,0},{1,3},{3,5},{5,7},{7,1},{8,10},{10,12},{12... | collective-permute-start | bytes 393224 | tf_op jit(solution)/shard_map/ppermute | solution.py:34
  23.3 5.3 %collective-permute-start.5 = (bf16[128,512]{1,0:T(8,128)(2,1)S(1)}, bf16[128,512]{1,0:T(8,128)(2,1)S(1)}, u32[]{:S(2)}, u32[]{:S(2)}) collective-permute-start(bf16[128,512]{1,0:T(8,128)(2,1)S(1)} %get-tuple-element.55), channel_id=1, source_target_pairs={{0,16},{8,24},{16,0},{24,8},{1,17},{9,25},{17,1},{25,9},{2,18},{10... | collective-permute-start | bytes 393224 | tf_op jit(solution)/shard_map/ppermute | solution.py:34
  24.3 5.7 %collective-permute-start.4 = (bf16[128,512]{1,0:T(8,128)(2,1)S(1)}, bf16[128,512]{1,0:T(8,128)(2,1)S(1)}, u32[]{:S(2)}, u32[]{:S(2)}) collective-permute-start(bf16[128,512]{1,0:T(8,128)(2,1)S(1)} %get-tuple-element.55), channel_id=1, source_target_pairs={{0,24},{8,0},{16,8},{24,16},{1,25},{9,1},{17,9},{25,17},{2,26},{10... | collective-permute-start | bytes 393224 | tf_op jit(solution)/shard_map/ppermute | solution.py:34
  25.5 6.7 %collective-permute-start.3 = (bf16[128,512]{1,0:T(8,128)(2,1)S(1)}, bf16[128,512]{1,0:T(8,128)(2,1)S(1)}, u32[]{:S(2)}, u32[]{:S(2)}) collective-permute-start(bf16[128,512]{1,0:T(8,128)(2,1)S(1)} %get-tuple-element.55), channel_id=1, source_target_pairs={{0,8},{8,16},{16,24},{24,0},{1,9},{9,17},{17,25},{25,1},{2,10},{10... | collective-permute-start | bytes 393224 | tf_op jit(solution)/shard_map/ppermute | solution.py:34
  32.2 10.3 %collective-permute-start.12 = (bf16[4,128,512]{2,1,0:T(8,128)(2,1)S(1)}, bf16[4,128,512]{2,1,0:T(8,128)(2,1)S(1)}, u32[]{:S(2)}, u32[]{:S(2)}) collective-permute-start(bf16[4,128,512]{2,1,0:T(8,128)(2,1)S(1)} %pad_maximum_fusion.1.refs_5_), channel_id=1, source_target_pairs={{0,24},{8,0},{16,8},{24,16},{1,25},{9,1},{17,9},{25,17},{2,26},{10... | collective-permute-start | bytes 1572872 | tf_op jit(solution)/shard_map/ppermute | solution.py:34
  32.4 10.4 %collective-permute-start.11 = (bf16[4,128,512]{2,1,0:T(8,128)(2,1)S(1)}, bf16[4,128,512]{2,1,0:T(8,128)(2,1)S(1)}, u32[]{:S(2)}, u32[]{:S(2)}) collective-permute-start(bf16[4,128,512]{2,1,0:T(8,128)(2,1)S(1)} %pad_maximum_fusion.1.refs_5_), channel_id=1, source_target_pairs={{0,8},{8,16},{16,24},{24,0},{1,9},{9,17},{17,25},{25,1},{2,10},{10... | collective-permute-start | bytes 1572872 | tf_op jit(solution)/shard_map/ppermute | solution.py:34
  33.8 9.7 %collective-permute-start.10 = (bf16[4,128,512]{2,1,0:T(8,128)(2,1)S(1)}, bf16[4,128,512]{2,1,0:T(8,128)(2,1)S(1)}, u32[]{:S(2)}, u32[]{:S(2)}) collective-permute-start(bf16[4,128,512]{2,1,0:T(8,128)(2,1)S(1)} %pad_maximum_fusion.refs_0_), channel_id=1, source_target_pairs={{0,6},{2,0},{4,2},{6,4},{1,7},{3,1},{5,3},{7,5},{8,14},{10,8},{12,... | collective-permute-start | bytes 1572872 | tf_op jit(solution)/shard_map/ppermute | solution.py:34
  34.7 9.5 %collective-permute-start.9 = (bf16[4,128,512]{2,1,0:T(8,128)(2,1)S(1)}, bf16[4,128,512]{2,1,0:T(8,128)(2,1)S(1)}, u32[]{:S(2)}, u32[]{:S(2)}) collective-permute-start(bf16[4,128,512]{2,1,0:T(8,128)(2,1)S(1)} %pad_maximum_fusion.refs_0_), channel_id=1, source_target_pairs={{0,2},{2,4},{4,6},{6,0},{1,3},{3,5},{5,7},{7,1},{8,10},{10,12},{12... | collective-permute-start | bytes 1572872 | tf_op jit(solution)/shard_map/ppermute | solution.py:34
  44.3 5.7 %collective-permute-start.16 = (bf16[2,128,512]{2,1,0:T(8,128)(2,1)S(1)}, bf16[2,128,512]{2,1,0:T(8,128)(2,1)S(1)}, u32[]{:S(2)}, u32[]{:S(2)}) collective-permute-start(bf16[2,128,512]{2,1,0:T(8,128)(2,1)S(1)} %slice.23), channel_id=1, source_target_pairs={{0,24},{8,0},{16,8},{24,16},{1,25},{9,1},{17,9},{25,17},{2,26},{10... | collective-permute-start | bytes 786440 | tf_op jit(solution)/shard_map/ppermute | solution.py:34
  46.6 6.8 %collective-permute-start.15 = (bf16[2,128,512]{2,1,0:T(8,128)(2,1)S(1)}, bf16[2,128,512]{2,1,0:T(8,128)(2,1)S(1)}, u32[]{:S(2)}, u32[]{:S(2)}) collective-permute-start(bf16[2,128,512]{2,1,0:T(8,128)(2,1)S(1)} %slice.22), channel_id=1, source_target_pairs={{0,8},{8,16},{16,24},{24,0},{1,9},{9,17},{17,25},{25,1},{2,10},{10... | collective-permute-start | bytes 786440 | tf_op jit(solution)/shard_map/ppermute | solution.py:34
  46.6 6.8 %collective-permute-start.14 = (bf16[2,128,512]{2,1,0:T(8,128)(2,1)S(1)}, bf16[2,128,512]{2,1,0:T(8,128)(2,1)S(1)}, u32[]{:S(2)}, u32[]{:S(2)}) collective-permute-start(bf16[2,128,512]{2,1,0:T(8,128)(2,1)S(1)} %slice.21), channel_id=1, source_target_pairs={{0,6},{2,0},{4,2},{6,4},{1,7},{3,1},{5,3},{7,5},{8,14},{10,8},{12,... | collective-permute-start | bytes 786440 | tf_op jit(solution)/shard_map/ppermute | solution.py:34
  46.8 6.8 %collective-permute-start.13 = (bf16[2,128,512]{2,1,0:T(8,128)(2,1)S(1)}, bf16[2,128,512]{2,1,0:T(8,128)(2,1)S(1)}, u32[]{:S(2)}, u32[]{:S(2)}) collective-permute-start(bf16[2,128,512]{2,1,0:T(8,128)(2,1)S(1)} %slice.20), channel_id=1, source_target_pairs={{0,2},{2,4},{4,6},{6,0},{1,3},{3,5},{5,7},{7,1},{8,10},{10,12},{12... | collective-permute-start | bytes 786440 | tf_op jit(solution)/shard_map/ppermute | solution.py:34
  144.5 18.6 %all-to-all-start.5 = ((f32[32,8,128]{2,1,0:T(8,128)}), f32[32,8,128]{2,1,0:T(8,128)S(1)}, u32[]{:S(2)}, u32[]{:S(2)}) async-start(f32[32,8,128]{2,1,0:T(8,128)} %get-tuple-element.81), calls=%async_computation.5 | async-start | bytes 262144 | tf_op jit(solution)/shard_map/all_to_all | solution.py:415
  148.3 11.1 %collective-permute-start.18 = (bf16[256,256]{1,0:T(8,128)(2,1)S(1)}, bf16[256,256]{1,0:T(8,128)(2,1)S(1)}, u32[]{:S(2)}, u32[]{:S(2)}) collective-permute-start(bf16[256,256]{1,0:T(8,128)(2,1)S(1)} %get-tuple-element.83), channel_id=1, source_target_pairs={{0,16},{8,24},{16,0},{24,8},{1,17},{9,25},{17,1},{25,9},{2,18},{10... | collective-permute-start | bytes 393224 | tf_op jit(solution)/shard_map/ppermute | solution.py:34
  151.0 12.1 %collective-permute-start.19 = (bf16[256,256]{1,0:T(8,128)(2,1)S(1)}, bf16[256,256]{1,0:T(8,128)(2,1)S(1)}, u32[]{:S(2)}, u32[]{:S(2)}) collective-permute-start(bf16[256,256]{1,0:T(8,128)(2,1)S(1)} %get-tuple-element.84), channel_id=1, source_target_pairs={{0,8},{8,16},{16,24},{24,0},{1,9},{9,17},{17,25},{25,1},{2,10},{10... | collective-permute-start | bytes 393224 | tf_op jit(solution)/shard_map/ppermute | solution.py:34
  151.3 11.8 %collective-permute-start.20 = (bf16[256,256]{1,0:T(8,128)(2,1)S(1)}, bf16[256,256]{1,0:T(8,128)(2,1)S(1)}, u32[]{:S(2)}, u32[]{:S(2)}) collective-permute-start(bf16[256,256]{1,0:T(8,128)(2,1)S(1)} %get-tuple-element.85), channel_id=1, source_target_pairs={{0,24},{8,0},{16,8},{24,16},{1,25},{9,1},{17,9},{25,17},{2,26},{10... | collective-permute-start | bytes 393224 | tf_op jit(solution)/shard_map/ppermute | solution.py:34
  171.1 9.5 %collective-permute-start.22 = (bf16[256,512]{1,0:T(8,128)(2,1)S(1)}, bf16[256,512]{1,0:T(8,128)(2,1)S(1)}, u32[]{:S(2)}, u32[]{:S(2)}) collective-permute-start(bf16[256,512]{1,0:T(8,128)(2,1)S(1)} %get-tuple-element.92), channel_id=1, source_target_pairs={{0,4},{2,6},{4,0},{6,2},{1,5},{3,7},{5,1},{7,3},{8,12},{10,14},{12... | collective-permute-start | bytes 786440 | tf_op jit(solution)/shard_map/ppermute | solution.py:34
  176.0 10.6 %collective-permute-start.23 = (bf16[256,512]{1,0:T(8,128)(2,1)S(1)}, bf16[256,512]{1,0:T(8,128)(2,1)S(1)}, u32[]{:S(2)}, u32[]{:S(2)}) collective-permute-start(bf16[256,512]{1,0:T(8,128)(2,1)S(1)} %get-tuple-element.93), channel_id=1, source_target_pairs={{0,2},{2,4},{4,6},{6,0},{1,3},{3,5},{5,7},{7,1},{8,10},{10,12},{12... | collective-permute-start | bytes 786440 | tf_op jit(solution)/shard_map/ppermute | solution.py:34
  176.4 10.2 %collective-permute-start.24 = (bf16[256,512]{1,0:T(8,128)(2,1)S(1)}, bf16[256,512]{1,0:T(8,128)(2,1)S(1)}, u32[]{:S(2)}, u32[]{:S(2)}) collective-permute-start(bf16[256,512]{1,0:T(8,128)(2,1)S(1)} %get-tuple-element.94), channel_id=1, source_target_pairs={{0,6},{2,0},{4,2},{6,4},{1,7},{3,1},{5,3},{7,5},{8,14},{10,8},{12,... | collective-permute-start | bytes 786440 | tf_op jit(solution)/shard_map/ppermute | solution.py:34
  (10 other events, 30.6 us)
Sparse Core Ops, SparseCore 0:
  17.7 46.5 all-gather.4
  67.4 95.2 all-gather.6

commit v16 on v12

--- a/solution.py
+++ b/solution.py
@@ -415,10 +415,10 @@
     w, pot_g = scale(place, columns, blocks)
     data_all, pot_g = lax.optimization_barrier((data_all, pot_g))
     got = shift(w, "core", 1)
-    opposite, data_all = transport(place, w, got, data_all, (2,), True)
-    up, down, data_all = transport(place, w, got, data_all, (1, 3), True)
+    up, data_all = transport(place, w, got, data_all, (1,), True)
+    opposite, down, data_all = transport(place, w, got, data_all, (2, 3), True)
     (target,) = transport(place, w, got, data_all, (0,), False)
-    for by, part in zip((2, 1, 3), (opposite, up, down)):
+    for by, part in zip((1, 2, 3), (up, opposite, down)):
         target = target + shift(part, "y", by).astype(F32)
     velocity = (target - noise.astype(F32)).astype(BF16)
     own = lax.dynamic_index_in_dim(f.reshape(2, X, 128), x, 1, False)

time: 195 us -> 197 us (1.010)
  waiting for transfers between devices: 49.2 us -> 51.3 us
    ppermute x25, waiting for transfers between devices: 41.1 us -> 43.1 us  [shift(): return lax.ppermute(x, axis, [(j, (j + by) % n) for j in range(n)])]
  transfers between devices with their start and end apart: 28 -> 28, of which waited for: 19 -> 21; matrix products, arithmetic and copies ran while one was open for 1% -> 1% of each run, Pallas kernels for 7% -> 7%
where the time goes in v16:
time: 197 us; the launch traced here: 196 us
  blocking collectives  64.2 us (33%)
  waiting for transfers between devices  51.3 us (26%)
  starting transfers between devices  34.8 us (18%)
  Pallas kernels  17.9 us (9%)
  between operations  14.2 us (7%)
  local copies, waits for them, and re-layouts  11.2 us (6%)
  other arithmetic  2.39 us (1%)
    all_to_all x3, blocking collectives, body(): parts = lax.all_to_all(rows, ('x', 'y', 'core'), 0, 0)  44.1 us
    ppermute x25, waiting for transfers between devices, shift(): return lax.ppermute(x, axis, [(j, (j + by) % n) for j in range(n)])  43.1 us
    ppermute x25, starting transfers between devices, shift(): return lax.ppermute(x, axis, [(j, (j + by) % n) for j in range(n)])  30.9 us
    all_to_all x2, blocking collectives, body(): columns = lax.all_to_all(columns, 'z', 0, 0)  20.1 us
    unnamed x12, local copies, waits for them, and re-layouts  10.1 us
    all_gather x1, waiting for transfers between devices, body(): lax.all_gather(swapped, ('z', 'core')).reshape(Y, C, C, X, QUARTER, SLICE)  8.12 us
    pallas_call x3, Pallas kernels, transport(): pl.pallas_call(functools.partial(transport_kernel, pieces), out_shape=kin...  4.35 us
  transfers between devices with their start and end apart: 28, of which 21 were waited for; matrix products, arithmetic and copies ran while one was open for 1% of the time, Pallas kernels for 7%

profile of v16, /device:TPU:1, one launch (start us, length us, event | category | flops | bytes accessed | tf_op | source)
XLA Modules:
  0.0 196.0 jit_solution(7752096010612199356)
XLA Ops:
  8.8 2.1 %collective-permute-start = (bf16[256,128]{1,0:T(8,128)(2,1)S(1)}, bf16[256,128]{1,0:T(8,128)(2,1)S(1)}, u32[]{:S(2)}, u32[]{:S(2)}) collective-permute-start(bf16[256,128]{1,0:T(8,128)(2,1)S(1)} %get-tuple-element.50), channel_id=1, source_target_pairs={{0,8},{8,16},{16,24},{24,0},{1,9},{9,17},{17,25},{25,1},{2,10},{10... | collective-permute-start | bytes 196616 | tf_op jit(solution)/shard_map/ppermute | solution.py:34
  10.9 2.5 %collective-permute-start.1 = (bf16[256,128]{1,0:T(8,128)(2,1)S(1)}, bf16[256,128]{1,0:T(8,128)(2,1)S(1)}, u32[]{:S(2)}, u32[]{:S(2)}) collective-permute-start(bf16[256,128]{1,0:T(8,128)(2,1)S(1)} %get-tuple-element.51), channel_id=1, source_target_pairs={{0,16},{8,24},{16,0},{24,8},{1,17},{9,25},{17,1},{25,9},{2,18},{10... | collective-permute-start | bytes 196616 | tf_op jit(solution)/shard_map/ppermute | solution.py:34
  18.6 3.2 %collective-permute-start.8 = (bf16[128,512]{1,0:T(8,128)(2,1)S(1)}, bf16[128,512]{1,0:T(8,128)(2,1)S(1)}, u32[]{:S(2)}, u32[]{:S(2)}) collective-permute-start(bf16[128,512]{1,0:T(8,128)(2,1)S(1)} %get-tuple-element.59), channel_id=1, source_target_pairs={{0,4},{2,6},{4,0},{6,2},{1,5},{3,7},{5,1},{7,3},{8,12},{10,14},{12... | collective-permute-start | bytes 393224 | tf_op jit(solution)/shard_map/ppermute | solution.py:34
  30.1 2.0 %collective-permute-done.3 = bf16[128,512]{1,0:T(8,128)(2,1)S(1)} collective-permute-done((bf16[128,512]{1,0:T(8,128)(2,1)S(1)}, bf16[128,512]{1,0:T(8,128)(2,1)S(1)}, u32[]{:S(2)}, u32[]{:S(2)}) %collective-permute-start.3) | collective-permute-done | bytes 131104 | tf_op jit(solution)/shard_map/ppermute | solution.py:34
  35.4 7.1 %collective-permute-done.12.refs_7_ = bf16[4,128,512]{2,1,0:T(8,128)(2,1)S(1)} collective-permute-done((bf16[4,128,512]{2,1,0:T(8,128)(2,1)S(1)}, bf16[4,128,512]{2,1,0:T(8,128)(2,1)S(1)}, u32[]{:S(2)}, u32[]{:S(2)}) %collective-permute-start.12) | collective-permute-done | bytes 524320 | tf_op jit(solution)/shard_map/ppermute | solution.py:34
  44.3 2.3 %collective-permute-start.16 = (bf16[2,128,512]{2,1,0:T(8,128)(2,1)S(1)}, bf16[2,128,512]{2,1,0:T(8,128)(2,1)S(1)}, u32[]{:S(2)}, u32[]{:S(2)}) collective-permute-start(bf16[2,128,512]{2,1,0:T(8,128)(2,1)S(1)} %slice.23), channel_id=1, source_target_pairs={{0,24},{8,0},{16,8},{24,16},{1,25},{9,1},{17,9},{25,17},{2,26},{10... | collective-permute-start | bytes 786440 | tf_op jit(solution)/shard_map/ppermute | solution.py:34
  48.1 1.9 collective-permute-done.16.refs_9_
  50.0 3.4 %collective-permute-done.15.refs_8_ = bf16[2,128,512]{2,1,0:T(8,128)(2,1)S(1)} collective-permute-done((bf16[2,128,512]{2,1,0:T(8,128)(2,1)S(1)}, bf16[2,128,512]{2,1,0:T(8,128)(2,1)S(1)}, u32[]{:S(2)}, u32[]{:S(2)}) %collective-permute-start.15) | collective-permute-done | bytes 262176 | tf_op jit(solution)/shard_map/ppermute | solution.py:34
  54.1 2.0 %copy-done.2 = bf16[1024,2048]{1,0:T(8,128)(2,1)} copy-done((bf16[1024,2048]{1,0:T(8,128)(2,1)}, bf16[1024,2048]{1,0:T(8,128)(2,1)S(1)}, u32[]{:S(2)}) %copy-start.2) | copy-done | bytes 4194328
  56.1 8.1 %all-gather.5.cloned.1.call-done = bf16[64,256,128]{2,1,0:T(8,128)(2,1)} async-done(((bf16[4,256,128]{2,1,0:T(8,128)(2,1)}), bf16[64,256,128]{2,1,0:T(8,128)(2,1)}) %all-gather.5.cloned.1.call-update) | async-done | bytes 4194320 | tf_op jit(solution)/shard_map/all_gather | solution.py:398
  64.3 3.0 %pick.1.data_ref = bf16[4,2,4,256,128]{4,3,2,1,0:T(8,128)(2,1)} custom-call(s32[4]{0:T(128)S(1)} %pad_add_fusion.place, bf16[4,2,2,4,256,128]{5,4,3,2,1,0:T(8,128)(2,1)} %bitcast.32), custom_call_target="tpu_custom_call" | custom-call | tf_op jit(solution)/shard_map/pick/pallas_call | solution.py:145
  68.8 2.2 %copy-done.3 = bf16[1024,2048]{1,0:T(8,128)(2,1)S(1)} copy-done((bf16[1024,2048]{1,0:T(8,128)(2,1)S(1)}, bf16[1024,2048]{1,0:T(8,128)(2,1)}, u32[]{:S(2)}) %copy-start.3) | copy-done | bytes 4194328
  76.3 16.4 %all_to_all.30.part_ref = f32[32,8,128]{2,1,0:T(8,128)S(1)} all-to-all(f32[32,8,128]{2,1,0:T(8,128)S(1)} %get-tuple-element.75), channel_id=1, replica_groups=mesh['z'=8,'x'=4,'y'=4,'core'=2] {'x','y','core'}, dimensions={0} | all-to-all | bytes 262144 | tf_op jit(solution)/shard_map/all_to_all | solution.py:408
  93.5 10.9 %all_to_all.31.part_ref = f32[8,8,128]{2,1,0:T(8,128)S(1)} all-to-all(f32[8,8,128]{2,1,0:T(8,128)S(1)} %get-tuple-element.76), channel_id=1, replica_groups=mesh['z'=8,'x'=4,'y'=4,'core'=2] {'z'}, dimensions={0} | all-to-all | bytes 65536 | tf_op jit(solution)/shard_map/all_to_all | solution.py:411
  104.8 14.0 %all_to_all.32.part_ref = f32[32,8,128]{2,1,0:T(8,128)S(1)} all-to-all(f32[32,8,128]{2,1,0:T(8,128)S(1)} %noise_lse.2), channel_id=1, replica_groups=mesh['z'=8,'x'=4,'y'=4,'core'=2] {'x','y','core'}, dimensions={0} | all-to-all | bytes 262144 | tf_op jit(solution)/shard_map/all_to_all | solution.py:408
  119.6 9.2 %all_to_all.33.part_ref = f32[8,8,128]{2,1,0:T(8,128)S(1)} all-to-all(f32[8,8,128]{2,1,0:T(8,128)S(1)} %get-tuple-element.77), channel_id=1, replica_groups=mesh['z'=8,'x'=4,'y'=4,'core'=2] {'z'}, dimensions={0} | all-to-all | bytes 65536 | tf_op jit(solution)/shard_map/all_to_all | solution.py:411
  129.2 13.7 %all_to_all.34.part_ref = f32[32,8,128]{2,1,0:T(8,128)S(1)} all-to-all(f32[32,8,128]{2,1,0:T(8,128)S(1)} %noise_lse.3), channel_id=1, replica_groups=mesh['z'=8,'x'=4,'y'=4,'core'=2] {'x','y','core'}, dimensions={0} | all-to-all | bytes 262144 | tf_op jit(solution)/shard_map/all_to_all | solution.py:408
  144.5 3.9 %all-to-all-start.5 = ((f32[32,8,128]{2,1,0:T(8,128)}), f32[32,8,128]{2,1,0:T(8,128)S(1)}, u32[]{:S(2)}, u32[]{:S(2)}) async-start(f32[32,8,128]{2,1,0:T(8,128)} %get-tuple-element.81), calls=%async_computation.5 | async-start | bytes 262144 | tf_op jit(solution)/shard_map/all_to_all | solution.py:414
  149.5 2.4 %collective-permute-start.19 = (bf16[256,256]{1,0:T(8,128)(2,1)S(1)}, bf16[256,256]{1,0:T(8,128)(2,1)S(1)}, u32[]{:S(2)}, u32[]{:S(2)}) collective-permute-start(bf16[256,256]{1,0:T(8,128)(2,1)S(1)} %get-tuple-element.84), channel_id=1, source_target_pairs={{0,16},{8,24},{16,0},{24,8},{1,17},{9,25},{17,1},{25,9},{2,18},{10... | collective-permute-start | bytes 393224 | tf_op jit(solution)/shard_map/ppermute | solution.py:34
  153.1 6.1 %collective-permute-done.18.refs_1_ = bf16[256,256]{1,0:T(8,128)(2,1)S(1)} collective-permute-done((bf16[256,256]{1,0:T(8,128)(2,1)S(1)}, bf16[256,256]{1,0:T(8,128)(2,1)S(1)}, u32[]{:S(2)}, u32[]{:S(2)}) %collective-permute-start.18) | collective-permute-done | bytes 131104 | tf_op jit(solution)/shard_map/ppermute | solution.py:34
  159.2 4.0 %collective-permute-done.19.refs_2_ = bf16[256,256]{1,0:T(8,128)(2,1)S(1)} collective-permute-done((bf16[256,256]{1,0:T(8,128)(2,1)S(1)}, bf16[256,256]{1,0:T(8,128)(2,1)S(1)}, u32[]{:S(2)}, u32[]{:S(2)}) %collective-permute-start.19) | collective-permute-done | bytes 131104 | tf_op jit(solution)/shard_map/ppermute | solution.py:34
  166.7 3.4 %copy-done = bf16[16,2,4,256,128]{4,3,2,1,0:T(8,128)(2,1)S(1)} copy-done((bf16[16,2,4,256,128]{4,3,2,1,0:T(8,128)(2,1)S(1)}, bf16[16,2,4,256,128]{4,3,2,1,0:T(8,128)(2,1)}, u32[]{:S(2)}) %copy-start) | copy-done | bytes 8388632
  174.7 2.5 %collective-permute-start.23 = (bf16[256,512]{1,0:T(8,128)(2,1)S(1)}, bf16[256,512]{1,0:T(8,128)(2,1)S(1)}, u32[]{:S(2)}, u32[]{:S(2)}) collective-permute-start(bf16[256,512]{1,0:T(8,128)(2,1)S(1)} %get-tuple-element.93), channel_id=1, source_target_pairs={{0,4},{2,6},{4,0},{6,2},{1,5},{3,7},{5,1},{7,3},{8,12},{10,14},{12... | collective-permute-start | bytes 786440 | tf_op jit(solution)/shard_map/ppermute | solution.py:34
  180.4 6.6 %collective-permute-done.23 = bf16[256,512]{1,0:T(8,128)(2,1)S(1)} collective-permute-done((bf16[256,512]{1,0:T(8,128)(2,1)S(1)}, bf16[256,512]{1,0:T(8,128)(2,1)S(1)}, u32[]{:S(2)}, u32[]{:S(2)}) %collective-permute-start.23) | collective-permute-done | bytes 262176 | tf_op jit(solution)/shard_map/ppermute | solution.py:34
  (78 shorter events, 48.8 us)
Async XLA Ops:
  7.2 57.1 %all-gather.5.cloned.1.call-start = ((), (), s32[]{:S(2)}) async-start(), calls=%async_computation.6 | async-start | bytes 4456448 | tf_op jit(solution)/shard_map/all_gather | solution.py:398
  8.8 5.7 %collective-permute-start = (bf16[256,128]{1,0:T(8,128)(2,1)S(1)}, bf16[256,128]{1,0:T(8,128)(2,1)S(1)}, u32[]{:S(2)}, u32[]{:S(2)}) collective-permute-start(bf16[256,128]{1,0:T(8,128)(2,1)S(1)} %get-tuple-element.50), channel_id=1, source_target_pairs={{0,8},{8,16},{16,24},{24,0},{1,9},{9,17},{17,25},{25,1},{2,10},{10... | collective-permute-start | bytes 196616 | tf_op jit(solution)/shard_map/ppermute | solution.py:34
  10.9 5.1 %collective-permute-start.1 = (bf16[256,128]{1,0:T(8,128)(2,1)S(1)}, bf16[256,128]{1,0:T(8,128)(2,1)S(1)}, u32[]{:S(2)}, u32[]{:S(2)}) collective-permute-start(bf16[256,128]{1,0:T(8,128)(2,1)S(1)} %get-tuple-element.51), channel_id=1, source_target_pairs={{0,16},{8,24},{16,0},{24,8},{1,17},{9,25},{17,1},{25,9},{2,18},{10... | collective-permute-start | bytes 196616 | tf_op jit(solution)/shard_map/ppermute | solution.py:34
  17.6 147.6 %all-gather.7.cloned.1.call-start = ((), (), s32[]{:S(2)}) async-start(), calls=%async_computation.7 | async-start | bytes 10485760 | tf_op jit(solution)/shard_map/all_gather | solution.py:401
  18.6 6.9 %collective-permute-start.8 = (bf16[128,512]{1,0:T(8,128)(2,1)S(1)}, bf16[128,512]{1,0:T(8,128)(2,1)S(1)}, u32[]{:S(2)}, u32[]{:S(2)}) collective-permute-start(bf16[128,512]{1,0:T(8,128)(2,1)S(1)} %get-tuple-element.59), channel_id=1, source_target_pairs={{0,4},{2,6},{4,0},{6,2},{1,5},{3,7},{5,1},{7,3},{8,12},{10,14},{12... | collective-permute-start | bytes 393224 | tf_op jit(solution)/shard_map/ppermute | solution.py:34
  22.6 6.0 %collective-permute-start.6 = (bf16[128,512]{1,0:T(8,128)(2,1)S(1)}, bf16[128,512]{1,0:T(8,128)(2,1)S(1)}, u32[]{:S(2)}, u32[]{:S(2)}) collective-permute-start(bf16[128,512]{1,0:T(8,128)(2,1)S(1)} %get-tuple-element.59), channel_id=1, source_target_pairs={{0,2},{2,4},{4,6},{6,0},{1,3},{3,5},{5,7},{7,1},{8,10},{10,12},{12... | collective-permute-start | bytes 393224 | tf_op jit(solution)/shard_map/ppermute | solution.py:34
  23.3 5.3 %collective-permute-start.5 = (bf16[128,512]{1,0:T(8,128)(2,1)S(1)}, bf16[128,512]{1,0:T(8,128)(2,1)S(1)}, u32[]{:S(2)}, u32[]{:S(2)}) collective-permute-start(bf16[128,512]{1,0:T(8,128)(2,1)S(1)} %get-tuple-element.55), channel_id=1, source_target_pairs={{0,16},{8,24},{16,0},{24,8},{1,17},{9,25},{17,1},{25,9},{2,18},{10... | collective-permute-start | bytes 393224 | tf_op jit(solution)/shard_map/ppermute | solution.py:34
  24.3 5.7 %collective-permute-start.4 = (bf16[128,512]{1,0:T(8,128)(2,1)S(1)}, bf16[128,512]{1,0:T(8,128)(2,1)S(1)}, u32[]{:S(2)}, u32[]{:S(2)}) collective-permute-start(bf16[128,512]{1,0:T(8,128)(2,1)S(1)} %get-tuple-element.55), channel_id=1, source_target_pairs={{0,24},{8,0},{16,8},{24,16},{1,25},{9,1},{17,9},{25,17},{2,26},{10... | collective-permute-start | bytes 393224 | tf_op jit(solution)/shard_map/ppermute | solution.py:34
  25.5 6.7 %collective-permute-start.3 = (bf16[128,512]{1,0:T(8,128)(2,1)S(1)}, bf16[128,512]{1,0:T(8,128)(2,1)S(1)}, u32[]{:S(2)}, u32[]{:S(2)}) collective-permute-start(bf16[128,512]{1,0:T(8,128)(2,1)S(1)} %get-tuple-element.55), channel_id=1, source_target_pairs={{0,8},{8,16},{16,24},{24,0},{1,9},{9,17},{17,25},{25,1},{2,10},{10... | collective-permute-start | bytes 393224 | tf_op jit(solution)/shard_map/ppermute | solution.py:34
  32.2 10.3 %collective-permute-start.12 = (bf16[4,128,512]{2,1,0:T(8,128)(2,1)S(1)}, bf16[4,128,512]{2,1,0:T(8,128)(2,1)S(1)}, u32[]{:S(2)}, u32[]{:S(2)}) collective-permute-start(bf16[4,128,512]{2,1,0:T(8,128)(2,1)S(1)} %pad_maximum_fusion.1.refs_5_), channel_id=1, source_target_pairs={{0,24},{8,0},{16,8},{24,16},{1,25},{9,1},{17,9},{25,17},{2,26},{10... | collective-permute-start | bytes 1572872 | tf_op jit(solution)/shard_map/ppermute | solution.py:34
  32.4 10.4 %collective-permute-start.11 = (bf16[4,128,512]{2,1,0:T(8,128)(2,1)S(1)}, bf16[4,128,512]{2,1,0:T(8,128)(2,1)S(1)}, u32[]{:S(2)}, u32[]{:S(2)}) collective-permute-start(bf16[4,128,512]{2,1,0:T(8,128)(2,1)S(1)} %pad_maximum_fusion.1.refs_5_), channel_id=1, source_target_pairs={{0,8},{8,16},{16,24},{24,0},{1,9},{9,17},{17,25},{25,1},{2,10},{10... | collective-permute-start | bytes 1572872 | tf_op jit(solution)/shard_map/ppermute | solution.py:34
  33.8 9.7 %collective-permute-start.10 = (bf16[4,128,512]{2,1,0:T(8,128)(2,1)S(1)}, bf16[4,128,512]{2,1,0:T(8,128)(2,1)S(1)}, u32[]{:S(2)}, u32[]{:S(2)}) collective-permute-start(bf16[4,128,512]{2,1,0:T(8,128)(2,1)S(1)} %pad_maximum_fusion.refs_0_), channel_id=1, source_target_pairs={{0,6},{2,0},{4,2},{6,4},{1,7},{3,1},{5,3},{7,5},{8,14},{10,8},{12,... | collective-permute-start | bytes 1572872 | tf_op jit(solution)/shard_map/ppermute | solution.py:34
  34.7 9.5 %collective-permute-start.9 = (bf16[4,128,512]{2,1,0:T(8,128)(2,1)S(1)}, bf16[4,128,512]{2,1,0:T(8,128)(2,1)S(1)}, u32[]{:S(2)}, u32[]{:S(2)}) collective-permute-start(bf16[4,128,512]{2,1,0:T(8,128)(2,1)S(1)} %pad_maximum_fusion.refs_0_), channel_id=1, source_target_pairs={{0,2},{2,4},{4,6},{6,0},{1,3},{3,5},{5,7},{7,1},{8,10},{10,12},{12... | collective-permute-start | bytes 1572872 | tf_op jit(solution)/shard_map/ppermute | solution.py:34
  44.3 5.7 %collective-permute-start.16 = (bf16[2,128,512]{2,1,0:T(8,128)(2,1)S(1)}, bf16[2,128,512]{2,1,0:T(8,128)(2,1)S(1)}, u32[]{:S(2)}, u32[]{:S(2)}) collective-permute-start(bf16[2,128,512]{2,1,0:T(8,128)(2,1)S(1)} %slice.23), channel_id=1, source_target_pairs={{0,24},{8,0},{16,8},{24,16},{1,25},{9,1},{17,9},{25,17},{2,26},{10... | collective-permute-start | bytes 786440 | tf_op jit(solution)/shard_map/ppermute | solution.py:34
  46.6 6.8 %collective-permute-start.15 = (bf16[2,128,512]{2,1,0:T(8,128)(2,1)S(1)}, bf16[2,128,512]{2,1,0:T(8,128)(2,1)S(1)}, u32[]{:S(2)}, u32[]{:S(2)}) collective-permute-start(bf16[2,128,512]{2,1,0:T(8,128)(2,1)S(1)} %slice.22), channel_id=1, source_target_pairs={{0,8},{8,16},{16,24},{24,0},{1,9},{9,17},{17,25},{25,1},{2,10},{10... | collective-permute-start | bytes 786440 | tf_op jit(solution)/shard_map/ppermute | solution.py:34
  46.6 6.8 %collective-permute-start.14 = (bf16[2,128,512]{2,1,0:T(8,128)(2,1)S(1)}, bf16[2,128,512]{2,1,0:T(8,128)(2,1)S(1)}, u32[]{:S(2)}, u32[]{:S(2)}) collective-permute-start(bf16[2,128,512]{2,1,0:T(8,128)(2,1)S(1)} %slice.21), channel_id=1, source_target_pairs={{0,6},{2,0},{4,2},{6,4},{1,7},{3,1},{5,3},{7,5},{8,14},{10,8},{12,... | collective-permute-start | bytes 786440 | tf_op jit(solution)/shard_map/ppermute | solution.py:34
  46.8 6.8 %collective-permute-start.13 = (bf16[2,128,512]{2,1,0:T(8,128)(2,1)S(1)}, bf16[2,128,512]{2,1,0:T(8,128)(2,1)S(1)}, u32[]{:S(2)}, u32[]{:S(2)}) collective-permute-start(bf16[2,128,512]{2,1,0:T(8,128)(2,1)S(1)} %slice.20), channel_id=1, source_target_pairs={{0,2},{2,4},{4,6},{6,0},{1,3},{3,5},{5,7},{7,1},{8,10},{10,12},{12... | collective-permute-start | bytes 786440 | tf_op jit(solution)/shard_map/ppermute | solution.py:34
  144.5 18.7 %all-to-all-start.5 = ((f32[32,8,128]{2,1,0:T(8,128)}), f32[32,8,128]{2,1,0:T(8,128)S(1)}, u32[]{:S(2)}, u32[]{:S(2)}) async-start(f32[32,8,128]{2,1,0:T(8,128)} %get-tuple-element.81), calls=%async_computation.5 | async-start | bytes 262144 | tf_op jit(solution)/shard_map/all_to_all | solution.py:414
  148.3 10.9 %collective-permute-start.18 = (bf16[256,256]{1,0:T(8,128)(2,1)S(1)}, bf16[256,256]{1,0:T(8,128)(2,1)S(1)}, u32[]{:S(2)}, u32[]{:S(2)}) collective-permute-start(bf16[256,256]{1,0:T(8,128)(2,1)S(1)} %get-tuple-element.83), channel_id=1, source_target_pairs={{0,8},{8,16},{16,24},{24,0},{1,9},{9,17},{17,25},{25,1},{2,10},{10... | collective-permute-start | bytes 393224 | tf_op jit(solution)/shard_map/ppermute | solution.py:34
  149.5 13.7 %collective-permute-start.19 = (bf16[256,256]{1,0:T(8,128)(2,1)S(1)}, bf16[256,256]{1,0:T(8,128)(2,1)S(1)}, u32[]{:S(2)}, u32[]{:S(2)}) collective-permute-start(bf16[256,256]{1,0:T(8,128)(2,1)S(1)} %get-tuple-element.84), channel_id=1, source_target_pairs={{0,16},{8,24},{16,0},{24,8},{1,17},{9,25},{17,1},{25,9},{2,18},{10... | collective-permute-start | bytes 393224 | tf_op jit(solution)/shard_map/ppermute | solution.py:34
  151.9 11.3 %collective-permute-start.20 = (bf16[256,256]{1,0:T(8,128)(2,1)S(1)}, bf16[256,256]{1,0:T(8,128)(2,1)S(1)}, u32[]{:S(2)}, u32[]{:S(2)}) collective-permute-start(bf16[256,256]{1,0:T(8,128)(2,1)S(1)} %get-tuple-element.85), channel_id=1, source_target_pairs={{0,24},{8,0},{16,8},{24,16},{1,25},{9,1},{17,9},{25,17},{2,26},{10... | collective-permute-start | bytes 393224 | tf_op jit(solution)/shard_map/ppermute | solution.py:34
  171.4 9.0 %collective-permute-start.22 = (bf16[256,512]{1,0:T(8,128)(2,1)S(1)}, bf16[256,512]{1,0:T(8,128)(2,1)S(1)}, u32[]{:S(2)}, u32[]{:S(2)}) collective-permute-start(bf16[256,512]{1,0:T(8,128)(2,1)S(1)} %get-tuple-element.92), channel_id=1, source_target_pairs={{0,2},{2,4},{4,6},{6,0},{1,3},{3,5},{5,7},{7,1},{8,10},{10,12},{12... | collective-permute-start | bytes 786440 | tf_op jit(solution)/shard_map/ppermute | solution.py:34
  174.7 12.3 %collective-permute-start.23 = (bf16[256,512]{1,0:T(8,128)(2,1)S(1)}, bf16[256,512]{1,0:T(8,128)(2,1)S(1)}, u32[]{:S(2)}, u32[]{:S(2)}) collective-permute-start(bf16[256,512]{1,0:T(8,128)(2,1)S(1)} %get-tuple-element.93), channel_id=1, source_target_pairs={{0,4},{2,6},{4,0},{6,2},{1,5},{3,7},{5,1},{7,3},{8,12},{10,14},{12... | collective-permute-start | bytes 786440 | tf_op jit(solution)/shard_map/ppermute | solution.py:34
  177.2 11.0 %collective-permute-start.24 = (bf16[256,512]{1,0:T(8,128)(2,1)S(1)}, bf16[256,512]{1,0:T(8,128)(2,1)S(1)}, u32[]{:S(2)}, u32[]{:S(2)}) collective-permute-start(bf16[256,512]{1,0:T(8,128)(2,1)S(1)} %get-tuple-element.94), channel_id=1, source_target_pairs={{0,6},{2,0},{4,2},{6,4},{1,7},{3,1},{5,3},{7,5},{8,14},{10,8},{12,... | collective-permute-start | bytes 786440 | tf_op jit(solution)/shard_map/ppermute | solution.py:34
  (10 other events, 32.9 us)
Sparse Core Ops, SparseCore 0:
  17.7 46.5 all-gather.4
  67.4 93.3 all-gather.6

commit v17 on v12

--- a/solution.py
+++ b/solution.py
@@ -270,7 +270,7 @@
 def data_kernel(q_ref, part_ref, out_ref, f_ref, lane_ref):
     f_ref[...] = -LOG2N - merged(part_ref)
     row = data_row(q_ref, f_ref, lane_ref)
-    out_ref[...] = jnp.broadcast_to(two_rows(row)[None], (Z, 8, 128))
+    out_ref[...] = jnp.broadcast_to(two_rows(row)[None, 0:2], (Z, 2, 128))
 
 
 def data_row(q_ref, f_ref, lane_ref):
@@ -291,7 +291,7 @@
 def data_lse(q, parts):
     return pl.pallas_call(
         data_kernel,
-        out_shape=(jax.ShapeDtypeStruct((Z, 8, 128), F32), jax.ShapeDtypeStruct((CHUNKS, 128), F32)),
+        out_shape=(jax.ShapeDtypeStruct((Z, 2, 128), F32), jax.ShapeDtypeStruct((CHUNKS, 128), F32)),
         in_specs=[VMEM] * 2,
         out_specs=(VMEM, VMEM),
         scratch_shapes=[pltpu.VMEM((QUARTER, 128), F32)],

time: 195 us -> 195 us (level)
  no operation moved by 1% of the time
where the time goes in v17:
time: 195 us
  blocking collectives  63.6 us (33%)
  waiting for transfers between devices  49.9 us (26%)
  starting transfers between devices  35.4 us (18%)
  Pallas kernels  17.9 us (9%)
  between operations  14.2 us (7%)
  local copies, waits for them, and re-layouts  11.2 us (6%)
  other arithmetic  2.39 us (1%)
    all_to_all x3, blocking collectives, body(): parts = lax.all_to_all(rows, ('x', 'y', 'core'), 0, 0)  44.1 us
    ppermute x25, waiting for transfers between devices, shift(): return lax.ppermute(x, axis, [(j, (j + by) % n) for j in range(n)])  41.7 us
    ppermute x25, starting transfers between devices, shift(): return lax.ppermute(x, axis, [(j, (j + by) % n) for j in range(n)])  31.5 us
    all_to_all x2, blocking collectives, body(): columns = lax.all_to_all(columns, 'z', 0, 0)  19.5 us
    unnamed x12, local copies, waits for them, and re-layouts  10.1 us
    all_gather x1, waiting for transfers between devices, body(): lax.all_gather(swapped, ('z', 'core')).reshape(Y, C, C, X, QUARTER, SLICE)  8.12 us
    pallas_call x3, Pallas kernels, transport(): pl.pallas_call(functools.partial(transport_kernel, pieces), out_shape=kin...  4.34 us
  transfers between devices with their start and end apart: 28, of which 19 were waited for; matrix products, arithmetic and copies ran while one was open for 1% of the time, Pallas kernels for 7%

profile of v17, /device:TPU:1, one launch (start us, length us, event | category | flops | bytes accessed | tf_op | source)
XLA Modules:
  0.0 194.5 jit_solution(2191095643850649937)
XLA Ops:
  8.8 2.1 %collective-permute-start = (bf16[256,128]{1,0:T(8,128)(2,1)S(1)}, bf16[256,128]{1,0:T(8,128)(2,1)S(1)}, u32[]{:S(2)}, u32[]{:S(2)}) collective-permute-start(bf16[256,128]{1,0:T(8,128)(2,1)S(1)} %get-tuple-element.50), channel_id=1, source_target_pairs={{0,8},{8,16},{16,24},{24,0},{1,9},{9,17},{17,25},{25,1},{2,10},{10... | collective-permute-start | bytes 196616 | tf_op jit(solution)/shard_map/ppermute | solution.py:34
  10.9 2.5 %collective-permute-start.1 = (bf16[256,128]{1,0:T(8,128)(2,1)S(1)}, bf16[256,128]{1,0:T(8,128)(2,1)S(1)}, u32[]{:S(2)}, u32[]{:S(2)}) collective-permute-start(bf16[256,128]{1,0:T(8,128)(2,1)S(1)} %get-tuple-element.51), channel_id=1, source_target_pairs={{0,16},{8,24},{16,0},{24,8},{1,17},{9,25},{17,1},{25,9},{2,18},{10... | collective-permute-start | bytes 196616 | tf_op jit(solution)/shard_map/ppermute | solution.py:34
  18.6 3.2 %collective-permute-start.8 = (bf16[128,512]{1,0:T(8,128)(2,1)S(1)}, bf16[128,512]{1,0:T(8,128)(2,1)S(1)}, u32[]{:S(2)}, u32[]{:S(2)}) collective-permute-start(bf16[128,512]{1,0:T(8,128)(2,1)S(1)} %get-tuple-element.59), channel_id=1, source_target_pairs={{0,4},{2,6},{4,0},{6,2},{1,5},{3,7},{5,1},{7,3},{8,12},{10,14},{12... | collective-permute-start | bytes 393224 | tf_op jit(solution)/shard_map/ppermute | solution.py:34
  30.1 2.0 %collective-permute-done.3 = bf16[128,512]{1,0:T(8,128)(2,1)S(1)} collective-permute-done((bf16[128,512]{1,0:T(8,128)(2,1)S(1)}, bf16[128,512]{1,0:T(8,128)(2,1)S(1)}, u32[]{:S(2)}, u32[]{:S(2)}) %collective-permute-start.3) | collective-permute-done | bytes 131104 | tf_op jit(solution)/shard_map/ppermute | solution.py:34
  35.4 7.1 %collective-permute-done.12.refs_7_ = bf16[4,128,512]{2,1,0:T(8,128)(2,1)S(1)} collective-permute-done((bf16[4,128,512]{2,1,0:T(8,128)(2,1)S(1)}, bf16[4,128,512]{2,1,0:T(8,128)(2,1)S(1)}, u32[]{:S(2)}, u32[]{:S(2)}) %collective-permute-start.12) | collective-permute-done | bytes 524320 | tf_op jit(solution)/shard_map/ppermute | solution.py:34
  44.3 2.3 %collective-permute-start.16 = (bf16[2,128,512]{2,1,0:T(8,128)(2,1)S(1)}, bf16[2,128,512]{2,1,0:T(8,128)(2,1)S(1)}, u32[]{:S(2)}, u32[]{:S(2)}) collective-permute-start(bf16[2,128,512]{2,1,0:T(8,128)(2,1)S(1)} %slice.23), channel_id=1, source_target_pairs={{0,24},{8,0},{16,8},{24,16},{1,25},{9,1},{17,9},{25,17},{2,26},{10... | collective-permute-start | bytes 786440 | tf_op jit(solution)/shard_map/ppermute | solution.py:34
  50.0 3.4 %collective-permute-done.15.refs_8_ = bf16[2,128,512]{2,1,0:T(8,128)(2,1)S(1)} collective-permute-done((bf16[2,128,512]{2,1,0:T(8,128)(2,1)S(1)}, bf16[2,128,512]{2,1,0:T(8,128)(2,1)S(1)}, u32[]{:S(2)}, u32[]{:S(2)}) %collective-permute-start.15) | collective-permute-done | bytes 262176 | tf_op jit(solution)/shard_map/ppermute | solution.py:34
  54.1 2.0 %copy-done.2 = bf16[1024,2048]{1,0:T(8,128)(2,1)} copy-done((bf16[1024,2048]{1,0:T(8,128)(2,1)}, bf16[1024,2048]{1,0:T(8,128)(2,1)S(1)}, u32[]{:S(2)}) %copy-start.2) | copy-done | bytes 4194328
  56.1 8.1 %all-gather.5.cloned.1.call-done = bf16[64,256,128]{2,1,0:T(8,128)(2,1)} async-done(((bf16[4,256,128]{2,1,0:T(8,128)(2,1)}), bf16[64,256,128]{2,1,0:T(8,128)(2,1)}) %all-gather.5.cloned.1.call-update) | async-done | bytes 4194320 | tf_op jit(solution)/shard_map/all_gather | solution.py:398
  64.3 3.0 %pick.1.data_ref = bf16[4,2,4,256,128]{4,3,2,1,0:T(8,128)(2,1)} custom-call(s32[4]{0:T(128)S(1)} %pad_add_fusion.place, bf16[4,2,2,4,256,128]{5,4,3,2,1,0:T(8,128)(2,1)} %bitcast.32), custom_call_target="tpu_custom_call" | custom-call | tf_op jit(solution)/shard_map/pick/pallas_call | solution.py:145
  68.8 2.2 %copy-done.3 = bf16[1024,2048]{1,0:T(8,128)(2,1)S(1)} copy-done((bf16[1024,2048]{1,0:T(8,128)(2,1)S(1)}, bf16[1024,2048]{1,0:T(8,128)(2,1)}, u32[]{:S(2)}) %copy-start.3) | copy-done | bytes 4194328
  76.3 16.4 %all_to_all.30.part_ref = f32[32,8,128]{2,1,0:T(8,128)S(1)} all-to-all(f32[32,8,128]{2,1,0:T(8,128)S(1)} %get-tuple-element.75), channel_id=1, replica_groups=mesh['z'=8,'x'=4,'y'=4,'core'=2] {'x','y','core'}, dimensions={0} | all-to-all | bytes 262144 | tf_op jit(solution)/shard_map/all_to_all | solution.py:408
  93.5 10.6 %all_to_all.31.part_ref = f32[8,2,128]{2,1,0:T(2,128)S(1)} all-to-all(f32[8,2,128]{2,1,0:T(2,128)S(1)} %get-tuple-element.76), channel_id=1, replica_groups=mesh['z'=8,'x'=4,'y'=4,'core'=2] {'z'}, dimensions={0} | all-to-all | bytes 16384 | tf_op jit(solution)/shard_map/all_to_all | solution.py:411
  104.5 14.0 %all_to_all.32.part_ref = f32[32,8,128]{2,1,0:T(8,128)S(1)} all-to-all(f32[32,8,128]{2,1,0:T(8,128)S(1)} %noise_lse.2), channel_id=1, replica_groups=mesh['z'=8,'x'=4,'y'=4,'core'=2] {'x','y','core'}, dimensions={0} | all-to-all | bytes 262144 | tf_op jit(solution)/shard_map/all_to_all | solution.py:408
  119.3 8.9 %all_to_all.33.part_ref = f32[8,2,128]{2,1,0:T(2,128)S(1)} all-to-all(f32[8,2,128]{2,1,0:T(2,128)S(1)} %get-tuple-element.77), channel_id=1, replica_groups=mesh['z'=8,'x'=4,'y'=4,'core'=2] {'z'}, dimensions={0} | all-to-all | bytes 16384 | tf_op jit(solution)/shard_map/all_to_all | solution.py:411
  128.6 13.7 %all_to_all.34.part_ref = f32[32,8,128]{2,1,0:T(8,128)S(1)} all-to-all(f32[32,8,128]{2,1,0:T(8,128)S(1)} %noise_lse.3), channel_id=1, replica_groups=mesh['z'=8,'x'=4,'y'=4,'core'=2] {'x','y','core'}, dimensions={0} | all-to-all | bytes 262144 | tf_op jit(solution)/shard_map/all_to_all | solution.py:408
  143.9 3.9 %all-to-all-start.5 = ((f32[32,8,128]{2,1,0:T(8,128)}), f32[32,8,128]{2,1,0:T(8,128)S(1)}, u32[]{:S(2)}, u32[]{:S(2)}) async-start(f32[32,8,128]{2,1,0:T(8,128)} %get-tuple-element.81), calls=%async_computation.5 | async-start | bytes 262144 | tf_op jit(solution)/shard_map/all_to_all | solution.py:414
  148.9 2.4 %collective-permute-start.19 = (bf16[256,256]{1,0:T(8,128)(2,1)S(1)}, bf16[256,256]{1,0:T(8,128)(2,1)S(1)}, u32[]{:S(2)}, u32[]{:S(2)}) collective-permute-start(bf16[256,256]{1,0:T(8,128)(2,1)S(1)} %get-tuple-element.84), channel_id=1, source_target_pairs={{0,16},{8,24},{16,0},{24,8},{1,17},{9,25},{17,1},{25,9},{2,18},{10... | collective-permute-start | bytes 393224 | tf_op jit(solution)/shard_map/ppermute | solution.py:34
  152.5 6.1 %collective-permute-done.18.refs_1_ = bf16[256,256]{1,0:T(8,128)(2,1)S(1)} collective-permute-done((bf16[256,256]{1,0:T(8,128)(2,1)S(1)}, bf16[256,256]{1,0:T(8,128)(2,1)S(1)}, u32[]{:S(2)}, u32[]{:S(2)}) %collective-permute-start.18) | collective-permute-done | bytes 131104 | tf_op jit(solution)/shard_map/ppermute | solution.py:34
  158.6 4.6 %collective-permute-done.19.refs_2_ = bf16[256,256]{1,0:T(8,128)(2,1)S(1)} collective-permute-done((bf16[256,256]{1,0:T(8,128)(2,1)S(1)}, bf16[256,256]{1,0:T(8,128)(2,1)S(1)}, u32[]{:S(2)}, u32[]{:S(2)}) %collective-permute-start.19) | collective-permute-done | bytes 131104 | tf_op jit(solution)/shard_map/ppermute | solution.py:34
  166.7 3.4 %copy-done = bf16[16,2,4,256,128]{4,3,2,1,0:T(8,128)(2,1)S(1)} copy-done((bf16[16,2,4,256,128]{4,3,2,1,0:T(8,128)(2,1)S(1)}, bf16[16,2,4,256,128]{4,3,2,1,0:T(8,128)(2,1)}, u32[]{:S(2)}) %copy-start) | copy-done | bytes 8388632
  171.4 3.0 %collective-permute-start.22 = (bf16[256,512]{1,0:T(8,128)(2,1)S(1)}, bf16[256,512]{1,0:T(8,128)(2,1)S(1)}, u32[]{:S(2)}, u32[]{:S(2)}) collective-permute-start(bf16[256,512]{1,0:T(8,128)(2,1)S(1)} %get-tuple-element.92), channel_id=1, source_target_pairs={{0,4},{2,6},{4,0},{6,2},{1,5},{3,7},{5,1},{7,3},{8,12},{10,14},{12... | collective-permute-start | bytes 786440 | tf_op jit(solution)/shard_map/ppermute | solution.py:34
  176.6 2.4 %collective-permute-start.24 = (bf16[256,512]{1,0:T(8,128)(2,1)S(1)}, bf16[256,512]{1,0:T(8,128)(2,1)S(1)}, u32[]{:S(2)}, u32[]{:S(2)}) collective-permute-start(bf16[256,512]{1,0:T(8,128)(2,1)S(1)} %get-tuple-element.94), channel_id=1, source_target_pairs={{0,6},{2,0},{4,2},{6,4},{1,7},{3,1},{5,3},{7,5},{8,14},{10,8},{12,... | collective-permute-start | bytes 786440 | tf_op jit(solution)/shard_map/ppermute | solution.py:34
  180.8 6.0 %collective-permute-done.23 = bf16[256,512]{1,0:T(8,128)(2,1)S(1)} collective-permute-done((bf16[256,512]{1,0:T(8,128)(2,1)S(1)}, bf16[256,512]{1,0:T(8,128)(2,1)S(1)}, u32[]{:S(2)}, u32[]{:S(2)}) %collective-permute-start.23) | collective-permute-done | bytes 262176 | tf_op jit(solution)/shard_map/ppermute | solution.py:34
  (78 shorter events, 47.0 us)
Async XLA Ops:
  7.2 57.1 %all-gather.5.cloned.1.call-start = ((), (), s32[]{:S(2)}) async-start(), calls=%async_computation.6 | async-start | bytes 4456448 | tf_op jit(solution)/shard_map/all_gather | solution.py:398
  8.8 5.7 %collective-permute-start = (bf16[256,128]{1,0:T(8,128)(2,1)S(1)}, bf16[256,128]{1,0:T(8,128)(2,1)S(1)}, u32[]{:S(2)}, u32[]{:S(2)}) collective-permute-start(bf16[256,128]{1,0:T(8,128)(2,1)S(1)} %get-tuple-element.50), channel_id=1, source_target_pairs={{0,8},{8,16},{16,24},{24,0},{1,9},{9,17},{17,25},{25,1},{2,10},{10... | collective-permute-start | bytes 196616 | tf_op jit(solution)/shard_map/ppermute | solution.py:34
  10.9 5.1 %collective-permute-start.1 = (bf16[256,128]{1,0:T(8,128)(2,1)S(1)}, bf16[256,128]{1,0:T(8,128)(2,1)S(1)}, u32[]{:S(2)}, u32[]{:S(2)}) collective-permute-start(bf16[256,128]{1,0:T(8,128)(2,1)S(1)} %get-tuple-element.51), channel_id=1, source_target_pairs={{0,16},{8,24},{16,0},{24,8},{1,17},{9,25},{17,1},{25,9},{2,18},{10... | collective-permute-start | bytes 196616 | tf_op jit(solution)/shard_map/ppermute | solution.py:34
  17.6 147.6 %all-gather.7.cloned.1.call-start = ((), (), s32[]{:S(2)}) async-start(), calls=%async_computation.7 | async-start | bytes 10485760 | tf_op jit(solution)/shard_map/all_gather | solution.py:401
  18.6 6.9 %collective-permute-start.8 = (bf16[128,512]{1,0:T(8,128)(2,1)S(1)}, bf16[128,512]{1,0:T(8,128)(2,1)S(1)}, u32[]{:S(2)}, u32[]{:S(2)}) collective-permute-start(bf16[128,512]{1,0:T(8,128)(2,1)S(1)} %get-tuple-element.59), channel_id=1, source_target_pairs={{0,4},{2,6},{4,0},{6,2},{1,5},{3,7},{5,1},{7,3},{8,12},{10,14},{12... | collective-permute-start | bytes 393224 | tf_op jit(solution)/shard_map/ppermute | solution.py:34
  22.6 6.0 %collective-permute-start.6 = (bf16[128,512]{1,0:T(8,128)(2,1)S(1)}, bf16[128,512]{1,0:T(8,128)(2,1)S(1)}, u32[]{:S(2)}, u32[]{:S(2)}) collective-permute-start(bf16[128,512]{1,0:T(8,128)(2,1)S(1)} %get-tuple-element.59), channel_id=1, source_target_pairs={{0,2},{2,4},{4,6},{6,0},{1,3},{3,5},{5,7},{7,1},{8,10},{10,12},{12... | collective-permute-start | bytes 393224 | tf_op jit(solution)/shard_map/ppermute | solution.py:34
  23.3 5.3 %collective-permute-start.5 = (bf16[128,512]{1,0:T(8,128)(2,1)S(1)}, bf16[128,512]{1,0:T(8,128)(2,1)S(1)}, u32[]{:S(2)}, u32[]{:S(2)}) collective-permute-start(bf16[128,512]{1,0:T(8,128)(2,1)S(1)} %get-tuple-element.55), channel_id=1, source_target_pairs={{0,16},{8,24},{16,0},{24,8},{1,17},{9,25},{17,1},{25,9},{2,18},{10... | collective-permute-start | bytes 393224 | tf_op jit(solution)/shard_map/ppermute | solution.py:34
  24.3 5.7 %collective-permute-start.4 = (bf16[128,512]{1,0:T(8,128)(2,1)S(1)}, bf16[128,512]{1,0:T(8,128)(2,1)S(1)}, u32[]{:S(2)}, u32[]{:S(2)}) collective-permute-start(bf16[128,512]{1,0:T(8,128)(2,1)S(1)} %get-tuple-element.55), channel_id=1, source_target_pairs={{0,24},{8,0},{16,8},{24,16},{1,25},{9,1},{17,9},{25,17},{2,26},{10... | collective-permute-start | bytes 393224 | tf_op jit(solution)/shard_map/ppermute | solution.py:34
  25.5 6.7 %collective-permute-start.3 = (bf16[128,512]{1,0:T(8,128)(2,1)S(1)}, bf16[128,512]{1,0:T(8,128)(2,1)S(1)}, u32[]{:S(2)}, u32[]{:S(2)}) collective-permute-start(bf16[128,512]{1,0:T(8,128)(2,1)S(1)} %get-tuple-element.55), channel_id=1, source_target_pairs={{0,8},{8,16},{16,24},{24,0},{1,9},{9,17},{17,25},{25,1},{2,10},{10... | collective-permute-start | bytes 393224 | tf_op jit(solution)/shard_map/ppermute | solution.py:34
  32.2 10.3 %collective-permute-start.12 = (bf16[4,128,512]{2,1,0:T(8,128)(2,1)S(1)}, bf16[4,128,512]{2,1,0:T(8,128)(2,1)S(1)}, u32[]{:S(2)}, u32[]{:S(2)}) collective-permute-start(bf16[4,128,512]{2,1,0:T(8,128)(2,1)S(1)} %pad_maximum_fusion.1.refs_5_), channel_id=1, source_target_pairs={{0,24},{8,0},{16,8},{24,16},{1,25},{9,1},{17,9},{25,17},{2,26},{10... | collective-permute-start | bytes 1572872 | tf_op jit(solution)/shard_map/ppermute | solution.py:34
  32.4 10.4 %collective-permute-start.11 = (bf16[4,128,512]{2,1,0:T(8,128)(2,1)S(1)}, bf16[4,128,512]{2,1,0:T(8,128)(2,1)S(1)}, u32[]{:S(2)}, u32[]{:S(2)}) collective-permute-start(bf16[4,128,512]{2,1,0:T(8,128)(2,1)S(1)} %pad_maximum_fusion.1.refs_5_), channel_id=1, source_target_pairs={{0,8},{8,16},{16,24},{24,0},{1,9},{9,17},{17,25},{25,1},{2,10},{10... | collective-permute-start | bytes 1572872 | tf_op jit(solution)/shard_map/ppermute | solution.py:34
  33.8 9.7 %collective-permute-start.10 = (bf16[4,128,512]{2,1,0:T(8,128)(2,1)S(1)}, bf16[4,128,512]{2,1,0:T(8,128)(2,1)S(1)}, u32[]{:S(2)}, u32[]{:S(2)}) collective-permute-start(bf16[4,128,512]{2,1,0:T(8,128)(2,1)S(1)} %pad_maximum_fusion.refs_0_), channel_id=1, source_target_pairs={{0,6},{2,0},{4,2},{6,4},{1,7},{3,1},{5,3},{7,5},{8,14},{10,8},{12,... | collective-permute-start | bytes 1572872 | tf_op jit(solution)/shard_map/ppermute | solution.py:34
  34.7 9.5 %collective-permute-start.9 = (bf16[4,128,512]{2,1,0:T(8,128)(2,1)S(1)}, bf16[4,128,512]{2,1,0:T(8,128)(2,1)S(1)}, u32[]{:S(2)}, u32[]{:S(2)}) collective-permute-start(bf16[4,128,512]{2,1,0:T(8,128)(2,1)S(1)} %pad_maximum_fusion.refs_0_), channel_id=1, source_target_pairs={{0,2},{2,4},{4,6},{6,0},{1,3},{3,5},{5,7},{7,1},{8,10},{10,12},{12... | collective-permute-start | bytes 1572872 | tf_op jit(solution)/shard_map/ppermute | solution.py:34
  44.3 5.7 %collective-permute-start.16 = (bf16[2,128,512]{2,1,0:T(8,128)(2,1)S(1)}, bf16[2,128,512]{2,1,0:T(8,128)(2,1)S(1)}, u32[]{:S(2)}, u32[]{:S(2)}) collective-permute-start(bf16[2,128,512]{2,1,0:T(8,128)(2,1)S(1)} %slice.23), channel_id=1, source_target_pairs={{0,24},{8,0},{16,8},{24,16},{1,25},{9,1},{17,9},{25,17},{2,26},{10... | collective-permute-start | bytes 786440 | tf_op jit(solution)/shard_map/ppermute | solution.py:34
  46.6 6.8 %collective-permute-start.15 = (bf16[2,128,512]{2,1,0:T(8,128)(2,1)S(1)}, bf16[2,128,512]{2,1,0:T(8,128)(2,1)S(1)}, u32[]{:S(2)}, u32[]{:S(2)}) collective-permute-start(bf16[2,128,512]{2,1,0:T(8,128)(2,1)S(1)} %slice.22), channel_id=1, source_target_pairs={{0,8},{8,16},{16,24},{24,0},{1,9},{9,17},{17,25},{25,1},{2,10},{10... | collective-permute-start | bytes 786440 | tf_op jit(solution)/shard_map/ppermute | solution.py:34
  46.6 6.8 %collective-permute-start.14 = (bf16[2,128,512]{2,1,0:T(8,128)(2,1)S(1)}, bf16[2,128,512]{2,1,0:T(8,128)(2,1)S(1)}, u32[]{:S(2)}, u32[]{:S(2)}) collective-permute-start(bf16[2,128,512]{2,1,0:T(8,128)(2,1)S(1)} %slice.21), channel_id=1, source_target_pairs={{0,6},{2,0},{4,2},{6,4},{1,7},{3,1},{5,3},{7,5},{8,14},{10,8},{12,... | collective-permute-start | bytes 786440 | tf_op jit(solution)/shard_map/ppermute | solution.py:34
  46.8 6.8 %collective-permute-start.13 = (bf16[2,128,512]{2,1,0:T(8,128)(2,1)S(1)}, bf16[2,128,512]{2,1,0:T(8,128)(2,1)S(1)}, u32[]{:S(2)}, u32[]{:S(2)}) collective-permute-start(bf16[2,128,512]{2,1,0:T(8,128)(2,1)S(1)} %slice.20), channel_id=1, source_target_pairs={{0,2},{2,4},{4,6},{6,0},{1,3},{3,5},{5,7},{7,1},{8,10},{10,12},{12... | collective-permute-start | bytes 786440 | tf_op jit(solution)/shard_map/ppermute | solution.py:34
  143.9 19.3 %all-to-all-start.5 = ((f32[32,8,128]{2,1,0:T(8,128)}), f32[32,8,128]{2,1,0:T(8,128)S(1)}, u32[]{:S(2)}, u32[]{:S(2)}) async-start(f32[32,8,128]{2,1,0:T(8,128)} %get-tuple-element.81), calls=%async_computation.5 | async-start | bytes 262144 | tf_op jit(solution)/shard_map/all_to_all | solution.py:414
  147.7 10.9 %collective-permute-start.18 = (bf16[256,256]{1,0:T(8,128)(2,1)S(1)}, bf16[256,256]{1,0:T(8,128)(2,1)S(1)}, u32[]{:S(2)}, u32[]{:S(2)}) collective-permute-start(bf16[256,256]{1,0:T(8,128)(2,1)S(1)} %get-tuple-element.83), channel_id=1, source_target_pairs={{0,8},{8,16},{16,24},{24,0},{1,9},{9,17},{17,25},{25,1},{2,10},{10... | collective-permute-start | bytes 393224 | tf_op jit(solution)/shard_map/ppermute | solution.py:34
  148.9 14.3 %collective-permute-start.19 = (bf16[256,256]{1,0:T(8,128)(2,1)S(1)}, bf16[256,256]{1,0:T(8,128)(2,1)S(1)}, u32[]{:S(2)}, u32[]{:S(2)}) collective-permute-start(bf16[256,256]{1,0:T(8,128)(2,1)S(1)} %get-tuple-element.84), channel_id=1, source_target_pairs={{0,16},{8,24},{16,0},{24,8},{1,17},{9,25},{17,1},{25,9},{2,18},{10... | collective-permute-start | bytes 393224 | tf_op jit(solution)/shard_map/ppermute | solution.py:34
  151.3 11.9 %collective-permute-start.20 = (bf16[256,256]{1,0:T(8,128)(2,1)S(1)}, bf16[256,256]{1,0:T(8,128)(2,1)S(1)}, u32[]{:S(2)}, u32[]{:S(2)}) collective-permute-start(bf16[256,256]{1,0:T(8,128)(2,1)S(1)} %get-tuple-element.85), channel_id=1, source_target_pairs={{0,24},{8,0},{16,8},{24,16},{1,25},{9,1},{17,9},{25,17},{2,26},{10... | collective-permute-start | bytes 393224 | tf_op jit(solution)/shard_map/ppermute | solution.py:34
  171.4 9.4 %collective-permute-start.22 = (bf16[256,512]{1,0:T(8,128)(2,1)S(1)}, bf16[256,512]{1,0:T(8,128)(2,1)S(1)}, u32[]{:S(2)}, u32[]{:S(2)}) collective-permute-start(bf16[256,512]{1,0:T(8,128)(2,1)S(1)} %get-tuple-element.92), channel_id=1, source_target_pairs={{0,4},{2,6},{4,0},{6,2},{1,5},{3,7},{5,1},{7,3},{8,12},{10,14},{12... | collective-permute-start | bytes 786440 | tf_op jit(solution)/shard_map/ppermute | solution.py:34
  176.2 10.6 %collective-permute-start.23 = (bf16[256,512]{1,0:T(8,128)(2,1)S(1)}, bf16[256,512]{1,0:T(8,128)(2,1)S(1)}, u32[]{:S(2)}, u32[]{:S(2)}) collective-permute-start(bf16[256,512]{1,0:T(8,128)(2,1)S(1)} %get-tuple-element.93), channel_id=1, source_target_pairs={{0,2},{2,4},{4,6},{6,0},{1,3},{3,5},{5,7},{7,1},{8,10},{10,12},{12... | collective-permute-start | bytes 786440 | tf_op jit(solution)/shard_map/ppermute | solution.py:34
  176.6 10.2 %collective-permute-start.24 = (bf16[256,512]{1,0:T(8,128)(2,1)S(1)}, bf16[256,512]{1,0:T(8,128)(2,1)S(1)}, u32[]{:S(2)}, u32[]{:S(2)}) collective-permute-start(bf16[256,512]{1,0:T(8,128)(2,1)S(1)} %get-tuple-element.94), channel_id=1, source_target_pairs={{0,6},{2,0},{4,2},{6,4},{1,7},{3,1},{5,3},{7,5},{8,14},{10,8},{12,... | collective-permute-start | bytes 786440 | tf_op jit(solution)/shard_map/ppermute | solution.py:34
  (10 other events, 30.9 us)
Sparse Core Ops, SparseCore 0:
  17.7 46.5 all-gather.4
  67.4 93.9 all-gather.6
